TPU v7x, 32 devices: a whole 2x2x4 slice. The times are simulated.
32 devices in a mesh: prompt: 4 (over y, x), tile: 8 (over z, core).
Axes of the slice: x: 2, y: 2, z: 4, core: 2. Of those that a mesh axis runs over, the one named last changes fastest.
Arguments:
- latent: bfloat16 [128, 160, 16], P(('prompt', 'tile')), parts along dimension 0, may hold values from -6 to 6
- cached_latent: bfloat16 [2, 128, 160, 16], P(None, ('prompt', 'tile')), parts along dimension 1, may hold values from -6 to 6
- cached_features: bfloat16 [2, 128, 160, 384], P(None, ('prompt', 'tile')), parts along dimension 1, may hold values from -5 to 5
- reward_grad: bfloat16 [256, 320, 192], P(('prompt', 'tile')), parts along dimension 0, may hold values from -6 to 6
- conv_in_weight: bfloat16 [3, 3, 3, 16, 384], replicated, may hold values from -0.3125 to 0.3125
- conv_mid_weight: bfloat16 [3, 3, 3, 384, 384], replicated, may hold values from -0.0625 to 0.0625
- conv_up_weight: bfloat16 [3, 3, 384, 192], replicated, may hold values from -0.109375 to 0.109375
- norm_gain: float32 [384], replicated, may hold values from 0.5 to 1.5
- out_gain: float32 [192], replicated, may hold values from 0.5 to 1.5
- shard_order: int32 [32], P('prompt'), parts along dimension 0, may hold values from 0 to 7, each once
Outputs:
- token_grad: float32 [5120, 64], P(('prompt', 'tile')), parts along dimension 0
There are 4 independent parts, one for each index of `prompt`. A program takes and returns all parts, laid end to end along the dimension named above; an argument that names none is the same for every part. Nothing has to cross between parts.
Inputs may be any that keep to these rules, and one draw needn't show every extreme that they name: shard_order is a permutation: each of 0 to 7 once.
All inputs are finite; a program needn't handle non-finite values.
Results may differ from a plain program's by a relative error of at most 0.0095.
Values may be sent and summed in bfloat16 or wider, within the bound.
No kernel may reach another device: no remote copies, remote signals or barrier semaphores. Data moves between devices by JAX's collectives and lax.ppermute only.
A program may use at most 64 MiB of HBM per device.

v0:
```python
import jax
import jax.numpy as jnp
from jax import lax
from jax.experimental import pallas as pl
from jax.experimental.pallas import tpu as pltpu
from jax.sharding import PartitionSpec as P

EPS = 1e-06
F32 = jnp.float32
BF16 = jnp.bfloat16
VM = pl.BlockSpec(memory_space=pltpu.VMEM)
SM = pl.BlockSpec(memory_space=pltpu.SMEM)


def call(body, outs, n_smem, n_vmem, scratch, flops, limit):
    specs = [SM] * n_smem + [VM] * n_vmem
    return pl.pallas_call(
        body,
        out_shape=[jax.ShapeDtypeStruct(s, d) for s, d in outs],
        in_specs=specs,
        out_specs=[VM] * len(outs),
        scratch_shapes=scratch,
        cost_estimate=pl.CostEstimate(flops=int(flops), bytes_accessed=2**20, transcendentals=0),
        compiler_params=pltpu.CompilerParams(vmem_limit_bytes=limit << 20),
    )


def mm(a, b):
    return jnp.dot(a, b, preferred_element_type=F32)


def mm_t(a, b):
    return lax.dot_general(a, b, (((1,), (1,)), ((), ())), preferred_element_type=F32)


def flag(info, k):
    return info[k].astype(F32)


def col_index(cols, lanes):
    return lax.broadcasted_iota(jnp.int32, (cols, lanes), 0)


def from_left(x):
    col = col_index(*x.shape)
    return jnp.where(col == 0, 0.0, pltpu.roll(x, 1, 0))


def from_right(x):
    cols = x.shape[0]
    col = col_index(*x.shape)
    return jnp.where(col == cols - 1, 0.0, pltpu.roll(x, cols - 1, 0))


def pack_body(rows, cols, o, chan):
    half = o - 128

    def body(info, reward, latent, cached, own, send_even, send_odd):
        x_index = lax.broadcasted_iota(jnp.int32, (cols, 2 * cols), 1)
        w_index = lax.broadcasted_iota(jnp.int32, (cols, 2 * cols), 0)
        pick = [(x_index == 2 * w_index + b).astype(F32).astype(BF16) for b in (0, 1)]
        zeros = jnp.zeros((128 - half, 2 * cols), BF16)
        for f in range(2 * rows):
            r = reward[f]
            first, rest = r[:128], r[128:]
            low = jnp.concatenate([first, rest, zeros], axis=0)
            high = jnp.concatenate([first, zeros, rest], axis=0)
            sides = (low, high) if f % 2 else (high, low)
            d0, d1 = mm_t(pick[0], sides[0]), mm_t(pick[1], sides[1])
            own[f, :, 0:128] = d0[:, :128].astype(BF16)
            own[f, :, 128:256] = d1[:, :128].astype(BF16)
            own[f, :, 256:384] = (d0[:, 128:] + d1[:, 128:]).astype(BF16)
        base = 3 * cols
        per = chan * rows
        for send, last in ((send_even, 1 - info[0]), (send_odd, info[0])):
            begin = last * (2 * rows - 3)
            for k in range(3):
                send[k * cols : (k + 1) * cols] = own[begin + k]
            for t in range(3):
                src = cached[t] if t < 2 else latent[...]
                lat = src.reshape(per, cols)
                send[base : base + per, t * 128 : t * 128 + 128] = lat[:, :128]
                send[base + per : base + 2 * per, t * 128 : t * 128 + cols - 128] = lat[:, 128:]

    return body


def taps_body(up, fwd, back_odd, back_even):
    def rows_of(q, j):
        parts = ((2,), (1, 2), (0, 1), (0,))[q]
        total = up[parts[0], j].astype(F32)
        for i in parts[1:]:
            total = total + up[i, j].astype(F32)
        return total

    for q in range(4):
        c0, c1, c2 = (rows_of(q, j) for j in range(3))
        tap = [t.astype(BF16) for t in (c2, c1 + c2, c0 + c1, c0)]
        for b, order in ((0, (3, 1)), (1, (2, 0))):
            place = q if b == 0 else (1, 0, 3, 2)[q]
            for side, p in enumerate(order):
                lanes = slice(side * 384, side * 384 + 384)
                fwd[b, q * 128 : q * 128 + 128, lanes] = tap[p][:128]
                fwd[b, 512 + place * 64 : 576 + place * 64, lanes] = tap[p][128:]
        target, side = ((back_odd, 1), (back_even, 0), (back_odd, 0), (back_even, 1))[q]
        lanes = slice(side * 384, side * 384 + 384)
        for block, (p0, p1) in enumerate(((1, 2), (3, 0))):
            base = block * 384
            target[base : base + 128, lanes] = tap[p0][:128]
            target[base + 128 : base + 256, lanes] = tap[p1][:128]
            low, high = (p0, p1) if q % 2 == 0 else (p1, p0)
            target[base + 256 : base + 320, lanes] = tap[low][128:]
            target[base + 320 : base + 384, lanes] = tap[high][128:]


def cached_body(rows, cols):
    size = rows * cols

    def body(info, features, mid, acc, send_even, send_odd, wide):
        for t in range(2):
            for r in range(rows):
                at = slice(r * cols, (r + 1) * cols)
                x = features[t, r]
                x32 = x.astype(F32)
                base = t * 1152
                wide[at, base : base + 384] = from_left(x32).astype(BF16)
                wide[at, base + 384 : base + 768] = x
                wide[at, base + 768 : base + 1152] = from_right(x32).astype(BF16)
        lhs = wide[...]
        kernels = [jnp.concatenate([mid[0, i], mid[1, i]], axis=0) for i in range(3)]
        pair = mm(lhs, jnp.concatenate([kernels[0], kernels[1]], axis=1))
        zero = jnp.zeros((cols, 384), F32)
        acc[0:cols] = zero
        acc[cols : 2 * cols] = zero
        acc[2 * cols :] = pair[:, :384]
        acc[cols : cols + size] += pair[:, 384:]
        acc[0:size] += mm(lhs, kernels[2])
        for send, last in ((send_even, 1 - info[0]), (send_odd, info[0])):
            send[...] = acc[pl.ds(pl.multiple_of(last * 3 * cols, 3 * cols), 3 * cols)].astype(BF16)

    return body


def current_body(rows, cols, chan):
    per = chan * rows
    base = 3 * cols

    def body(info, latent, cached, got_even, got_odd, w_in, mid, gain, hidden, conv, lat, tall, wide, w_order):
        even = info[0] == 0
        lat[...] = jnp.zeros_like(lat)

        def fill(first_row, got, ok):
            scale = ok.astype(F32)
            for t in range(3):
                x = got[base : base + per, t * 128 : t * 128 + 128].astype(F32) * scale
                y = got[base + per : base + 2 * per, t * 128 : t * 128 + cols - 128].astype(F32) * scale
                for r in range(rows):
                    at = pl.ds((first_row + r) * 3 * chan + t * chan, chan)
                    lat[at, 0:128] = x[r * chan : (r + 1) * chan]
                    lat[at, 128:cols] = y[r * chan : (r + 1) * chan]

        @pl.when(even)
        def _():
            fill(0, got_odd, info[1])
            fill(2 * rows, got_even, info[2])

        @pl.when(jnp.logical_not(even))
        def _():
            fill(0, got_even, info[1])
            fill(2 * rows, got_odd, info[2])

        for t in range(3):
            for r in range(rows):
                at = pl.ds((rows + r) * 3 * chan + t * chan, chan)
                lat[at, 0:cols] = (cached[t, r] if t < 2 else latent[r]).astype(F32)

        for r in range(3 * rows):
            for t in range(3):
                x = lat[pl.ds((r * 3 + t) * chan, chan), :]
                at = (r * 3 + t) * 3 * chan
                tall[at : at + chan] = pltpu.roll(x, 1, 1).astype(BF16)
                tall[at + chan : at + 2 * chan] = x.astype(BF16)
                tall[at + 2 * chan : at + 3 * chan] = pltpu.roll(x, 255, 1).astype(BF16)
        for i in range(3):
            for t in range(3):
                at = (i * 3 + t) * 3 * chan
                w_order[at : at + 3 * chan] = w_in[t, i]

        deep = 27 * chan
        for k in range(rows + 6):
            lhs = tall[k * 9 * chan : k * 9 * chan + deep, 0:cols]
            h = lax.dot_general(lhs, w_order[...], (((0,), (0,)), ((), ())), preferred_element_type=F32)
            h = h.astype(BF16)
            if 1 <= k <= rows + 4:
                hidden[k - 1] = h
            v = h.astype(F32)
            inv = lax.rsqrt(jnp.mean(v * v, axis=1, keepdims=True) + EPS)
            y = v * inv * gain[...]
            act = y * (0.5 * jnp.tanh(0.5 * y) + 0.5)
            if k < 3:
                act = act * flag(info, 1)
            if k >= rows + 3:
                act = act * flag(info, 2)
            at = slice(k * cols, (k + 1) * cols)
            wide[at, 0:384] = from_left(act).astype(BF16)
            wide[at, 384:768] = act.astype(BF16)
            wide[at, 768:1152] = from_right(act).astype(BF16)

        size = rows * cols
        for part in range(2):
            start = part * size
            total = mm(wide[start : start + size], mid[2, 0])
            total += mm(wide[start + cols : start + cols + size], mid[2, 1])
            total += mm(wide[start + 2 * cols : start + 2 * cols + size], mid[2, 2])
            conv[start : start + size] = total

    return body


def pull_scale(y):
    sig = 0.5 * jnp.tanh(0.5 * y) + 0.5
    return sig * (1.0 + y * (1.0 - sig))


def back_body(rows, cols, chan, count, o):
    deep_rows = rows + 4
    size = rows * cols
    width = 2 * cols // count

    def body(
        info, hidden, conv, acc, got_even, got_odd, packed_even, packed_odd, own, fwd, back_odd, back_even, mid, w_in, gain,
        out_gain, payload, reward, edge, p0, p1, g_odd, g_even, wide, lines,
    ):
        even = info[0] == 0
        top, bottom = flag(info, 1), flag(info, 2)

        def take(got, packed, before):
            ok = top if before else bottom
            place = 0 if before else 3
            for k in range(3):
                at = slice(k * cols, (k + 1) * cols)
                edge[(place + k) * cols : (place + k + 1) * cols] = got[at].astype(F32) * ok
                reward[k if before else 2 * rows + 3 + k] = (packed[at].astype(F32) * ok).astype(BF16)

        @pl.when(even)
        def _():
            take(got_odd, packed_odd, True)
            take(got_even, packed_even, False)

        @pl.when(jnp.logical_not(even))
        def _():
            take(got_even, packed_even, True)
            take(got_odd, packed_odd, False)

        reward[3 : 2 * rows + 3] = own[...]

        def row(ref, k):
            return ref[k * cols : (k + 1) * cols]

        state_rows = []
        for k in range(deep_rows):
            x = hidden[k].astype(F32) + row(conv, k)
            if 1 <= k <= rows + 2:
                x = x + row(acc, k - 1)
            if k < 3:
                x = x + row(edge, k)
            if k >= rows + 1:
                x = x + row(edge, k - rows + 2)
            if k < 2:
                x = x * top
            if k >= rows + 2:
                x = x * bottom
            x = x.astype(BF16)
            x32 = x.astype(F32)
            at = slice(k * cols, (k + 1) * cols)
            wide[at, 0:384] = from_left(x32).astype(BF16)
            wide[at, 384:768] = x
            wide[at, 768:1152] = from_right(x32).astype(BF16)

        for part in range(2):
            at = slice(part * size, (part + 1) * size)
            p0[at] = mm_t(wide[at, 0:768], fwd[0])
            p1[at] = mm_t(wide[at, 384:1152], fwd[1])

        lane = lax.broadcasted_iota(jnp.int32, (cols, 128), 1)
        low = lane < 64
        gains = [out_gain[:, 0:128], out_gain[:, 128:256]]

        def pull(v0, v1, vm, r, zero_low):
            mine = low if zero_low else jnp.logical_not(low)
            v0, v1, vm = (v.astype(BF16).astype(F32) for v in (v0, v1, vm))

            def both(a0, a1, am):
                s0 = jnp.sum(a0 + jnp.where(mine, am, 0.0), axis=1, keepdims=True)
                s1 = jnp.sum(a1 + jnp.where(mine, 0.0, am), axis=1, keepdims=True)
                return s0 * (1.0 / o), s1 * (1.0 / o)

            q0, q1 = both(v0 * v0, v1 * v1, vm * vm)
            i0, i1 = lax.rsqrt(q0 + EPS), lax.rsqrt(q1 + EPS)
            im = jnp.where(mine, i0, i1)
            out = []
            for v, i, g, k in ((v0, i0, gains[0], 0), (v1, i1, gains[0], 1), (vm, im, gains[1], 2)):
                s = v * i
                y = s * g
                d = r[:, k * 128 : k * 128 + 128].astype(F32) * pull_scale(y) * g
                out.append((s, d))
            m0, m1 = both(*(s * d for s, d in out))
            mm_ = jnp.where(mine, m0, m1)
            return [i * (d - s * m) for (s, d), i, m in zip(out, (i0, i1, im), (m0, m1, mm_))], mine

        def store(g, target, k):
            (a0, a1, am), mine = g
            at = slice(k * cols, (k + 1) * cols)
            target[at, 0:128] = a0.astype(BF16)
            target[at, 128:256] = a1.astype(BF16)
            target[at, 256:384] = am.astype(BF16)
            target[at, 384:512] = from_right(a0).astype(BF16)
            target[at, 512:640] = from_left(a1).astype(BF16)
            target[at, 640:768] = jnp.where(mine, from_right(am), from_left(am)).astype(BF16)

        fine = rows + 3
        for k in range(fine):
            a, b = slice(k * cols, (k + 1) * cols), slice((k + 1) * cols, (k + 2) * cols)
            v0 = p0[a, 256:384] + p0[b, 0:128]
            v1 = p1[a, 256:384] + p1[b, 0:128]
            vm = jnp.where(low, p0[a, 640:768] + p0[b, 512:640], p1[a, 640:768] + p1[b, 512:640])
            store(pull(v0, v1, vm, reward[2 * k], True), g_odd, k)
            v0 = p0[b, 128:256] + p0[a, 384:512]
            v1 = p1[b, 128:256] + p1[a, 384:512]
            vm = jnp.where(low, p1[b, 512:640] + p1[a, 640:768], p0[b, 512:640] + p0[a, 640:768])
            store(pull(v0, v1, vm, reward[2 * k + 1], False), g_even, k)

        span = fine * cols
        p0[0:span] = mm(g_odd[...], back_odd[...])
        p1[0:span] = mm(g_even[...], back_even[...])
        for k in range(rows + 2):
            a, b = slice(k * cols, (k + 1) * cols), slice((k + 1) * cols, (k + 2) * cols)
            x = p0[b, 0:384] + p0[a, 384:768] + p1[a, 0:384] + p1[b, 384:768]
            if k == 0:
                x = x * top
            if k == rows + 1:
                x = x * bottom
            x = x.astype(BF16)
            x32 = x.astype(F32)
            wide[a, 0:384] = from_right(x32).astype(BF16)
            wide[a, 384:768] = x
            wide[a, 768:1152] = from_left(x32).astype(BF16)

        total = None
        for i in range(3):
            kernel = jnp.concatenate([mid[2, i, j * 384 : (j + 1) * 384] for j in range(3)], axis=1)
            term = mm_t(wide[(2 - i) * cols : (2 - i) * cols + size], kernel)
            total = term if total is None else total + term
        p0[0:size, 0:384] = total
        g = gain[...]
        for k in range(rows):
            at = slice(k * cols, (k + 1) * cols)
            v = hidden[k + 2].astype(F32)
            inv = lax.rsqrt(jnp.mean(v * v, axis=1, keepdims=True) + EPS)
            s = v * inv
            d = p0[at, 0:384] * pull_scale(s * g) * g
            dv = inv * (d - s * jnp.mean(d * s, axis=1, keepdims=True))
            block = wide[(k + 1) * cols : (k + 2) * cols, 384:768].astype(F32)
            g_odd[at, 0:384] = (block + dv).astype(BF16)

        z = mm_t(w_in[...], g_odd[0:size, 0:384])
        place = lax.broadcasted_iota(jnp.int32, (chan, size), 1)
        col = lax.rem(place, cols)
        sums = []
        for i in range(3):
            z0, z1, z2 = (z[(i * 3 + j) * chan : (i * 3 + j + 1) * chan] for j in range(3))
            left = jnp.where(col == cols - 1, 0.0, pltpu.roll(z0, size - 1, 1))
            right = jnp.where(col == 0, 0.0, pltpu.roll(z2, 1, 1))
            sums.append(left + z1 + right)
        inner = sums[1]
        inner = inner + jnp.where(place < size - cols, pltpu.roll(sums[0], size - cols, 1), 0.0)
        inner = inner + jnp.where(place >= cols, pltpu.roll(sums[2], cols, 1), 0.0)
        lines[0:chan] = inner
        lines[chan : 2 * chan] = sums[0]
        lines[2 * chan : 3 * chan] = sums[2]
        per_row = count // 2
        for u in range(count):
            pair, piece = u // per_row, u % per_row
            for a in range(2):
                at = (2 * pair + a) * cols + piece * width
                payload[u, a * chan : (a + 1) * chan] = lines[0:chan, at : at + width].astype(BF16)
            if pair == 0:
                at = (rows - 1) * cols + piece * width
                payload[u, 2 * chan : 3 * chan] = lines[2 * chan : 3 * chan, at : at + width].astype(BF16)
            else:
                at = piece * width
                payload[u, 2 * chan : 3 * chan] = lines[chan : 2 * chan, at : at + width].astype(BF16)

    return body


def place_body(count, chan, width, tokens):
    piece = width // 2

    def body(info, order, got, out):
        pair = info[3]
        w = lax.broadcasted_iota(jnp.int32, (width, tokens), 0)
        pos = lax.broadcasted_iota(jnp.int32, (width, tokens), 1)
        inner, outer = [None, None], [None, None]
        for t in range(count):
            step = t + 1 - 2 * pair
            valid = jnp.logical_and(step >= 0, step < count)
            beside = order[jnp.clip(step, 0, count - 1)]
            for b in range(2):
                want = 2 * pos + b - w
                sel = (want == 2 * piece * order[t]).astype(F32).astype(BF16)
                sel_e = (want == jnp.where(valid, 2 * piece * beside, -99999)).astype(F32).astype(BF16)
                x = mm(got[t, 0 : 2 * chan], sel)
                e = mm(got[t, 2 * chan : 3 * chan], sel_e)
                inner[b] = x if inner[b] is None else inner[b] + x
                outer[b] = e if outer[b] is None else outer[b] + e
        for a in range(2):
            mine = (pair == a).astype(F32)
            for b in range(2):
                at = (2 * a + b) * chan
                out[at : at + chan] = inner[b][a * chan : (a + 1) * chan] + outer[b] * mine

    return body


def swaps(count):
    within = [(i, i ^ 1) for i in range(count)]
    across = [(0, 0), (count - 1, count - 1)]
    for i in range(1, count - 1, 2):
        across += [(i, i + 1), (i + 1, i)]
    return within, sorted(across)


def shards(
    latent, cached_latent, cached_features, reward_grad, conv_in_weight, conv_mid_weight, conv_up_weight, norm_gain, out_gain, shard_order
):
    count = lax.axis_size("tile")
    rows, cols, chan = latent.shape
    mid_chan = norm_gain.shape[0]
    o = out_gain.shape[0]
    tile = lax.axis_index("tile")
    info = jnp.stack(
        [tile % 2, (tile > 0).astype(jnp.int32), (tile < count - 1).astype(jnp.int32), (tile >= count // 2).astype(jnp.int32)]
    ).astype(jnp.int32)
    lat = jnp.transpose(latent, (0, 2, 1))
    lat_cached = jnp.transpose(cached_latent, (0, 1, 3, 2))
    reward_t = jnp.transpose(reward_grad, (0, 2, 1))
    up_t = jnp.transpose(conv_up_weight, (0, 1, 3, 2))
    mid = conv_mid_weight.reshape(3, 3, 3 * mid_chan, mid_chan)
    w_in = conv_in_weight.reshape(3, 3, 3 * chan, mid_chan)
    gain = norm_gain.reshape(1, mid_chan)
    gain_out = jnp.concatenate([out_gain, out_gain[128:]]).reshape(1, 256)
    within, across = swaps(count)
    size = rows * cols
    edge_rows = 3 * cols + 2 * chan * rows

    own, send_even, send_odd = call(
        pack_body(rows, cols, o, chan),
        [((2 * rows, cols, 384), BF16), ((edge_rows, 384), BF16), ((edge_rows, 384), BF16)],
        1, 3, [], 2e9, 16,
    )(info, reward_t, lat, lat_cached)
    packed_even = lax.ppermute(send_even, "tile", within)
    packed_odd = lax.ppermute(send_odd, "tile", across)

    fwd, back_odd, back_even = call(
        taps_body, [((2, 768, 768), BF16), ((768, 768), BF16), ((768, 768), BF16)], 0, 1, [], 1e9, 16
    )(up_t)

    acc, part_even, part_odd = call(
        cached_body(rows, cols),
        [((6 * cols, 384), F32), ((3 * cols, 384), BF16), ((3 * cols, 384), BF16)],
        1, 2, [pltpu.VMEM((size, 2304), BF16)], 4e9, 24,
    )(info, cached_features, mid)
    got_even = lax.ppermute(part_even, "tile", within)
    got_odd = lax.ppermute(part_odd, "tile", across)

    hidden, conv = call(
        current_body(rows, cols, chan),
        [((rows + 4, cols, 384), BF16), ((2 * size, 384), F32)],
        1, 7,
        [
            pltpu.VMEM((9 * rows * chan, 256), F32),
            pltpu.VMEM((27 * rows * chan, 256), BF16),
            pltpu.VMEM(((rows + 6) * cols, 1152), BF16),
            pltpu.VMEM((27 * chan, 384), BF16),
        ],
        5e9, 24,
    )(info, lat, lat_cached, packed_even, packed_odd, w_in, mid, gain)

    width = 2 * cols // count
    (payload,) = call(
        back_body(rows, cols, chan, count, o),
        [((count, 3 * chan, width), BF16)],
        1, 15,
        [
            pltpu.VMEM((2 * rows + 6, cols, 384), BF16),
            pltpu.VMEM((6 * cols, 384), F32),
            pltpu.VMEM(((rows + 4) * cols, 768), F32),
            pltpu.VMEM(((rows + 4) * cols, 768), F32),
            pltpu.VMEM(((rows + 3) * cols, 768), BF16),
            pltpu.VMEM(((rows + 3) * cols, 768), BF16),
            pltpu.VMEM(((rows + 4) * cols, 1152), BF16),
            pltpu.VMEM((3 * chan, size), F32),
        ],
        8e9, 32,
    )(
        info, hidden, conv, acc, got_even, got_odd, packed_even, packed_odd, own, fwd, back_odd, back_even, mid,
        w_in[2].reshape(9 * chan, mid_chan), gain, gain_out,
    )
    received = lax.all_to_all(payload, "tile", split_axis=0, concat_axis=0, tiled=True)
    tokens = size // 4
    (placed,) = call(place_body(count, chan, width, tokens), [((4 * chan, tokens), F32)], 2, 1, [], 1e7, 16)(
        info, shard_order, received
    )
    return placed.T


def solution(mesh):
    return jax.shard_map(
        shards,
        mesh=mesh,
        in_specs=(
            P(("prompt", "tile"), None, None),
            P(None, ("prompt", "tile"), None, None),
            P(None, ("prompt", "tile"), None, None),
            P(("prompt", "tile"), None, None),
            P(),
            P(),
            P(),
            P(),
            P(),
            P("prompt"),
        ),
        out_specs=P(("prompt", "tile"), None),
        check_vma=False,
    )
```

profile of v0, /device:TPU:0, one launch (start us, length us, event | category | flops | bytes accessed | tf_op | source)
XLA Modules:
  0.0 55.3 jit_solution(4867702096052372440)
XLA Ops:
  0.0 0.1 pad_add_fusion.info
  0.1 1.3 %copy-done.5 = bf16[8,320,192]{1,2,0:T(8,128)(2,1)S(1)} copy-done((bf16[8,320,192]{1,2,0:T(8,128)(2,1)S(1)}, bf16[8,320,192]{1,2,0:T(8,128)(2,1)}, u32[]{:S(2)}) %copy-start.5) | copy-done | bytes 983064
  1.4 0.8 %copy-done.7 = bf16[2,4,160,16]{2,3,1,0:T(8,128)(2,1)S(1)} copy-done((bf16[2,4,160,16]{2,3,1,0:T(8,128)(2,1)S(1)}, bf16[2,4,160,16]{2,3,1,0:T(8,128)(2,1)}, u32[]{:S(2)}) %copy-start.7) | copy-done | bytes 40984
  2.2 0.8 %copy-done.9 = bf16[4,160,16]{1,2,0:T(8,128)(2,1)S(1)} copy-done((bf16[4,160,16]{1,2,0:T(8,128)(2,1)S(1)}, bf16[4,160,16]{1,2,0:T(8,128)(2,1)}, u32[]{:S(2)}) %copy-start.9) | copy-done | bytes 20504
  3.0 1.7 %shard_map.100 = (bf16[8,160,384]{2,1,0:T(8,128)(2,1)S(1)}, bf16[608,384]{1,0:T(8,128)(2,1)S(1)}, bf16[608,384]{1,0:T(8,128)(2,1)S(1)}) custom-call(s32[4]{0:T(128)S(1)} %pad_add_fusion.info, bf16[8,192,320]{2,1,0:T(8,128)(2,1)S(1)} %bitcast.22, bf16[4,16,160]{2,1,0:T(8,128)(2,1)S(1)} %bitcast.25, bf16[2,4,16,160]{3,2,1,0:T(8,128)(2,1)S(1)} %bitcast.23), custom_call_target="tpu_custom_call" | custom-call | flops 2000000000 | bytes 1048576 | tf_op jit(solution)/shard_map/pallas_call | solution.py:457
  4.7 0.5 collective-permute-start
  5.2 0.7 %collective-permute-start.1 = (bf16[608,384]{1,0:T(8,128)(2,1)S(1)}, bf16[608,384]{1,0:T(8,128)(2,1)S(1)}, u32[]{:S(2)}, u32[]{:S(2)}) collective-permute-start(bf16[608,384]{1,0:T(8,128)(2,1)S(1)} %get-tuple-element.17), channel_id=1, source_target_pairs={{0,0},{1,2},{2,1},{3,4},{4,3},{5,6},{6,5},{7,7},{8,8},{9,10},{10,9... | collective-permute-start | bytes 1400840 | tf_op jit(solution)/shard_map/ppermute | solution.py:463
  5.9 0.0 copy-done.6
  5.9 0.0 copy-start.2
  5.9 3.3 %copy-done.2 = bf16[3,3,3,384,384]{4,3,2,1,0:T(8,128)(2,1)S(1)} copy-done((bf16[3,3,3,384,384]{4,3,2,1,0:T(8,128)(2,1)S(1)}, bf16[3,3,3,384,384]{4,3,2,1,0:T(8,128)(2,1)}, u32[]{:S(2)}) %copy-start.2) | copy-done | bytes 7962648
  9.1 4.7 %shard_map.102 = (f32[960,384]{1,0:T(8,128)S(1)}, bf16[480,384]{1,0:T(8,128)(2,1)S(1)}, bf16[480,384]{1,0:T(8,128)(2,1)S(1)}) custom-call(s32[4]{0:T(128)S(1)} %pad_add_fusion.info, bf16[2,4,160,384]{3,2,1,0:T(8,128)(2,1)S(1)} %copy-done.6, bf16[3,3,1152,384]{3,2,1,0:T(8,128)(2,1)S(1)} %bitcast.18), custom_call_target="tpu_custom_call" | custom-call | flops 4000000000 | bytes 1048576 | tf_op jit(solution)/shard_map/pallas_call | solution.py:469
  13.8 4.0 %collective-permute-start.2 = (bf16[480,384]{1,0:T(8,128)(2,1)S(1)}, bf16[480,384]{1,0:T(8,128)(2,1)S(1)}, u32[]{:S(2)}, u32[]{:S(2)}) collective-permute-start(bf16[480,384]{1,0:T(8,128)(2,1)S(1)} %get-tuple-element.21), channel_id=1, source_target_pairs={{0,1},{1,0},{2,3},{3,2},{4,5},{5,4},{6,7},{7,6},{8,9},{9,8},{10,11... | collective-permute-start | bytes 1105928 | tf_op jit(solution)/shard_map/ppermute | solution.py:474
  17.8 0.7 %collective-permute-start.3 = (bf16[480,384]{1,0:T(8,128)(2,1)S(1)}, bf16[480,384]{1,0:T(8,128)(2,1)S(1)}, u32[]{:S(2)}, u32[]{:S(2)}) collective-permute-start(bf16[480,384]{1,0:T(8,128)(2,1)S(1)} %get-tuple-element.22), channel_id=1, source_target_pairs={{0,0},{1,2},{2,1},{3,4},{4,3},{5,6},{6,5},{7,7},{8,8},{9,10},{10,9... | collective-permute-start | bytes 1105928 | tf_op jit(solution)/shard_map/ppermute | solution.py:475
  18.6 0.0 copy-done.4
  18.6 0.0 copy-start.8
  18.6 0.0 copy-start.10
  18.6 0.6 %shard_map.103 = (bf16[2,768,768]{2,1,0:T(8,128)(2,1)S(1)}, bf16[768,768]{1,0:T(8,128)(2,1)S(1)}, bf16[768,768]{1,0:T(8,128)(2,1)S(1)}) custom-call(bf16[3,3,192,384]{3,2,1,0:T(8,128)(2,1)S(1)} %bitcast.21), custom_call_target="tpu_custom_call" | custom-call | flops 1000000000 | bytes 1048576 | tf_op jit(solution)/shard_map/pallas_call | solution.py:465
  19.2 0.1 pad_maximum_fusion
  19.3 0.0 collective-permute-done.got_even.packed_even
  19.3 0.0 collective-permute-done.1.got_odd.packed_odd
  19.3 0.2 copy-done.8
  19.4 8.3 %shard_map.101 = (bf16[8,160,384]{2,1,0:T(8,128)(2,1)S(1)}, f32[1280,384]{1,0:T(8,128)S(1)}) custom-call(s32[4]{0:T(128)S(1)} %pad_add_fusion.info, bf16[4,16,160]{2,1,0:T(8,128)(2,1)S(1)} %bitcast.26, bf16[2,4,16,160]{3,2,1,0:T(8,128)(2,1)S(1)} %bitcast.24, bf16[608,384]{1,0:T(8,128)(2,1)S(1)} %collective-permute-done.got_even.packed_even, ...), custom_call_target="tpu_custom_call" | custom-call | flops 5000000000 | bytes 1048576 | tf_op jit(solution)/shard_map/pallas_call | solution.py:477
  27.7 0.0 collective-permute-done.2.got_even
  27.8 0.0 collective-permute-done.3.got_odd
  27.8 0.0 copy-start.1
  27.8 13.8 %shard_map.104 = bf16[8,48,40]{2,1,0:T(8,128)(2,1)S(1)} custom-call(s32[4]{0:T(128)S(1)} %pad_add_fusion.info, bf16[8,160,384]{2,1,0:T(8,128)(2,1)S(1)} %get-tuple-element.18.hidden, f32[1280,384]{1,0:T(8,128)S(1)} %get-tuple-element.19.conv, f32[960,384]{1,0:T(8,128)S(1)} %get-tuple-element.20.acc, bf16[480,384]{1,0:T(8,128)(2,1)S(1)} %collective-permute-done.2.got_even, ...), custom_call_target="tpu_custom_call" | custom-call | flops 8000000000 | bytes 1048576 | tf_op jit(solution)/shard_map/pallas_call | solution.py:491
  41.6 0.1 copy.11
  41.7 0.1 reshape.21
  41.8 11.7 %all_to_all.5 = bf16[8,2,960]{2,1,0:T(2,128)(2,1)S(1)} all-to-all(bf16[8,2,960]{2,1,0:T(2,128)(2,1)S(1)} %reshape.21), channel_id=1, replica_groups=mesh['prompt'=4,'tile'=8] {'tile'}, dimensions={0} | all-to-all | bytes 61440 | tf_op jit(solution)/shard_map/all_to_all | solution.py:510
  53.5 0.1 reshape.22
  53.7 0.1 copy.12.got
  53.8 1.5 %shard_map.105 = f32[64,160]{1,0:T(8,128)} custom-call(s32[4]{0:T(128)S(1)} %pad_add_fusion.info, s32[8]{0:T(128)S(1)} %copy-done.1, bf16[8,48,40]{2,1,0:T(8,128)(2,1)S(1)} %copy.12.got), custom_call_target="tpu_custom_call" | custom-call | flops 10000000 | bytes 1048576 | tf_op jit(solution)/shard_map/pallas_call | solution.py:512
  (18 shorter events, 0.0 us)
Async XLA Ops:
  0.1 1.3 %copy-start.5 = (bf16[8,320,192]{1,2,0:T(8,128)(2,1)S(1)}, bf16[8,320,192]{1,2,0:T(8,128)(2,1)}, u32[]{:S(2)}) copy-start(bf16[8,320,192]{1,2,0:T(8,128)(2,1)} %param.13) | copy-start | bytes 2949124
  1.4 0.8 %copy-start.7 = (bf16[2,4,160,16]{2,3,1,0:T(8,128)(2,1)S(1)}, bf16[2,4,160,16]{2,3,1,0:T(8,128)(2,1)}, u32[]{:S(2)}) copy-start(bf16[2,4,160,16]{2,3,1,0:T(8,128)(2,1)} %param.11) | copy-start | bytes 122884
  2.2 0.8 %copy-start.9 = (bf16[4,160,16]{1,2,0:T(8,128)(2,1)S(1)}, bf16[4,160,16]{1,2,0:T(8,128)(2,1)}, u32[]{:S(2)}) copy-start(bf16[4,160,16]{1,2,0:T(8,128)(2,1)} %param.10) | copy-start | bytes 61444
  2.9 2.9 %copy-start.6 = (bf16[2,4,160,384]{3,2,1,0:T(8,128)(2,1)S(1)}, bf16[2,4,160,384]{3,2,1,0:T(8,128)(2,1)}, u32[]{:S(2)}) copy-start(bf16[2,4,160,384]{3,2,1,0:T(8,128)(2,1)} %features.1) | copy-start | bytes 2949124
  4.7 14.6 %collective-permute-start = (bf16[608,384]{1,0:T(8,128)(2,1)S(1)}, bf16[608,384]{1,0:T(8,128)(2,1)S(1)}, u32[]{:S(2)}, u32[]{:S(2)}) collective-permute-start(bf16[608,384]{1,0:T(8,128)(2,1)S(1)} %get-tuple-element.16), channel_id=1, source_target_pairs={{0,1},{1,0},{2,3},{3,2},{4,5},{5,4},{6,7},{7,6},{8,9},{9,8},{10,11... | collective-permute-start | bytes 1400840 | tf_op jit(solution)/shard_map/ppermute | solution.py:462
  5.2 14.1 %collective-permute-start.1 = (bf16[608,384]{1,0:T(8,128)(2,1)S(1)}, bf16[608,384]{1,0:T(8,128)(2,1)S(1)}, u32[]{:S(2)}, u32[]{:S(2)}) collective-permute-start(bf16[608,384]{1,0:T(8,128)(2,1)S(1)} %get-tuple-element.17), channel_id=1, source_target_pairs={{0,0},{1,2},{2,1},{3,4},{4,3},{5,6},{6,5},{7,7},{8,8},{9,10},{10,9... | collective-permute-start | bytes 1400840 | tf_op jit(solution)/shard_map/ppermute | solution.py:463
  5.9 3.3 %copy-start.2 = (bf16[3,3,3,384,384]{4,3,2,1,0:T(8,128)(2,1)S(1)}, bf16[3,3,3,384,384]{4,3,2,1,0:T(8,128)(2,1)}, u32[]{:S(2)}) copy-start(bf16[3,3,3,384,384]{4,3,2,1,0:T(8,128)(2,1)} %param.15) | copy-start | bytes 23887876
  9.1 9.4 %copy-start.12 = (f32[192]{0:T(256)S(1)}, f32[192]{0:T(256)}, u32[]{:S(2)}) copy-start(f32[192]{0:T(256)} %param.18) | copy-start | bytes 2308
  9.1 9.4 %copy-start.11 = (f32[384]{0:T(512)S(1)}, f32[384]{0:T(512)}, u32[]{:S(2)}) copy-start(f32[384]{0:T(512)} %param.17) | copy-start | bytes 4612
  9.1 9.4 %copy-start = (bf16[3,3,3,16,384]{4,3,2,1,0:T(8,128)(2,1)S(1)}, bf16[3,3,3,16,384]{4,3,2,1,0:T(8,128)(2,1)}, u32[]{:S(2)}) copy-start(bf16[3,3,3,16,384]{4,3,2,1,0:T(8,128)(2,1)} %param.14) | copy-start | bytes 995332
  9.1 9.5 %copy-start.4 = (bf16[3,3,384,192]{2,3,1,0:T(8,128)(2,1)S(1)}, bf16[3,3,384,192]{2,3,1,0:T(8,128)(2,1)}, u32[]{:S(2)}) copy-start(bf16[3,3,384,192]{2,3,1,0:T(8,128)(2,1)} %param.16) | copy-start | bytes 3981316
  9.1 10.1 %copy-start.3 = (bf16[3,3,3,384,384]{4,3,2,1,0:T(8,128)(2,1)S(1)}, bf16[3,3,3,384,384]{4,3,2,1,0:T(8,128)(2,1)}, u32[]{:S(2)}) copy-start(bf16[3,3,3,384,384]{4,3,2,1,0:T(8,128)(2,1)} %param.15) | copy-start | bytes 23887876
  13.8 13.9 %collective-permute-start.2 = (bf16[480,384]{1,0:T(8,128)(2,1)S(1)}, bf16[480,384]{1,0:T(8,128)(2,1)S(1)}, u32[]{:S(2)}, u32[]{:S(2)}) collective-permute-start(bf16[480,384]{1,0:T(8,128)(2,1)S(1)} %get-tuple-element.21), channel_id=1, source_target_pairs={{0,1},{1,0},{2,3},{3,2},{4,5},{5,4},{6,7},{7,6},{8,9},{9,8},{10,11... | collective-permute-start | bytes 1105928 | tf_op jit(solution)/shard_map/ppermute | solution.py:474
  17.8 9.9 %collective-permute-start.3 = (bf16[480,384]{1,0:T(8,128)(2,1)S(1)}, bf16[480,384]{1,0:T(8,128)(2,1)S(1)}, u32[]{:S(2)}, u32[]{:S(2)}) collective-permute-start(bf16[480,384]{1,0:T(8,128)(2,1)S(1)} %get-tuple-element.22), channel_id=1, source_target_pairs={{0,0},{1,2},{2,1},{3,4},{4,3},{5,6},{6,5},{7,7},{8,8},{9,10},{10,9... | collective-permute-start | bytes 1105928 | tf_op jit(solution)/shard_map/ppermute | solution.py:475
  18.6 0.8 %copy-start.8 = (bf16[2,4,160,16]{2,3,1,0:T(8,128)(2,1)S(1)}, bf16[2,4,160,16]{2,3,1,0:T(8,128)(2,1)}, u32[]{:S(2)}) copy-start(bf16[2,4,160,16]{2,3,1,0:T(8,128)(2,1)} %param.11) | copy-start | bytes 122884
  18.6 0.8 %copy-start.10 = (bf16[4,160,16]{1,2,0:T(8,128)(2,1)S(1)}, bf16[4,160,16]{1,2,0:T(8,128)(2,1)}, u32[]{:S(2)}) copy-start(bf16[4,160,16]{1,2,0:T(8,128)(2,1)} %param.10) | copy-start | bytes 61444
  27.8 26.0 %copy-start.1 = (s32[8]{0:T(128)S(1)}, s32[8]{0:T(128)}, u32[]{:S(2)}) copy-start(s32[8]{0:T(128)} %order.1) | copy-start | bytes 100
where the time goes:
time: 55.6 us; the launch traced here: 55.3 us
  Pallas kernels  30.5 us (55%)
  blocking collectives  11.7 us (21%)
  local copies, waits for them, and re-layouts  6.83 us (12%)
  starting transfers between devices  5.86 us (11%)
    pallas_call x1, Pallas kernels, shards(): call(back_body(rows, cols, chan, count, o), [((count, 3 * chan, width), B...  13.8 us
    all_to_all x1, blocking collectives, shards(): lax.all_to_all(payload, 'tile', split_axis=0, concat_axis=0, tiled=True)  11.7 us
    pallas_call x1, Pallas kernels, shards(): call(current_body(rows, cols, chan), [((rows + 4, cols, 384), BF16), ((2...  8.3 us
    unnamed x28, local copies, waits for them, and re-layouts  6.59 us
    pallas_call x1, Pallas kernels, shards(): call(cached_body(rows, cols), [((6 * cols, 384), F32), ((3 * cols, 384),...  4.68 us
    ppermute x1, starting transfers between devices, shards(): got_even = lax.ppermute(part_even, 'tile', within)  4 us
    pallas_call x1, Pallas kernels, shards(): call(pack_body(rows, cols, o, chan), [((2 * rows, cols, 384), BF16), ((ed...  1.69 us
    pallas_call x1, Pallas kernels, shards(): call(place_body(count, chan, width, tokens), [((4 * chan, tokens), F32)],...  1.45 us
  transfers between devices with their start and end apart: 4, of which 0 were waited for; matrix products, arithmetic and copies ran while one was open for 0% of the time, Pallas kernels for 25%

commit v1 on v0

--- a/solution.py
+++ b/solution.py
@@ -234,23 +234,23 @@
         even = info[0] == 0
         top, bottom = flag(info, 1), flag(info, 2)
 
-        def take(got, packed, before):
+        def take(got, packed, before, slot):
             ok = top if before else bottom
             place = 0 if before else 3
             for k in range(3):
                 at = slice(k * cols, (k + 1) * cols)
-                edge[(place + k) * cols : (place + k + 1) * cols] = got[at].astype(F32) * ok
+                edge[(place + k) * cols : (place + k + 1) * cols] = got[slot, at].astype(F32) * ok
                 reward[k if before else 2 * rows + 3 + k] = (packed[at].astype(F32) * ok).astype(BF16)
 
         @pl.when(even)
         def _():
-            take(got_odd, packed_odd, True)
-            take(got_even, packed_even, False)
+            take(got_odd, packed_odd, True, 0)
+            take(got_even, packed_even, False, 1)
 
         @pl.when(jnp.logical_not(even))
         def _():
-            take(got_even, packed_even, True)
-            take(got_odd, packed_odd, False)
+            take(got_even, packed_even, True, 0)
+            take(got_odd, packed_odd, False, 1)
 
         reward[3 : 2 * rows + 3] = own[...]
 
@@ -471,8 +471,10 @@
         [((6 * cols, 384), F32), ((3 * cols, 384), BF16), ((3 * cols, 384), BF16)],
         1, 2, [pltpu.VMEM((size, 2304), BF16)], 4e9, 24,
     )(info, cached_features, mid)
-    got_even = lax.ppermute(part_even, "tile", within)
-    got_odd = lax.ppermute(part_odd, "tile", across)
+    pairs = [[i, i + 1] for i in range(0, count, 2)]
+    cross = [[i, i + 1] for i in range(1, count - 1, 2)] + [[count - 1, 0]]
+    got_even = lax.all_gather(part_even, "tile", axis_index_groups=pairs)
+    got_odd = lax.all_gather(part_odd, "tile", axis_index_groups=cross)
 
     hidden, conv = call(
         current_body(rows, cols, chan),
@@ -507,7 +509,8 @@
         info, hidden, conv, acc, got_even, got_odd, packed_even, packed_odd, own, fwd, back_odd, back_even, mid,
         w_in[2].reshape(9 * chan, mid_chan), gain, gain_out,
     )
-    received = lax.all_to_all(payload, "tile", split_axis=0, concat_axis=0, tiled=True)
+    gathered = lax.all_gather(payload, "tile")
+    received = lax.dynamic_index_in_dim(gathered, tile, 1, keepdims=False)
     tokens = size // 4
     (placed,) = call(place_body(count, chan, width, tokens), [((4 * chan, tokens), F32)], 2, 1, [], 1e7, 16)(
         info, shard_order, received

time: 55.6 us -> 78.6 us (1.41)
  blocking collectives: 11.7 us -> 32.6 us
  local copies, waits for them, and re-layouts: 6.83 us -> 11.8 us
  starting transfers between devices: 5.86 us -> 2.11 us
  Pallas kernels: 30.5 us -> 31.4 us
    all_gather x0 -> x3, blocking collectives: none -> 32.6 us  [the longest x1 14.9 us: shards(): gathered = lax.all_gather(payload, 'tile')]
    all_to_all x1 -> x0, blocking collectives: 11.7 us -> none  [shards(): lax.all_to_all(payload, 'tile', split_axis=0, concat_axis=0, tiled=True)]
    unnamed x28 -> x37, local copies, waits for them, and re-layouts: 6.59 us -> 11.6 us
    ppermute x2 -> x0, starting transfers between devices: 4.67 us -> none  [the longest x1 4 us: shards(): got_even = lax.ppermute(part_even, 'tile', within)]
    ppermute x1, starting transfers between devices: 0.68 us -> 1.67 us  [shards(): packed_odd = lax.ppermute(send_odd, 'tile', across)]
    pallas_call x1, Pallas kernels: 1.69 us -> 2.59 us  [shards(): call(pack_body(rows, cols, o, chan), [((2 * rows, cols, 384), BF16), ((ed...]
  transfers between devices with their start and end apart: 4 -> 2, of which waited for: 0 -> 0; matrix products, arithmetic and copies ran while one was open for 0% -> 0% of each run, Pallas kernels for 25% -> 7%
where the time goes in v1:
time: 78.6 us; the launch traced here: 78.2 us
  blocking collectives  32.6 us (41%)
  Pallas kernels  31.4 us (40%)
  local copies, waits for them, and re-layouts  11.8 us (15%)
  starting transfers between devices  2.11 us (3%)
    all_gather x1, blocking collectives, shards(): gathered = lax.all_gather(payload, 'tile')  14.9 us
    pallas_call x1, Pallas kernels, shards(): call(back_body(rows, cols, chan, count, o), [((count, 3 * chan, width), B...  13.8 us
    all_gather x1, blocking collectives, shards(): got_odd = lax.all_gather(part_odd, 'tile', axis_index_groups=cross)  12.6 us
    unnamed x37, local copies, waits for them, and re-layouts  11.6 us
    pallas_call x1, Pallas kernels, shards(): call(current_body(rows, cols, chan), [((rows + 4, cols, 384), BF16), ((2...  8.29 us
    all_gather x1, blocking collectives, shards(): got_even = lax.all_gather(part_even, 'tile', axis_index_groups=pairs)  5.05 us
    pallas_call x1, Pallas kernels, shards(): call(cached_body(rows, cols), [((6 * cols, 384), F32), ((3 * cols, 384),...  4.67 us
    pallas_call x1, Pallas kernels, shards(): call(pack_body(rows, cols, o, chan), [((2 * rows, cols, 384), BF16), ((ed...  2.59 us
  transfers between devices with their start and end apart: 2, of which 0 were waited for; matrix products, arithmetic and copies ran while one was open for 0% of the time, Pallas kernels for 7%

profile of v1, /device:TPU:0, one launch (start us, length us, event | category | flops | bytes accessed | tf_op | source)
XLA Modules:
  0.0 78.2 jit_solution(15370165372601279402)
XLA Ops:
  0.0 0.1 pad_add_fusion.info
  0.1 1.3 %copy-done.6 = bf16[8,320,192]{1,2,0:T(8,128)(2,1)S(1)} copy-done((bf16[8,320,192]{1,2,0:T(8,128)(2,1)S(1)}, bf16[8,320,192]{1,2,0:T(8,128)(2,1)}, u32[]{:S(2)}) %copy-start.6) | copy-done | bytes 983064
  1.4 0.8 %copy-done.8 = bf16[2,4,160,16]{2,3,1,0:T(8,128)(2,1)S(1)} copy-done((bf16[2,4,160,16]{2,3,1,0:T(8,128)(2,1)S(1)}, bf16[2,4,160,16]{2,3,1,0:T(8,128)(2,1)}, u32[]{:S(2)}) %copy-start.8) | copy-done | bytes 40984
  2.2 0.8 copy-done.10
  3.0 2.6 %shard_map.100 = (bf16[8,160,384]{2,1,0:T(8,128)(2,1)S(1)}, bf16[608,384]{1,0:T(8,128)(2,1)}, bf16[608,384]{1,0:T(8,128)(2,1)}) custom-call(s32[4]{0:T(128)S(1)} %pad_add_fusion.info, bf16[8,192,320]{2,1,0:T(8,128)(2,1)S(1)} %bitcast.27, bf16[4,16,160]{2,1,0:T(8,128)(2,1)S(1)} %bitcast.30, bf16[2,4,16,160]{3,2,1,0:T(8,128)(2,1)S(1)} %bitcast.28), custom_call_target="tpu_custom_call" | custom-call | flops 2000000000 | bytes 1048576 | tf_op jit(solution)/shard_map/pallas_call | solution.py:457
  5.5 1.0 %copy-done.14 = bf16[8,160,384]{2,1,0:T(8,128)(2,1)} copy-done((bf16[8,160,384]{2,1,0:T(8,128)(2,1)}, bf16[8,160,384]{2,1,0:T(8,128)(2,1)S(1)}, u32[]{:S(2)}) %copy-start.14) | copy-done | bytes 983064
  6.5 0.4 collective-permute-start
  6.9 1.7 %collective-permute-start.1 = (bf16[608,384]{1,0:T(8,128)(2,1)}, bf16[608,384]{1,0:T(8,128)(2,1)S(1)}, u32[]{:S(2)}, u32[]{:S(2)}) collective-permute-start(bf16[608,384]{1,0:T(8,128)(2,1)} %get-tuple-element.17), channel_id=1, source_target_pairs={{0,0},{1,2},{2,1},{3,4},{4,3},{5,6},{6,5},{7,7},{8,8},{9,10},{10,9... | collective-permute-start | bytes 1400840 | tf_op jit(solution)/shard_map/ppermute | solution.py:463
  8.6 0.0 copy-done.7
  8.6 0.0 copy-start.2
  8.6 3.3 %copy-done.2 = bf16[3,3,3,384,384]{4,3,2,1,0:T(8,128)(2,1)S(1)} copy-done((bf16[3,3,3,384,384]{4,3,2,1,0:T(8,128)(2,1)S(1)}, bf16[3,3,3,384,384]{4,3,2,1,0:T(8,128)(2,1)}, u32[]{:S(2)}) %copy-start.2) | copy-done | bytes 7962648
  11.9 4.7 %shard_map.102 = (f32[960,384]{1,0:T(8,128)S(1)}, bf16[480,384]{1,0:T(8,128)(2,1)S(1)}, bf16[480,384]{1,0:T(8,128)(2,1)S(1)}) custom-call(s32[4]{0:T(128)S(1)} %pad_add_fusion.info, bf16[2,4,160,384]{3,2,1,0:T(8,128)(2,1)S(1)} %copy-done.7, bf16[3,3,1152,384]{3,2,1,0:T(8,128)(2,1)S(1)} %bitcast.23), custom_call_target="tpu_custom_call" | custom-call | flops 4000000000 | bytes 1048576 | tf_op jit(solution)/shard_map/pallas_call | solution.py:469
  16.6 0.0 copy-start.12
  16.6 1.1 %copy-done.12 = f32[960,384]{1,0:T(8,128)} copy-done((f32[960,384]{1,0:T(8,128)}, f32[960,384]{1,0:T(8,128)S(1)}, u32[]{:S(2)}) %copy-start.12) | copy-done | bytes 1474584
  17.7 0.1 pad_maximum_fusion
  17.8 0.0 copy-done.5
  17.8 0.6 shard_map.103
  18.4 0.0 copy-start.9
  18.4 0.0 copy-start.11
  18.4 5.1 %all-gather = bf16[960,384]{1,0:T(8,128)(2,1)S(1)} all-gather(bf16[480,384]{1,0:T(8,128)(2,1)S(1)} %get-tuple-element.21), channel_id=2, replica_groups={{0,1},{2,3},{4,5},{6,7},{8,9},{10,11},{12,13},{14,15},{16,17},{18,19},{..., dimensions={0}, use_global_device_ids=true | all-gather | bytes 1105920 | tf_op jit(solution)/shard_map/all_gather | solution.py:476
  23.5 12.6 %all-gather.1 = bf16[960,384]{1,0:T(8,128)(2,1)S(1)} all-gather(bf16[480,384]{1,0:T(8,128)(2,1)S(1)} %get-tuple-element.22), channel_id=3, replica_groups={{1,2},{3,4},{5,6},{7,0},{9,10},{11,12},{13,14},{15,8},{17,18},{19,20},{..., dimensions={0}, use_global_device_ids=true | all-gather | bytes 1105920 | tf_op jit(solution)/shard_map/all_gather | solution.py:477
  36.1 0.0 collective-permute-done.got_even.packed_even
  36.1 0.0 collective-permute-done.1.got_odd.packed_odd
  36.1 0.0 copy-start.3
  36.1 3.3 %copy-done.3 = bf16[3,3,3,384,384]{4,3,2,1,0:T(8,128)(2,1)S(1)} copy-done((bf16[3,3,3,384,384]{4,3,2,1,0:T(8,128)(2,1)S(1)}, bf16[3,3,3,384,384]{4,3,2,1,0:T(8,128)(2,1)}, u32[]{:S(2)}) %copy-start.3) | copy-done | bytes 7962648
  39.4 8.3 %shard_map.101 = (bf16[8,160,384]{2,1,0:T(8,128)(2,1)S(1)}, f32[1280,384]{1,0:T(8,128)S(1)}) custom-call(s32[4]{0:T(128)S(1)} %pad_add_fusion.info, bf16[4,16,160]{2,1,0:T(8,128)(2,1)S(1)} %bitcast.31, bf16[2,4,16,160]{3,2,1,0:T(8,128)(2,1)S(1)} %bitcast.29, bf16[608,384]{1,0:T(8,128)(2,1)S(1)} %collective-permute-done.got_even.packed_even, ...), custom_call_target="tpu_custom_call" | custom-call | flops 5000000000 | bytes 1048576 | tf_op jit(solution)/shard_map/pallas_call | solution.py:479
  47.7 0.0 copy-start.1
  47.7 13.8 %shard_map.104 = bf16[8,48,40]{2,1,0:T(8,128)(2,1)S(1)} custom-call(s32[4]{0:T(128)S(1)} %pad_add_fusion.info, bf16[8,160,384]{2,1,0:T(8,128)(2,1)S(1)} %get-tuple-element.18.hidden, f32[1280,384]{1,0:T(8,128)S(1)} %get-tuple-element.19.conv, f32[960,384]{1,0:T(8,128)S(1)} %copy-done.13, bf16[2,480,384]{2,1,0:T(8,128)(2,1)S(1)} %bitcast.17, ...), custom_call_target="tpu_custom_call" | custom-call | flops 8000000000 | bytes 1048576 | tf_op jit(solution)/shard_map/pallas_call | solution.py:493
  61.5 0.1 copy.12
  61.7 14.9 %all-gather.2 = bf16[64,48,40]{1,2,0:T(8,128)(2,1)S(1)} all-gather(bf16[8,48,40]{1,2,0:T(8,128)(2,1)S(1)} %copy.12), channel_id=4, replica_groups=mesh['prompt'=4,'tile'=8] {'tile'}, dimensions={0}, use_global_device_ids=true | all-gather | bytes 276480 | tf_op jit(solution)/shard_map/all_gather | solution.py:512
  76.6 0.1 copy.14
  76.7 1.5 %shard_map.105 = f32[64,160]{1,0:T(8,128)} custom-call(s32[4]{0:T(128)S(1)} %pad_add_fusion.info, s32[8]{0:T(128)S(1)} %copy-done.1, bf16[8,48,40]{2,1,0:T(8,128)(2,1)S(1)} %bitcast.19), custom_call_target="tpu_custom_call" | custom-call | flops 10000000 | bytes 1048576 | tf_op jit(solution)/shard_map/pallas_call | solution.py:515
  (25 shorter events, 0.1 us)
Async XLA Ops:
  0.1 1.3 %copy-start.6 = (bf16[8,320,192]{1,2,0:T(8,128)(2,1)S(1)}, bf16[8,320,192]{1,2,0:T(8,128)(2,1)}, u32[]{:S(2)}) copy-start(bf16[8,320,192]{1,2,0:T(8,128)(2,1)} %param.13) | copy-start | bytes 2949124
  1.4 0.8 %copy-start.8 = (bf16[2,4,160,16]{2,3,1,0:T(8,128)(2,1)S(1)}, bf16[2,4,160,16]{2,3,1,0:T(8,128)(2,1)}, u32[]{:S(2)}) copy-start(bf16[2,4,160,16]{2,3,1,0:T(8,128)(2,1)} %param.11) | copy-start | bytes 122884
  2.2 0.8 copy-start.10
  2.9 5.7 %copy-start.17 = (f32[192]{0:T(256)S(1)}, f32[192]{0:T(256)}, u32[]{:S(2)}) copy-start(f32[192]{0:T(256)} %param.18) | copy-start | bytes 2308
  3.0 5.7 %copy-start.7 = (bf16[2,4,160,384]{3,2,1,0:T(8,128)(2,1)S(1)}, bf16[2,4,160,384]{3,2,1,0:T(8,128)(2,1)}, u32[]{:S(2)}) copy-start(bf16[2,4,160,384]{3,2,1,0:T(8,128)(2,1)} %features.1) | copy-start | bytes 2949124
  5.5 1.0 %copy-start.14 = (bf16[8,160,384]{2,1,0:T(8,128)(2,1)}, bf16[8,160,384]{2,1,0:T(8,128)(2,1)S(1)}, u32[]{:S(2)}) copy-start(bf16[8,160,384]{2,1,0:T(8,128)(2,1)S(1)} %get-tuple-element.23.own) | copy-start | bytes 2949124
  6.5 29.6 %collective-permute-start = (bf16[608,384]{1,0:T(8,128)(2,1)}, bf16[608,384]{1,0:T(8,128)(2,1)S(1)}, u32[]{:S(2)}, u32[]{:S(2)}) collective-permute-start(bf16[608,384]{1,0:T(8,128)(2,1)} %get-tuple-element.16), channel_id=1, source_target_pairs={{0,1},{1,0},{2,3},{3,2},{4,5},{5,4},{6,7},{7,6},{8,9},{9,8},{10,11... | collective-permute-start | bytes 1400840 | tf_op jit(solution)/shard_map/ppermute | solution.py:462
  6.9 29.1 %collective-permute-start.1 = (bf16[608,384]{1,0:T(8,128)(2,1)}, bf16[608,384]{1,0:T(8,128)(2,1)S(1)}, u32[]{:S(2)}, u32[]{:S(2)}) collective-permute-start(bf16[608,384]{1,0:T(8,128)(2,1)} %get-tuple-element.17), channel_id=1, source_target_pairs={{0,0},{1,2},{2,1},{3,4},{4,3},{5,6},{6,5},{7,7},{8,8},{9,10},{10,9... | collective-permute-start | bytes 1400840 | tf_op jit(solution)/shard_map/ppermute | solution.py:463
  8.6 3.3 %copy-start.2 = (bf16[3,3,3,384,384]{4,3,2,1,0:T(8,128)(2,1)S(1)}, bf16[3,3,3,384,384]{4,3,2,1,0:T(8,128)(2,1)}, u32[]{:S(2)}) copy-start(bf16[3,3,3,384,384]{4,3,2,1,0:T(8,128)(2,1)} %param.15) | copy-start | bytes 23887876
  11.9 5.9 %copy-start.16 = (f32[384]{0:T(512)S(1)}, f32[384]{0:T(512)}, u32[]{:S(2)}) copy-start(f32[384]{0:T(512)} %param.17) | copy-start | bytes 4612
  11.9 5.9 %copy-start = (bf16[3,3,3,16,384]{4,3,2,1,0:T(8,128)(2,1)S(1)}, bf16[3,3,3,16,384]{4,3,2,1,0:T(8,128)(2,1)}, u32[]{:S(2)}) copy-start(bf16[3,3,3,16,384]{4,3,2,1,0:T(8,128)(2,1)} %param.14) | copy-start | bytes 995332
  11.9 5.9 %copy-start.5 = (bf16[3,3,384,192]{2,3,1,0:T(8,128)(2,1)S(1)}, bf16[3,3,384,192]{2,3,1,0:T(8,128)(2,1)}, u32[]{:S(2)}) copy-start(bf16[3,3,384,192]{2,3,1,0:T(8,128)(2,1)} %param.16) | copy-start | bytes 3981316
  16.6 1.1 %copy-start.12 = (f32[960,384]{1,0:T(8,128)}, f32[960,384]{1,0:T(8,128)S(1)}, u32[]{:S(2)}) copy-start(f32[960,384]{1,0:T(8,128)S(1)} %get-tuple-element.20.acc) | copy-start | bytes 4423684
  18.4 17.7 %copy-start.9 = (bf16[2,4,160,16]{2,3,1,0:T(8,128)(2,1)S(1)}, bf16[2,4,160,16]{2,3,1,0:T(8,128)(2,1)}, u32[]{:S(2)}) copy-start(bf16[2,4,160,16]{2,3,1,0:T(8,128)(2,1)} %param.11) | copy-start | bytes 122884
  18.4 17.7 %copy-start.11 = (bf16[4,160,16]{1,2,0:T(8,128)(2,1)S(1)}, bf16[4,160,16]{1,2,0:T(8,128)(2,1)}, u32[]{:S(2)}) copy-start(bf16[4,160,16]{1,2,0:T(8,128)(2,1)} %param.10) | copy-start | bytes 61444
  36.1 3.3 %copy-start.3 = (bf16[3,3,3,384,384]{4,3,2,1,0:T(8,128)(2,1)S(1)}, bf16[3,3,3,384,384]{4,3,2,1,0:T(8,128)(2,1)}, u32[]{:S(2)}) copy-start(bf16[3,3,3,384,384]{4,3,2,1,0:T(8,128)(2,1)} %param.15) | copy-start | bytes 23887876
  39.4 8.3 %copy-start.4 = (bf16[3,3,3,384,384]{4,3,2,1,0:T(8,128)(2,1)S(1)}, bf16[3,3,3,384,384]{4,3,2,1,0:T(8,128)(2,1)}, u32[]{:S(2)}) copy-start(bf16[3,3,3,384,384]{4,3,2,1,0:T(8,128)(2,1)} %param.15) | copy-start | bytes 23887876
  39.4 8.3 %copy-start.13 = (f32[960,384]{1,0:T(8,128)S(1)}, f32[960,384]{1,0:T(8,128)}, u32[]{:S(2)}) copy-start(f32[960,384]{1,0:T(8,128)} %copy-done.12) | copy-start | bytes 4423684
  39.4 8.3 %copy-start.15 = (bf16[8,160,384]{2,1,0:T(8,128)(2,1)S(1)}, bf16[8,160,384]{2,1,0:T(8,128)(2,1)}, u32[]{:S(2)}) copy-start(bf16[8,160,384]{2,1,0:T(8,128)(2,1)} %copy-done.14) | copy-start | bytes 2949124
  47.7 29.0 %copy-start.1 = (s32[8]{0:T(128)S(1)}, s32[8]{0:T(128)}, u32[]{:S(2)}) copy-start(s32[8]{0:T(128)} %order.1) | copy-start | bytes 100

commit v2 on v0

--- a/solution.py
+++ b/solution.py
@@ -12,13 +12,23 @@
 SM = pl.BlockSpec(memory_space=pltpu.SMEM)
 
 
-def call(body, outs, n_smem, n_vmem, scratch, flops, limit):
+def weave(*groups):
+    total = max(len(g) for g in groups)
+    done = [0] * len(groups)
+    for k in range(total):
+        for n, g in enumerate(groups):
+            while done[n] * total < (k + 1) * len(g):
+                g[done[n]]()
+                done[n] += 1
+
+
+def call(body, outs, n_smem, n_vmem, scratch, flops, limit, smem_outs=0):
     specs = [SM] * n_smem + [VM] * n_vmem
     return pl.pallas_call(
         body,
         out_shape=[jax.ShapeDtypeStruct(s, d) for s, d in outs],
         in_specs=specs,
-        out_specs=[VM] * len(outs),
+        out_specs=[SM] * smem_outs + [VM] * (len(outs) - smem_outs),
         scratch_shapes=scratch,
         cost_estimate=pl.CostEstimate(flops=int(flops), bytes_accessed=2**20, transcendentals=0),
         compiler_params=pltpu.CompilerParams(vmem_limit_bytes=limit << 20),
@@ -85,7 +95,10 @@
     return body
 
 
-def taps_body(up, fwd, back_odd, back_even):
+def taps_body(info, up, info_out, fwd, back_odd, back_even):
+    for k in range(4):
+        info_out[k] = info[k]
+
     def rows_of(q, j):
         parts = ((2,), (1, 2), (0, 1), (0,))[q]
         total = up[parts[0], j].astype(F32)
@@ -187,7 +200,8 @@
                 w_order[at : at + 3 * chan] = w_in[t, i]
 
         deep = 27 * chan
-        for k in range(rows + 6):
+
+        def hidden_row(k):
             lhs = tall[k * 9 * chan : k * 9 * chan + deep, 0:cols]
             h = lax.dot_general(lhs, w_order[...], (((0,), (0,)), ((), ())), preferred_element_type=F32)
             h = h.astype(BF16)
@@ -206,13 +220,23 @@
             wide[at, 384:768] = act.astype(BF16)
             wide[at, 768:1152] = from_right(act).astype(BF16)
 
-        size = rows * cols
-        for part in range(2):
-            start = part * size
-            total = mm(wide[start : start + size], mid[2, 0])
-            total += mm(wide[start + cols : start + cols + size], mid[2, 1])
-            total += mm(wide[start + 2 * cols : start + 2 * cols + size], mid[2, 2])
-            conv[start : start + size] = total
+        def conv_rows(p, lanes):
+            start = 2 * p * cols
+            lhs = [wide[start + i * cols : start + (i + 2) * cols] for i in range(3)]
+            rhs = [mid[2, i, :, lanes] for i in range(3)]
+            conv[start : start + 2 * cols, lanes] = mm(jnp.concatenate(lhs, axis=1), jnp.concatenate(rhs, axis=0))
+
+        def rows_step(k):
+            return lambda: hidden_row(k)
+
+        def conv_step(p):
+            return [lambda: conv_rows(p, slice(0, 256)), lambda: conv_rows(p, slice(256, 384))]
+
+        for k in range(4):
+            hidden_row(k)
+        for p in range(rows // 2 + 2):
+            after = [rows_step(k) for k in (2 * p + 4, 2 * p + 5) if k < rows + 6]
+            weave(conv_step(p), after) if after else weave(conv_step(p))
 
     return body
 
@@ -229,7 +253,7 @@
 
     def body(
         info, hidden, conv, acc, got_even, got_odd, packed_even, packed_odd, own, fwd, back_odd, back_even, mid, w_in, gain,
-        out_gain, payload, reward, edge, p0, p1, g_odd, g_even, wide, lines,
+        out_gain, payload, reward, edge, p0, p1, g_odd, g_even, wide, t_odd, t_even, back, act_grad, hid, lines,
     ):
         even = info[0] == 0
         top, bottom = flag(info, 1), flag(info, 2)
@@ -257,8 +281,7 @@
         def row(ref, k):
             return ref[k * cols : (k + 1) * cols]
 
-        state_rows = []
-        for k in range(deep_rows):
+        def state_row(k):
             x = hidden[k].astype(F32) + row(conv, k)
             if 1 <= k <= rows + 2:
                 x = x + row(acc, k - 1)
@@ -277,10 +300,10 @@
             wide[at, 384:768] = x
             wide[at, 768:1152] = from_right(x32).astype(BF16)
 
-        for part in range(2):
-            at = slice(part * size, (part + 1) * size)
-            p0[at] = mm_t(wide[at, 0:768], fwd[0])
-            p1[at] = mm_t(wide[at, 384:1152], fwd[1])
+        def up_dot(p, b, n):
+            at = slice(2 * p * cols, (2 * p + 2) * cols)
+            lanes = slice(n * 256, n * 256 + 256)
+            (p0, p1)[b][at, lanes] = mm_t(wide[at, b * 384 : b * 384 + 768], fwd[b, lanes])
 
         lane = lax.broadcasted_iota(jnp.int32, (cols, 128), 1)
         low = lane < 64
@@ -305,8 +328,8 @@
                 d = r[:, k * 128 : k * 128 + 128].astype(F32) * pull_scale(y) * g
                 out.append((s, d))
             m0, m1 = both(*(s * d for s, d in out))
-            mm_ = jnp.where(mine, m0, m1)
-            return [i * (d - s * m) for (s, d), i, m in zip(out, (i0, i1, im), (m0, m1, mm_))], mine
+            mx = jnp.where(mine, m0, m1)
+            return [i * (d - s * m) for (s, d), i, m in zip(out, (i0, i1, im), (m0, m1, mx))], mine
 
         def store(g, target, k):
             (a0, a1, am), mine = g
@@ -318,52 +341,88 @@
             target[at, 512:640] = from_left(a1).astype(BF16)
             target[at, 640:768] = jnp.where(mine, from_right(am), from_left(am)).astype(BF16)
 
-        fine = rows + 3
-        for k in range(fine):
+        def pull_odd(k):
             a, b = slice(k * cols, (k + 1) * cols), slice((k + 1) * cols, (k + 2) * cols)
             v0 = p0[a, 256:384] + p0[b, 0:128]
             v1 = p1[a, 256:384] + p1[b, 0:128]
             vm = jnp.where(low, p0[a, 640:768] + p0[b, 512:640], p1[a, 640:768] + p1[b, 512:640])
             store(pull(v0, v1, vm, reward[2 * k], True), g_odd, k)
+
+        def pull_even(k):
+            a, b = slice(k * cols, (k + 1) * cols), slice((k + 1) * cols, (k + 2) * cols)
             v0 = p0[b, 128:256] + p0[a, 384:512]
             v1 = p1[b, 128:256] + p1[a, 384:512]
             vm = jnp.where(low, p1[b, 512:640] + p1[a, 640:768], p0[b, 512:640] + p0[a, 640:768])
             store(pull(v0, v1, vm, reward[2 * k + 1], False), g_even, k)
 
-        span = fine * cols
-        p0[0:span] = mm(g_odd[...], back_odd[...])
-        p1[0:span] = mm(g_even[...], back_even[...])
-        for k in range(rows + 2):
+        fine = rows + 3
+
+        def down_dot(first, number, odd, n):
+            at = slice(first * cols, (first + number) * cols)
+            lanes = slice(n * 256, n * 256 + 256)
+            if odd:
+                t_odd[at, lanes] = mm(g_odd[at], back_odd[:, lanes])
+            else:
+                t_even[at, lanes] = mm(g_even[at], back_even[:, lanes])
+
+        def block_row(k):
             a, b = slice(k * cols, (k + 1) * cols), slice((k + 1) * cols, (k + 2) * cols)
-            x = p0[b, 0:384] + p0[a, 384:768] + p1[a, 0:384] + p1[b, 384:768]
+            x = t_odd[b, 0:384] + t_odd[a, 384:768] + t_even[a, 0:384] + t_even[b, 384:768]
             if k == 0:
                 x = x * top
             if k == rows + 1:
                 x = x * bottom
             x = x.astype(BF16)
             x32 = x.astype(F32)
-            wide[a, 0:384] = from_right(x32).astype(BF16)
-            wide[a, 384:768] = x
-            wide[a, 768:1152] = from_left(x32).astype(BF16)
-
-        total = None
-        for i in range(3):
-            kernel = jnp.concatenate([mid[2, i, j * 384 : (j + 1) * 384] for j in range(3)], axis=1)
-            term = mm_t(wide[(2 - i) * cols : (2 - i) * cols + size], kernel)
-            total = term if total is None else total + term
-        p0[0:size, 0:384] = total
-        g = gain[...]
-        for k in range(rows):
+            back[a, 0:384] = from_right(x32).astype(BF16)
+            back[a, 384:768] = x
+            back[a, 768:1152] = from_left(x32).astype(BF16)
+
+        def mid_dot(p, n):
+            lanes = slice(n * 256, min(384, n * 256 + 256))
+            lhs = [back[(2 * p + 2 - i) * cols : (2 * p + 4 - i) * cols] for i in range(3)]
+            rhs = [mid[2, i, j * 384 + lanes.start : j * 384 + lanes.stop] for i in range(3) for j in range(3)]
+            at = slice(2 * p * cols, (2 * p + 2) * cols)
+            act_grad[at, lanes] = mm_t(jnp.concatenate(lhs, axis=1), jnp.concatenate(rhs, axis=1))
+
+        def hidden_pull(k):
+            g = gain[...]
             at = slice(k * cols, (k + 1) * cols)
             v = hidden[k + 2].astype(F32)
             inv = lax.rsqrt(jnp.mean(v * v, axis=1, keepdims=True) + EPS)
             s = v * inv
-            d = p0[at, 0:384] * pull_scale(s * g) * g
+            d = act_grad[at] * pull_scale(s * g) * g
             dv = inv * (d - s * jnp.mean(d * s, axis=1, keepdims=True))
-            block = wide[(k + 1) * cols : (k + 2) * cols, 384:768].astype(F32)
-            g_odd[at, 0:384] = (block + dv).astype(BF16)
-
-        z = mm_t(w_in[...], g_odd[0:size, 0:384])
+            block = back[(k + 1) * cols : (k + 2) * cols, 384:768].astype(F32)
+            hid[at] = (block + dv).astype(BF16)
+
+        def steps(f, *keys):
+            return [lambda key=key: f(*key) for key in keys]
+
+        def ups(p):
+            return steps(up_dot, *[(p, b, n) for n in range(3) for b in range(2)])
+
+        def downs(first, number):
+            return steps(down_dot, *[(first, number, odd, n) for odd in (True, False) for n in range(3)])
+
+        def pulls(*ks):
+            return [step for k in ks for step in steps(pull_odd, (k,)) + steps(pull_even, (k,))]
+
+        state_row(0)
+        state_row(1)
+        weave(ups(0), steps(state_row, (2,), (3,)))
+        weave(ups(1), steps(state_row, (4,), (5,)) + pulls(0))
+        weave(ups(2), steps(state_row, (6,), (7,)) + pulls(1, 2))
+        weave(ups(3) + downs(0, 2), pulls(3, 4))
+        weave(downs(2, 2), pulls(5, 6) + steps(block_row, (0,)))
+        weave(downs(4, 3), steps(block_row, (1,), (2,)))
+        block_row(3)
+        weave(steps(mid_dot, (0, 0), (0, 1)), steps(block_row, (4,), (5,)))
+        weave(steps(mid_dot, (1, 0), (1, 1)), steps(hidden_pull, (0,), (1,)))
+        hidden_pull(2)
+        hidden_pull(3)
+
+        z = mm_t(w_in[...], hid[...])
         place = lax.broadcasted_iota(jnp.int32, (chan, size), 1)
         col = lax.rem(place, cols)
         sums = []
@@ -381,15 +440,15 @@
         per_row = count // 2
         for u in range(count):
             pair, piece = u // per_row, u % per_row
+            parts = []
             for a in range(2):
                 at = (2 * pair + a) * cols + piece * width
-                payload[u, a * chan : (a + 1) * chan] = lines[0:chan, at : at + width].astype(BF16)
-            if pair == 0:
-                at = (rows - 1) * cols + piece * width
-                payload[u, 2 * chan : 3 * chan] = lines[2 * chan : 3 * chan, at : at + width].astype(BF16)
-            else:
-                at = piece * width
-                payload[u, 2 * chan : 3 * chan] = lines[chan : 2 * chan, at : at + width].astype(BF16)
+                parts.append(lines[0:chan, at : at + width])
+            at = piece * width + (0 if pair else (rows - 1) * cols)
+            first = chan if pair else 2 * chan
+            parts.append(lines[first : first + chan, at : at + width])
+            parts.append(jnp.zeros((chan, 128 - 3 * width), F32))
+            payload[u] = jnp.concatenate(parts, axis=1).astype(BF16)
 
     return body
 
@@ -399,26 +458,24 @@
 
     def body(info, order, got, out):
         pair = info[3]
-        w = lax.broadcasted_iota(jnp.int32, (width, tokens), 0)
-        pos = lax.broadcasted_iota(jnp.int32, (width, tokens), 1)
-        inner, outer = [None, None], [None, None]
+        lane = lax.broadcasted_iota(jnp.int32, (128, 4 * tokens), 0)
+        column = lax.broadcasted_iota(jnp.int32, (128, 4 * tokens), 1)
+        group = (lane >= width).astype(jnp.int32) + (lane >= 2 * width).astype(jnp.int32)
+        w = lane - group * width
+        part = jnp.where(group == 2, pair, group)
+        fixed = (2 * part + (w & 1)) * tokens + (w >> 1) - column
+        fixed = jnp.where(lane < 3 * width, fixed, -99999)
+        total = None
         for t in range(count):
             step = t + 1 - 2 * pair
             valid = jnp.logical_and(step >= 0, step < count)
-            beside = order[jnp.clip(step, 0, count - 1)]
-            for b in range(2):
-                want = 2 * pos + b - w
-                sel = (want == 2 * piece * order[t]).astype(F32).astype(BF16)
-                sel_e = (want == jnp.where(valid, 2 * piece * beside, -99999)).astype(F32).astype(BF16)
-                x = mm(got[t, 0 : 2 * chan], sel)
-                e = mm(got[t, 2 * chan : 3 * chan], sel_e)
-                inner[b] = x if inner[b] is None else inner[b] + x
-                outer[b] = e if outer[b] is None else outer[b] + e
-        for a in range(2):
-            mine = (pair == a).astype(F32)
-            for b in range(2):
-                at = (2 * a + b) * chan
-                out[at : at + chan] = inner[b][a * chan : (a + 1) * chan] + outer[b] * mine
+            beside = jnp.where(valid, piece * order[jnp.clip(step, 0, count - 1)], -9999)
+            begin = jnp.where(group == 2, beside, piece * order[t])
+            sel = (fixed + begin == 0).astype(F32).astype(BF16)
+            x = mm(got[t], sel)
+            total = x if total is None else total + x
+        for k in range(4):
+            out[k * chan : (k + 1) * chan] = total[:, k * tokens : (k + 1) * tokens]
 
     return body
 
@@ -454,17 +511,19 @@
     size = rows * cols
     edge_rows = 3 * cols + 2 * chan * rows
 
+    info, fwd, back_odd, back_even = call(
+        taps_body,
+        [((4,), jnp.int32), ((2, 768, 768), BF16), ((768, 768), BF16), ((768, 768), BF16)],
+        1, 1, [], 1e10, 16, 1,
+    )(info, up_t)
+
     own, send_even, send_odd = call(
         pack_body(rows, cols, o, chan),
         [((2 * rows, cols, 384), BF16), ((edge_rows, 384), BF16), ((edge_rows, 384), BF16)],
-        1, 3, [], 2e9, 16,
+        1, 3, [], 1e10, 16,
     )(info, reward_t, lat, lat_cached)
     packed_even = lax.ppermute(send_even, "tile", within)
     packed_odd = lax.ppermute(send_odd, "tile", across)
-
-    fwd, back_odd, back_even = call(
-        taps_body, [((2, 768, 768), BF16), ((768, 768), BF16), ((768, 768), BF16)], 0, 1, [], 1e9, 16
-    )(up_t)
 
     acc, part_even, part_odd = call(
         cached_body(rows, cols),
@@ -490,7 +549,7 @@
     width = 2 * cols // count
     (payload,) = call(
         back_body(rows, cols, chan, count, o),
-        [((count, 3 * chan, width), BF16)],
+        [((count, chan, 128), BF16)],
         1, 15,
         [
             pltpu.VMEM((2 * rows + 6, cols, 384), BF16),
@@ -500,9 +559,14 @@
             pltpu.VMEM(((rows + 3) * cols, 768), BF16),
             pltpu.VMEM(((rows + 3) * cols, 768), BF16),
             pltpu.VMEM(((rows + 4) * cols, 1152), BF16),
+            pltpu.VMEM(((rows + 3) * cols, 768), F32),
+            pltpu.VMEM(((rows + 3) * cols, 768), F32),
+            pltpu.VMEM(((rows + 2) * cols, 1152), BF16),
+            pltpu.VMEM((size, 384), F32),
+            pltpu.VMEM((size, 384), BF16),
             pltpu.VMEM((3 * chan, size), F32),
         ],
-        8e9, 32,
+        8e9, 36,
     )(
         info, hidden, conv, acc, got_even, got_odd, packed_even, packed_odd, own, fwd, back_odd, back_even, mid,
         w_in[2].reshape(9 * chan, mid_chan), gain, gain_out,

time: 55.6 us -> 51.2 us (0.921)
  local copies, waits for them, and re-layouts: 6.83 us -> 1.48 us
  Pallas kernels: 30.5 us -> 31.6 us
    unnamed x28 -> x22, local copies, waits for them, and re-layouts: 6.59 us -> 1.46 us
    pallas_call x2, Pallas kernels: 14.4 us -> 16.4 us  [the longest x1 15.3 us: shards(): call(back_body(rows, cols, chan, count, o), [((count, chan, 128), BF16)],...]
    pallas_call x1, Pallas kernels: 8.3 us -> 7.16 us  [shards(): call(current_body(rows, cols, chan), [((rows + 4, cols, 384), BF16), ((2...]
  transfers between devices with their start and end apart: 4 -> 4, of which waited for: 0 -> 0; matrix products, arithmetic and copies ran while one was open for 0% -> 0% of each run, Pallas kernels for 25% -> 23%
where the time goes in v2:
time: 51.2 us; the launch traced here: 51 us
  Pallas kernels  31.6 us (62%)
  blocking collectives  11.7 us (23%)
  starting transfers between devices  5.89 us (12%)
  local copies, waits for them, and re-layouts  1.48 us (3%)
    pallas_call x1, Pallas kernels, shards(): call(back_body(rows, cols, chan, count, o), [((count, chan, 128), BF16)],...  15.3 us
    all_to_all x1, blocking collectives, shards(): lax.all_to_all(payload, 'tile', split_axis=0, concat_axis=0, tiled=True)  11.7 us
    pallas_call x1, Pallas kernels, shards(): call(current_body(rows, cols, chan), [((rows + 4, cols, 384), BF16), ((2...  7.16 us
    pallas_call x1, Pallas kernels, shards(): call(cached_body(rows, cols), [((6 * cols, 384), F32), ((3 * cols, 384),...  4.7 us
    ppermute x1, starting transfers between devices, shards(): got_even = lax.ppermute(part_even, 'tile', within)  4.02 us
    pallas_call x1, Pallas kernels, shards(): call(pack_body(rows, cols, o, chan), [((2 * rows, cols, 384), BF16), ((ed...  1.7 us
    pallas_call x1, Pallas kernels, shards(): call(place_body(count, chan, width, tokens), [((4 * chan, tokens), F32)],...  1.6 us
    unnamed x22, local copies, waits for them, and re-layouts  1.46 us
  transfers between devices with their start and end apart: 4, of which 0 were waited for; matrix products, arithmetic and copies ran while one was open for 0% of the time, Pallas kernels for 23%

profile of v2, /device:TPU:0, one launch (start us, length us, event | category | flops | bytes accessed | tf_op | source)
XLA Modules:
  0.0 51.0 jit_solution(6496678566425689086)
XLA Ops:
  0.0 0.1 pad_add_fusion.info
  0.1 1.3 %copy-done.2 = bf16[3,3,384,192]{2,3,1,0:T(8,128)(2,1)S(1)} copy-done((bf16[3,3,384,192]{2,3,1,0:T(8,128)(2,1)S(1)}, bf16[3,3,384,192]{2,3,1,0:T(8,128)(2,1)}, u32[]{:S(2)}) %copy-start.2) | copy-done | bytes 1327128
  1.4 1.1 %shard_map.100 = (s32[4]{0:T(128)S(1)}, bf16[2,768,768]{2,1,0:T(8,128)(2,1)S(1)}, bf16[768,768]{1,0:T(8,128)(2,1)S(1)}, bf16[768,768]{1,0:T(8,128)(2,1)S(1)}) custom-call(s32[4]{0:T(128)S(1)} %pad_add_fusion.info, bf16[3,3,192,384]{3,2,1,0:T(8,128)(2,1)S(1)} %bitcast.21), custom_call_target="tpu_custom_call" | custom-call | flops 10000000000 | bytes 1048576 | tf_op jit(solution)/shard_map/pallas_call | solution.py:514
  2.6 0.0 slice-start.1
  2.6 0.1 copy-done.3
  2.7 0.0 copy-done.5
  2.7 0.0 copy-done.6
  2.7 1.7 %shard_map.101 = (bf16[8,160,384]{2,1,0:T(8,128)(2,1)S(1)}, bf16[608,384]{1,0:T(8,128)(2,1)S(1)}, bf16[608,384]{1,0:T(8,128)(2,1)S(1)}) custom-call(s32[4]{0:T(128)S(1)} %get-tuple-element.17.info, bf16[8,192,320]{2,1,0:T(8,128)(2,1)S(1)} %bitcast.22, bf16[4,16,160]{2,1,0:T(8,128)(2,1)S(1)} %bitcast.25, bf16[2,4,16,160]{3,2,1,0:T(8,128)(2,1)S(1)} %bitcast.23), custom_call_target="tpu_custom_call" | custom-call | flops 10000000000 | bytes 1048576 | tf_op jit(solution)/shard_map/pallas_call | solution.py:520
  4.4 0.5 %collective-permute-start = (bf16[608,384]{1,0:T(8,128)(2,1)S(1)}, bf16[608,384]{1,0:T(8,128)(2,1)S(1)}, u32[]{:S(2)}, u32[]{:S(2)}) collective-permute-start(bf16[608,384]{1,0:T(8,128)(2,1)S(1)} %get-tuple-element.18), channel_id=1, source_target_pairs={{0,1},{1,0},{2,3},{3,2},{4,5},{5,4},{6,7},{7,6},{8,9},{9,8},{10,11... | collective-permute-start | bytes 1400840 | tf_op jit(solution)/shard_map/ppermute | solution.py:525
  4.9 0.7 %collective-permute-start.1 = (bf16[608,384]{1,0:T(8,128)(2,1)S(1)}, bf16[608,384]{1,0:T(8,128)(2,1)S(1)}, u32[]{:S(2)}, u32[]{:S(2)}) collective-permute-start(bf16[608,384]{1,0:T(8,128)(2,1)S(1)} %get-tuple-element.19), channel_id=1, source_target_pairs={{0,0},{1,2},{2,1},{3,4},{4,3},{5,6},{6,5},{7,7},{8,8},{9,10},{10,9... | collective-permute-start | bytes 1400840 | tf_op jit(solution)/shard_map/ppermute | solution.py:526
  5.6 0.0 slice-done
  5.6 0.0 slice-done.1
  5.6 0.0 copy-done.4
  5.6 0.0 copy-start.8
  5.6 0.0 copy-start.7
  5.7 0.0 copy-start
  5.7 4.7 %shard_map.103 = (f32[960,384]{1,0:T(8,128)S(1)}, bf16[480,384]{1,0:T(8,128)(2,1)S(1)}, bf16[480,384]{1,0:T(8,128)(2,1)S(1)}) custom-call(s32[4]{0:T(128)S(1)} %get-tuple-element.17.info, bf16[2,4,160,384]{3,2,1,0:T(8,128)(2,1)S(1)} %copy-done.4, bf16[3,3,1152,384]{3,2,1,0:T(8,128)(2,1)S(1)} %bitcast.19), custom_call_target="tpu_custom_call" | custom-call | flops 4000000000 | bytes 1048576 | tf_op jit(solution)/shard_map/pallas_call | solution.py:528
  10.4 4.0 %collective-permute-start.2 = (bf16[480,384]{1,0:T(8,128)(2,1)S(1)}, bf16[480,384]{1,0:T(8,128)(2,1)S(1)}, u32[]{:S(2)}, u32[]{:S(2)}) collective-permute-start(bf16[480,384]{1,0:T(8,128)(2,1)S(1)} %get-tuple-element.23), channel_id=1, source_target_pairs={{0,1},{1,0},{2,3},{3,2},{4,5},{5,4},{6,7},{7,6},{8,9},{9,8},{10,11... | collective-permute-start | bytes 1105928 | tf_op jit(solution)/shard_map/ppermute | solution.py:533
  14.4 0.7 %collective-permute-start.3 = (bf16[480,384]{1,0:T(8,128)(2,1)S(1)}, bf16[480,384]{1,0:T(8,128)(2,1)S(1)}, u32[]{:S(2)}, u32[]{:S(2)}) collective-permute-start(bf16[480,384]{1,0:T(8,128)(2,1)S(1)} %get-tuple-element.24), channel_id=1, source_target_pairs={{0,0},{1,2},{2,1},{3,4},{4,3},{5,6},{6,5},{7,7},{8,8},{9,10},{10,9... | collective-permute-start | bytes 1105928 | tf_op jit(solution)/shard_map/ppermute | solution.py:534
  15.1 0.0 copy-done.8
  15.1 0.0 copy-done.7
  15.1 0.0 copy-done
  15.1 0.1 pad_maximum_fusion
  15.2 0.0 collective-permute-done.got_even.packed_even
  15.2 0.0 collective-permute-done.1.got_odd.packed_odd
  15.2 7.2 %shard_map.102 = (bf16[8,160,384]{2,1,0:T(8,128)(2,1)S(1)}, f32[1280,384]{1,0:T(8,128)S(1)}) custom-call(s32[4]{0:T(128)S(1)} %get-tuple-element.17.info, bf16[4,16,160]{2,1,0:T(8,128)(2,1)S(1)} %bitcast.26, bf16[2,4,16,160]{3,2,1,0:T(8,128)(2,1)S(1)} %bitcast.24, bf16[608,384]{1,0:T(8,128)(2,1)S(1)} %collective-permute-done.got_even.packed_even, ...), custom_call_target="tpu_custom_call" | custom-call | flops 5000000000 | bytes 1048576 | tf_op jit(solution)/shard_map/pallas_call | solution.py:536
  22.4 0.0 collective-permute-done.2.got_even
  22.4 0.0 collective-permute-done.3.got_odd
  22.4 0.0 copy-start.1
  22.4 15.3 %shard_map.104 = bf16[8,16,128]{2,1,0:T(8,128)(2,1)S(1)} custom-call(s32[4]{0:T(128)S(1)} %get-tuple-element.17.info, bf16[8,160,384]{2,1,0:T(8,128)(2,1)S(1)} %get-tuple-element.20.hidden, f32[1280,384]{1,0:T(8,128)S(1)} %get-tuple-element.21.conv, f32[960,384]{1,0:T(8,128)S(1)} %get-tuple-element.22.acc, ...), custom_call_target="tpu_custom_call" | custom-call | flops 8000000000 | bytes 1048576 | tf_op jit(solution)/shard_map/pallas_call | solution.py:550
  37.7 11.7 %all_to_all.5.got = bf16[8,16,128]{2,1,0:T(8,128)(2,1)S(1)} all-to-all(bf16[8,16,128]{2,1,0:T(8,128)(2,1)S(1)} %shard_map.104), channel_id=1, replica_groups=mesh['prompt'=4,'tile'=8] {'tile'}, dimensions={0} | all-to-all | bytes 65536 | tf_op jit(solution)/shard_map/all_to_all | solution.py:574
  49.4 1.6 %shard_map.105 = f32[64,160]{1,0:T(8,128)} custom-call(s32[4]{0:T(128)S(1)} %get-tuple-element.17.info, s32[8]{0:T(128)S(1)} %copy-done.1, bf16[8,16,128]{2,1,0:T(8,128)(2,1)S(1)} %all_to_all.5.got), custom_call_target="tpu_custom_call" | custom-call | flops 10000000 | bytes 1048576 | tf_op jit(solution)/shard_map/pallas_call | solution.py:576
  (11 shorter events, 0.0 us)
Async XLA Ops:
  0.1 1.3 %copy-start.2 = (bf16[3,3,384,192]{2,3,1,0:T(8,128)(2,1)S(1)}, bf16[3,3,384,192]{2,3,1,0:T(8,128)(2,1)}, u32[]{:S(2)}) copy-start(bf16[3,3,384,192]{2,3,1,0:T(8,128)(2,1)} %param.16) | copy-start | bytes 3981316
  1.4 1.3 %copy-start.3 = (bf16[8,320,192]{1,2,0:T(8,128)(2,1)S(1)}, bf16[8,320,192]{1,2,0:T(8,128)(2,1)}, u32[]{:S(2)}) copy-start(bf16[8,320,192]{1,2,0:T(8,128)(2,1)} %param.13) | copy-start | bytes 2949124
  1.4 1.3 %copy-start.5 = (bf16[2,4,160,16]{2,3,1,0:T(8,128)(2,1)S(1)}, bf16[2,4,160,16]{2,3,1,0:T(8,128)(2,1)}, u32[]{:S(2)}) copy-start(bf16[2,4,160,16]{2,3,1,0:T(8,128)(2,1)} %param.11) | copy-start | bytes 122884
  1.4 1.3 %copy-start.6 = (bf16[4,160,16]{1,2,0:T(8,128)(2,1)S(1)}, bf16[4,160,16]{1,2,0:T(8,128)(2,1)}, u32[]{:S(2)}) copy-start(bf16[4,160,16]{1,2,0:T(8,128)(2,1)} %param.10) | copy-start | bytes 61444
  1.4 4.2 %slice-start = ((s8[7962624]{0:T(1024)(128)(4,1)}), s8[4194304]{0:T(1024)(128)(4,1)S(1)}, s32[]{:S(2)}) async-start(s8[7962624]{0:T(1024)(128)(4,1)} %bitcast.17), calls=%async_computation.1 | async-start | bytes 8388608
  2.6 3.0 %slice-start.1 = ((s8[7962624]{0:T(1024)(128)(4,1)}), s8[3768320]{0:T(1024)(128)(4,1)S(1)}, s32[]{:S(2)}) async-start(s8[7962624]{0:T(1024)(128)(4,1)} %bitcast.17), calls=%async_computation.2 | async-start | bytes 7536640
  2.7 2.9 %copy-start.4 = (bf16[2,4,160,384]{3,2,1,0:T(8,128)(2,1)S(1)}, bf16[2,4,160,384]{3,2,1,0:T(8,128)(2,1)}, u32[]{:S(2)}) copy-start(bf16[2,4,160,384]{3,2,1,0:T(8,128)(2,1)} %features.1) | copy-start | bytes 2949124
  4.4 10.8 %collective-permute-start = (bf16[608,384]{1,0:T(8,128)(2,1)S(1)}, bf16[608,384]{1,0:T(8,128)(2,1)S(1)}, u32[]{:S(2)}, u32[]{:S(2)}) collective-permute-start(bf16[608,384]{1,0:T(8,128)(2,1)S(1)} %get-tuple-element.18), channel_id=1, source_target_pairs={{0,1},{1,0},{2,3},{3,2},{4,5},{5,4},{6,7},{7,6},{8,9},{9,8},{10,11... | collective-permute-start | bytes 1400840 | tf_op jit(solution)/shard_map/ppermute | solution.py:525
  4.9 10.3 %collective-permute-start.1 = (bf16[608,384]{1,0:T(8,128)(2,1)S(1)}, bf16[608,384]{1,0:T(8,128)(2,1)S(1)}, u32[]{:S(2)}, u32[]{:S(2)}) collective-permute-start(bf16[608,384]{1,0:T(8,128)(2,1)S(1)} %get-tuple-element.19), channel_id=1, source_target_pairs={{0,0},{1,2},{2,1},{3,4},{4,3},{5,6},{6,5},{7,7},{8,8},{9,10},{10,9... | collective-permute-start | bytes 1400840 | tf_op jit(solution)/shard_map/ppermute | solution.py:526
  5.6 9.4 %copy-start.8 = (f32[192]{0:T(256)S(1)}, f32[192]{0:T(256)}, u32[]{:S(2)}) copy-start(f32[192]{0:T(256)} %param.18) | copy-start | bytes 2308
  5.6 9.5 %copy-start.7 = (f32[384]{0:T(512)S(1)}, f32[384]{0:T(512)}, u32[]{:S(2)}) copy-start(f32[384]{0:T(512)} %param.17) | copy-start | bytes 4612
  5.7 9.5 %copy-start = (bf16[3,3,3,16,384]{4,3,2,1,0:T(8,128)(2,1)S(1)}, bf16[3,3,3,16,384]{4,3,2,1,0:T(8,128)(2,1)}, u32[]{:S(2)}) copy-start(bf16[3,3,3,16,384]{4,3,2,1,0:T(8,128)(2,1)} %param.14) | copy-start | bytes 995332
  10.4 12.0 %collective-permute-start.2 = (bf16[480,384]{1,0:T(8,128)(2,1)S(1)}, bf16[480,384]{1,0:T(8,128)(2,1)S(1)}, u32[]{:S(2)}, u32[]{:S(2)}) collective-permute-start(bf16[480,384]{1,0:T(8,128)(2,1)S(1)} %get-tuple-element.23), channel_id=1, source_target_pairs={{0,1},{1,0},{2,3},{3,2},{4,5},{5,4},{6,7},{7,6},{8,9},{9,8},{10,11... | collective-permute-start | bytes 1105928 | tf_op jit(solution)/shard_map/ppermute | solution.py:533
  14.4 8.0 %collective-permute-start.3 = (bf16[480,384]{1,0:T(8,128)(2,1)S(1)}, bf16[480,384]{1,0:T(8,128)(2,1)S(1)}, u32[]{:S(2)}, u32[]{:S(2)}) collective-permute-start(bf16[480,384]{1,0:T(8,128)(2,1)S(1)} %get-tuple-element.24), channel_id=1, source_target_pairs={{0,0},{1,2},{2,1},{3,4},{4,3},{5,6},{6,5},{7,7},{8,8},{9,10},{10,9... | collective-permute-start | bytes 1105928 | tf_op jit(solution)/shard_map/ppermute | solution.py:534
  22.4 27.0 %copy-start.1 = (s32[8]{0:T(128)S(1)}, s32[8]{0:T(128)}, u32[]{:S(2)}) copy-start(s32[8]{0:T(128)} %order.1) | copy-start | bytes 100

commit v3 on v2

--- a/solution.py
+++ b/solution.py
@@ -106,15 +106,19 @@
             total = total + up[i, j].astype(F32)
         return total
 
+    rest = []
     for q in range(4):
         c0, c1, c2 = (rows_of(q, j) for j in range(3))
         tap = [t.astype(BF16) for t in (c2, c1 + c2, c0 + c1, c0)]
+        rest.append([t[128:] for t in tap])
         for b, order in ((0, (3, 1)), (1, (2, 0))):
-            place = q if b == 0 else (1, 0, 3, 2)[q]
             for side, p in enumerate(order):
-                lanes = slice(side * 384, side * 384 + 384)
-                fwd[b, q * 128 : q * 128 + 128, lanes] = tap[p][:128]
-                fwd[b, 512 + place * 64 : 576 + place * 64, lanes] = tap[p][128:]
+                fwd[b, side * 384 : side * 384 + 384, q * 128 : q * 128 + 128] = tap[p][:128].T
+                if q % 2 == 1:
+                    pair = (q - 1, q) if b == 0 else (q, q - 1)
+                    both = jnp.concatenate([rest[k][p] for k in pair], axis=0)
+                    at = 512 + (q // 2) * 128
+                    fwd[b, side * 384 : side * 384 + 384, at : at + 128] = both.T
         target, side = ((back_odd, 1), (back_even, 0), (back_odd, 0), (back_even, 1))[q]
         lanes = slice(side * 384, side * 384 + 384)
         for block, (p0, p1) in enumerate(((1, 2), (3, 0))):
@@ -126,10 +130,10 @@
             target[base + 320 : base + 384, lanes] = tap[high][128:]
 
 
-def cached_body(rows, cols):
+def cached_body(rows, cols, count, width, tokens):
     size = rows * cols
 
-    def body(info, features, mid, acc, send_even, send_odd, wide):
+    def body(info, order, features, mid, acc, send_even, send_odd, mid_t, sel, wide):
         for t in range(2):
             for r in range(rows):
                 at = slice(r * cols, (r + 1) * cols)
@@ -142,6 +146,11 @@
         lhs = wide[...]
         kernels = [jnp.concatenate([mid[0, i], mid[1, i]], axis=0) for i in range(3)]
         pair = mm(lhs, jnp.concatenate([kernels[0], kernels[1]], axis=1))
+        for i in range(3):
+            for j in range(3):
+                at = (i * 3 + j) * 384
+                mid_t[at : at + 384] = mid[2, i, j * 384 : (j + 1) * 384].T
+        placing(info, order, sel, count, width, tokens)
         zero = jnp.zeros((cols, 384), F32)
         acc[0:cols] = zero
         acc[cols : 2 * cols] = zero
@@ -158,7 +167,7 @@
     per = chan * rows
     base = 3 * cols
 
-    def body(info, latent, cached, got_even, got_odd, w_in, mid, gain, hidden, conv, lat, tall, wide, w_order):
+    def body(info, latent, cached, got_even, got_odd, w_in, mid, gain, hidden, conv, lat, tall, wide, w_order, flat):
         even = info[0] == 0
         lat[...] = jnp.zeros_like(lat)
 
@@ -194,16 +203,16 @@
                 tall[at : at + chan] = pltpu.roll(x, 1, 1).astype(BF16)
                 tall[at + chan : at + 2 * chan] = x.astype(BF16)
                 tall[at + 2 * chan : at + 3 * chan] = pltpu.roll(x, 255, 1).astype(BF16)
+            flat[r, :, 0 : 9 * chan] = tall[r * 9 * chan : (r + 1) * 9 * chan, 0:cols].T
         for i in range(3):
             for t in range(3):
                 at = (i * 3 + t) * 3 * chan
                 w_order[at : at + 3 * chan] = w_in[t, i]
 
-        deep = 27 * chan
+        deep = 9 * chan
 
         def hidden_row(k):
-            lhs = tall[k * 9 * chan : k * 9 * chan + deep, 0:cols]
-            h = lax.dot_general(lhs, w_order[...], (((0,), (0,)), ((), ())), preferred_element_type=F32)
+            h = sum(mm(flat[k + i, :, 0:deep], w_order[i * deep : (i + 1) * deep]) for i in range(3))
             h = h.astype(BF16)
             if 1 <= k <= rows + 4:
                 hidden[k - 1] = h
@@ -252,7 +261,7 @@
     width = 2 * cols // count
 
     def body(
-        info, hidden, conv, acc, got_even, got_odd, packed_even, packed_odd, own, fwd, back_odd, back_even, mid, w_in, gain,
+        info, hidden, conv, acc, got_even, got_odd, packed_even, packed_odd, own, fwd, back_odd, back_even, mid_t, w_in, gain,
         out_gain, payload, reward, edge, p0, p1, g_odd, g_even, wide, t_odd, t_even, back, act_grad, hid, lines,
     ):
         even = info[0] == 0
@@ -303,7 +312,7 @@
         def up_dot(p, b, n):
             at = slice(2 * p * cols, (2 * p + 2) * cols)
             lanes = slice(n * 256, n * 256 + 256)
-            (p0, p1)[b][at, lanes] = mm_t(wide[at, b * 384 : b * 384 + 768], fwd[b, lanes])
+            (p0, p1)[b][at, lanes] = mm(wide[at, b * 384 : b * 384 + 768], fwd[b, :, lanes])
 
         lane = lax.broadcasted_iota(jnp.int32, (cols, 128), 1)
         low = lane < 64
@@ -381,9 +390,8 @@
         def mid_dot(p, n):
             lanes = slice(n * 256, min(384, n * 256 + 256))
             lhs = [back[(2 * p + 2 - i) * cols : (2 * p + 4 - i) * cols] for i in range(3)]
-            rhs = [mid[2, i, j * 384 + lanes.start : j * 384 + lanes.stop] for i in range(3) for j in range(3)]
             at = slice(2 * p * cols, (2 * p + 2) * cols)
-            act_grad[at, lanes] = mm_t(jnp.concatenate(lhs, axis=1), jnp.concatenate(rhs, axis=1))
+            act_grad[at, lanes] = mm(jnp.concatenate(lhs, axis=1), mid_t[:, lanes])
 
         def hidden_pull(k):
             g = gain[...]
@@ -453,27 +461,29 @@
     return body
 
 
-def place_body(count, chan, width, tokens):
+def placing(info, order, sel, count, width, tokens):
     piece = width // 2
-
-    def body(info, order, got, out):
-        pair = info[3]
-        lane = lax.broadcasted_iota(jnp.int32, (128, 4 * tokens), 0)
-        column = lax.broadcasted_iota(jnp.int32, (128, 4 * tokens), 1)
-        group = (lane >= width).astype(jnp.int32) + (lane >= 2 * width).astype(jnp.int32)
-        w = lane - group * width
-        part = jnp.where(group == 2, pair, group)
-        fixed = (2 * part + (w & 1)) * tokens + (w >> 1) - column
-        fixed = jnp.where(lane < 3 * width, fixed, -99999)
-        total = None
-        for t in range(count):
-            step = t + 1 - 2 * pair
-            valid = jnp.logical_and(step >= 0, step < count)
-            beside = jnp.where(valid, piece * order[jnp.clip(step, 0, count - 1)], -9999)
-            begin = jnp.where(group == 2, beside, piece * order[t])
-            sel = (fixed + begin == 0).astype(F32).astype(BF16)
-            x = mm(got[t], sel)
-            total = x if total is None else total + x
+    pair = info[3]
+    lane = lax.broadcasted_iota(jnp.int32, (128, 4 * tokens), 0)
+    column = lax.broadcasted_iota(jnp.int32, (128, 4 * tokens), 1)
+    group = (lane >= width).astype(jnp.int32) + (lane >= 2 * width).astype(jnp.int32)
+    w = lane - group * width
+    part = jnp.where(group == 2, pair, group)
+    fixed = (2 * part + (w & 1)) * tokens + (w >> 1) - column
+    fixed = jnp.where(lane < 3 * width, fixed, -99999)
+    for t in range(count):
+        step = t + 1 - 2 * pair
+        valid = jnp.logical_and(step >= 0, step < count)
+        beside = jnp.where(valid, piece * order[jnp.clip(step, 0, count - 1)], -9999)
+        begin = jnp.where(group == 2, beside, piece * order[t])
+        sel[t] = (fixed + begin == 0).astype(F32).astype(BF16)
+
+
+def place_body(count, chan, tokens):
+    def body(sel, got, out):
+        total = mm(got[0], sel[0])
+        for t in range(1, count):
+            total += mm(got[t], sel[t])
         for k in range(4):
             out[k * chan : (k + 1) * chan] = total[:, k * tokens : (k + 1) * tokens]
 
@@ -525,11 +535,16 @@
     packed_even = lax.ppermute(send_even, "tile", within)
     packed_odd = lax.ppermute(send_odd, "tile", across)
 
-    acc, part_even, part_odd = call(
-        cached_body(rows, cols),
-        [((6 * cols, 384), F32), ((3 * cols, 384), BF16), ((3 * cols, 384), BF16)],
-        1, 2, [pltpu.VMEM((size, 2304), BF16)], 4e9, 24,
-    )(info, cached_features, mid)
+    width = 2 * cols // count
+    tokens = size // 4
+    acc, part_even, part_odd, mid_t, sel = call(
+        cached_body(rows, cols, count, width, tokens),
+        [
+            ((6 * cols, 384), F32), ((3 * cols, 384), BF16), ((3 * cols, 384), BF16), ((3456, 384), BF16),
+            ((count, 128, 4 * tokens), BF16),
+        ],
+        2, 2, [pltpu.VMEM((size, 2304), BF16)], 4e9, 24,
+    )(info, shard_order, cached_features, mid)
     got_even = lax.ppermute(part_even, "tile", within)
     got_odd = lax.ppermute(part_odd, "tile", across)
 
@@ -542,11 +557,11 @@
             pltpu.VMEM((27 * rows * chan, 256), BF16),
             pltpu.VMEM(((rows + 6) * cols, 1152), BF16),
             pltpu.VMEM((27 * chan, 384), BF16),
+            pltpu.VMEM((3 * rows, cols, 256), BF16),
         ],
         5e9, 24,
     )(info, lat, lat_cached, packed_even, packed_odd, w_in, mid, gain)
 
-    width = 2 * cols // count
     (payload,) = call(
         back_body(rows, cols, chan, count, o),
         [((count, chan, 128), BF16)],
@@ -568,14 +583,11 @@
         ],
         8e9, 36,
     )(
-        info, hidden, conv, acc, got_even, got_odd, packed_even, packed_odd, own, fwd, back_odd, back_even, mid,
+        info, hidden, conv, acc, got_even, got_odd, packed_even, packed_odd, own, fwd, back_odd, back_even, mid_t,
         w_in[2].reshape(9 * chan, mid_chan), gain, gain_out,
     )
     received = lax.all_to_all(payload, "tile", split_axis=0, concat_axis=0, tiled=True)
-    tokens = size // 4
-    (placed,) = call(place_body(count, chan, width, tokens), [((4 * chan, tokens), F32)], 2, 1, [], 1e7, 16)(
-        info, shard_order, received
-    )
+    (placed,) = call(place_body(count, chan, tokens), [((4 * chan, tokens), F32)], 0, 2, [], 1e7, 16)(sel, received)
     return placed.T
 
 

time: 51.2 us -> 50.1 us (0.979)
  Pallas kernels: 31.6 us -> 30.5 us
    pallas_call x1, Pallas kernels: 15.3 us -> 13 us  [shards(): call(back_body(rows, cols, chan, count, o), [((count, chan, 128), BF16)],...]
    pallas_call x1, Pallas kernels: 1.15 us -> 1.93 us  [shards(): call(taps_body, [((4,), jnp.int32), ((2, 768, 768), BF16), ((768, 768), B...]
    pallas_call x1, Pallas kernels: 7.16 us -> 7.67 us  [shards(): call(current_body(rows, cols, chan), [((rows + 4, cols, 384), BF16), ((2...]
  transfers between devices with their start and end apart: 4 -> 4, of which waited for: 0 -> 0; matrix products, arithmetic and copies ran while one was open for 0% -> 0% of each run, Pallas kernels for 23% -> 26%
where the time goes in v3:
time: 50.1 us; the launch traced here: 49.9 us
  Pallas kernels  30.5 us (61%)
  blocking collectives  11.7 us (23%)
  starting transfers between devices  5.87 us (12%)
  local copies, waits for them, and re-layouts  1.4 us (3%)
    pallas_call x1, Pallas kernels, shards(): call(back_body(rows, cols, chan, count, o), [((count, chan, 128), BF16)],...  13 us
    all_to_all x1, blocking collectives, shards(): lax.all_to_all(payload, 'tile', split_axis=0, concat_axis=0, tiled=True)  11.7 us
    pallas_call x1, Pallas kernels, shards(): call(current_body(rows, cols, chan), [((rows + 4, cols, 384), BF16), ((2...  7.67 us
    pallas_call x1, Pallas kernels, shards(): call(cached_body(rows, cols, count, width, tokens), [((6 * cols, 384), F3...  5.26 us
    ppermute x1, starting transfers between devices, shards(): got_even = lax.ppermute(part_even, 'tile', within)  4 us
    pallas_call x1, Pallas kernels, shards(): call(taps_body, [((4,), jnp.int32), ((2, 768, 768), BF16), ((768, 768), B...  1.93 us
    pallas_call x1, Pallas kernels, shards(): call(pack_body(rows, cols, o, chan), [((2 * rows, cols, 384), BF16), ((ed...  1.7 us
    unnamed x22, local copies, waits for them, and re-layouts  1.38 us
  transfers between devices with their start and end apart: 4, of which 0 were waited for; matrix products, arithmetic and copies ran while one was open for 0% of the time, Pallas kernels for 26%

profile of v3, /device:TPU:0, one launch (start us, length us, event | category | flops | bytes accessed | tf_op | source)
XLA Modules:
  0.0 49.9 jit_solution(10436193743762542880)
XLA Ops:
  0.0 0.1 pad_add_fusion.info
  0.1 1.3 %copy-done.1 = bf16[3,3,384,192]{2,3,1,0:T(8,128)(2,1)S(1)} copy-done((bf16[3,3,384,192]{2,3,1,0:T(8,128)(2,1)S(1)}, bf16[3,3,384,192]{2,3,1,0:T(8,128)(2,1)}, u32[]{:S(2)}) %copy-start.1) | copy-done | bytes 1327128
  1.4 1.9 %shard_map.100 = (s32[4]{0:T(128)S(1)}, bf16[2,768,768]{2,1,0:T(8,128)(2,1)S(1)}, bf16[768,768]{1,0:T(8,128)(2,1)S(1)}, bf16[768,768]{1,0:T(8,128)(2,1)S(1)}) custom-call(s32[4]{0:T(128)S(1)} %pad_add_fusion.info, bf16[3,3,192,384]{3,2,1,0:T(8,128)(2,1)S(1)} %bitcast.20), custom_call_target="tpu_custom_call" | custom-call | flops 10000000000 | bytes 1048576 | tf_op jit(solution)/shard_map/pallas_call | solution.py:524
  3.4 0.0 slice-start.1
  3.4 0.0 copy-done.2
  3.4 0.0 copy-done.4
  3.4 0.0 copy-done.5
  3.4 0.0 copy-start.3
  3.4 0.0 copy-start.6
  3.4 1.7 %shard_map.102 = (bf16[8,160,384]{2,1,0:T(8,128)(2,1)S(1)}, bf16[608,384]{1,0:T(8,128)(2,1)S(1)}, bf16[608,384]{1,0:T(8,128)(2,1)S(1)}) custom-call(s32[4]{0:T(128)S(1)} %get-tuple-element.19.info, bf16[8,192,320]{2,1,0:T(8,128)(2,1)S(1)} %bitcast.21, bf16[4,16,160]{2,1,0:T(8,128)(2,1)S(1)} %bitcast.24, bf16[2,4,16,160]{3,2,1,0:T(8,128)(2,1)S(1)} %bitcast.22), custom_call_target="tpu_custom_call" | custom-call | flops 10000000000 | bytes 1048576 | tf_op jit(solution)/shard_map/pallas_call | solution.py:530
  5.1 0.5 %collective-permute-start = (bf16[608,384]{1,0:T(8,128)(2,1)S(1)}, bf16[608,384]{1,0:T(8,128)(2,1)S(1)}, u32[]{:S(2)}, u32[]{:S(2)}) collective-permute-start(bf16[608,384]{1,0:T(8,128)(2,1)S(1)} %get-tuple-element.21), channel_id=1, source_target_pairs={{0,1},{1,0},{2,3},{3,2},{4,5},{5,4},{6,7},{7,6},{8,9},{9,8},{10,11... | collective-permute-start | bytes 1400840 | tf_op jit(solution)/shard_map/ppermute | solution.py:535
  5.6 0.7 %collective-permute-start.1 = (bf16[608,384]{1,0:T(8,128)(2,1)S(1)}, bf16[608,384]{1,0:T(8,128)(2,1)S(1)}, u32[]{:S(2)}, u32[]{:S(2)}) collective-permute-start(bf16[608,384]{1,0:T(8,128)(2,1)S(1)} %get-tuple-element.22), channel_id=1, source_target_pairs={{0,0},{1,2},{2,1},{3,4},{4,3},{5,6},{6,5},{7,7},{8,8},{9,10},{10,9... | collective-permute-start | bytes 1400840 | tf_op jit(solution)/shard_map/ppermute | solution.py:536
  6.3 0.0 slice-done
  6.3 0.0 slice-done.1
  6.4 0.0 copy-done.3
  6.4 0.0 copy-done.6
  6.4 0.0 copy-start.7
  6.4 0.0 copy-start
  6.4 0.0 copy-start.8
  6.4 5.3 %shard_map.101 = (f32[960,384]{1,0:T(8,128)S(1)}, bf16[480,384]{1,0:T(8,128)(2,1)S(1)}, bf16[480,384]{1,0:T(8,128)(2,1)S(1)}, bf16[3456,384]{1,0:T(8,128)(2,1)S(1)}, bf16[8,128,640]{2,1,0:T(8,128)(2,1)S(1)}) custom-call(s32[4]{0:T(128)S(1)} %get-tuple-element.19.info, s32[8]{0:T(128)S(1)} %copy-done.6, bf16[2,4,160,384]{3,2,1,0:T(8,128)(2,1)S(1)} %copy-done.3, ...), custom_call_target="tpu_custom_call" | custom-call | flops 4000000000 | bytes 1048576 | tf_op jit(solution)/shard_map/pallas_call | solution.py:540
  11.7 4.0 %collective-permute-start.2 = (bf16[480,384]{1,0:T(8,128)(2,1)S(1)}, bf16[480,384]{1,0:T(8,128)(2,1)S(1)}, u32[]{:S(2)}, u32[]{:S(2)}) collective-permute-start(bf16[480,384]{1,0:T(8,128)(2,1)S(1)} %get-tuple-element.26), channel_id=1, source_target_pairs={{0,1},{1,0},{2,3},{3,2},{4,5},{5,4},{6,7},{7,6},{8,9},{9,8},{10,11... | collective-permute-start | bytes 1105928 | tf_op jit(solution)/shard_map/ppermute | solution.py:548
  15.7 0.7 %collective-permute-start.3 = (bf16[480,384]{1,0:T(8,128)(2,1)S(1)}, bf16[480,384]{1,0:T(8,128)(2,1)S(1)}, u32[]{:S(2)}, u32[]{:S(2)}) collective-permute-start(bf16[480,384]{1,0:T(8,128)(2,1)S(1)} %get-tuple-element.27), channel_id=1, source_target_pairs={{0,0},{1,2},{2,1},{3,4},{4,3},{5,6},{6,5},{7,7},{8,8},{9,10},{10,9... | collective-permute-start | bytes 1105928 | tf_op jit(solution)/shard_map/ppermute | solution.py:549
  16.4 0.0 copy-done.7
  16.4 0.1 pad_maximum_fusion
  16.5 0.0 collective-permute-done.got_even.packed_even
  16.5 0.0 collective-permute-done.1.got_odd.packed_odd
  16.5 7.7 %shard_map.103 = (bf16[8,160,384]{2,1,0:T(8,128)(2,1)S(1)}, f32[1280,384]{1,0:T(8,128)S(1)}) custom-call(s32[4]{0:T(128)S(1)} %get-tuple-element.19.info, bf16[4,16,160]{2,1,0:T(8,128)(2,1)S(1)} %bitcast.25, bf16[2,4,16,160]{3,2,1,0:T(8,128)(2,1)S(1)} %bitcast.23, bf16[608,384]{1,0:T(8,128)(2,1)S(1)} %collective-permute-done.got_even.packed_even, ...), custom_call_target="tpu_custom_call" | custom-call | flops 5000000000 | bytes 1048576 | tf_op jit(solution)/shard_map/pallas_call | solution.py:551
  24.2 0.0 collective-permute-done.2.got_even
  24.2 0.0 collective-permute-done.3.got_odd
  24.2 13.0 %shard_map.104 = bf16[8,16,128]{2,1,0:T(8,128)(2,1)S(1)} custom-call(s32[4]{0:T(128)S(1)} %get-tuple-element.19.info, bf16[8,160,384]{2,1,0:T(8,128)(2,1)S(1)} %get-tuple-element.23.hidden, f32[1280,384]{1,0:T(8,128)S(1)} %get-tuple-element.24.conv, f32[960,384]{1,0:T(8,128)S(1)} %get-tuple-element.25.acc, ...), custom_call_target="tpu_custom_call" | custom-call | flops 8000000000 | bytes 1048576 | tf_op jit(solution)/shard_map/pallas_call | solution.py:565
  37.2 11.7 %all_to_all.5.got = bf16[8,16,128]{2,1,0:T(8,128)(2,1)S(1)} all-to-all(bf16[8,16,128]{2,1,0:T(8,128)(2,1)S(1)} %shard_map.104), channel_id=1, replica_groups=mesh['prompt'=4,'tile'=8] {'tile'}, dimensions={0} | all-to-all | bytes 65536 | tf_op jit(solution)/shard_map/all_to_all | solution.py:589
  48.9 1.0 %shard_map.105 = f32[64,160]{1,0:T(8,128)} custom-call(bf16[8,128,640]{2,1,0:T(8,128)(2,1)S(1)} %get-tuple-element.20.sel, bf16[8,16,128]{2,1,0:T(8,128)(2,1)S(1)} %all_to_all.5.got), custom_call_target="tpu_custom_call" | custom-call | flops 10000000 | bytes 1048576 | tf_op jit(solution)/shard_map/pallas_call | solution.py:590
  (11 shorter events, 0.0 us)
Async XLA Ops:
  0.1 1.3 %copy-start.1 = (bf16[3,3,384,192]{2,3,1,0:T(8,128)(2,1)S(1)}, bf16[3,3,384,192]{2,3,1,0:T(8,128)(2,1)}, u32[]{:S(2)}) copy-start(bf16[3,3,384,192]{2,3,1,0:T(8,128)(2,1)} %param.16) | copy-start | bytes 3981316
  1.4 2.0 %copy-start.2 = (bf16[8,320,192]{1,2,0:T(8,128)(2,1)S(1)}, bf16[8,320,192]{1,2,0:T(8,128)(2,1)}, u32[]{:S(2)}) copy-start(bf16[8,320,192]{1,2,0:T(8,128)(2,1)} %param.13) | copy-start | bytes 2949124
  1.4 2.0 %copy-start.4 = (bf16[2,4,160,16]{2,3,1,0:T(8,128)(2,1)S(1)}, bf16[2,4,160,16]{2,3,1,0:T(8,128)(2,1)}, u32[]{:S(2)}) copy-start(bf16[2,4,160,16]{2,3,1,0:T(8,128)(2,1)} %param.11) | copy-start | bytes 122884
  1.4 2.0 %copy-start.5 = (bf16[4,160,16]{1,2,0:T(8,128)(2,1)S(1)}, bf16[4,160,16]{1,2,0:T(8,128)(2,1)}, u32[]{:S(2)}) copy-start(bf16[4,160,16]{1,2,0:T(8,128)(2,1)} %param.10) | copy-start | bytes 61444
  1.4 4.9 %slice-start = ((s8[7962624]{0:T(1024)(128)(4,1)}), s8[4194304]{0:T(1024)(128)(4,1)S(1)}, s32[]{:S(2)}) async-start(s8[7962624]{0:T(1024)(128)(4,1)} %bitcast.16), calls=%async_computation.1 | async-start | bytes 8388608
  3.4 3.0 %slice-start.1 = ((s8[7962624]{0:T(1024)(128)(4,1)}), s8[3768320]{0:T(1024)(128)(4,1)S(1)}, s32[]{:S(2)}) async-start(s8[7962624]{0:T(1024)(128)(4,1)} %bitcast.16), calls=%async_computation.2 | async-start | bytes 7536640
  3.4 3.0 %copy-start.3 = (bf16[2,4,160,384]{3,2,1,0:T(8,128)(2,1)S(1)}, bf16[2,4,160,384]{3,2,1,0:T(8,128)(2,1)}, u32[]{:S(2)}) copy-start(bf16[2,4,160,384]{3,2,1,0:T(8,128)(2,1)} %features.1) | copy-start | bytes 2949124
  3.4 3.0 %copy-start.6 = (s32[8]{0:T(128)S(1)}, s32[8]{0:T(128)}, u32[]{:S(2)}) copy-start(s32[8]{0:T(128)} %order.1) | copy-start | bytes 100
  5.1 11.4 %collective-permute-start = (bf16[608,384]{1,0:T(8,128)(2,1)S(1)}, bf16[608,384]{1,0:T(8,128)(2,1)S(1)}, u32[]{:S(2)}, u32[]{:S(2)}) collective-permute-start(bf16[608,384]{1,0:T(8,128)(2,1)S(1)} %get-tuple-element.21), channel_id=1, source_target_pairs={{0,1},{1,0},{2,3},{3,2},{4,5},{5,4},{6,7},{7,6},{8,9},{9,8},{10,11... | collective-permute-start | bytes 1400840 | tf_op jit(solution)/shard_map/ppermute | solution.py:535
  5.6 10.9 %collective-permute-start.1 = (bf16[608,384]{1,0:T(8,128)(2,1)S(1)}, bf16[608,384]{1,0:T(8,128)(2,1)S(1)}, u32[]{:S(2)}, u32[]{:S(2)}) collective-permute-start(bf16[608,384]{1,0:T(8,128)(2,1)S(1)} %get-tuple-element.22), channel_id=1, source_target_pairs={{0,0},{1,2},{2,1},{3,4},{4,3},{5,6},{6,5},{7,7},{8,8},{9,10},{10,9... | collective-permute-start | bytes 1400840 | tf_op jit(solution)/shard_map/ppermute | solution.py:536
  6.4 10.0 %copy-start.7 = (f32[384]{0:T(512)S(1)}, f32[384]{0:T(512)}, u32[]{:S(2)}) copy-start(f32[384]{0:T(512)} %param.17) | copy-start | bytes 4612
  6.4 10.0 %copy-start = (bf16[3,3,3,16,384]{4,3,2,1,0:T(8,128)(2,1)S(1)}, bf16[3,3,3,16,384]{4,3,2,1,0:T(8,128)(2,1)}, u32[]{:S(2)}) copy-start(bf16[3,3,3,16,384]{4,3,2,1,0:T(8,128)(2,1)} %param.14) | copy-start | bytes 995332
  6.4 10.0 %copy-start.8 = (f32[192]{0:T(256)S(1)}, f32[192]{0:T(256)}, u32[]{:S(2)}) copy-start(f32[192]{0:T(256)} %param.18) | copy-start | bytes 2308
  11.7 12.5 %collective-permute-start.2 = (bf16[480,384]{1,0:T(8,128)(2,1)S(1)}, bf16[480,384]{1,0:T(8,128)(2,1)S(1)}, u32[]{:S(2)}, u32[]{:S(2)}) collective-permute-start(bf16[480,384]{1,0:T(8,128)(2,1)S(1)} %get-tuple-element.26), channel_id=1, source_target_pairs={{0,1},{1,0},{2,3},{3,2},{4,5},{5,4},{6,7},{7,6},{8,9},{9,8},{10,11... | collective-permute-start | bytes 1105928 | tf_op jit(solution)/shard_map/ppermute | solution.py:548
  15.7 8.5 %collective-permute-start.3 = (bf16[480,384]{1,0:T(8,128)(2,1)S(1)}, bf16[480,384]{1,0:T(8,128)(2,1)S(1)}, u32[]{:S(2)}, u32[]{:S(2)}) collective-permute-start(bf16[480,384]{1,0:T(8,128)(2,1)S(1)} %get-tuple-element.27), channel_id=1, source_target_pairs={{0,0},{1,2},{2,1},{3,4},{4,3},{5,6},{6,5},{7,7},{8,8},{9,10},{10,9... | collective-permute-start | bytes 1105928 | tf_op jit(solution)/shard_map/ppermute | solution.py:549

commit v4 on v3

--- a/solution.py
+++ b/solution.py
@@ -10,16 +10,6 @@
 BF16 = jnp.bfloat16
 VM = pl.BlockSpec(memory_space=pltpu.VMEM)
 SM = pl.BlockSpec(memory_space=pltpu.SMEM)
-
-
-def weave(*groups):
-    total = max(len(g) for g in groups)
-    done = [0] * len(groups)
-    for k in range(total):
-        for n, g in enumerate(groups):
-            while done[n] * total < (k + 1) * len(g):
-                g[done[n]]()
-                done[n] += 1
 
 
 def call(body, outs, n_smem, n_vmem, scratch, flops, limit, smem_outs=0):
@@ -151,14 +141,17 @@
                 at = (i * 3 + j) * 384
                 mid_t[at : at + 384] = mid[2, i, j * 384 : (j + 1) * 384].T
         placing(info, order, sel, count, width, tokens)
-        zero = jnp.zeros((cols, 384), F32)
-        acc[0:cols] = zero
-        acc[cols : 2 * cols] = zero
-        acc[2 * cols :] = pair[:, :384]
-        acc[cols : cols + size] += pair[:, 384:]
-        acc[0:size] += mm(lhs, kernels[2])
+        last_kernel = mm(lhs, kernels[2])
+        for k in range(rows + 4):
+            total = jnp.zeros((cols, 384), F32)
+            for i, part in enumerate((pair[:, :384], pair[:, 384:], last_kernel)):
+                r = k - 3 + i
+                if 0 <= r < rows:
+                    total = total + part[r * cols : (r + 1) * cols]
+            acc[k] = total
         for send, last in ((send_even, 1 - info[0]), (send_odd, info[0])):
-            send[...] = acc[pl.ds(pl.multiple_of(last * 3 * cols, 3 * cols), 3 * cols)].astype(BF16)
+            for k in range(3):
+                send[k * cols : (k + 1) * cols] = acc[1 + last * 3 + k].astype(BF16)
 
     return body
 
@@ -167,7 +160,7 @@
     per = chan * rows
     base = 3 * cols
 
-    def body(info, latent, cached, got_even, got_odd, w_in, mid, gain, hidden, conv, lat, tall, wide, w_order, flat):
+    def body(info, latent, cached, got_even, got_odd, w_in, mid, half_gain, hidden, conv, lat, tall, wide, w_order):
         even = info[0] == 0
         lat[...] = jnp.zeros_like(lat)
 
@@ -199,81 +192,74 @@
         for r in range(3 * rows):
             for t in range(3):
                 x = lat[pl.ds((r * 3 + t) * chan, chan), :]
-                at = (r * 3 + t) * 3 * chan
-                tall[at : at + chan] = pltpu.roll(x, 1, 1).astype(BF16)
-                tall[at + chan : at + 2 * chan] = x.astype(BF16)
-                tall[at + 2 * chan : at + 3 * chan] = pltpu.roll(x, 255, 1).astype(BF16)
-            flat[r, :, 0 : 9 * chan] = tall[r * 9 * chan : (r + 1) * 9 * chan, 0:cols].T
+                at = t * 3 * chan
+                tall[r, at : at + chan] = pltpu.roll(x, 1, 1).astype(BF16)
+                tall[r, at + chan : at + 2 * chan] = x.astype(BF16)
+                tall[r, at + 2 * chan : at + 3 * chan] = pltpu.roll(x, 255, 1).astype(BF16)
         for i in range(3):
             for t in range(3):
                 at = (i * 3 + t) * 3 * chan
                 w_order[at : at + 3 * chan] = w_in[t, i]
 
-        deep = 9 * chan
-
         def hidden_row(k):
-            h = sum(mm(flat[k + i, :, 0:deep], w_order[i * deep : (i + 1) * deep]) for i in range(3))
+            lhs = tall[pl.ds(k, 3)].reshape(27 * chan, 256)[:, 0:cols]
+            h = lax.dot_general(lhs, w_order[...], (((0,), (0,)), ((), ())), preferred_element_type=F32)
             h = h.astype(BF16)
-            if 1 <= k <= rows + 4:
-                hidden[k - 1] = h
+            hidden[k] = h
             v = h.astype(F32)
             inv = lax.rsqrt(jnp.mean(v * v, axis=1, keepdims=True) + EPS)
-            y = v * inv * gain[...]
-            act = y * (0.5 * jnp.tanh(0.5 * y) + 0.5)
-            if k < 3:
-                act = act * flag(info, 1)
-            if k >= rows + 3:
-                act = act * flag(info, 2)
-            at = slice(k * cols, (k + 1) * cols)
-            wide[at, 0:384] = from_left(act).astype(BF16)
-            wide[at, 384:768] = act.astype(BF16)
-            wide[at, 768:1152] = from_right(act).astype(BF16)
-
-        def conv_rows(p, lanes):
-            start = 2 * p * cols
-            lhs = [wide[start + i * cols : start + (i + 2) * cols] for i in range(3)]
-            rhs = [mid[2, i, :, lanes] for i in range(3)]
-            conv[start : start + 2 * cols, lanes] = mm(jnp.concatenate(lhs, axis=1), jnp.concatenate(rhs, axis=0))
-
-        def rows_step(k):
-            return lambda: hidden_row(k)
-
-        def conv_step(p):
-            return [lambda: conv_rows(p, slice(0, 256)), lambda: conv_rows(p, slice(256, 384))]
-
-        for k in range(4):
+            half = v * inv * half_gain[...]
+            inside = jnp.where(k < 3, info[1], jnp.where(k >= rows + 3, info[2], 1)).astype(F32)
+            act = half * (jnp.tanh(half) + 1.0) * inside
+            wide[k, :, 0:384] = from_left(act).astype(BF16)
+            wide[k, :, 384:768] = act.astype(BF16)
+            wide[k, :, 768:1152] = from_right(act).astype(BF16)
+
+        def conv_row(p):
+            lhs = jnp.concatenate([wide[p], wide[p + 1], wide[p + 2]], axis=1)
+            conv[p] = mm(lhs, mid[2].reshape(3456, 384))
+
+        @pl.loop(0, 3)
+        def _(k):
             hidden_row(k)
-        for p in range(rows // 2 + 2):
-            after = [rows_step(k) for k in (2 * p + 4, 2 * p + 5) if k < rows + 6]
-            weave(conv_step(p), after) if after else weave(conv_step(p))
+
+        @pl.loop(3, rows + 6)
+        def _(k):
+            conv_row(k - 3)
+            hidden_row(k)
+
+        conv_row(rows + 3)
 
     return body
 
 
-def pull_scale(y):
-    sig = 0.5 * jnp.tanh(0.5 * y) + 0.5
-    return sig * (1.0 + y * (1.0 - sig))
+def pulled(s, half_gain, grad):
+    h = s * half_gain
+    t = jnp.tanh(h)
+    return (grad * half_gain) * ((1.0 + t) * (1.0 + h * (1.0 - t)))
 
 
 def back_body(rows, cols, chan, count, o):
-    deep_rows = rows + 4
     size = rows * cols
     width = 2 * cols // count
 
     def body(
-        info, hidden, conv, acc, got_even, got_odd, packed_even, packed_odd, own, fwd, back_odd, back_even, mid_t, w_in, gain,
-        out_gain, payload, reward, edge, p0, p1, g_odd, g_even, wide, t_odd, t_even, back, act_grad, hid, lines,
+        info, hidden, conv, acc, got_even, got_odd, packed_even, packed_odd, own, fwd, back_odd, back_even, mid_t, w_in, half_gain,
+        half_out, payload, reward, edge, p0, p1, g_odd, g_even, wide, t_odd, t_even, back, act_grad, hid, lines,
     ):
         even = info[0] == 0
         top, bottom = flag(info, 1), flag(info, 2)
 
         def take(got, packed, before):
             ok = top if before else bottom
-            place = 0 if before else 3
+            place = 0 if before else rows + 1
             for k in range(3):
                 at = slice(k * cols, (k + 1) * cols)
-                edge[(place + k) * cols : (place + k + 1) * cols] = got[at].astype(F32) * ok
+                edge[place + k] = got[at].astype(F32) * ok
                 reward[k if before else 2 * rows + 3 + k] = (packed[at].astype(F32) * ok).astype(BF16)
+
+        for k in range(3, rows + 1):
+            edge[k] = jnp.zeros((cols, 384), F32)
 
         @pl.when(even)
         def _():
@@ -287,41 +273,31 @@
 
         reward[3 : 2 * rows + 3] = own[...]
 
-        def row(ref, k):
-            return ref[k * cols : (k + 1) * cols]
-
-        def state_row(k):
-            x = hidden[k].astype(F32) + row(conv, k)
-            if 1 <= k <= rows + 2:
-                x = x + row(acc, k - 1)
-            if k < 3:
-                x = x + row(edge, k)
-            if k >= rows + 1:
-                x = x + row(edge, k - rows + 2)
-            if k < 2:
-                x = x * top
-            if k >= rows + 2:
-                x = x * bottom
+        def inside(k, first, last):
+            return jnp.where(k < first, info[1], jnp.where(k >= last, info[2], 1)).astype(F32)
+
+        def spread(ref, k, x, ahead):
             x = x.astype(BF16)
             x32 = x.astype(F32)
-            at = slice(k * cols, (k + 1) * cols)
-            wide[at, 0:384] = from_left(x32).astype(BF16)
-            wide[at, 384:768] = x
-            wide[at, 768:1152] = from_right(x32).astype(BF16)
-
-        def up_dot(p, b, n):
-            at = slice(2 * p * cols, (2 * p + 2) * cols)
-            lanes = slice(n * 256, n * 256 + 256)
-            (p0, p1)[b][at, lanes] = mm(wide[at, b * 384 : b * 384 + 768], fwd[b, :, lanes])
+            sides = (from_right(x32), from_left(x32)) if ahead else (from_left(x32), from_right(x32))
+            ref[k, :, 0:384] = sides[0].astype(BF16)
+            ref[k, :, 384:768] = x
+            ref[k, :, 768:1152] = sides[1].astype(BF16)
+
+        def state_row(k):
+            x = hidden[k + 1].astype(F32) + conv[k] + acc[k] + edge[k]
+            spread(wide, k, x * inside(k, 2, rows + 2), False)
+
+        def up_row(k):
+            p0[k] = mm(wide[k, :, 0:768], fwd[0])
+            p1[k] = mm(wide[k, :, 384:1152], fwd[1])
 
         lane = lax.broadcasted_iota(jnp.int32, (cols, 128), 1)
         low = lane < 64
-        gains = [out_gain[:, 0:128], out_gain[:, 128:256]]
+        gains = [half_out[:, 0:128], half_out[:, 128:256]]
 
         def pull(v0, v1, vm, r, zero_low):
             mine = low if zero_low else jnp.logical_not(low)
-            v0, v1, vm = (v.astype(BF16).astype(F32) for v in (v0, v1, vm))
-
             def both(a0, a1, am):
                 s0 = jnp.sum(a0 + jnp.where(mine, am, 0.0), axis=1, keepdims=True)
                 s1 = jnp.sum(a1 + jnp.where(mine, 0.0, am), axis=1, keepdims=True)
@@ -333,104 +309,87 @@
             out = []
             for v, i, g, k in ((v0, i0, gains[0], 0), (v1, i1, gains[0], 1), (vm, im, gains[1], 2)):
                 s = v * i
-                y = s * g
-                d = r[:, k * 128 : k * 128 + 128].astype(F32) * pull_scale(y) * g
-                out.append((s, d))
+                out.append((s, pulled(s, g, r[:, k * 128 : k * 128 + 128].astype(F32))))
             m0, m1 = both(*(s * d for s, d in out))
             mx = jnp.where(mine, m0, m1)
             return [i * (d - s * m) for (s, d), i, m in zip(out, (i0, i1, im), (m0, m1, mx))], mine
 
         def store(g, target, k):
             (a0, a1, am), mine = g
-            at = slice(k * cols, (k + 1) * cols)
-            target[at, 0:128] = a0.astype(BF16)
-            target[at, 128:256] = a1.astype(BF16)
-            target[at, 256:384] = am.astype(BF16)
-            target[at, 384:512] = from_right(a0).astype(BF16)
-            target[at, 512:640] = from_left(a1).astype(BF16)
-            target[at, 640:768] = jnp.where(mine, from_right(am), from_left(am)).astype(BF16)
-
-        def pull_odd(k):
-            a, b = slice(k * cols, (k + 1) * cols), slice((k + 1) * cols, (k + 2) * cols)
-            v0 = p0[a, 256:384] + p0[b, 0:128]
-            v1 = p1[a, 256:384] + p1[b, 0:128]
-            vm = jnp.where(low, p0[a, 640:768] + p0[b, 512:640], p1[a, 640:768] + p1[b, 512:640])
+            target[k, :, 0:128] = a0.astype(BF16)
+            target[k, :, 128:256] = a1.astype(BF16)
+            target[k, :, 256:384] = am.astype(BF16)
+            target[k, :, 384:512] = from_right(a0).astype(BF16)
+            target[k, :, 512:640] = from_left(a1).astype(BF16)
+            target[k, :, 640:768] = jnp.where(mine, from_right(am), from_left(am)).astype(BF16)
+
+        def pull_rows(k):
+            v0 = p0[k, :, 256:384] + p0[k + 1, :, 0:128]
+            v1 = p1[k, :, 256:384] + p1[k + 1, :, 0:128]
+            vm = jnp.where(low, p0[k, :, 640:768] + p0[k + 1, :, 512:640], p1[k, :, 640:768] + p1[k + 1, :, 512:640])
             store(pull(v0, v1, vm, reward[2 * k], True), g_odd, k)
-
-        def pull_even(k):
-            a, b = slice(k * cols, (k + 1) * cols), slice((k + 1) * cols, (k + 2) * cols)
-            v0 = p0[b, 128:256] + p0[a, 384:512]
-            v1 = p1[b, 128:256] + p1[a, 384:512]
-            vm = jnp.where(low, p1[b, 512:640] + p1[a, 640:768], p0[b, 512:640] + p0[a, 640:768])
+            v0 = p0[k + 1, :, 128:256] + p0[k, :, 384:512]
+            v1 = p1[k + 1, :, 128:256] + p1[k, :, 384:512]
+            vm = jnp.where(low, p1[k + 1, :, 512:640] + p1[k, :, 640:768], p0[k + 1, :, 512:640] + p0[k, :, 640:768])
             store(pull(v0, v1, vm, reward[2 * k + 1], False), g_even, k)
 
-        fine = rows + 3
-
-        def down_dot(first, number, odd, n):
-            at = slice(first * cols, (first + number) * cols)
-            lanes = slice(n * 256, n * 256 + 256)
-            if odd:
-                t_odd[at, lanes] = mm(g_odd[at], back_odd[:, lanes])
-            else:
-                t_even[at, lanes] = mm(g_even[at], back_even[:, lanes])
+        def down_row(k):
+            t_odd[k] = mm(g_odd[k], back_odd[...])
+            t_even[k] = mm(g_even[k], back_even[...])
 
         def block_row(k):
-            a, b = slice(k * cols, (k + 1) * cols), slice((k + 1) * cols, (k + 2) * cols)
-            x = t_odd[b, 0:384] + t_odd[a, 384:768] + t_even[a, 0:384] + t_even[b, 384:768]
-            if k == 0:
-                x = x * top
-            if k == rows + 1:
-                x = x * bottom
-            x = x.astype(BF16)
-            x32 = x.astype(F32)
-            back[a, 0:384] = from_right(x32).astype(BF16)
-            back[a, 384:768] = x
-            back[a, 768:1152] = from_left(x32).astype(BF16)
-
-        def mid_dot(p, n):
-            lanes = slice(n * 256, min(384, n * 256 + 256))
-            lhs = [back[(2 * p + 2 - i) * cols : (2 * p + 4 - i) * cols] for i in range(3)]
-            at = slice(2 * p * cols, (2 * p + 2) * cols)
-            act_grad[at, lanes] = mm(jnp.concatenate(lhs, axis=1), mid_t[:, lanes])
+            x = t_odd[k + 1, :, 0:384] + t_odd[k, :, 384:768] + t_even[k, :, 0:384] + t_even[k + 1, :, 384:768]
+            spread(back, k, x * inside(k, 1, rows + 1), True)
+
+        def mid_row(p):
+            act_grad[p] = mm(jnp.concatenate([back[p + 2], back[p + 1], back[p]], axis=1), mid_t[...])
 
         def hidden_pull(k):
-            g = gain[...]
-            at = slice(k * cols, (k + 1) * cols)
-            v = hidden[k + 2].astype(F32)
+            v = hidden[k + 3].astype(F32)
             inv = lax.rsqrt(jnp.mean(v * v, axis=1, keepdims=True) + EPS)
             s = v * inv
-            d = act_grad[at] * pull_scale(s * g) * g
+            d = pulled(s, half_gain[...], act_grad[k])
             dv = inv * (d - s * jnp.mean(d * s, axis=1, keepdims=True))
-            block = back[(k + 1) * cols : (k + 2) * cols, 384:768].astype(F32)
-            hid[at] = (block + dv).astype(BF16)
-
-        def steps(f, *keys):
-            return [lambda key=key: f(*key) for key in keys]
-
-        def ups(p):
-            return steps(up_dot, *[(p, b, n) for n in range(3) for b in range(2)])
-
-        def downs(first, number):
-            return steps(down_dot, *[(first, number, odd, n) for odd in (True, False) for n in range(3)])
-
-        def pulls(*ks):
-            return [step for k in ks for step in steps(pull_odd, (k,)) + steps(pull_even, (k,))]
-
-        state_row(0)
-        state_row(1)
-        weave(ups(0), steps(state_row, (2,), (3,)))
-        weave(ups(1), steps(state_row, (4,), (5,)) + pulls(0))
-        weave(ups(2), steps(state_row, (6,), (7,)) + pulls(1, 2))
-        weave(ups(3) + downs(0, 2), pulls(3, 4))
-        weave(downs(2, 2), pulls(5, 6) + steps(block_row, (0,)))
-        weave(downs(4, 3), steps(block_row, (1,), (2,)))
-        block_row(3)
-        weave(steps(mid_dot, (0, 0), (0, 1)), steps(block_row, (4,), (5,)))
-        weave(steps(mid_dot, (1, 0), (1, 1)), steps(hidden_pull, (0,), (1,)))
-        hidden_pull(2)
-        hidden_pull(3)
-
-        z = mm_t(w_in[...], hid[...])
+            hid[k] = (back[k + 1, :, 384:768].astype(F32) + dv).astype(BF16)
+
+        fine = rows + 3
+
+        @pl.loop(0, 4)
+        def _(k):
+            state_row(k)
+
+        @pl.loop(0, 2)
+        def _(k):
+            up_row(k)
+
+        up_row(2)
+        pull_rows(0)
+
+        @pl.loop(1, fine - 1)
+        def _(k):
+            up_row(k + 2)
+            pull_rows(k)
+            down_row(k - 1)
+            state_row(jnp.minimum(k + 3, rows + 3))
+
+        pull_rows(fine - 1)
+        down_row(fine - 2)
+        down_row(fine - 1)
+
+        @pl.loop(0, 3)
+        def _(k):
+            block_row(k)
+
+        @pl.loop(0, rows - 1)
+        def _(p):
+            mid_row(p)
+            block_row(p + 3)
+
+        mid_row(rows - 1)
+        for k in range(rows):
+            hidden_pull(k)
+
+        z = mm_t(w_in[...], hid[...].reshape(size, 384))
         place = lax.broadcasted_iota(jnp.int32, (chan, size), 1)
         col = lax.rem(place, cols)
         sums = []
@@ -515,8 +474,8 @@
     up_t = jnp.transpose(conv_up_weight, (0, 1, 3, 2))
     mid = conv_mid_weight.reshape(3, 3, 3 * mid_chan, mid_chan)
     w_in = conv_in_weight.reshape(3, 3, 3 * chan, mid_chan)
-    gain = norm_gain.reshape(1, mid_chan)
-    gain_out = jnp.concatenate([out_gain, out_gain[128:]]).reshape(1, 256)
+    gain = 0.5 * norm_gain.reshape(1, mid_chan)
+    gain_out = 0.5 * jnp.concatenate([out_gain, out_gain[128:]]).reshape(1, 256)
     within, across = swaps(count)
     size = rows * cols
     edge_rows = 3 * cols + 2 * chan * rows
@@ -540,7 +499,7 @@
     acc, part_even, part_odd, mid_t, sel = call(
         cached_body(rows, cols, count, width, tokens),
         [
-            ((6 * cols, 384), F32), ((3 * cols, 384), BF16), ((3 * cols, 384), BF16), ((3456, 384), BF16),
+            ((rows + 4, cols, 384), F32), ((3 * cols, 384), BF16), ((3 * cols, 384), BF16), ((3456, 384), BF16),
             ((count, 128, 4 * tokens), BF16),
         ],
         2, 2, [pltpu.VMEM((size, 2304), BF16)], 4e9, 24,
@@ -550,14 +509,13 @@
 
     hidden, conv = call(
         current_body(rows, cols, chan),
-        [((rows + 4, cols, 384), BF16), ((2 * size, 384), F32)],
+        [((rows + 6, cols, 384), BF16), ((rows + 4, cols, 384), F32)],
         1, 7,
         [
             pltpu.VMEM((9 * rows * chan, 256), F32),
-            pltpu.VMEM((27 * rows * chan, 256), BF16),
-            pltpu.VMEM(((rows + 6) * cols, 1152), BF16),
+            pltpu.VMEM((3 * rows, 9 * chan, 256), BF16),
+            pltpu.VMEM((rows + 6, cols, 1152), BF16),
             pltpu.VMEM((27 * chan, 384), BF16),
-            pltpu.VMEM((3 * rows, cols, 256), BF16),
         ],
         5e9, 24,
     )(info, lat, lat_cached, packed_even, packed_odd, w_in, mid, gain)
@@ -568,17 +526,17 @@
         1, 15,
         [
             pltpu.VMEM((2 * rows + 6, cols, 384), BF16),
-            pltpu.VMEM((6 * cols, 384), F32),
-            pltpu.VMEM(((rows + 4) * cols, 768), F32),
-            pltpu.VMEM(((rows + 4) * cols, 768), F32),
-            pltpu.VMEM(((rows + 3) * cols, 768), BF16),
-            pltpu.VMEM(((rows + 3) * cols, 768), BF16),
-            pltpu.VMEM(((rows + 4) * cols, 1152), BF16),
-            pltpu.VMEM(((rows + 3) * cols, 768), F32),
-            pltpu.VMEM(((rows + 3) * cols, 768), F32),
-            pltpu.VMEM(((rows + 2) * cols, 1152), BF16),
-            pltpu.VMEM((size, 384), F32),
-            pltpu.VMEM((size, 384), BF16),
+            pltpu.VMEM((rows + 4, cols, 384), F32),
+            pltpu.VMEM((rows + 4, cols, 768), F32),
+            pltpu.VMEM((rows + 4, cols, 768), F32),
+            pltpu.VMEM((rows + 3, cols, 768), BF16),
+            pltpu.VMEM((rows + 3, cols, 768), BF16),
+            pltpu.VMEM((rows + 4, cols, 1152), BF16),
+            pltpu.VMEM((rows + 3, cols, 768), F32),
+            pltpu.VMEM((rows + 3, cols, 768), F32),
+            pltpu.VMEM((rows + 2, cols, 1152), BF16),
+            pltpu.VMEM((rows, cols, 384), F32),
+            pltpu.VMEM((rows, cols, 384), BF16),
             pltpu.VMEM((3 * chan, size), F32),
         ],
         8e9, 36,

time: 50.1 us -> 55.6 us (1.11)
  Pallas kernels: 30.5 us -> 35.9 us
    pallas_call x1, Pallas kernels: 13 us -> 16 us  [shards(): call(back_body(rows, cols, chan, count, o), [((count, chan, 128), BF16)],...]
    pallas_call x2, Pallas kernels: 12.9 us -> 15.3 us  [the longest x1 10.1 us: shards(): call(current_body(rows, cols, chan), [((rows + 6, cols, 384), BF16), ((ro...]
  transfers between devices with their start and end apart: 4 -> 4, of which waited for: 0 -> 0; matrix products, arithmetic and copies ran while one was open for 0% -> 0% of each run, Pallas kernels for 26% -> 28%
where the time goes in v4:
time: 55.6 us; the launch traced here: 55.4 us
  Pallas kernels  35.9 us (65%)
  blocking collectives  11.7 us (21%)
  starting transfers between devices  5.87 us (11%)
  local copies, waits for them, and re-layouts  1.4 us (3%)
    pallas_call x1, Pallas kernels, shards(): call(back_body(rows, cols, chan, count, o), [((count, chan, 128), BF16)],...  16 us
    all_to_all x1, blocking collectives, shards(): lax.all_to_all(payload, 'tile', split_axis=0, concat_axis=0, tiled=True)  11.7 us
    pallas_call x1, Pallas kernels, shards(): call(current_body(rows, cols, chan), [((rows + 6, cols, 384), BF16), ((ro...  10.1 us
    pallas_call x1, Pallas kernels, shards(): call(cached_body(rows, cols, count, width, tokens), [((rows + 4, cols, 38...  5.27 us
    ppermute x1, starting transfers between devices, shards(): got_even = lax.ppermute(part_even, 'tile', within)  3.97 us
    pallas_call x1, Pallas kernels, shards(): call(taps_body, [((4,), jnp.int32), ((2, 768, 768), BF16), ((768, 768), B...  1.93 us
    pallas_call x1, Pallas kernels, shards(): call(pack_body(rows, cols, o, chan), [((2 * rows, cols, 384), BF16), ((ed...  1.7 us
    unnamed x22, local copies, waits for them, and re-layouts  1.38 us
  transfers between devices with their start and end apart: 4, of which 0 were waited for; matrix products, arithmetic and copies ran while one was open for 0% of the time, Pallas kernels for 28%

profile of v4, /device:TPU:0, one launch (start us, length us, event | category | flops | bytes accessed | tf_op | source)
XLA Modules:
  0.0 55.4 jit_solution(10432153081804118409)
XLA Ops:
  0.0 0.1 pad_add_fusion.info
  0.1 1.3 %copy-done.1 = bf16[3,3,384,192]{2,3,1,0:T(8,128)(2,1)S(1)} copy-done((bf16[3,3,384,192]{2,3,1,0:T(8,128)(2,1)S(1)}, bf16[3,3,384,192]{2,3,1,0:T(8,128)(2,1)}, u32[]{:S(2)}) %copy-start.1) | copy-done | bytes 1327128
  1.4 1.9 %shard_map.100 = (s32[4]{0:T(128)S(1)}, bf16[2,768,768]{2,1,0:T(8,128)(2,1)S(1)}, bf16[768,768]{1,0:T(8,128)(2,1)S(1)}, bf16[768,768]{1,0:T(8,128)(2,1)S(1)}) custom-call(s32[4]{0:T(128)S(1)} %pad_add_fusion.info, bf16[3,3,192,384]{3,2,1,0:T(8,128)(2,1)S(1)} %bitcast.21), custom_call_target="tpu_custom_call" | custom-call | flops 10000000000 | bytes 1048576 | tf_op jit(solution)/shard_map/pallas_call | solution.py:483
  3.4 0.0 slice-start.1
  3.4 0.0 copy-done.2
  3.4 0.0 copy-done.4
  3.4 0.0 copy-done.5
  3.4 0.0 copy-start.3
  3.4 0.0 copy-start.6
  3.4 1.7 %shard_map.102 = (bf16[8,160,384]{2,1,0:T(8,128)(2,1)S(1)}, bf16[608,384]{1,0:T(8,128)(2,1)S(1)}, bf16[608,384]{1,0:T(8,128)(2,1)S(1)}) custom-call(s32[4]{0:T(128)S(1)} %get-tuple-element.19.info, bf16[8,192,320]{2,1,0:T(8,128)(2,1)S(1)} %bitcast.22, bf16[4,16,160]{2,1,0:T(8,128)(2,1)S(1)} %bitcast.25, bf16[2,4,16,160]{3,2,1,0:T(8,128)(2,1)S(1)} %bitcast.23), custom_call_target="tpu_custom_call" | custom-call | flops 10000000000 | bytes 1048576 | tf_op jit(solution)/shard_map/pallas_call | solution.py:489
  5.1 0.6 collective-permute-start
  5.7 0.7 %collective-permute-start.1 = (bf16[608,384]{1,0:T(8,128)(2,1)S(1)}, bf16[608,384]{1,0:T(8,128)(2,1)S(1)}, u32[]{:S(2)}, u32[]{:S(2)}) collective-permute-start(bf16[608,384]{1,0:T(8,128)(2,1)S(1)} %get-tuple-element.22), channel_id=1, source_target_pairs={{0,0},{1,2},{2,1},{3,4},{4,3},{5,6},{6,5},{7,7},{8,8},{9,10},{10,9... | collective-permute-start | bytes 1400840 | tf_op jit(solution)/shard_map/ppermute | solution.py:495
  6.4 0.0 slice-done
  6.4 0.0 slice-done.1
  6.4 0.0 copy-done.3
  6.4 0.0 copy-done.6
  6.4 0.0 copy-start.7
  6.4 0.0 copy-start
  6.4 0.0 copy-start.8
  6.5 5.3 %shard_map.101 = (f32[8,160,384]{2,1,0:T(8,128)S(1)}, bf16[480,384]{1,0:T(8,128)(2,1)S(1)}, bf16[480,384]{1,0:T(8,128)(2,1)S(1)}, bf16[3456,384]{1,0:T(8,128)(2,1)S(1)}, bf16[8,128,640]{2,1,0:T(8,128)(2,1)S(1)}) custom-call(s32[4]{0:T(128)S(1)} %get-tuple-element.19.info, s32[8]{0:T(128)S(1)} %copy-done.6, bf16[2,4,160,384]{3,2,1,0:T(8,128)(2,1)S(1)} %copy-done.3, ...), custom_call_target="tpu_custom_call" | custom-call | flops 4000000000 | bytes 1048576 | tf_op jit(solution)/shard_map/pallas_call | solution.py:499
  11.7 4.0 %collective-permute-start.2 = (bf16[480,384]{1,0:T(8,128)(2,1)S(1)}, bf16[480,384]{1,0:T(8,128)(2,1)S(1)}, u32[]{:S(2)}, u32[]{:S(2)}) collective-permute-start(bf16[480,384]{1,0:T(8,128)(2,1)S(1)} %get-tuple-element.26), channel_id=1, source_target_pairs={{0,1},{1,0},{2,3},{3,2},{4,5},{5,4},{6,7},{7,6},{8,9},{9,8},{10,11... | collective-permute-start | bytes 1105928 | tf_op jit(solution)/shard_map/ppermute | solution.py:507
  15.7 0.7 %collective-permute-start.3 = (bf16[480,384]{1,0:T(8,128)(2,1)S(1)}, bf16[480,384]{1,0:T(8,128)(2,1)S(1)}, u32[]{:S(2)}, u32[]{:S(2)}) collective-permute-start(bf16[480,384]{1,0:T(8,128)(2,1)S(1)} %get-tuple-element.27), channel_id=1, source_target_pairs={{0,0},{1,2},{2,1},{3,4},{4,3},{5,6},{6,5},{7,7},{8,8},{9,10},{10,9... | collective-permute-start | bytes 1105928 | tf_op jit(solution)/shard_map/ppermute | solution.py:508
  16.4 0.0 copy-done
  16.5 0.1 maximum_multiply_fusion.half_out
  16.5 0.0 collective-permute-done.got_even.packed_even
  16.5 0.0 collective-permute-done.1.got_odd.packed_odd
  16.5 10.1 %shard_map.103 = (bf16[10,160,384]{2,1,0:T(8,128)(2,1)S(1)}, f32[8,160,384]{2,1,0:T(8,128)S(1)}) custom-call(s32[4]{0:T(128)S(1)} %get-tuple-element.19.info, bf16[4,16,160]{2,1,0:T(8,128)(2,1)S(1)} %bitcast.26, bf16[2,4,16,160]{3,2,1,0:T(8,128)(2,1)S(1)} %bitcast.24, bf16[608,384]{1,0:T(8,128)(2,1)S(1)} %collective-permute-done.got_even.packed_even, ...), custom_call_target="tpu_custom_call" | custom-call | flops 5000000000 | bytes 1048576 | tf_op jit(solution)/shard_map/pallas_call | solution.py:510
  26.6 0.0 collective-permute-done.2.got_even
  26.6 0.0 collective-permute-done.3.got_odd
  26.6 16.0 %shard_map.104 = bf16[8,16,128]{2,1,0:T(8,128)(2,1)S(1)} custom-call(s32[4]{0:T(128)S(1)} %get-tuple-element.19.info, bf16[10,160,384]{2,1,0:T(8,128)(2,1)S(1)} %get-tuple-element.23.hidden, f32[8,160,384]{2,1,0:T(8,128)S(1)} %get-tuple-element.24.conv, f32[8,160,384]{2,1,0:T(8,128)S(1)} %get-tuple-element.25.acc, ...), custom_call_target="tpu_custom_call" | custom-call | flops 8000000000 | bytes 1048576 | tf_op jit(solution)/shard_map/pallas_call | solution.py:523
  42.6 11.7 %all_to_all.5.got = bf16[8,16,128]{2,1,0:T(8,128)(2,1)S(1)} all-to-all(bf16[8,16,128]{2,1,0:T(8,128)(2,1)S(1)} %shard_map.104), channel_id=1, replica_groups=mesh['prompt'=4,'tile'=8] {'tile'}, dimensions={0} | all-to-all | bytes 65536 | tf_op jit(solution)/shard_map/all_to_all | solution.py:547
  54.3 1.0 %shard_map.105 = f32[64,160]{1,0:T(8,128)} custom-call(bf16[8,128,640]{2,1,0:T(8,128)(2,1)S(1)} %get-tuple-element.20.sel, bf16[8,16,128]{2,1,0:T(8,128)(2,1)S(1)} %all_to_all.5.got), custom_call_target="tpu_custom_call" | custom-call | flops 10000000 | bytes 1048576 | tf_op jit(solution)/shard_map/pallas_call | solution.py:548
  (12 shorter events, 0.0 us)
Async XLA Ops:
  0.1 1.3 %copy-start.1 = (bf16[3,3,384,192]{2,3,1,0:T(8,128)(2,1)S(1)}, bf16[3,3,384,192]{2,3,1,0:T(8,128)(2,1)}, u32[]{:S(2)}) copy-start(bf16[3,3,384,192]{2,3,1,0:T(8,128)(2,1)} %param.16) | copy-start | bytes 3981316
  1.4 2.0 %copy-start.2 = (bf16[8,320,192]{1,2,0:T(8,128)(2,1)S(1)}, bf16[8,320,192]{1,2,0:T(8,128)(2,1)}, u32[]{:S(2)}) copy-start(bf16[8,320,192]{1,2,0:T(8,128)(2,1)} %param.13) | copy-start | bytes 2949124
  1.4 2.0 %copy-start.4 = (bf16[2,4,160,16]{2,3,1,0:T(8,128)(2,1)S(1)}, bf16[2,4,160,16]{2,3,1,0:T(8,128)(2,1)}, u32[]{:S(2)}) copy-start(bf16[2,4,160,16]{2,3,1,0:T(8,128)(2,1)} %param.11) | copy-start | bytes 122884
  1.4 2.0 %copy-start.5 = (bf16[4,160,16]{1,2,0:T(8,128)(2,1)S(1)}, bf16[4,160,16]{1,2,0:T(8,128)(2,1)}, u32[]{:S(2)}) copy-start(bf16[4,160,16]{1,2,0:T(8,128)(2,1)} %param.10) | copy-start | bytes 61444
  1.4 5.0 %slice-start = ((s8[7962624]{0:T(1024)(128)(4,1)}), s8[4194304]{0:T(1024)(128)(4,1)S(1)}, s32[]{:S(2)}) async-start(s8[7962624]{0:T(1024)(128)(4,1)} %bitcast.17), calls=%async_computation.1 | async-start | bytes 8388608
  3.4 3.0 %slice-start.1 = ((s8[7962624]{0:T(1024)(128)(4,1)}), s8[3768320]{0:T(1024)(128)(4,1)S(1)}, s32[]{:S(2)}) async-start(s8[7962624]{0:T(1024)(128)(4,1)} %bitcast.17), calls=%async_computation.2 | async-start | bytes 7536640
  3.4 3.0 %copy-start.3 = (bf16[2,4,160,384]{3,2,1,0:T(8,128)(2,1)S(1)}, bf16[2,4,160,384]{3,2,1,0:T(8,128)(2,1)}, u32[]{:S(2)}) copy-start(bf16[2,4,160,384]{3,2,1,0:T(8,128)(2,1)} %features.1) | copy-start | bytes 2949124
  3.4 3.0 %copy-start.6 = (s32[8]{0:T(128)S(1)}, s32[8]{0:T(128)}, u32[]{:S(2)}) copy-start(s32[8]{0:T(128)} %order.1) | copy-start | bytes 100
  5.1 11.4 %collective-permute-start = (bf16[608,384]{1,0:T(8,128)(2,1)S(1)}, bf16[608,384]{1,0:T(8,128)(2,1)S(1)}, u32[]{:S(2)}, u32[]{:S(2)}) collective-permute-start(bf16[608,384]{1,0:T(8,128)(2,1)S(1)} %get-tuple-element.21), channel_id=1, source_target_pairs={{0,1},{1,0},{2,3},{3,2},{4,5},{5,4},{6,7},{7,6},{8,9},{9,8},{10,11... | collective-permute-start | bytes 1400840 | tf_op jit(solution)/shard_map/ppermute | solution.py:494
  5.7 10.9 %collective-permute-start.1 = (bf16[608,384]{1,0:T(8,128)(2,1)S(1)}, bf16[608,384]{1,0:T(8,128)(2,1)S(1)}, u32[]{:S(2)}, u32[]{:S(2)}) collective-permute-start(bf16[608,384]{1,0:T(8,128)(2,1)S(1)} %get-tuple-element.22), channel_id=1, source_target_pairs={{0,0},{1,2},{2,1},{3,4},{4,3},{5,6},{6,5},{7,7},{8,8},{9,10},{10,9... | collective-permute-start | bytes 1400840 | tf_op jit(solution)/shard_map/ppermute | solution.py:495
  6.4 10.0 %copy-start.7 = (f32[384]{0:T(512)S(1)}, f32[384]{0:T(512)}, u32[]{:S(2)}) copy-start(f32[384]{0:T(512)} %param.17) | copy-start | bytes 4612
  6.4 10.0 %copy-start = (bf16[3,3,3,16,384]{4,3,2,1,0:T(8,128)(2,1)S(1)}, bf16[3,3,3,16,384]{4,3,2,1,0:T(8,128)(2,1)}, u32[]{:S(2)}) copy-start(bf16[3,3,3,16,384]{4,3,2,1,0:T(8,128)(2,1)} %param.14) | copy-start | bytes 995332
  6.4 10.0 %copy-start.8 = (f32[192]{0:T(256)S(1)}, f32[192]{0:T(256)}, u32[]{:S(2)}) copy-start(f32[192]{0:T(256)} %param.18) | copy-start | bytes 2308
  11.7 14.9 %collective-permute-start.2 = (bf16[480,384]{1,0:T(8,128)(2,1)S(1)}, bf16[480,384]{1,0:T(8,128)(2,1)S(1)}, u32[]{:S(2)}, u32[]{:S(2)}) collective-permute-start(bf16[480,384]{1,0:T(8,128)(2,1)S(1)} %get-tuple-element.26), channel_id=1, source_target_pairs={{0,1},{1,0},{2,3},{3,2},{4,5},{5,4},{6,7},{7,6},{8,9},{9,8},{10,11... | collective-permute-start | bytes 1105928 | tf_op jit(solution)/shard_map/ppermute | solution.py:507
  15.7 10.9 %collective-permute-start.3 = (bf16[480,384]{1,0:T(8,128)(2,1)S(1)}, bf16[480,384]{1,0:T(8,128)(2,1)S(1)}, u32[]{:S(2)}, u32[]{:S(2)}) collective-permute-start(bf16[480,384]{1,0:T(8,128)(2,1)S(1)} %get-tuple-element.27), channel_id=1, source_target_pairs={{0,0},{1,2},{2,1},{3,4},{4,3},{5,6},{6,5},{7,7},{8,8},{9,10},{10,9... | collective-permute-start | bytes 1105928 | tf_op jit(solution)/shard_map/ppermute | solution.py:508

commit v5 on v4

--- a/solution.py
+++ b/solution.py
@@ -202,33 +202,33 @@
                 w_order[at : at + 3 * chan] = w_in[t, i]
 
         def hidden_row(k):
-            lhs = tall[pl.ds(k, 3)].reshape(27 * chan, 256)[:, 0:cols]
+            lhs = tall[k : k + 3].reshape(27 * chan, 256)[:, 0:cols]
             h = lax.dot_general(lhs, w_order[...], (((0,), (0,)), ((), ())), preferred_element_type=F32)
             h = h.astype(BF16)
             hidden[k] = h
             v = h.astype(F32)
             inv = lax.rsqrt(jnp.mean(v * v, axis=1, keepdims=True) + EPS)
             half = v * inv * half_gain[...]
-            inside = jnp.where(k < 3, info[1], jnp.where(k >= rows + 3, info[2], 1)).astype(F32)
-            act = half * (jnp.tanh(half) + 1.0) * inside
+            act = half * (jnp.tanh(half) + 1.0)
+            if k < 3:
+                act = act * flag(info, 1)
+            if k >= rows + 3:
+                act = act * flag(info, 2)
             wide[k, :, 0:384] = from_left(act).astype(BF16)
             wide[k, :, 384:768] = act.astype(BF16)
             wide[k, :, 768:1152] = from_right(act).astype(BF16)
 
-        def conv_row(p):
-            lhs = jnp.concatenate([wide[p], wide[p + 1], wide[p + 2]], axis=1)
-            conv[p] = mm(lhs, mid[2].reshape(3456, 384))
-
-        @pl.loop(0, 3)
-        def _(k):
+        def conv_rows(p, count):
+            lhs = [wide[p + i : p + i + count].reshape(count * cols, 1152) for i in range(3)]
+            total = mm(jnp.concatenate(lhs, axis=1), mid[2].reshape(3456, 384))
+            conv[p : p + count] = total.reshape(count, cols, 384)
+
+        for k in range(rows + 2):
             hidden_row(k)
-
-        @pl.loop(3, rows + 6)
-        def _(k):
-            conv_row(k - 3)
+        conv_rows(0, rows)
+        for k in range(rows + 2, rows + 6):
             hidden_row(k)
-
-        conv_row(rows + 3)
+        conv_rows(rows, 4)
 
     return body
 
@@ -258,9 +258,6 @@
                 edge[place + k] = got[at].astype(F32) * ok
                 reward[k if before else 2 * rows + 3 + k] = (packed[at].astype(F32) * ok).astype(BF16)
 
-        for k in range(3, rows + 1):
-            edge[k] = jnp.zeros((cols, 384), F32)
-
         @pl.when(even)
         def _():
             take(got_odd, packed_odd, True)
@@ -273,8 +270,8 @@
 
         reward[3 : 2 * rows + 3] = own[...]
 
-        def inside(k, first, last):
-            return jnp.where(k < first, info[1], jnp.where(k >= last, info[2], 1)).astype(F32)
+        def inside(x, k, first, last):
+            return x * top if k < first else x * bottom if k >= last else x
 
         def spread(ref, k, x, ahead):
             x = x.astype(BF16)
@@ -285,12 +282,17 @@
             ref[k, :, 768:1152] = sides[1].astype(BF16)
 
         def state_row(k):
-            x = hidden[k + 1].astype(F32) + conv[k] + acc[k] + edge[k]
-            spread(wide, k, x * inside(k, 2, rows + 2), False)
-
-        def up_row(k):
-            p0[k] = mm(wide[k, :, 0:768], fwd[0])
-            p1[k] = mm(wide[k, :, 384:1152], fwd[1])
+            x = hidden[k + 1].astype(F32) + conv[k]
+            if 1 <= k <= rows + 2:
+                x = x + acc[k]
+            if k < 3 or k > rows:
+                x = x + edge[k]
+            spread(wide, k, inside(x, k, 2, rows + 2), False)
+
+        def up_rows(k, count):
+            x = wide[k : k + count].reshape(count * cols, 1152)
+            p0[k : k + count] = mm(x[:, 0:768], fwd[0]).reshape(count, cols, 768)
+            p1[k : k + count] = mm(x[:, 384:1152], fwd[1]).reshape(count, cols, 768)
 
         lane = lax.broadcasted_iota(jnp.int32, (cols, 128), 1)
         low = lane < 64
@@ -333,16 +335,9 @@
             vm = jnp.where(low, p1[k + 1, :, 512:640] + p1[k, :, 640:768], p0[k + 1, :, 512:640] + p0[k, :, 640:768])
             store(pull(v0, v1, vm, reward[2 * k + 1], False), g_even, k)
 
-        def down_row(k):
-            t_odd[k] = mm(g_odd[k], back_odd[...])
-            t_even[k] = mm(g_even[k], back_even[...])
-
         def block_row(k):
             x = t_odd[k + 1, :, 0:384] + t_odd[k, :, 384:768] + t_even[k, :, 0:384] + t_even[k + 1, :, 384:768]
-            spread(back, k, x * inside(k, 1, rows + 1), True)
-
-        def mid_row(p):
-            act_grad[p] = mm(jnp.concatenate([back[p + 2], back[p + 1], back[p]], axis=1), mid_t[...])
+            spread(back, k, inside(x, k, 1, rows + 1), True)
 
         def hidden_pull(k):
             v = hidden[k + 3].astype(F32)
@@ -353,39 +348,20 @@
             hid[k] = (back[k + 1, :, 384:768].astype(F32) + dv).astype(BF16)
 
         fine = rows + 3
-
-        @pl.loop(0, 4)
-        def _(k):
+        for k in range(rows):
             state_row(k)
-
-        @pl.loop(0, 2)
-        def _(k):
-            up_row(k)
-
-        up_row(2)
-        pull_rows(0)
-
-        @pl.loop(1, fine - 1)
-        def _(k):
-            up_row(k + 2)
+        up_rows(0, rows)
+        for k in range(rows, rows + 4):
+            state_row(k)
+        up_rows(rows, 4)
+        for k in range(fine):
             pull_rows(k)
-            down_row(k - 1)
-            state_row(jnp.minimum(k + 3, rows + 3))
-
-        pull_rows(fine - 1)
-        down_row(fine - 2)
-        down_row(fine - 1)
-
-        @pl.loop(0, 3)
-        def _(k):
+        t_odd[...] = mm(g_odd[...].reshape(fine * cols, 768), back_odd[...]).reshape(fine, cols, 768)
+        t_even[...] = mm(g_even[...].reshape(fine * cols, 768), back_even[...]).reshape(fine, cols, 768)
+        for k in range(rows + 2):
             block_row(k)
-
-        @pl.loop(0, rows - 1)
-        def _(p):
-            mid_row(p)
-            block_row(p + 3)
-
-        mid_row(rows - 1)
+        lhs = [back[2 - i : 2 - i + rows].reshape(size, 1152) for i in range(3)]
+        act_grad[...] = mm(jnp.concatenate(lhs, axis=1), mid_t[...]).reshape(rows, cols, 384)
         for k in range(rows):
             hidden_pull(k)
 

time: 55.6 us -> 49.8 us (0.90)
  Pallas kernels: 35.9 us -> 30.1 us
    pallas_call x1, Pallas kernels: 16 us -> 12.8 us  [shards(): call(back_body(rows, cols, chan, count, o), [((count, chan, 128), BF16)],...]
    pallas_call x1, Pallas kernels: 10.1 us -> 7.45 us  [shards(): call(current_body(rows, cols, chan), [((rows + 6, cols, 384), BF16), ((ro...]
  transfers between devices with their start and end apart: 4 -> 4, of which waited for: 0 -> 0; matrix products, arithmetic and copies ran while one was open for 0% -> 0% of each run, Pallas kernels for 28% -> 26%
where the time goes in v5:
time: 49.8 us; the launch traced here: 49.6 us
  Pallas kernels  30.1 us (60%)
  blocking collectives  11.7 us (23%)
  starting transfers between devices  5.87 us (12%)
  local copies, waits for them, and re-layouts  1.4 us (3%)
    pallas_call x1, Pallas kernels, shards(): call(back_body(rows, cols, chan, count, o), [((count, chan, 128), BF16)],...  12.8 us
    all_to_all x1, blocking collectives, shards(): lax.all_to_all(payload, 'tile', split_axis=0, concat_axis=0, tiled=True)  11.7 us
    pallas_call x1, Pallas kernels, shards(): call(current_body(rows, cols, chan), [((rows + 6, cols, 384), BF16), ((ro...  7.45 us
    pallas_call x1, Pallas kernels, shards(): call(cached_body(rows, cols, count, width, tokens), [((rows + 4, cols, 38...  5.27 us
    ppermute x1, starting transfers between devices, shards(): got_even = lax.ppermute(part_even, 'tile', within)  3.97 us
    pallas_call x1, Pallas kernels, shards(): call(taps_body, [((4,), jnp.int32), ((2, 768, 768), BF16), ((768, 768), B...  1.93 us
    pallas_call x1, Pallas kernels, shards(): call(pack_body(rows, cols, o, chan), [((2 * rows, cols, 384), BF16), ((ed...  1.7 us
    unnamed x22, local copies, waits for them, and re-layouts  1.38 us
  transfers between devices with their start and end apart: 4, of which 0 were waited for; matrix products, arithmetic and copies ran while one was open for 0% of the time, Pallas kernels for 26%

profile of v5, /device:TPU:0, one launch (start us, length us, event | category | flops | bytes accessed | tf_op | source)
XLA Modules:
  0.0 49.6 jit_solution(17840058037425263502)
XLA Ops:
  0.0 0.1 pad_add_fusion.info
  0.1 1.3 %copy-done.1 = bf16[3,3,384,192]{2,3,1,0:T(8,128)(2,1)S(1)} copy-done((bf16[3,3,384,192]{2,3,1,0:T(8,128)(2,1)S(1)}, bf16[3,3,384,192]{2,3,1,0:T(8,128)(2,1)}, u32[]{:S(2)}) %copy-start.1) | copy-done | bytes 1327128
  1.4 1.9 %shard_map.100 = (s32[4]{0:T(128)S(1)}, bf16[2,768,768]{2,1,0:T(8,128)(2,1)S(1)}, bf16[768,768]{1,0:T(8,128)(2,1)S(1)}, bf16[768,768]{1,0:T(8,128)(2,1)S(1)}) custom-call(s32[4]{0:T(128)S(1)} %pad_add_fusion.info, bf16[3,3,192,384]{3,2,1,0:T(8,128)(2,1)S(1)} %bitcast.21), custom_call_target="tpu_custom_call" | custom-call | flops 10000000000 | bytes 1048576 | tf_op jit(solution)/shard_map/pallas_call | solution.py:459
  3.4 0.0 slice-start.1
  3.4 0.0 copy-done.2
  3.4 0.0 copy-done.4
  3.4 0.0 copy-done.5
  3.4 0.0 copy-start.3
  3.4 0.0 copy-start.6
  3.4 1.7 %shard_map.102 = (bf16[8,160,384]{2,1,0:T(8,128)(2,1)S(1)}, bf16[608,384]{1,0:T(8,128)(2,1)S(1)}, bf16[608,384]{1,0:T(8,128)(2,1)S(1)}) custom-call(s32[4]{0:T(128)S(1)} %get-tuple-element.19.info, bf16[8,192,320]{2,1,0:T(8,128)(2,1)S(1)} %bitcast.22, bf16[4,16,160]{2,1,0:T(8,128)(2,1)S(1)} %bitcast.25, bf16[2,4,16,160]{3,2,1,0:T(8,128)(2,1)S(1)} %bitcast.23), custom_call_target="tpu_custom_call" | custom-call | flops 10000000000 | bytes 1048576 | tf_op jit(solution)/shard_map/pallas_call | solution.py:465
  5.1 0.6 %collective-permute-start = (bf16[608,384]{1,0:T(8,128)(2,1)S(1)}, bf16[608,384]{1,0:T(8,128)(2,1)S(1)}, u32[]{:S(2)}, u32[]{:S(2)}) collective-permute-start(bf16[608,384]{1,0:T(8,128)(2,1)S(1)} %get-tuple-element.21), channel_id=1, source_target_pairs={{0,1},{1,0},{2,3},{3,2},{4,5},{5,4},{6,7},{7,6},{8,9},{9,8},{10,11... | collective-permute-start | bytes 1400840 | tf_op jit(solution)/shard_map/ppermute | solution.py:470
  5.7 0.7 %collective-permute-start.1 = (bf16[608,384]{1,0:T(8,128)(2,1)S(1)}, bf16[608,384]{1,0:T(8,128)(2,1)S(1)}, u32[]{:S(2)}, u32[]{:S(2)}) collective-permute-start(bf16[608,384]{1,0:T(8,128)(2,1)S(1)} %get-tuple-element.22), channel_id=1, source_target_pairs={{0,0},{1,2},{2,1},{3,4},{4,3},{5,6},{6,5},{7,7},{8,8},{9,10},{10,9... | collective-permute-start | bytes 1400840 | tf_op jit(solution)/shard_map/ppermute | solution.py:471
  6.4 0.0 slice-done
  6.4 0.0 slice-done.1
  6.4 0.0 copy-done.3
  6.4 0.0 copy-done.6
  6.4 0.0 copy-start.7
  6.4 0.0 copy-start
  6.4 0.0 copy-start.8
  6.5 5.3 %shard_map.101 = (f32[8,160,384]{2,1,0:T(8,128)S(1)}, bf16[480,384]{1,0:T(8,128)(2,1)S(1)}, bf16[480,384]{1,0:T(8,128)(2,1)S(1)}, bf16[3456,384]{1,0:T(8,128)(2,1)S(1)}, bf16[8,128,640]{2,1,0:T(8,128)(2,1)S(1)}) custom-call(s32[4]{0:T(128)S(1)} %get-tuple-element.19.info, s32[8]{0:T(128)S(1)} %copy-done.6, bf16[2,4,160,384]{3,2,1,0:T(8,128)(2,1)S(1)} %copy-done.3, ...), custom_call_target="tpu_custom_call" | custom-call | flops 4000000000 | bytes 1048576 | tf_op jit(solution)/shard_map/pallas_call | solution.py:475
  11.7 4.0 %collective-permute-start.2 = (bf16[480,384]{1,0:T(8,128)(2,1)S(1)}, bf16[480,384]{1,0:T(8,128)(2,1)S(1)}, u32[]{:S(2)}, u32[]{:S(2)}) collective-permute-start(bf16[480,384]{1,0:T(8,128)(2,1)S(1)} %get-tuple-element.26), channel_id=1, source_target_pairs={{0,1},{1,0},{2,3},{3,2},{4,5},{5,4},{6,7},{7,6},{8,9},{9,8},{10,11... | collective-permute-start | bytes 1105928 | tf_op jit(solution)/shard_map/ppermute | solution.py:483
  15.7 0.7 %collective-permute-start.3 = (bf16[480,384]{1,0:T(8,128)(2,1)S(1)}, bf16[480,384]{1,0:T(8,128)(2,1)S(1)}, u32[]{:S(2)}, u32[]{:S(2)}) collective-permute-start(bf16[480,384]{1,0:T(8,128)(2,1)S(1)} %get-tuple-element.27), channel_id=1, source_target_pairs={{0,0},{1,2},{2,1},{3,4},{4,3},{5,6},{6,5},{7,7},{8,8},{9,10},{10,9... | collective-permute-start | bytes 1105928 | tf_op jit(solution)/shard_map/ppermute | solution.py:484
  16.4 0.0 copy-done
  16.5 0.1 maximum_multiply_fusion.half_out
  16.5 0.0 collective-permute-done.got_even.packed_even
  16.5 0.0 collective-permute-done.1.got_odd.packed_odd
  16.5 7.5 %shard_map.103 = (bf16[10,160,384]{2,1,0:T(8,128)(2,1)S(1)}, f32[8,160,384]{2,1,0:T(8,128)S(1)}) custom-call(s32[4]{0:T(128)S(1)} %get-tuple-element.19.info, bf16[4,16,160]{2,1,0:T(8,128)(2,1)S(1)} %bitcast.26, bf16[2,4,16,160]{3,2,1,0:T(8,128)(2,1)S(1)} %bitcast.24, bf16[608,384]{1,0:T(8,128)(2,1)S(1)} %collective-permute-done.got_even.packed_even, ...), custom_call_target="tpu_custom_call" | custom-call | flops 5000000000 | bytes 1048576 | tf_op jit(solution)/shard_map/pallas_call | solution.py:486
  24.0 0.0 collective-permute-done.2.got_even
  24.0 0.0 collective-permute-done.3.got_odd
  24.0 12.8 %shard_map.104 = bf16[8,16,128]{2,1,0:T(8,128)(2,1)S(1)} custom-call(s32[4]{0:T(128)S(1)} %get-tuple-element.19.info, bf16[10,160,384]{2,1,0:T(8,128)(2,1)S(1)} %get-tuple-element.23.hidden, f32[8,160,384]{2,1,0:T(8,128)S(1)} %get-tuple-element.24.conv, f32[8,160,384]{2,1,0:T(8,128)S(1)} %get-tuple-element.25.acc, ...), custom_call_target="tpu_custom_call" | custom-call | flops 8000000000 | bytes 1048576 | tf_op jit(solution)/shard_map/pallas_call | solution.py:499
  36.8 11.7 %all_to_all.5.got = bf16[8,16,128]{2,1,0:T(8,128)(2,1)S(1)} all-to-all(bf16[8,16,128]{2,1,0:T(8,128)(2,1)S(1)} %shard_map.104), channel_id=1, replica_groups=mesh['prompt'=4,'tile'=8] {'tile'}, dimensions={0} | all-to-all | bytes 65536 | tf_op jit(solution)/shard_map/all_to_all | solution.py:523
  48.5 1.0 %shard_map.105 = f32[64,160]{1,0:T(8,128)} custom-call(bf16[8,128,640]{2,1,0:T(8,128)(2,1)S(1)} %get-tuple-element.20.sel, bf16[8,16,128]{2,1,0:T(8,128)(2,1)S(1)} %all_to_all.5.got), custom_call_target="tpu_custom_call" | custom-call | flops 10000000 | bytes 1048576 | tf_op jit(solution)/shard_map/pallas_call | solution.py:524
  (12 shorter events, 0.0 us)
Async XLA Ops:
  0.1 1.3 %copy-start.1 = (bf16[3,3,384,192]{2,3,1,0:T(8,128)(2,1)S(1)}, bf16[3,3,384,192]{2,3,1,0:T(8,128)(2,1)}, u32[]{:S(2)}) copy-start(bf16[3,3,384,192]{2,3,1,0:T(8,128)(2,1)} %param.16) | copy-start | bytes 3981316
  1.4 2.0 %copy-start.2 = (bf16[8,320,192]{1,2,0:T(8,128)(2,1)S(1)}, bf16[8,320,192]{1,2,0:T(8,128)(2,1)}, u32[]{:S(2)}) copy-start(bf16[8,320,192]{1,2,0:T(8,128)(2,1)} %param.13) | copy-start | bytes 2949124
  1.4 2.0 %copy-start.4 = (bf16[2,4,160,16]{2,3,1,0:T(8,128)(2,1)S(1)}, bf16[2,4,160,16]{2,3,1,0:T(8,128)(2,1)}, u32[]{:S(2)}) copy-start(bf16[2,4,160,16]{2,3,1,0:T(8,128)(2,1)} %param.11) | copy-start | bytes 122884
  1.4 2.0 %copy-start.5 = (bf16[4,160,16]{1,2,0:T(8,128)(2,1)S(1)}, bf16[4,160,16]{1,2,0:T(8,128)(2,1)}, u32[]{:S(2)}) copy-start(bf16[4,160,16]{1,2,0:T(8,128)(2,1)} %param.10) | copy-start | bytes 61444
  1.4 5.0 %slice-start = ((s8[7962624]{0:T(1024)(128)(4,1)}), s8[4194304]{0:T(1024)(128)(4,1)S(1)}, s32[]{:S(2)}) async-start(s8[7962624]{0:T(1024)(128)(4,1)} %bitcast.17), calls=%async_computation.1 | async-start | bytes 8388608
  3.4 3.0 %slice-start.1 = ((s8[7962624]{0:T(1024)(128)(4,1)}), s8[3768320]{0:T(1024)(128)(4,1)S(1)}, s32[]{:S(2)}) async-start(s8[7962624]{0:T(1024)(128)(4,1)} %bitcast.17), calls=%async_computation.2 | async-start | bytes 7536640
  3.4 3.0 %copy-start.3 = (bf16[2,4,160,384]{3,2,1,0:T(8,128)(2,1)S(1)}, bf16[2,4,160,384]{3,2,1,0:T(8,128)(2,1)}, u32[]{:S(2)}) copy-start(bf16[2,4,160,384]{3,2,1,0:T(8,128)(2,1)} %features.1) | copy-start | bytes 2949124
  3.4 3.0 %copy-start.6 = (s32[8]{0:T(128)S(1)}, s32[8]{0:T(128)}, u32[]{:S(2)}) copy-start(s32[8]{0:T(128)} %order.1) | copy-start | bytes 100
  5.1 11.4 %collective-permute-start = (bf16[608,384]{1,0:T(8,128)(2,1)S(1)}, bf16[608,384]{1,0:T(8,128)(2,1)S(1)}, u32[]{:S(2)}, u32[]{:S(2)}) collective-permute-start(bf16[608,384]{1,0:T(8,128)(2,1)S(1)} %get-tuple-element.21), channel_id=1, source_target_pairs={{0,1},{1,0},{2,3},{3,2},{4,5},{5,4},{6,7},{7,6},{8,9},{9,8},{10,11... | collective-permute-start | bytes 1400840 | tf_op jit(solution)/shard_map/ppermute | solution.py:470
  5.7 10.9 %collective-permute-start.1 = (bf16[608,384]{1,0:T(8,128)(2,1)S(1)}, bf16[608,384]{1,0:T(8,128)(2,1)S(1)}, u32[]{:S(2)}, u32[]{:S(2)}) collective-permute-start(bf16[608,384]{1,0:T(8,128)(2,1)S(1)} %get-tuple-element.22), channel_id=1, source_target_pairs={{0,0},{1,2},{2,1},{3,4},{4,3},{5,6},{6,5},{7,7},{8,8},{9,10},{10,9... | collective-permute-start | bytes 1400840 | tf_op jit(solution)/shard_map/ppermute | solution.py:471
  6.4 10.0 %copy-start.7 = (f32[384]{0:T(512)S(1)}, f32[384]{0:T(512)}, u32[]{:S(2)}) copy-start(f32[384]{0:T(512)} %param.17) | copy-start | bytes 4612
  6.4 10.0 %copy-start = (bf16[3,3,3,16,384]{4,3,2,1,0:T(8,128)(2,1)S(1)}, bf16[3,3,3,16,384]{4,3,2,1,0:T(8,128)(2,1)}, u32[]{:S(2)}) copy-start(bf16[3,3,3,16,384]{4,3,2,1,0:T(8,128)(2,1)} %param.14) | copy-start | bytes 995332
  6.4 10.0 %copy-start.8 = (f32[192]{0:T(256)S(1)}, f32[192]{0:T(256)}, u32[]{:S(2)}) copy-start(f32[192]{0:T(256)} %param.18) | copy-start | bytes 2308
  11.7 12.3 %collective-permute-start.2 = (bf16[480,384]{1,0:T(8,128)(2,1)S(1)}, bf16[480,384]{1,0:T(8,128)(2,1)S(1)}, u32[]{:S(2)}, u32[]{:S(2)}) collective-permute-start(bf16[480,384]{1,0:T(8,128)(2,1)S(1)} %get-tuple-element.26), channel_id=1, source_target_pairs={{0,1},{1,0},{2,3},{3,2},{4,5},{5,4},{6,7},{7,6},{8,9},{9,8},{10,11... | collective-permute-start | bytes 1105928 | tf_op jit(solution)/shard_map/ppermute | solution.py:483
  15.7 8.3 %collective-permute-start.3 = (bf16[480,384]{1,0:T(8,128)(2,1)S(1)}, bf16[480,384]{1,0:T(8,128)(2,1)S(1)}, u32[]{:S(2)}, u32[]{:S(2)}) collective-permute-start(bf16[480,384]{1,0:T(8,128)(2,1)S(1)} %get-tuple-element.27), channel_id=1, source_target_pairs={{0,0},{1,2},{2,1},{3,4},{4,3},{5,6},{6,5},{7,7},{8,8},{9,10},{10,9... | collective-permute-start | bytes 1105928 | tf_op jit(solution)/shard_map/ppermute | solution.py:484

commit v6 on v5

--- a/solution.py
+++ b/solution.py
@@ -10,6 +10,22 @@
 BF16 = jnp.bfloat16
 VM = pl.BlockSpec(memory_space=pltpu.VMEM)
 SM = pl.BlockSpec(memory_space=pltpu.SMEM)
+
+
+def phase(info, *groups):
+    @pl.when(info[1] >= 0)
+    def _():
+        total = max(len(g) for g in groups)
+        done = [0] * len(groups)
+        for k in range(total):
+            for n, g in enumerate(groups):
+                while done[n] * total < (k + 1) * len(g):
+                    g[done[n]]()
+                    done[n] += 1
+
+
+def steps(f, *keys):
+    return [lambda key=key: f(*key) for key in keys]
 
 
 def call(body, outs, n_smem, n_vmem, scratch, flops, limit, smem_outs=0):
@@ -123,32 +139,43 @@
 def cached_body(rows, cols, count, width, tokens):
     size = rows * cols
 
-    def body(info, order, features, mid, acc, send_even, send_odd, mid_t, sel, wide):
-        for t in range(2):
-            for r in range(rows):
-                at = slice(r * cols, (r + 1) * cols)
-                x = features[t, r]
-                x32 = x.astype(F32)
-                base = t * 1152
-                wide[at, base : base + 384] = from_left(x32).astype(BF16)
-                wide[at, base + 384 : base + 768] = x
-                wide[at, base + 768 : base + 1152] = from_right(x32).astype(BF16)
-        lhs = wide[...]
-        kernels = [jnp.concatenate([mid[0, i], mid[1, i]], axis=0) for i in range(3)]
-        pair = mm(lhs, jnp.concatenate([kernels[0], kernels[1]], axis=1))
-        for i in range(3):
-            for j in range(3):
-                at = (i * 3 + j) * 384
-                mid_t[at : at + 384] = mid[2, i, j * 384 : (j + 1) * 384].T
-        placing(info, order, sel, count, width, tokens)
-        last_kernel = mm(lhs, kernels[2])
-        for k in range(rows + 4):
+    def body(info, order, features, mid, acc, send_even, send_odd, mid_t, sel, wide, parts):
+        def spread(t, r):
+            at = slice(r * cols, (r + 1) * cols)
+            x = features[t, r]
+            x32 = x.astype(F32)
+            base = t * 1152
+            wide[at, base : base + 384] = from_left(x32).astype(BF16)
+            wide[at, base + 384 : base + 768] = x
+            wide[at, base + 768 : base + 1152] = from_right(x32).astype(BF16)
+
+        def product(i, lanes):
+            parts[i, :, lanes] = mm(wide[...], jnp.concatenate([mid[0, i, :, lanes], mid[1, i, :, lanes]], axis=0))
+
+        def double():
+            left = jnp.concatenate([mid[0, 0, :, 256:384], mid[1, 0, :, 256:384]], axis=0)
+            right = jnp.concatenate([mid[0, 1, :, 256:384], mid[1, 1, :, 256:384]], axis=0)
+            both = mm(wide[...], jnp.concatenate([left, right], axis=1))
+            parts[0, :, 256:384] = both[:, :128]
+            parts[1, :, 256:384] = both[:, 128:]
+
+        def turn(i, j):
+            at = (i * 3 + j) * 384
+            mid_t[at : at + 384] = mid[2, i, j * 384 : (j + 1) * 384].T
+
+        def total_row(k):
             total = jnp.zeros((cols, 384), F32)
-            for i, part in enumerate((pair[:, :384], pair[:, 384:], last_kernel)):
+            for i in range(3):
                 r = k - 3 + i
                 if 0 <= r < rows:
-                    total = total + part[r * cols : (r + 1) * cols]
+                    total = total + parts[i, r * cols : (r + 1) * cols]
             acc[k] = total
+
+        most, rest = slice(0, 256), slice(256, 384)
+        phase(info, steps(spread, *[(t, r) for t in range(2) for r in range(rows)]))
+        phase(info, steps(product, (0, most), (1, most)) + steps(double, ()), steps(turn, *[(i, j) for i in range(3) for j in range(3)]))
+        phase(info, steps(product, (2, most), (2, rest)), steps(placing(info, order, sel, count, width, tokens), *[(t,) for t in range(count)]))
+        phase(info, steps(total_row, *[(k,) for k in range(rows + 4)]))
         for send, last in ((send_even, 1 - info[0]), (send_odd, info[0])):
             for k in range(3):
                 send[k * cols : (k + 1) * cols] = acc[1 + last * 3 + k].astype(BF16)
@@ -218,17 +245,21 @@
             wide[k, :, 384:768] = act.astype(BF16)
             wide[k, :, 768:1152] = from_right(act).astype(BF16)
 
-        def conv_rows(p, count):
-            lhs = [wide[p + i : p + i + count].reshape(count * cols, 1152) for i in range(3)]
-            total = mm(jnp.concatenate(lhs, axis=1), mid[2].reshape(3456, 384))
-            conv[p : p + count] = total.reshape(count, cols, 384)
-
-        for k in range(rows + 2):
-            hidden_row(k)
-        conv_rows(0, rows)
-        for k in range(rows + 2, rows + 6):
-            hidden_row(k)
-        conv_rows(rows, 4)
+        def conv_rows(p, number, lanes):
+            lhs = [wide[p + i : p + i + number].reshape(number * cols, 1152) for i in range(3)]
+            total = mm(jnp.concatenate(lhs, axis=1), mid[2, :, :, lanes].reshape(3456, lanes.stop - lanes.start))
+            conv[p : p + number, :, lanes] = total.reshape(number, cols, lanes.stop - lanes.start)
+
+        def hiddens(first, last):
+            return steps(hidden_row, *[(k,) for k in range(first, last)])
+
+        def convs(p, number):
+            return steps(conv_rows, (p, number, slice(0, 256)), (p, number, slice(256, 384)))
+
+        phase(info, hiddens(0, 4))
+        phase(info, convs(0, 2), hiddens(4, rows + 3))
+        phase(info, convs(2, rows - 1), hiddens(rows + 3, rows + 6))
+        phase(info, convs(rows + 1, 3))
 
     return body
 
@@ -289,10 +320,21 @@
                 x = x + edge[k]
             spread(wide, k, inside(x, k, 2, rows + 2), False)
 
-        def up_rows(k, count):
-            x = wide[k : k + count].reshape(count * cols, 1152)
-            p0[k : k + count] = mm(x[:, 0:768], fwd[0]).reshape(count, cols, 768)
-            p1[k : k + count] = mm(x[:, 384:1152], fwd[1]).reshape(count, cols, 768)
+        def up_rows(k, number, b, n):
+            x = wide[k : k + number, :, b * 384 : b * 384 + 768].reshape(number * cols, 768)
+            lanes = slice(n * 256, n * 256 + 256)
+            (p0, p1)[b][k : k + number, :, lanes] = mm(x, fwd[b, :, lanes]).reshape(number, cols, 256)
+
+        def down_rows(k, number, odd, n):
+            g, kernel, t = (g_odd, back_odd, t_odd) if odd else (g_even, back_even, t_even)
+            lanes = slice(n * 256, n * 256 + 256)
+            x = g[k : k + number].reshape(number * cols, 768)
+            t[k : k + number, :, lanes] = mm(x, kernel[:, lanes]).reshape(number, cols, 256)
+
+        def mid_rows(k, number, lanes):
+            lhs = [back[k + 2 - i : k + 2 - i + number].reshape(number * cols, 1152) for i in range(3)]
+            total = mm(jnp.concatenate(lhs, axis=1), mid_t[:, lanes])
+            act_grad[k : k + number, :, lanes] = total.reshape(number, cols, lanes.stop - lanes.start)
 
         lane = lax.broadcasted_iota(jnp.int32, (cols, 128), 1)
         low = lane < 64
@@ -325,11 +367,13 @@
             target[k, :, 512:640] = from_left(a1).astype(BF16)
             target[k, :, 640:768] = jnp.where(mine, from_right(am), from_left(am)).astype(BF16)
 
-        def pull_rows(k):
+        def pull_odd(k):
             v0 = p0[k, :, 256:384] + p0[k + 1, :, 0:128]
             v1 = p1[k, :, 256:384] + p1[k + 1, :, 0:128]
             vm = jnp.where(low, p0[k, :, 640:768] + p0[k + 1, :, 512:640], p1[k, :, 640:768] + p1[k + 1, :, 512:640])
             store(pull(v0, v1, vm, reward[2 * k], True), g_odd, k)
+
+        def pull_even(k):
             v0 = p0[k + 1, :, 128:256] + p0[k, :, 384:512]
             v1 = p1[k + 1, :, 128:256] + p1[k, :, 384:512]
             vm = jnp.where(low, p1[k + 1, :, 512:640] + p1[k, :, 640:768], p0[k + 1, :, 512:640] + p0[k, :, 640:768])
@@ -347,22 +391,30 @@
             dv = inv * (d - s * jnp.mean(d * s, axis=1, keepdims=True))
             hid[k] = (back[k + 1, :, 384:768].astype(F32) + dv).astype(BF16)
 
-        fine = rows + 3
-        for k in range(rows):
-            state_row(k)
-        up_rows(0, rows)
-        for k in range(rows, rows + 4):
-            state_row(k)
-        up_rows(rows, 4)
-        for k in range(fine):
-            pull_rows(k)
-        t_odd[...] = mm(g_odd[...].reshape(fine * cols, 768), back_odd[...]).reshape(fine, cols, 768)
-        t_even[...] = mm(g_even[...].reshape(fine * cols, 768), back_even[...]).reshape(fine, cols, 768)
-        for k in range(rows + 2):
-            block_row(k)
-        lhs = [back[2 - i : 2 - i + rows].reshape(size, 1152) for i in range(3)]
-        act_grad[...] = mm(jnp.concatenate(lhs, axis=1), mid_t[...]).reshape(rows, cols, 384)
-        for k in range(rows):
+        def each(f, first, last):
+            return steps(f, *[(k,) for k in range(first, last)])
+
+        def ups(k, number):
+            return steps(up_rows, *[(k, number, b, n) for n in range(3) for b in range(2)])
+
+        def downs(k, number):
+            return steps(down_rows, *[(k, number, odd, n) for n in range(3) for odd in (True, False)])
+
+        def mids(k, number):
+            return steps(mid_rows, (k, number, slice(0, 256)), (k, number, slice(256, 384)))
+
+        def pulls(first, last):
+            return [step for k in range(first, last) for step in steps(pull_odd, (k,)) + steps(pull_even, (k,))]
+
+        phase(info, each(state_row, 0, rows))
+        phase(info, ups(0, rows), each(state_row, rows, rows + 4))
+        phase(info, ups(rows, 4), pulls(0, rows - 1))
+        phase(info, downs(0, rows - 1), pulls(rows - 1, rows + 1))
+        phase(info, downs(rows - 1, 2), pulls(rows + 1, rows + 3), each(block_row, 0, 2))
+        phase(info, downs(rows + 1, 2), each(block_row, 2, rows))
+        phase(info, each(block_row, rows, rows + 2), mids(0, 2))
+        phase(info, mids(2, rows - 2), each(hidden_pull, 0, 2))
+        for k in range(2, rows):
             hidden_pull(k)
 
         z = mm_t(w_in[...], hid[...].reshape(size, 384))
@@ -406,12 +458,15 @@
     part = jnp.where(group == 2, pair, group)
     fixed = (2 * part + (w & 1)) * tokens + (w >> 1) - column
     fixed = jnp.where(lane < 3 * width, fixed, -99999)
-    for t in range(count):
+
+    def one(t):
         step = t + 1 - 2 * pair
         valid = jnp.logical_and(step >= 0, step < count)
         beside = jnp.where(valid, piece * order[jnp.clip(step, 0, count - 1)], -9999)
         begin = jnp.where(group == 2, beside, piece * order[t])
         sel[t] = (fixed + begin == 0).astype(F32).astype(BF16)
+
+    return one
 
 
 def place_body(count, chan, tokens):
@@ -478,7 +533,7 @@
             ((rows + 4, cols, 384), F32), ((3 * cols, 384), BF16), ((3 * cols, 384), BF16), ((3456, 384), BF16),
             ((count, 128, 4 * tokens), BF16),
         ],
-        2, 2, [pltpu.VMEM((size, 2304), BF16)], 4e9, 24,
+        2, 2, [pltpu.VMEM((size, 2304), BF16), pltpu.VMEM((3, size, 384), F32)], 4e9, 24,
     )(info, shard_order, cached_features, mid)
     got_even = lax.ppermute(part_even, "tile", within)
     got_odd = lax.ppermute(part_odd, "tile", across)

time: 49.8 us -> 51.8 us (1.040)
  Pallas kernels: 30.1 us -> 32.2 us
    pallas_call x1, Pallas kernels: 12.8 us -> 13.7 us  [shards(): call(back_body(rows, cols, chan, count, o), [((count, chan, 128), BF16)],...]
    pallas_call x1, Pallas kernels: 7.45 us -> 8.1 us  [shards(): call(current_body(rows, cols, chan), [((rows + 6, cols, 384), BF16), ((ro...]
  transfers between devices with their start and end apart: 4 -> 4, of which waited for: 0 -> 0; matrix products, arithmetic and copies ran while one was open for 0% -> 0% of each run, Pallas kernels for 26% -> 27%
where the time goes in v6:
time: 51.8 us; the launch traced here: 51.6 us
  Pallas kernels  32.2 us (62%)
  blocking collectives  11.7 us (23%)
  starting transfers between devices  5.87 us (11%)
  local copies, waits for them, and re-layouts  1.4 us (3%)
    pallas_call x1, Pallas kernels, shards(): call(back_body(rows, cols, chan, count, o), [((count, chan, 128), BF16)],...  13.7 us
    all_to_all x1, blocking collectives, shards(): lax.all_to_all(payload, 'tile', split_axis=0, concat_axis=0, tiled=True)  11.7 us
    pallas_call x1, Pallas kernels, shards(): call(current_body(rows, cols, chan), [((rows + 6, cols, 384), BF16), ((ro...  8.1 us
    pallas_call x1, Pallas kernels, shards(): call(cached_body(rows, cols, count, width, tokens), [((rows + 4, cols, 38...  5.72 us
    ppermute x1, starting transfers between devices, shards(): got_even = lax.ppermute(part_even, 'tile', within)  3.97 us
    pallas_call x1, Pallas kernels, shards(): call(taps_body, [((4,), jnp.int32), ((2, 768, 768), BF16), ((768, 768), B...  1.93 us
    pallas_call x1, Pallas kernels, shards(): call(pack_body(rows, cols, o, chan), [((2 * rows, cols, 384), BF16), ((ed...  1.7 us
    unnamed x22, local copies, waits for them, and re-layouts  1.38 us
  transfers between devices with their start and end apart: 4, of which 0 were waited for; matrix products, arithmetic and copies ran while one was open for 0% of the time, Pallas kernels for 27%

profile of v6, /device:TPU:0, one launch (start us, length us, event | category | flops | bytes accessed | tf_op | source)
XLA Modules:
  0.0 51.6 jit_solution(11343851556278153733)
XLA Ops:
  0.0 0.1 pad_add_fusion.info
  0.1 1.3 %copy-done.1 = bf16[3,3,384,192]{2,3,1,0:T(8,128)(2,1)S(1)} copy-done((bf16[3,3,384,192]{2,3,1,0:T(8,128)(2,1)S(1)}, bf16[3,3,384,192]{2,3,1,0:T(8,128)(2,1)}, u32[]{:S(2)}) %copy-start.1) | copy-done | bytes 1327128
  1.4 1.9 %shard_map.100 = (s32[4]{0:T(128)S(1)}, bf16[2,768,768]{2,1,0:T(8,128)(2,1)S(1)}, bf16[768,768]{1,0:T(8,128)(2,1)S(1)}, bf16[768,768]{1,0:T(8,128)(2,1)S(1)}) custom-call(s32[4]{0:T(128)S(1)} %pad_add_fusion.info, bf16[3,3,192,384]{3,2,1,0:T(8,128)(2,1)S(1)} %bitcast.21), custom_call_target="tpu_custom_call" | custom-call | flops 10000000000 | bytes 1048576 | tf_op jit(solution)/shard_map/pallas_call | solution.py:514
  3.4 0.0 slice-start.1
  3.4 0.0 copy-done.2
  3.4 0.0 copy-done.4
  3.4 0.0 copy-done.5
  3.4 0.0 copy-start.3
  3.4 0.0 copy-start.6
  3.4 1.7 %shard_map.102 = (bf16[8,160,384]{2,1,0:T(8,128)(2,1)S(1)}, bf16[608,384]{1,0:T(8,128)(2,1)S(1)}, bf16[608,384]{1,0:T(8,128)(2,1)S(1)}) custom-call(s32[4]{0:T(128)S(1)} %get-tuple-element.19.info, bf16[8,192,320]{2,1,0:T(8,128)(2,1)S(1)} %bitcast.22, bf16[4,16,160]{2,1,0:T(8,128)(2,1)S(1)} %bitcast.25, bf16[2,4,16,160]{3,2,1,0:T(8,128)(2,1)S(1)} %bitcast.23), custom_call_target="tpu_custom_call" | custom-call | flops 10000000000 | bytes 1048576 | tf_op jit(solution)/shard_map/pallas_call | solution.py:520
  5.1 0.6 %collective-permute-start = (bf16[608,384]{1,0:T(8,128)(2,1)S(1)}, bf16[608,384]{1,0:T(8,128)(2,1)S(1)}, u32[]{:S(2)}, u32[]{:S(2)}) collective-permute-start(bf16[608,384]{1,0:T(8,128)(2,1)S(1)} %get-tuple-element.21), channel_id=1, source_target_pairs={{0,1},{1,0},{2,3},{3,2},{4,5},{5,4},{6,7},{7,6},{8,9},{9,8},{10,11... | collective-permute-start | bytes 1400840 | tf_op jit(solution)/shard_map/ppermute | solution.py:525
  5.7 0.7 %collective-permute-start.1 = (bf16[608,384]{1,0:T(8,128)(2,1)S(1)}, bf16[608,384]{1,0:T(8,128)(2,1)S(1)}, u32[]{:S(2)}, u32[]{:S(2)}) collective-permute-start(bf16[608,384]{1,0:T(8,128)(2,1)S(1)} %get-tuple-element.22), channel_id=1, source_target_pairs={{0,0},{1,2},{2,1},{3,4},{4,3},{5,6},{6,5},{7,7},{8,8},{9,10},{10,9... | collective-permute-start | bytes 1400840 | tf_op jit(solution)/shard_map/ppermute | solution.py:526
  6.4 0.0 slice-done
  6.4 0.0 slice-done.1
  6.4 0.0 copy-done.3
  6.4 0.0 copy-done.6
  6.4 0.0 copy-start.7
  6.4 0.0 copy-start
  6.4 0.0 copy-start.8
  6.5 5.7 %shard_map.101 = (f32[8,160,384]{2,1,0:T(8,128)S(1)}, bf16[480,384]{1,0:T(8,128)(2,1)S(1)}, bf16[480,384]{1,0:T(8,128)(2,1)S(1)}, bf16[3456,384]{1,0:T(8,128)(2,1)S(1)}, bf16[8,128,640]{2,1,0:T(8,128)(2,1)S(1)}) custom-call(s32[4]{0:T(128)S(1)} %get-tuple-element.19.info, s32[8]{0:T(128)S(1)} %copy-done.6, bf16[2,4,160,384]{3,2,1,0:T(8,128)(2,1)S(1)} %copy-done.3, ...), custom_call_target="tpu_custom_call" | custom-call | flops 4000000000 | bytes 1048576 | tf_op jit(solution)/shard_map/pallas_call | solution.py:530
  12.2 4.0 %collective-permute-start.2 = (bf16[480,384]{1,0:T(8,128)(2,1)S(1)}, bf16[480,384]{1,0:T(8,128)(2,1)S(1)}, u32[]{:S(2)}, u32[]{:S(2)}) collective-permute-start(bf16[480,384]{1,0:T(8,128)(2,1)S(1)} %get-tuple-element.26), channel_id=1, source_target_pairs={{0,1},{1,0},{2,3},{3,2},{4,5},{5,4},{6,7},{7,6},{8,9},{9,8},{10,11... | collective-permute-start | bytes 1105928 | tf_op jit(solution)/shard_map/ppermute | solution.py:538
  16.1 0.7 %collective-permute-start.3 = (bf16[480,384]{1,0:T(8,128)(2,1)S(1)}, bf16[480,384]{1,0:T(8,128)(2,1)S(1)}, u32[]{:S(2)}, u32[]{:S(2)}) collective-permute-start(bf16[480,384]{1,0:T(8,128)(2,1)S(1)} %get-tuple-element.27), channel_id=1, source_target_pairs={{0,0},{1,2},{2,1},{3,4},{4,3},{5,6},{6,5},{7,7},{8,8},{9,10},{10,9... | collective-permute-start | bytes 1105928 | tf_op jit(solution)/shard_map/ppermute | solution.py:539
  16.8 0.0 copy-done.7
  16.9 0.1 maximum_multiply_fusion.half_out
  17.0 0.0 collective-permute-done.got_even.packed_even
  17.0 0.0 collective-permute-done.1.got_odd.packed_odd
  17.0 8.1 %shard_map.103 = (bf16[10,160,384]{2,1,0:T(8,128)(2,1)S(1)}, f32[8,160,384]{2,1,0:T(8,128)S(1)}) custom-call(s32[4]{0:T(128)S(1)} %get-tuple-element.19.info, bf16[4,16,160]{2,1,0:T(8,128)(2,1)S(1)} %bitcast.26, bf16[2,4,16,160]{3,2,1,0:T(8,128)(2,1)S(1)} %bitcast.24, bf16[608,384]{1,0:T(8,128)(2,1)S(1)} %collective-permute-done.got_even.packed_even, ...), custom_call_target="tpu_custom_call" | custom-call | flops 5000000000 | bytes 1048576 | tf_op jit(solution)/shard_map/pallas_call | solution.py:541
  25.1 0.0 collective-permute-done.2.got_even
  25.1 0.0 collective-permute-done.3.got_odd
  25.1 13.7 %shard_map.104 = bf16[8,16,128]{2,1,0:T(8,128)(2,1)S(1)} custom-call(s32[4]{0:T(128)S(1)} %get-tuple-element.19.info, bf16[10,160,384]{2,1,0:T(8,128)(2,1)S(1)} %get-tuple-element.23.hidden, f32[8,160,384]{2,1,0:T(8,128)S(1)} %get-tuple-element.24.conv, f32[8,160,384]{2,1,0:T(8,128)S(1)} %get-tuple-element.25.acc, ...), custom_call_target="tpu_custom_call" | custom-call | flops 8000000000 | bytes 1048576 | tf_op jit(solution)/shard_map/pallas_call | solution.py:554
  38.8 11.7 %all_to_all.5.got = bf16[8,16,128]{2,1,0:T(8,128)(2,1)S(1)} all-to-all(bf16[8,16,128]{2,1,0:T(8,128)(2,1)S(1)} %shard_map.104), channel_id=1, replica_groups=mesh['prompt'=4,'tile'=8] {'tile'}, dimensions={0} | all-to-all | bytes 65536 | tf_op jit(solution)/shard_map/all_to_all | solution.py:578
  50.5 1.0 %shard_map.105 = f32[64,160]{1,0:T(8,128)} custom-call(bf16[8,128,640]{2,1,0:T(8,128)(2,1)S(1)} %get-tuple-element.20.sel, bf16[8,16,128]{2,1,0:T(8,128)(2,1)S(1)} %all_to_all.5.got), custom_call_target="tpu_custom_call" | custom-call | flops 10000000 | bytes 1048576 | tf_op jit(solution)/shard_map/pallas_call | solution.py:579
  (12 shorter events, 0.0 us)
Async XLA Ops:
  0.1 1.3 %copy-start.1 = (bf16[3,3,384,192]{2,3,1,0:T(8,128)(2,1)S(1)}, bf16[3,3,384,192]{2,3,1,0:T(8,128)(2,1)}, u32[]{:S(2)}) copy-start(bf16[3,3,384,192]{2,3,1,0:T(8,128)(2,1)} %param.16) | copy-start | bytes 3981316
  1.4 2.0 %copy-start.2 = (bf16[8,320,192]{1,2,0:T(8,128)(2,1)S(1)}, bf16[8,320,192]{1,2,0:T(8,128)(2,1)}, u32[]{:S(2)}) copy-start(bf16[8,320,192]{1,2,0:T(8,128)(2,1)} %param.13) | copy-start | bytes 2949124
  1.4 2.0 %copy-start.4 = (bf16[2,4,160,16]{2,3,1,0:T(8,128)(2,1)S(1)}, bf16[2,4,160,16]{2,3,1,0:T(8,128)(2,1)}, u32[]{:S(2)}) copy-start(bf16[2,4,160,16]{2,3,1,0:T(8,128)(2,1)} %param.11) | copy-start | bytes 122884
  1.4 2.0 %copy-start.5 = (bf16[4,160,16]{1,2,0:T(8,128)(2,1)S(1)}, bf16[4,160,16]{1,2,0:T(8,128)(2,1)}, u32[]{:S(2)}) copy-start(bf16[4,160,16]{1,2,0:T(8,128)(2,1)} %param.10) | copy-start | bytes 61444
  1.4 5.0 %slice-start = ((s8[7962624]{0:T(1024)(128)(4,1)}), s8[4194304]{0:T(1024)(128)(4,1)S(1)}, s32[]{:S(2)}) async-start(s8[7962624]{0:T(1024)(128)(4,1)} %bitcast.17), calls=%async_computation.1 | async-start | bytes 8388608
  3.4 3.0 %slice-start.1 = ((s8[7962624]{0:T(1024)(128)(4,1)}), s8[3768320]{0:T(1024)(128)(4,1)S(1)}, s32[]{:S(2)}) async-start(s8[7962624]{0:T(1024)(128)(4,1)} %bitcast.17), calls=%async_computation.2 | async-start | bytes 7536640
  3.4 3.0 %copy-start.3 = (bf16[2,4,160,384]{3,2,1,0:T(8,128)(2,1)S(1)}, bf16[2,4,160,384]{3,2,1,0:T(8,128)(2,1)}, u32[]{:S(2)}) copy-start(bf16[2,4,160,384]{3,2,1,0:T(8,128)(2,1)} %features.1) | copy-start | bytes 2949124
  3.4 3.0 %copy-start.6 = (s32[8]{0:T(128)S(1)}, s32[8]{0:T(128)}, u32[]{:S(2)}) copy-start(s32[8]{0:T(128)} %order.1) | copy-start | bytes 100
  5.1 11.9 %collective-permute-start = (bf16[608,384]{1,0:T(8,128)(2,1)S(1)}, bf16[608,384]{1,0:T(8,128)(2,1)S(1)}, u32[]{:S(2)}, u32[]{:S(2)}) collective-permute-start(bf16[608,384]{1,0:T(8,128)(2,1)S(1)} %get-tuple-element.21), channel_id=1, source_target_pairs={{0,1},{1,0},{2,3},{3,2},{4,5},{5,4},{6,7},{7,6},{8,9},{9,8},{10,11... | collective-permute-start | bytes 1400840 | tf_op jit(solution)/shard_map/ppermute | solution.py:525
  5.7 11.3 %collective-permute-start.1 = (bf16[608,384]{1,0:T(8,128)(2,1)S(1)}, bf16[608,384]{1,0:T(8,128)(2,1)S(1)}, u32[]{:S(2)}, u32[]{:S(2)}) collective-permute-start(bf16[608,384]{1,0:T(8,128)(2,1)S(1)} %get-tuple-element.22), channel_id=1, source_target_pairs={{0,0},{1,2},{2,1},{3,4},{4,3},{5,6},{6,5},{7,7},{8,8},{9,10},{10,9... | collective-permute-start | bytes 1400840 | tf_op jit(solution)/shard_map/ppermute | solution.py:526
  6.4 10.4 %copy-start.7 = (f32[384]{0:T(512)S(1)}, f32[384]{0:T(512)}, u32[]{:S(2)}) copy-start(f32[384]{0:T(512)} %param.17) | copy-start | bytes 4612
  6.4 10.4 %copy-start = (bf16[3,3,3,16,384]{4,3,2,1,0:T(8,128)(2,1)S(1)}, bf16[3,3,3,16,384]{4,3,2,1,0:T(8,128)(2,1)}, u32[]{:S(2)}) copy-start(bf16[3,3,3,16,384]{4,3,2,1,0:T(8,128)(2,1)} %param.14) | copy-start | bytes 995332
  6.4 10.4 %copy-start.8 = (f32[192]{0:T(256)S(1)}, f32[192]{0:T(256)}, u32[]{:S(2)}) copy-start(f32[192]{0:T(256)} %param.18) | copy-start | bytes 2308
  12.2 12.9 %collective-permute-start.2 = (bf16[480,384]{1,0:T(8,128)(2,1)S(1)}, bf16[480,384]{1,0:T(8,128)(2,1)S(1)}, u32[]{:S(2)}, u32[]{:S(2)}) collective-permute-start(bf16[480,384]{1,0:T(8,128)(2,1)S(1)} %get-tuple-element.26), channel_id=1, source_target_pairs={{0,1},{1,0},{2,3},{3,2},{4,5},{5,4},{6,7},{7,6},{8,9},{9,8},{10,11... | collective-permute-start | bytes 1105928 | tf_op jit(solution)/shard_map/ppermute | solution.py:538
  16.1 9.0 %collective-permute-start.3 = (bf16[480,384]{1,0:T(8,128)(2,1)S(1)}, bf16[480,384]{1,0:T(8,128)(2,1)S(1)}, u32[]{:S(2)}, u32[]{:S(2)}) collective-permute-start(bf16[480,384]{1,0:T(8,128)(2,1)S(1)} %get-tuple-element.27), channel_id=1, source_target_pairs={{0,0},{1,2},{2,1},{3,4},{4,3},{5,6},{6,5},{7,7},{8,8},{9,10},{10,9... | collective-permute-start | bytes 1105928 | tf_op jit(solution)/shard_map/ppermute | solution.py:539

commit v7 on v5

--- a/solution.py
+++ b/solution.py
@@ -37,19 +37,27 @@
     return info[k].astype(F32)
 
 
-def col_index(cols, lanes):
-    return lax.broadcasted_iota(jnp.int32, (cols, lanes), 0)
-
-
 def from_left(x):
-    col = col_index(*x.shape)
-    return jnp.where(col == 0, 0.0, pltpu.roll(x, 1, 0))
+    moved = pltpu.roll(x, 1, 0)
+    first = lax.broadcasted_iota(jnp.int32, (8, x.shape[1]), 0) == 0
+    return jnp.concatenate([jnp.where(first, 0.0, moved[:8]), moved[8:]], axis=0)
 
 
 def from_right(x):
-    cols = x.shape[0]
-    col = col_index(*x.shape)
-    return jnp.where(col == cols - 1, 0.0, pltpu.roll(x, cols - 1, 0))
+    size = x.shape[0]
+    moved = pltpu.roll(x, size - 1, 0)
+    last = lax.broadcasted_iota(jnp.int32, (8, x.shape[1]), 0) == 7
+    return jnp.concatenate([moved[: size - 8], jnp.where(last, 0.0, moved[size - 8 :])], axis=0)
+
+
+def beside(target, base, lanes, x, ahead):
+    sides = (from_right, from_left) if ahead else (from_left, from_right)
+    for group, value in enumerate((sides[0](x), x, sides[1](x))):
+        at = base + group * 384 + lanes
+        target[:, at : at + 128] = value.astype(BF16)
+
+
+CHUNK = 32
 
 
 def pack_body(rows, cols, o, chan):
@@ -89,35 +97,42 @@
     for k in range(4):
         info_out[k] = info[k]
 
-    def rows_of(q, j):
-        parts = ((2,), (1, 2), (0, 1), (0,))[q]
-        total = up[parts[0], j].astype(F32)
-        for i in parts[1:]:
-            total = total + up[i, j].astype(F32)
-        return total
-
-    rest = []
-    for q in range(4):
-        c0, c1, c2 = (rows_of(q, j) for j in range(3))
-        tap = [t.astype(BF16) for t in (c2, c1 + c2, c0 + c1, c0)]
-        rest.append([t[128:] for t in tap])
-        for b, order in ((0, (3, 1)), (1, (2, 0))):
-            for side, p in enumerate(order):
-                fwd[b, side * 384 : side * 384 + 384, q * 128 : q * 128 + 128] = tap[p][:128].T
-                if q % 2 == 1:
-                    pair = (q - 1, q) if b == 0 else (q, q - 1)
-                    both = jnp.concatenate([rest[k][p] for k in pair], axis=0)
-                    at = 512 + (q // 2) * 128
-                    fwd[b, side * 384 : side * 384 + 384, at : at + 128] = both.T
-        target, side = ((back_odd, 1), (back_even, 0), (back_odd, 0), (back_even, 1))[q]
-        lanes = slice(side * 384, side * 384 + 384)
-        for block, (p0, p1) in enumerate(((1, 2), (3, 0))):
-            base = block * 384
-            target[base : base + 128, lanes] = tap[p0][:128]
-            target[base + 128 : base + 256, lanes] = tap[p1][:128]
-            low, high = (p0, p1) if q % 2 == 0 else (p1, p0)
-            target[base + 256 : base + 320, lanes] = tap[low][128:]
-            target[base + 320 : base + 384, lanes] = tap[high][128:]
+    parts = ((2,), (1, 2), (0, 1), (0,))
+    targets = ((back_odd, 1), (back_even, 0), (back_odd, 0), (back_even, 1))
+
+    def home(q, p, tile):
+        block, second = ((1, 1), (0, 0), (0, 1), (1, 0))[p]
+        target, side = targets[q]
+        if tile < 2:
+            row = block * 384 + second * 128 + tile * 64
+        else:
+            row = block * 384 + 256 + 64 * (second if q % 2 == 0 else 1 - second)
+        return target, row, side * 384
+
+    for tile in range(3):
+        for lanes in range(0, 384, 128):
+            w = [[up[i, j, tile * 64 : tile * 64 + 64, lanes : lanes + 128].astype(F32) for j in range(3)] for i in range(3)]
+            for q in range(4):
+                c = [w[parts[q][0]][j] + w[parts[q][1]][j] if len(parts[q]) > 1 else w[parts[q][0]][j] for j in range(3)]
+                for p, tap in enumerate((c[2], c[1] + c[2], c[0] + c[1], c[0])):
+                    target, row, side = home(q, p, tile)
+                    target[row : row + 64, side + lanes : side + lanes + 128] = tap.astype(BF16)
+
+    def tap_tile(q, p, tile, lanes):
+        target, row, side = home(q, p, tile)
+        return target[row : row + 64, side + lanes : side + lanes + 128]
+
+    for b, order in ((0, (3, 1)), (1, (2, 0))):
+        for side, p in enumerate(order):
+            for lanes in range(0, 384, 128):
+                at = slice(side * 384 + lanes, side * 384 + lanes + 128)
+                for q in range(4):
+                    both = jnp.concatenate([tap_tile(q, p, 0, lanes), tap_tile(q, p, 1, lanes)], axis=0)
+                    fwd[b, at, q * 128 : q * 128 + 128] = both.T
+                for half in range(2):
+                    pair = (2 * half, 2 * half + 1) if b == 0 else (2 * half + 1, 2 * half)
+                    both = jnp.concatenate([tap_tile(q, p, 2, lanes) for q in pair], axis=0)
+                    fwd[b, at, 512 + half * 128 : 640 + half * 128] = both.T
 
 
 def cached_body(rows, cols, count, width, tokens):
@@ -126,13 +141,9 @@
     def body(info, order, features, mid, acc, send_even, send_odd, mid_t, sel, wide):
         for t in range(2):
             for r in range(rows):
-                at = slice(r * cols, (r + 1) * cols)
-                x = features[t, r]
-                x32 = x.astype(F32)
-                base = t * 1152
-                wide[at, base : base + 384] = from_left(x32).astype(BF16)
-                wide[at, base + 384 : base + 768] = x
-                wide[at, base + 768 : base + 1152] = from_right(x32).astype(BF16)
+                for lanes in range(0, 384, 128):
+                    x = features[t, r, :, lanes : lanes + 128].astype(F32)
+                    beside(wide.at[r * cols : (r + 1) * cols], t * 1152, lanes, x, False)
         lhs = wide[...]
         kernels = [jnp.concatenate([mid[0, i], mid[1, i]], axis=0) for i in range(3)]
         pair = mm(lhs, jnp.concatenate([kernels[0], kernels[1]], axis=1))
@@ -160,7 +171,7 @@
     per = chan * rows
     base = 3 * cols
 
-    def body(info, latent, cached, got_even, got_odd, w_in, mid, half_gain, hidden, conv, lat, tall, wide, w_order):
+    def body(info, latent, cached, got_even, got_odd, w_in, mid, half_gain, hidden, conv, lat, tall, wide, w_order, plain):
         even = info[0] == 0
         lat[...] = jnp.zeros_like(lat)
 
@@ -204,19 +215,22 @@
         def hidden_row(k):
             lhs = tall[k : k + 3].reshape(27 * chan, 256)[:, 0:cols]
             h = lax.dot_general(lhs, w_order[...], (((0,), (0,)), ((), ())), preferred_element_type=F32)
-            h = h.astype(BF16)
-            hidden[k] = h
-            v = h.astype(F32)
-            inv = lax.rsqrt(jnp.mean(v * v, axis=1, keepdims=True) + EPS)
-            half = v * inv * half_gain[...]
-            act = half * (jnp.tanh(half) + 1.0)
-            if k < 3:
-                act = act * flag(info, 1)
-            if k >= rows + 3:
-                act = act * flag(info, 2)
-            wide[k, :, 0:384] = from_left(act).astype(BF16)
-            wide[k, :, 384:768] = act.astype(BF16)
-            wide[k, :, 768:1152] = from_right(act).astype(BF16)
+            plain[k % 2] = h
+            for c in range(0, cols, CHUNK):
+                at = slice(c, c + CHUNK)
+                v = plain[k % 2, at].astype(BF16)
+                hidden[k, at] = v
+                v = v.astype(F32)
+                inv = lax.rsqrt(jnp.mean(v * v, axis=1, keepdims=True) + EPS)
+                half = v * inv * half_gain[...]
+                act = half * (jnp.tanh(half) + 1.0)
+                if k < 3:
+                    act = act * flag(info, 1)
+                if k >= rows + 3:
+                    act = act * flag(info, 2)
+                plain[k % 2, at] = act
+            for lanes in range(0, 384, 128):
+                beside(wide.at[k], 0, lanes, plain[k % 2, :, lanes : lanes + 128], False)
 
         def conv_rows(p, count):
             lhs = [wide[p + i : p + i + count].reshape(count * cols, 1152) for i in range(3)]
@@ -245,7 +259,7 @@
 
     def body(
         info, hidden, conv, acc, got_even, got_odd, packed_even, packed_odd, own, fwd, back_odd, back_even, mid_t, w_in, half_gain,
-        half_out, payload, reward, edge, p0, p1, g_odd, g_even, wide, t_odd, t_even, back, act_grad, hid, lines,
+        half_out, payload, reward, edge, p0, p1, g_odd, g_even, wide, t_odd, t_even, back, act_grad, hid, tmp_odd, tmp_even, lines,
     ):
         even = info[0] == 0
         top, bottom = flag(info, 1), flag(info, 2)
@@ -273,29 +287,23 @@
         def inside(x, k, first, last):
             return x * top if k < first else x * bottom if k >= last else x
 
-        def spread(ref, k, x, ahead):
-            x = x.astype(BF16)
-            x32 = x.astype(F32)
-            sides = (from_right(x32), from_left(x32)) if ahead else (from_left(x32), from_right(x32))
-            ref[k, :, 0:384] = sides[0].astype(BF16)
-            ref[k, :, 384:768] = x
-            ref[k, :, 768:1152] = sides[1].astype(BF16)
-
         def state_row(k):
-            x = hidden[k + 1].astype(F32) + conv[k]
-            if 1 <= k <= rows + 2:
-                x = x + acc[k]
-            if k < 3 or k > rows:
-                x = x + edge[k]
-            spread(wide, k, inside(x, k, 2, rows + 2), False)
+            for lanes in range(0, 384, 128):
+                at = slice(lanes, lanes + 128)
+                x = hidden[k + 1, :, at].astype(F32) + conv[k, :, at]
+                if 1 <= k <= rows + 2:
+                    x = x + acc[k, :, at]
+                if k < 3 or k > rows:
+                    x = x + edge[k, :, at]
+                beside(wide.at[k], 0, lanes, inside(x, k, 2, rows + 2), False)
 
         def up_rows(k, count):
             x = wide[k : k + count].reshape(count * cols, 1152)
             p0[k : k + count] = mm(x[:, 0:768], fwd[0]).reshape(count, cols, 768)
             p1[k : k + count] = mm(x[:, 384:1152], fwd[1]).reshape(count, cols, 768)
 
-        lane = lax.broadcasted_iota(jnp.int32, (cols, 128), 1)
-        low = lane < 64
+        low = lax.broadcasted_iota(jnp.int32, (CHUNK, 128), 1) < 64
+        tall_low = lax.broadcasted_iota(jnp.int32, (cols, 128), 1) < 64
         gains = [half_out[:, 0:128], half_out[:, 128:256]]
 
         def pull(v0, v1, vm, r, zero_low):
@@ -314,38 +322,48 @@
                 out.append((s, pulled(s, g, r[:, k * 128 : k * 128 + 128].astype(F32))))
             m0, m1 = both(*(s * d for s, d in out))
             mx = jnp.where(mine, m0, m1)
-            return [i * (d - s * m) for (s, d), i, m in zip(out, (i0, i1, im), (m0, m1, mx))], mine
-
-        def store(g, target, k):
-            (a0, a1, am), mine = g
-            target[k, :, 0:128] = a0.astype(BF16)
-            target[k, :, 128:256] = a1.astype(BF16)
-            target[k, :, 256:384] = am.astype(BF16)
-            target[k, :, 384:512] = from_right(a0).astype(BF16)
-            target[k, :, 512:640] = from_left(a1).astype(BF16)
-            target[k, :, 640:768] = jnp.where(mine, from_right(am), from_left(am)).astype(BF16)
-
-        def pull_rows(k):
-            v0 = p0[k, :, 256:384] + p0[k + 1, :, 0:128]
-            v1 = p1[k, :, 256:384] + p1[k + 1, :, 0:128]
-            vm = jnp.where(low, p0[k, :, 640:768] + p0[k + 1, :, 512:640], p1[k, :, 640:768] + p1[k + 1, :, 512:640])
-            store(pull(v0, v1, vm, reward[2 * k], True), g_odd, k)
-            v0 = p0[k + 1, :, 128:256] + p0[k, :, 384:512]
-            v1 = p1[k + 1, :, 128:256] + p1[k, :, 384:512]
-            vm = jnp.where(low, p1[k + 1, :, 512:640] + p1[k, :, 640:768], p0[k + 1, :, 512:640] + p0[k, :, 640:768])
-            store(pull(v0, v1, vm, reward[2 * k + 1], False), g_even, k)
+            return [i * (d - s * m) for (s, d), i, m in zip(out, (i0, i1, im), (m0, m1, mx))]
+
+        def pull_row(k, odd):
+            target, tmp = (g_odd, tmp_odd) if odd else (g_even, tmp_even)
+            for c in range(0, cols, CHUNK):
+                at = slice(c, c + CHUNK)
+                if odd:
+                    v0 = p0[k, at, 256:384] + p0[k + 1, at, 0:128]
+                    v1 = p1[k, at, 256:384] + p1[k + 1, at, 0:128]
+                    m0 = p0[k, at, 640:768] + p0[k + 1, at, 512:640]
+                    m1 = p1[k, at, 640:768] + p1[k + 1, at, 512:640]
+                else:
+                    v0 = p0[k + 1, at, 128:256] + p0[k, at, 384:512]
+                    v1 = p1[k + 1, at, 128:256] + p1[k, at, 384:512]
+                    m0 = p1[k + 1, at, 512:640] + p1[k, at, 640:768]
+                    m1 = p0[k + 1, at, 512:640] + p0[k, at, 640:768]
+                out = pull(v0, v1, jnp.where(low, m0, m1), reward[2 * k + (0 if odd else 1), at], odd)
+                for n, value in enumerate(out):
+                    lanes = slice(n * 128, n * 128 + 128)
+                    target[k, at, lanes] = value.astype(BF16)
+                    tmp[k % 2, at, lanes] = value
+            target[k, :, 384:512] = from_right(tmp[k % 2, :, 0:128]).astype(BF16)
+            target[k, :, 512:640] = from_left(tmp[k % 2, :, 128:256]).astype(BF16)
+            x = tmp[k % 2, :, 256:384]
+            sides = (from_right(x), from_left(x)) if odd else (from_left(x), from_right(x))
+            target[k, :, 640:768] = jnp.where(tall_low, *sides).astype(BF16)
 
         def block_row(k):
-            x = t_odd[k + 1, :, 0:384] + t_odd[k, :, 384:768] + t_even[k, :, 0:384] + t_even[k + 1, :, 384:768]
-            spread(back, k, inside(x, k, 1, rows + 1), True)
+            for lanes in range(0, 384, 128):
+                at, far = slice(lanes, lanes + 128), slice(lanes + 384, lanes + 512)
+                x = t_odd[k + 1, :, at] + t_odd[k, :, far] + t_even[k, :, at] + t_even[k + 1, :, far]
+                beside(back.at[k], 0, lanes, inside(x, k, 1, rows + 1), True)
 
         def hidden_pull(k):
-            v = hidden[k + 3].astype(F32)
-            inv = lax.rsqrt(jnp.mean(v * v, axis=1, keepdims=True) + EPS)
-            s = v * inv
-            d = pulled(s, half_gain[...], act_grad[k])
-            dv = inv * (d - s * jnp.mean(d * s, axis=1, keepdims=True))
-            hid[k] = (back[k + 1, :, 384:768].astype(F32) + dv).astype(BF16)
+            for c in range(0, cols, CHUNK):
+                at = slice(c, c + CHUNK)
+                v = hidden[k + 3, at].astype(F32)
+                inv = lax.rsqrt(jnp.mean(v * v, axis=1, keepdims=True) + EPS)
+                s = v * inv
+                d = pulled(s, half_gain[...], act_grad[k, at])
+                dv = inv * (d - s * jnp.mean(d * s, axis=1, keepdims=True))
+                hid[k, at] = (back[k + 1, at, 384:768].astype(F32) + dv).astype(BF16)
 
         fine = rows + 3
         for k in range(rows):
@@ -355,7 +373,8 @@
             state_row(k)
         up_rows(rows, 4)
         for k in range(fine):
-            pull_rows(k)
+            pull_row(k, True)
+            pull_row(k, False)
         t_odd[...] = mm(g_odd[...].reshape(fine * cols, 768), back_odd[...]).reshape(fine, cols, 768)
         t_even[...] = mm(g_even[...].reshape(fine * cols, 768), back_even[...]).reshape(fine, cols, 768)
         for k in range(rows + 2):
@@ -492,6 +511,7 @@
             pltpu.VMEM((3 * rows, 9 * chan, 256), BF16),
             pltpu.VMEM((rows + 6, cols, 1152), BF16),
             pltpu.VMEM((27 * chan, 384), BF16),
+            pltpu.VMEM((2, cols, 384), F32),
         ],
         5e9, 24,
     )(info, lat, lat_cached, packed_even, packed_odd, w_in, mid, gain)
@@ -513,6 +533,8 @@
             pltpu.VMEM((rows + 2, cols, 1152), BF16),
             pltpu.VMEM((rows, cols, 384), F32),
             pltpu.VMEM((rows, cols, 384), BF16),
+            pltpu.VMEM((2, cols, 384), F32),
+            pltpu.VMEM((2, cols, 384), F32),
             pltpu.VMEM((3 * chan, size), F32),
         ],
         8e9, 36,

time: 49.8 us -> 50 us (level)
  no operation moved by 1% of the time
where the time goes in v7:
time: 50 us; the launch traced here: 49.8 us
  Pallas kernels  30.4 us (61%)
  blocking collectives  11.7 us (23%)
  starting transfers between devices  5.86 us (12%)
  local copies, waits for them, and re-layouts  1.4 us (3%)
    pallas_call x1, Pallas kernels, shards(): call(back_body(rows, cols, chan, count, o), [((count, chan, 128), BF16)],...  12.9 us
    all_to_all x1, blocking collectives, shards(): lax.all_to_all(payload, 'tile', split_axis=0, concat_axis=0, tiled=True)  11.7 us
    pallas_call x1, Pallas kernels, shards(): call(current_body(rows, cols, chan), [((rows + 6, cols, 384), BF16), ((ro...  7.52 us
    pallas_call x1, Pallas kernels, shards(): call(cached_body(rows, cols, count, width, tokens), [((rows + 4, cols, 38...  5.3 us
    ppermute x1, starting transfers between devices, shards(): got_even = lax.ppermute(part_even, 'tile', within)  3.99 us
    pallas_call x1, Pallas kernels, shards(): call(taps_body, [((4,), jnp.int32), ((2, 768, 768), BF16), ((768, 768), B...  2 us
    pallas_call x1, Pallas kernels, shards(): call(pack_body(rows, cols, o, chan), [((2 * rows, cols, 384), BF16), ((ed...  1.7 us
    unnamed x22, local copies, waits for them, and re-layouts  1.38 us
  transfers between devices with their start and end apart: 4, of which 0 were waited for; matrix products, arithmetic and copies ran while one was open for 0% of the time, Pallas kernels for 26%

profile of v7, /device:TPU:0, one launch (start us, length us, event | category | flops | bytes accessed | tf_op | source)
XLA Modules:
  0.0 49.8 jit_solution(13004873946550692519)
XLA Ops:
  0.0 0.1 pad_add_fusion.info
  0.1 1.3 %copy-done.1 = bf16[3,3,384,192]{2,3,1,0:T(8,128)(2,1)S(1)} copy-done((bf16[3,3,384,192]{2,3,1,0:T(8,128)(2,1)S(1)}, bf16[3,3,384,192]{2,3,1,0:T(8,128)(2,1)}, u32[]{:S(2)}) %copy-start.1) | copy-done | bytes 1327128
  1.4 2.0 %shard_map.100 = (s32[4]{0:T(128)S(1)}, bf16[2,768,768]{2,1,0:T(8,128)(2,1)S(1)}, bf16[768,768]{1,0:T(8,128)(2,1)S(1)}, bf16[768,768]{1,0:T(8,128)(2,1)S(1)}) custom-call(s32[4]{0:T(128)S(1)} %pad_add_fusion.info, bf16[3,3,192,384]{3,2,1,0:T(8,128)(2,1)S(1)} %bitcast.21), custom_call_target="tpu_custom_call" | custom-call | flops 10000000000 | bytes 1048576 | tf_op jit(solution)/shard_map/pallas_call | solution.py:478
  3.4 0.0 slice-start.1
  3.4 0.0 copy-done.2
  3.4 0.0 copy-done.4
  3.5 0.0 copy-done.5
  3.5 0.0 copy-start.3
  3.5 0.0 copy-start.6
  3.5 1.7 %shard_map.102 = (bf16[8,160,384]{2,1,0:T(8,128)(2,1)S(1)}, bf16[608,384]{1,0:T(8,128)(2,1)S(1)}, bf16[608,384]{1,0:T(8,128)(2,1)S(1)}) custom-call(s32[4]{0:T(128)S(1)} %get-tuple-element.19.info, bf16[8,192,320]{2,1,0:T(8,128)(2,1)S(1)} %bitcast.22, bf16[4,16,160]{2,1,0:T(8,128)(2,1)S(1)} %bitcast.25, bf16[2,4,16,160]{3,2,1,0:T(8,128)(2,1)S(1)} %bitcast.23), custom_call_target="tpu_custom_call" | custom-call | flops 10000000000 | bytes 1048576 | tf_op jit(solution)/shard_map/pallas_call | solution.py:484
  5.2 0.5 %collective-permute-start = (bf16[608,384]{1,0:T(8,128)(2,1)S(1)}, bf16[608,384]{1,0:T(8,128)(2,1)S(1)}, u32[]{:S(2)}, u32[]{:S(2)}) collective-permute-start(bf16[608,384]{1,0:T(8,128)(2,1)S(1)} %get-tuple-element.21), channel_id=1, source_target_pairs={{0,1},{1,0},{2,3},{3,2},{4,5},{5,4},{6,7},{7,6},{8,9},{9,8},{10,11... | collective-permute-start | bytes 1400840 | tf_op jit(solution)/shard_map/ppermute | solution.py:489
  5.7 0.7 %collective-permute-start.1 = (bf16[608,384]{1,0:T(8,128)(2,1)S(1)}, bf16[608,384]{1,0:T(8,128)(2,1)S(1)}, u32[]{:S(2)}, u32[]{:S(2)}) collective-permute-start(bf16[608,384]{1,0:T(8,128)(2,1)S(1)} %get-tuple-element.22), channel_id=1, source_target_pairs={{0,0},{1,2},{2,1},{3,4},{4,3},{5,6},{6,5},{7,7},{8,8},{9,10},{10,9... | collective-permute-start | bytes 1400840 | tf_op jit(solution)/shard_map/ppermute | solution.py:490
  6.4 0.0 slice-done
  6.4 0.0 slice-done.1
  6.4 0.0 copy-done.3
  6.4 0.0 copy-done.6
  6.4 0.0 copy-start.7
  6.5 0.0 copy-start
  6.5 0.0 copy-start.8
  6.5 5.3 %shard_map.101 = (f32[8,160,384]{2,1,0:T(8,128)S(1)}, bf16[480,384]{1,0:T(8,128)(2,1)S(1)}, bf16[480,384]{1,0:T(8,128)(2,1)S(1)}, bf16[3456,384]{1,0:T(8,128)(2,1)S(1)}, bf16[8,128,640]{2,1,0:T(8,128)(2,1)S(1)}) custom-call(s32[4]{0:T(128)S(1)} %get-tuple-element.19.info, s32[8]{0:T(128)S(1)} %copy-done.6, bf16[2,4,160,384]{3,2,1,0:T(8,128)(2,1)S(1)} %copy-done.3, ...), custom_call_target="tpu_custom_call" | custom-call | flops 4000000000 | bytes 1048576 | tf_op jit(solution)/shard_map/pallas_call | solution.py:494
  11.8 4.0 %collective-permute-start.2 = (bf16[480,384]{1,0:T(8,128)(2,1)S(1)}, bf16[480,384]{1,0:T(8,128)(2,1)S(1)}, u32[]{:S(2)}, u32[]{:S(2)}) collective-permute-start(bf16[480,384]{1,0:T(8,128)(2,1)S(1)} %get-tuple-element.26), channel_id=1, source_target_pairs={{0,1},{1,0},{2,3},{3,2},{4,5},{5,4},{6,7},{7,6},{8,9},{9,8},{10,11... | collective-permute-start | bytes 1105928 | tf_op jit(solution)/shard_map/ppermute | solution.py:502
  15.8 0.7 %collective-permute-start.3 = (bf16[480,384]{1,0:T(8,128)(2,1)S(1)}, bf16[480,384]{1,0:T(8,128)(2,1)S(1)}, u32[]{:S(2)}, u32[]{:S(2)}) collective-permute-start(bf16[480,384]{1,0:T(8,128)(2,1)S(1)} %get-tuple-element.27), channel_id=1, source_target_pairs={{0,0},{1,2},{2,1},{3,4},{4,3},{5,6},{6,5},{7,7},{8,8},{9,10},{10,9... | collective-permute-start | bytes 1105928 | tf_op jit(solution)/shard_map/ppermute | solution.py:503
  16.5 0.0 copy-done.8
  16.6 0.1 maximum_multiply_fusion.half_out
  16.6 0.0 collective-permute-done.got_even.packed_even
  16.6 0.0 collective-permute-done.1.got_odd.packed_odd
  16.6 7.5 %shard_map.103 = (bf16[10,160,384]{2,1,0:T(8,128)(2,1)S(1)}, f32[8,160,384]{2,1,0:T(8,128)S(1)}) custom-call(s32[4]{0:T(128)S(1)} %get-tuple-element.19.info, bf16[4,16,160]{2,1,0:T(8,128)(2,1)S(1)} %bitcast.26, bf16[2,4,16,160]{3,2,1,0:T(8,128)(2,1)S(1)} %bitcast.24, bf16[608,384]{1,0:T(8,128)(2,1)S(1)} %collective-permute-done.got_even.packed_even, ...), custom_call_target="tpu_custom_call" | custom-call | flops 5000000000 | bytes 1048576 | tf_op jit(solution)/shard_map/pallas_call | solution.py:505
  24.2 0.0 collective-permute-done.2.got_even
  24.2 0.0 collective-permute-done.3.got_odd
  24.2 12.9 %shard_map.104 = bf16[8,16,128]{2,1,0:T(8,128)(2,1)S(1)} custom-call(s32[4]{0:T(128)S(1)} %get-tuple-element.19.info, bf16[10,160,384]{2,1,0:T(8,128)(2,1)S(1)} %get-tuple-element.23.hidden, f32[8,160,384]{2,1,0:T(8,128)S(1)} %get-tuple-element.24.conv, f32[8,160,384]{2,1,0:T(8,128)S(1)} %get-tuple-element.25.acc, ...), custom_call_target="tpu_custom_call" | custom-call | flops 8000000000 | bytes 1048576 | tf_op jit(solution)/shard_map/pallas_call | solution.py:519
  37.1 11.7 %all_to_all.5.got = bf16[8,16,128]{2,1,0:T(8,128)(2,1)S(1)} all-to-all(bf16[8,16,128]{2,1,0:T(8,128)(2,1)S(1)} %shard_map.104), channel_id=1, replica_groups=mesh['prompt'=4,'tile'=8] {'tile'}, dimensions={0} | all-to-all | bytes 65536 | tf_op jit(solution)/shard_map/all_to_all | solution.py:545
  48.8 1.0 %shard_map.105 = f32[64,160]{1,0:T(8,128)} custom-call(bf16[8,128,640]{2,1,0:T(8,128)(2,1)S(1)} %get-tuple-element.20.sel, bf16[8,16,128]{2,1,0:T(8,128)(2,1)S(1)} %all_to_all.5.got), custom_call_target="tpu_custom_call" | custom-call | flops 10000000 | bytes 1048576 | tf_op jit(solution)/shard_map/pallas_call | solution.py:546
  (12 shorter events, 0.0 us)
Async XLA Ops:
  0.1 1.3 %copy-start.1 = (bf16[3,3,384,192]{2,3,1,0:T(8,128)(2,1)S(1)}, bf16[3,3,384,192]{2,3,1,0:T(8,128)(2,1)}, u32[]{:S(2)}) copy-start(bf16[3,3,384,192]{2,3,1,0:T(8,128)(2,1)} %param.16) | copy-start | bytes 3981316
  1.4 2.0 %copy-start.2 = (bf16[8,320,192]{1,2,0:T(8,128)(2,1)S(1)}, bf16[8,320,192]{1,2,0:T(8,128)(2,1)}, u32[]{:S(2)}) copy-start(bf16[8,320,192]{1,2,0:T(8,128)(2,1)} %param.13) | copy-start | bytes 2949124
  1.4 2.0 %copy-start.4 = (bf16[2,4,160,16]{2,3,1,0:T(8,128)(2,1)S(1)}, bf16[2,4,160,16]{2,3,1,0:T(8,128)(2,1)}, u32[]{:S(2)}) copy-start(bf16[2,4,160,16]{2,3,1,0:T(8,128)(2,1)} %param.11) | copy-start | bytes 122884
  1.4 2.0 %copy-start.5 = (bf16[4,160,16]{1,2,0:T(8,128)(2,1)S(1)}, bf16[4,160,16]{1,2,0:T(8,128)(2,1)}, u32[]{:S(2)}) copy-start(bf16[4,160,16]{1,2,0:T(8,128)(2,1)} %param.10) | copy-start | bytes 61444
  1.4 5.0 %slice-start = ((s8[7962624]{0:T(1024)(128)(4,1)}), s8[4194304]{0:T(1024)(128)(4,1)S(1)}, s32[]{:S(2)}) async-start(s8[7962624]{0:T(1024)(128)(4,1)} %bitcast.17), calls=%async_computation.1 | async-start | bytes 8388608
  3.4 3.0 %slice-start.1 = ((s8[7962624]{0:T(1024)(128)(4,1)}), s8[3768320]{0:T(1024)(128)(4,1)S(1)}, s32[]{:S(2)}) async-start(s8[7962624]{0:T(1024)(128)(4,1)} %bitcast.17), calls=%async_computation.2 | async-start | bytes 7536640
  3.5 3.0 %copy-start.3 = (bf16[2,4,160,384]{3,2,1,0:T(8,128)(2,1)S(1)}, bf16[2,4,160,384]{3,2,1,0:T(8,128)(2,1)}, u32[]{:S(2)}) copy-start(bf16[2,4,160,384]{3,2,1,0:T(8,128)(2,1)} %features.1) | copy-start | bytes 2949124
  3.5 3.0 %copy-start.6 = (s32[8]{0:T(128)S(1)}, s32[8]{0:T(128)}, u32[]{:S(2)}) copy-start(s32[8]{0:T(128)} %order.1) | copy-start | bytes 100
  5.2 11.4 %collective-permute-start = (bf16[608,384]{1,0:T(8,128)(2,1)S(1)}, bf16[608,384]{1,0:T(8,128)(2,1)S(1)}, u32[]{:S(2)}, u32[]{:S(2)}) collective-permute-start(bf16[608,384]{1,0:T(8,128)(2,1)S(1)} %get-tuple-element.21), channel_id=1, source_target_pairs={{0,1},{1,0},{2,3},{3,2},{4,5},{5,4},{6,7},{7,6},{8,9},{9,8},{10,11... | collective-permute-start | bytes 1400840 | tf_op jit(solution)/shard_map/ppermute | solution.py:489
  5.7 10.9 %collective-permute-start.1 = (bf16[608,384]{1,0:T(8,128)(2,1)S(1)}, bf16[608,384]{1,0:T(8,128)(2,1)S(1)}, u32[]{:S(2)}, u32[]{:S(2)}) collective-permute-start(bf16[608,384]{1,0:T(8,128)(2,1)S(1)} %get-tuple-element.22), channel_id=1, source_target_pairs={{0,0},{1,2},{2,1},{3,4},{4,3},{5,6},{6,5},{7,7},{8,8},{9,10},{10,9... | collective-permute-start | bytes 1400840 | tf_op jit(solution)/shard_map/ppermute | solution.py:490
  6.4 10.0 %copy-start.7 = (f32[384]{0:T(512)S(1)}, f32[384]{0:T(512)}, u32[]{:S(2)}) copy-start(f32[384]{0:T(512)} %param.17) | copy-start | bytes 4612
  6.5 10.0 %copy-start = (bf16[3,3,3,16,384]{4,3,2,1,0:T(8,128)(2,1)S(1)}, bf16[3,3,3,16,384]{4,3,2,1,0:T(8,128)(2,1)}, u32[]{:S(2)}) copy-start(bf16[3,3,3,16,384]{4,3,2,1,0:T(8,128)(2,1)} %param.14) | copy-start | bytes 995332
  6.5 10.1 %copy-start.8 = (f32[192]{0:T(256)S(1)}, f32[192]{0:T(256)}, u32[]{:S(2)}) copy-start(f32[192]{0:T(256)} %param.18) | copy-start | bytes 2308
  11.8 12.4 %collective-permute-start.2 = (bf16[480,384]{1,0:T(8,128)(2,1)S(1)}, bf16[480,384]{1,0:T(8,128)(2,1)S(1)}, u32[]{:S(2)}, u32[]{:S(2)}) collective-permute-start(bf16[480,384]{1,0:T(8,128)(2,1)S(1)} %get-tuple-element.26), channel_id=1, source_target_pairs={{0,1},{1,0},{2,3},{3,2},{4,5},{5,4},{6,7},{7,6},{8,9},{9,8},{10,11... | collective-permute-start | bytes 1105928 | tf_op jit(solution)/shard_map/ppermute | solution.py:502
  15.8 8.4 %collective-permute-start.3 = (bf16[480,384]{1,0:T(8,128)(2,1)S(1)}, bf16[480,384]{1,0:T(8,128)(2,1)S(1)}, u32[]{:S(2)}, u32[]{:S(2)}) collective-permute-start(bf16[480,384]{1,0:T(8,128)(2,1)S(1)} %get-tuple-element.27), channel_id=1, source_target_pairs={{0,0},{1,2},{2,1},{3,4},{4,3},{5,6},{6,5},{7,7},{8,8},{9,10},{10,9... | collective-permute-start | bytes 1105928 | tf_op jit(solution)/shard_map/ppermute | solution.py:503

commit v8 on v7

--- a/solution.py
+++ b/solution.py
@@ -10,6 +10,20 @@
 BF16 = jnp.bfloat16
 VM = pl.BlockSpec(memory_space=pltpu.VMEM)
 SM = pl.BlockSpec(memory_space=pltpu.SMEM)
+
+
+def weave(*groups):
+    total = max(len(g) for g in groups)
+    done = [0] * len(groups)
+    for k in range(total):
+        for n, g in enumerate(groups):
+            while done[n] * total < (k + 1) * len(g):
+                g[done[n]]()
+                done[n] += 1
+
+
+def steps(f, *keys):
+    return [lambda key=key: f(*key) for key in keys]
 
 
 def call(body, outs, n_smem, n_vmem, scratch, flops, limit, smem_outs=0):
@@ -60,28 +74,36 @@
 CHUNK = 32
 
 
+def picker(cols, o):
+    half = o - 128
+    x_index = lax.broadcasted_iota(jnp.int32, (cols, 2 * cols), 1)
+    w_index = lax.broadcasted_iota(jnp.int32, (cols, 2 * cols), 0)
+    pick = [(x_index == 2 * w_index + b).astype(F32).astype(BF16) for b in (0, 1)]
+    zeros = jnp.zeros((128 - half, 2 * cols), BF16)
+
+    def one(reward, f, own, k):
+        r = reward[f]
+        first, rest = r[:128], r[128:]
+        low = jnp.concatenate([first, rest, zeros], axis=0)
+        high = jnp.concatenate([first, zeros, rest], axis=0)
+        sides = (low, high) if f % 2 else (high, low)
+        d0, d1 = mm_t(pick[0], sides[0]), mm_t(pick[1], sides[1])
+        own[k, :, 0:128] = d0[:, :128].astype(BF16)
+        own[k, :, 128:256] = d1[:, :128].astype(BF16)
+        own[k, :, 256:384] = (d0[:, 128:] + d1[:, 128:]).astype(BF16)
+
+    return one
+
+
 def pack_body(rows, cols, o, chan):
-    half = o - 128
-
     def body(info, reward, latent, cached, own, send_even, send_odd):
-        x_index = lax.broadcasted_iota(jnp.int32, (cols, 2 * cols), 1)
-        w_index = lax.broadcasted_iota(jnp.int32, (cols, 2 * cols), 0)
-        pick = [(x_index == 2 * w_index + b).astype(F32).astype(BF16) for b in (0, 1)]
-        zeros = jnp.zeros((128 - half, 2 * cols), BF16)
-        for f in range(2 * rows):
-            r = reward[f]
-            first, rest = r[:128], r[128:]
-            low = jnp.concatenate([first, rest, zeros], axis=0)
-            high = jnp.concatenate([first, zeros, rest], axis=0)
-            sides = (low, high) if f % 2 else (high, low)
-            d0, d1 = mm_t(pick[0], sides[0]), mm_t(pick[1], sides[1])
-            own[f, :, 0:128] = d0[:, :128].astype(BF16)
-            own[f, :, 128:256] = d1[:, :128].astype(BF16)
-            own[f, :, 256:384] = (d0[:, 128:] + d1[:, 128:]).astype(BF16)
+        one = picker(cols, o)
+        for k in range(6):
+            one(reward, k if k < 3 else 2 * rows - 6 + k, own, k)
         base = 3 * cols
         per = chan * rows
         for send, last in ((send_even, 1 - info[0]), (send_odd, info[0])):
-            begin = last * (2 * rows - 3)
+            begin = last * 3
             for k in range(3):
                 send[k * cols : (k + 1) * cols] = own[begin + k]
             for t in range(3):
@@ -93,21 +115,43 @@
     return body
 
 
-def taps_body(info, up, info_out, fwd, back_odd, back_even):
+def home(targets, q, p, tile):
+    block, second = ((1, 1), (0, 0), (0, 1), (1, 0))[p]
+    target, side = targets[q]
+    if tile < 2:
+        row = block * 384 + second * 128 + tile * 64
+    else:
+        row = block * 384 + 256 + 64 * (second if q % 2 == 0 else 1 - second)
+    return target, row, side * 384
+
+
+def turning(back_odd, back_even, fwd):
+    targets = ((back_odd, 1), (back_even, 0), (back_odd, 0), (back_even, 1))
+
+    def tap_tile(q, p, tile, lanes):
+        target, row, side = home(targets, q, p, tile)
+        return target[row : row + 64, side + lanes : side + lanes + 128]
+
+    def one(b, side, lanes):
+        p = ((3, 1), (2, 0))[b][side]
+        at = slice(side * 384 + lanes, side * 384 + lanes + 128)
+        for q in range(4):
+            both = jnp.concatenate([tap_tile(q, p, 0, lanes), tap_tile(q, p, 1, lanes)], axis=0)
+            fwd[b, at, q * 128 : q * 128 + 128] = both.T
+        for half in range(2):
+            pair = (2 * half, 2 * half + 1) if b == 0 else (2 * half + 1, 2 * half)
+            both = jnp.concatenate([tap_tile(q, p, 2, lanes) for q in pair], axis=0)
+            fwd[b, at, 512 + half * 128 : 640 + half * 128] = both.T
+
+    return steps(one, *[(b, side, lanes) for b in range(2) for side in range(2) for lanes in range(0, 384, 128)])
+
+
+def taps_body(info, up, info_out, back_odd, back_even):
     for k in range(4):
         info_out[k] = info[k]
 
     parts = ((2,), (1, 2), (0, 1), (0,))
     targets = ((back_odd, 1), (back_even, 0), (back_odd, 0), (back_even, 1))
-
-    def home(q, p, tile):
-        block, second = ((1, 1), (0, 0), (0, 1), (1, 0))[p]
-        target, side = targets[q]
-        if tile < 2:
-            row = block * 384 + second * 128 + tile * 64
-        else:
-            row = block * 384 + 256 + 64 * (second if q % 2 == 0 else 1 - second)
-        return target, row, side * 384
 
     for tile in range(3):
         for lanes in range(0, 384, 128):
@@ -115,50 +159,49 @@
             for q in range(4):
                 c = [w[parts[q][0]][j] + w[parts[q][1]][j] if len(parts[q]) > 1 else w[parts[q][0]][j] for j in range(3)]
                 for p, tap in enumerate((c[2], c[1] + c[2], c[0] + c[1], c[0])):
-                    target, row, side = home(q, p, tile)
+                    target, row, side = home(targets, q, p, tile)
                     target[row : row + 64, side + lanes : side + lanes + 128] = tap.astype(BF16)
 
-    def tap_tile(q, p, tile, lanes):
-        target, row, side = home(q, p, tile)
-        return target[row : row + 64, side + lanes : side + lanes + 128]
-
-    for b, order in ((0, (3, 1)), (1, (2, 0))):
-        for side, p in enumerate(order):
-            for lanes in range(0, 384, 128):
-                at = slice(side * 384 + lanes, side * 384 + lanes + 128)
-                for q in range(4):
-                    both = jnp.concatenate([tap_tile(q, p, 0, lanes), tap_tile(q, p, 1, lanes)], axis=0)
-                    fwd[b, at, q * 128 : q * 128 + 128] = both.T
-                for half in range(2):
-                    pair = (2 * half, 2 * half + 1) if b == 0 else (2 * half + 1, 2 * half)
-                    both = jnp.concatenate([tap_tile(q, p, 2, lanes) for q in pair], axis=0)
-                    fwd[b, at, 512 + half * 128 : 640 + half * 128] = both.T
-
-
-def cached_body(rows, cols, count, width, tokens):
+
+def cached_body(rows, cols, count, width, tokens, o):
     size = rows * cols
 
-    def body(info, order, features, mid, acc, send_even, send_odd, mid_t, sel, wide):
+    def body(
+        info, order, features, mid, back_odd, back_even, reward, acc, send_even, send_odd, mid_t, sel, fwd, own, wide, parts
+    ):
         for t in range(2):
             for r in range(rows):
                 for lanes in range(0, 384, 128):
                     x = features[t, r, :, lanes : lanes + 128].astype(F32)
                     beside(wide.at[r * cols : (r + 1) * cols], t * 1152, lanes, x, False)
-        lhs = wide[...]
-        kernels = [jnp.concatenate([mid[0, i], mid[1, i]], axis=0) for i in range(3)]
-        pair = mm(lhs, jnp.concatenate([kernels[0], kernels[1]], axis=1))
-        for i in range(3):
-            for j in range(3):
-                at = (i * 3 + j) * 384
-                mid_t[at : at + 384] = mid[2, i, j * 384 : (j + 1) * 384].T
-        placing(info, order, sel, count, width, tokens)
-        last_kernel = mm(lhs, kernels[2])
+        def product(i, lanes):
+            parts[i, :, lanes] = mm(wide[...], jnp.concatenate([mid[0, i, :, lanes], mid[1, i, :, lanes]], axis=0))
+
+        def double():
+            left = jnp.concatenate([mid[0, 0, :, 256:384], mid[1, 0, :, 256:384]], axis=0)
+            right = jnp.concatenate([mid[0, 1, :, 256:384], mid[1, 1, :, 256:384]], axis=0)
+            both = mm(wide[...], jnp.concatenate([left, right], axis=1))
+            parts[0, :, 256:384] = both[:, :128]
+            parts[1, :, 256:384] = both[:, 128:]
+
+        def turn(i, j):
+            at = (i * 3 + j) * 384
+            mid_t[at : at + 384] = mid[2, i, j * 384 : (j + 1) * 384].T
+
+        most, rest = slice(0, 256), slice(256, 384)
+        products = steps(product, (0, most), (1, most)) + steps(double, ()) + steps(product, (2, most), (2, rest))
+        one = picker(cols, o)
+        others = steps(turn, *[(i, j) for i in range(3) for j in range(3)])
+        others += turning(back_odd, back_even, fwd)
+        others += steps(placing(info, order, sel, count, width, tokens), *[(t,) for t in range(count)])
+        others += steps(one, (reward, rows - 1, own, 0), (reward, rows, own, 1))
+        weave(others, products)
         for k in range(rows + 4):
             total = jnp.zeros((cols, 384), F32)
-            for i, part in enumerate((pair[:, :384], pair[:, 384:], last_kernel)):
+            for i in range(3):
                 r = k - 3 + i
                 if 0 <= r < rows:
-                    total = total + part[r * cols : (r + 1) * cols]
+                    total = total + parts[i, r * cols : (r + 1) * cols]
             acc[k] = total
         for send, last in ((send_even, 1 - info[0]), (send_odd, info[0])):
             for k in range(3):
@@ -232,17 +275,18 @@
             for lanes in range(0, 384, 128):
                 beside(wide.at[k], 0, lanes, plain[k % 2, :, lanes : lanes + 128], False)
 
-        def conv_rows(p, count):
-            lhs = [wide[p + i : p + i + count].reshape(count * cols, 1152) for i in range(3)]
-            total = mm(jnp.concatenate(lhs, axis=1), mid[2].reshape(3456, 384))
-            conv[p : p + count] = total.reshape(count, cols, 384)
+        def conv_rows(p, number, lanes):
+            lhs = [wide[p + i : p + i + number].reshape(number * cols, 1152) for i in range(3)]
+            total = mm(jnp.concatenate(lhs, axis=1), mid[2, :, :, lanes].reshape(3456, lanes.stop - lanes.start))
+            conv[p : p + number, :, lanes] = total.reshape(number, cols, lanes.stop - lanes.start)
+
+        def convs(p, number):
+            return steps(conv_rows, (p, number, slice(0, 256)), (p, number, slice(256, 384)))
 
         for k in range(rows + 2):
             hidden_row(k)
-        conv_rows(0, rows)
-        for k in range(rows + 2, rows + 6):
-            hidden_row(k)
-        conv_rows(rows, 4)
+        weave(steps(hidden_row, *[(k,) for k in range(rows + 2, rows + 6)]), convs(0, rows))
+        weave(convs(rows, 4))
 
     return body
 
@@ -258,7 +302,7 @@
     width = 2 * cols // count
 
     def body(
-        info, hidden, conv, acc, got_even, got_odd, packed_even, packed_odd, own, fwd, back_odd, back_even, mid_t, w_in, half_gain,
+        info, hidden, conv, acc, got_even, got_odd, packed_even, packed_odd, own, own_mid, fwd, back_odd, back_even, mid_t, w_in, half_gain,
         half_out, payload, reward, edge, p0, p1, g_odd, g_even, wide, t_odd, t_even, back, act_grad, hid, tmp_odd, tmp_even, lines,
     ):
         even = info[0] == 0
@@ -282,7 +326,9 @@
             take(got_even, packed_even, True)
             take(got_odd, packed_odd, False)
 
-        reward[3 : 2 * rows + 3] = own[...]
+        reward[3:6] = own[0:3]
+        reward[6 : 2 * rows] = own_mid[...]
+        reward[2 * rows : 2 * rows + 3] = own[3:6]
 
         def inside(x, k, first, last):
             return x * top if k < first else x * bottom if k >= last else x
@@ -297,10 +343,16 @@
                     x = x + edge[k, :, at]
                 beside(wide.at[k], 0, lanes, inside(x, k, 2, rows + 2), False)
 
-        def up_rows(k, count):
-            x = wide[k : k + count].reshape(count * cols, 1152)
-            p0[k : k + count] = mm(x[:, 0:768], fwd[0]).reshape(count, cols, 768)
-            p1[k : k + count] = mm(x[:, 384:1152], fwd[1]).reshape(count, cols, 768)
+        def up_rows(k, number, b, n):
+            x = wide[k : k + number, :, b * 384 : b * 384 + 768].reshape(number * cols, 768)
+            lanes = slice(n * 256, n * 256 + 256)
+            (p0, p1)[b][k : k + number, :, lanes] = mm(x, fwd[b, :, lanes]).reshape(number, cols, 256)
+
+        def down_rows(k, number, odd, n):
+            g, kernel, t = (g_odd, back_odd, t_odd) if odd else (g_even, back_even, t_even)
+            lanes = slice(n * 256, n * 256 + 256)
+            x = g[k : k + number].reshape(number * cols, 768)
+            t[k : k + number, :, lanes] = mm(x, kernel[:, lanes]).reshape(number, cols, 256)
 
         low = lax.broadcasted_iota(jnp.int32, (CHUNK, 128), 1) < 64
         tall_low = lax.broadcasted_iota(jnp.int32, (cols, 128), 1) < 64
@@ -365,20 +417,24 @@
                 dv = inv * (d - s * jnp.mean(d * s, axis=1, keepdims=True))
                 hid[k, at] = (back[k + 1, at, 384:768].astype(F32) + dv).astype(BF16)
 
-        fine = rows + 3
-        for k in range(rows):
-            state_row(k)
-        up_rows(0, rows)
-        for k in range(rows, rows + 4):
-            state_row(k)
-        up_rows(rows, 4)
-        for k in range(fine):
-            pull_row(k, True)
-            pull_row(k, False)
-        t_odd[...] = mm(g_odd[...].reshape(fine * cols, 768), back_odd[...]).reshape(fine, cols, 768)
-        t_even[...] = mm(g_even[...].reshape(fine * cols, 768), back_even[...]).reshape(fine, cols, 768)
-        for k in range(rows + 2):
-            block_row(k)
+        def each(f, first, last):
+            return steps(f, *[(k,) for k in range(first, last)])
+
+        def ups(k, number):
+            return steps(up_rows, *[(k, number, b, n) for n in range(3) for b in range(2)])
+
+        def downs(k, number):
+            return steps(down_rows, *[(k, number, odd, n) for n in range(3) for odd in (True, False)])
+
+        def pulls(first, last):
+            return steps(pull_row, *[(k, odd) for k in range(first, last) for odd in (True, False)])
+
+        weave(each(state_row, 0, rows))
+        weave(each(state_row, rows, rows + 4), ups(0, rows))
+        weave(pulls(0, rows - 1), ups(rows, 4))
+        weave(pulls(rows - 1, rows + 3), downs(0, rows - 1))
+        weave(each(block_row, 0, rows - 2), downs(rows - 1, 4))
+        weave(each(block_row, rows - 2, rows + 2))
         lhs = [back[2 - i : 2 - i + rows].reshape(size, 1152) for i in range(3)]
         act_grad[...] = mm(jnp.concatenate(lhs, axis=1), mid_t[...]).reshape(rows, cols, 384)
         for k in range(rows):
@@ -425,12 +481,15 @@
     part = jnp.where(group == 2, pair, group)
     fixed = (2 * part + (w & 1)) * tokens + (w >> 1) - column
     fixed = jnp.where(lane < 3 * width, fixed, -99999)
-    for t in range(count):
+
+    def one(t):
         step = t + 1 - 2 * pair
         valid = jnp.logical_and(step >= 0, step < count)
         beside = jnp.where(valid, piece * order[jnp.clip(step, 0, count - 1)], -9999)
         begin = jnp.where(group == 2, beside, piece * order[t])
         sel[t] = (fixed + begin == 0).astype(F32).astype(BF16)
+
+    return one
 
 
 def place_body(count, chan, tokens):
@@ -475,30 +534,30 @@
     size = rows * cols
     edge_rows = 3 * cols + 2 * chan * rows
 
-    info, fwd, back_odd, back_even = call(
+    info, back_odd, back_even = call(
         taps_body,
-        [((4,), jnp.int32), ((2, 768, 768), BF16), ((768, 768), BF16), ((768, 768), BF16)],
-        1, 1, [], 1e10, 16, 1,
+        [((4,), jnp.int32), ((768, 768), BF16), ((768, 768), BF16)],
+        1, 1, [], 1e10, 8, 1,
     )(info, up_t)
 
     own, send_even, send_odd = call(
         pack_body(rows, cols, o, chan),
-        [((2 * rows, cols, 384), BF16), ((edge_rows, 384), BF16), ((edge_rows, 384), BF16)],
-        1, 3, [], 1e10, 16,
+        [((6, cols, 384), BF16), ((edge_rows, 384), BF16), ((edge_rows, 384), BF16)],
+        1, 3, [], 1e10, 8,
     )(info, reward_t, lat, lat_cached)
     packed_even = lax.ppermute(send_even, "tile", within)
     packed_odd = lax.ppermute(send_odd, "tile", across)
 
     width = 2 * cols // count
     tokens = size // 4
-    acc, part_even, part_odd, mid_t, sel = call(
-        cached_body(rows, cols, count, width, tokens),
+    acc, part_even, part_odd, mid_t, sel, fwd, own_mid = call(
+        cached_body(rows, cols, count, width, tokens, o),
         [
             ((rows + 4, cols, 384), F32), ((3 * cols, 384), BF16), ((3 * cols, 384), BF16), ((3456, 384), BF16),
-            ((count, 128, 4 * tokens), BF16),
+            ((count, 128, 4 * tokens), BF16), ((2, 768, 768), BF16), ((2, cols, 384), BF16),
         ],
-        2, 2, [pltpu.VMEM((size, 2304), BF16)], 4e9, 24,
-    )(info, shard_order, cached_features, mid)
+        2, 5, [pltpu.VMEM((size, 2304), BF16), pltpu.VMEM((3, size, 384), F32)], 4e9, 14,
+    )(info, shard_order, cached_features, mid, back_odd, back_even, reward_t)
     got_even = lax.ppermute(part_even, "tile", within)
     got_odd = lax.ppermute(part_odd, "tile", across)
 
@@ -513,13 +572,13 @@
             pltpu.VMEM((27 * chan, 384), BF16),
             pltpu.VMEM((2, cols, 384), F32),
         ],
-        5e9, 24,
+        5e9, 14,
     )(info, lat, lat_cached, packed_even, packed_odd, w_in, mid, gain)
 
     (payload,) = call(
         back_body(rows, cols, chan, count, o),
         [((count, chan, 128), BF16)],
-        1, 15,
+        1, 16,
         [
             pltpu.VMEM((2 * rows + 6, cols, 384), BF16),
             pltpu.VMEM((rows + 4, cols, 384), F32),
@@ -537,13 +596,13 @@
             pltpu.VMEM((2, cols, 384), F32),
             pltpu.VMEM((3 * chan, size), F32),
         ],
-        8e9, 36,
+        8e9, 34,
     )(
-        info, hidden, conv, acc, got_even, got_odd, packed_even, packed_odd, own, fwd, back_odd, back_even, mid_t,
+        info, hidden, conv, acc, got_even, got_odd, packed_even, packed_odd, own, own_mid, fwd, back_odd, back_even, mid_t,
         w_in[2].reshape(9 * chan, mid_chan), gain, gain_out,
     )
     received = lax.all_to_all(payload, "tile", split_axis=0, concat_axis=0, tiled=True)
-    (placed,) = call(place_body(count, chan, tokens), [((4 * chan, tokens), F32)], 0, 2, [], 1e7, 16)(sel, received)
+    (placed,) = call(place_body(count, chan, tokens), [((4 * chan, tokens), F32)], 0, 2, [], 1e7, 8)(sel, received)
     return placed.T
 
 

time: 50 us -> 49.5 us (0.990)
  Pallas kernels: 30.4 us -> 29.7 us
    pallas_call x3, Pallas kernels: 9 us -> 8.03 us  [the longest x1 5.43 us: shards(): call(cached_body(rows, cols, count, width, tokens, o), [((rows + 4, cols,...]
where the time goes in v8:
time: 49.5 us; the launch traced here: 49.3 us
  Pallas kernels  29.7 us (60%)
  blocking collectives  11.7 us (24%)
  starting transfers between devices  5.95 us (12%)
  local copies, waits for them, and re-layouts  1.58 us (3%)
    pallas_call x1, Pallas kernels, shards(): call(back_body(rows, cols, chan, count, o), [((count, chan, 128), BF16)],...  13.2 us
    all_to_all x1, blocking collectives, shards(): lax.all_to_all(payload, 'tile', split_axis=0, concat_axis=0, tiled=True)  11.7 us
    pallas_call x1, Pallas kernels, shards(): call(current_body(rows, cols, chan), [((rows + 6, cols, 384), BF16), ((ro...  7.44 us
    pallas_call x1, Pallas kernels, shards(): call(cached_body(rows, cols, count, width, tokens, o), [((rows + 4, cols,...  5.43 us
    ppermute x1, starting transfers between devices, shards(): got_even = lax.ppermute(part_even, 'tile', within)  4.05 us
    unnamed x22, local copies, waits for them, and re-layouts  1.56 us
    pallas_call x1, Pallas kernels, shards(): call(pack_body(rows, cols, o, chan), [((6, cols, 384), BF16), ((edge_rows...  1.45 us
    pallas_call x1, Pallas kernels, shards(): call(taps_body, [((4,), jnp.int32), ((768, 768), BF16), ((768, 768), BF16...  1.15 us
  transfers between devices with their start and end apart: 4, of which 0 were waited for; matrix products, arithmetic and copies ran while one was open for 0% of the time, Pallas kernels for 26%

profile of v8, /device:TPU:0, one launch (start us, length us, event | category | flops | bytes accessed | tf_op | source)
XLA Modules:
  0.0 49.3 jit_solution(3435818508899576672)
XLA Ops:
  0.0 0.1 pad_add_fusion.info
  0.1 0.0 copy-start.1
  0.1 1.3 %copy-done.1 = bf16[3,3,384,192]{2,3,1,0:T(8,128)(2,1)S(1)} copy-done((bf16[3,3,384,192]{2,3,1,0:T(8,128)(2,1)S(1)}, bf16[3,3,384,192]{2,3,1,0:T(8,128)(2,1)}, u32[]{:S(2)}) %copy-start.1) | copy-done | bytes 1327128
  1.4 0.0 copy-start.2
  1.4 0.0 copy-start.4
  1.4 1.1 %shard_map.100 = (s32[4]{0:T(128)S(1)}, bf16[768,768]{1,0:T(8,128)(2,1)S(1)}, bf16[768,768]{1,0:T(8,128)(2,1)S(1)}) custom-call(s32[4]{0:T(128)S(1)} %pad_add_fusion.info, bf16[3,3,192,384]{3,2,1,0:T(8,128)(2,1)S(1)} %bitcast.21), custom_call_target="tpu_custom_call" | custom-call | flops 10000000000 | bytes 1048576 | tf_op jit(solution)/shard_map/pallas_call | solution.py:537
  2.6 0.1 copy-done.2
  2.7 0.0 copy-done.4
  2.7 0.0 copy-done.5
  2.7 0.0 copy-start.6
  2.7 1.5 %shard_map.102 = (bf16[6,160,384]{2,1,0:T(8,128)(2,1)S(1)}, bf16[608,384]{1,0:T(8,128)(2,1)S(1)}, bf16[608,384]{1,0:T(8,128)(2,1)S(1)}) custom-call(s32[4]{0:T(128)S(1)} %get-tuple-element.20.info, bf16[8,192,320]{2,1,0:T(8,128)(2,1)S(1)} %bitcast.22, bf16[4,16,160]{2,1,0:T(8,128)(2,1)S(1)} %bitcast.26, bf16[2,4,16,160]{3,2,1,0:T(8,128)(2,1)S(1)} %bitcast.24), custom_call_target="tpu_custom_call" | custom-call | flops 10000000000 | bytes 1048576 | tf_op jit(solution)/shard_map/pallas_call | solution.py:543
  4.2 0.5 %collective-permute-start = (bf16[608,384]{1,0:T(8,128)(2,1)S(1)}, bf16[608,384]{1,0:T(8,128)(2,1)S(1)}, u32[]{:S(2)}, u32[]{:S(2)}) collective-permute-start(bf16[608,384]{1,0:T(8,128)(2,1)S(1)} %get-tuple-element.24), channel_id=1, source_target_pairs={{0,1},{1,0},{2,3},{3,2},{4,5},{5,4},{6,7},{7,6},{8,9},{9,8},{10,11... | collective-permute-start | bytes 1400840 | tf_op jit(solution)/shard_map/ppermute | solution.py:548
  4.7 0.7 %collective-permute-start.1 = (bf16[608,384]{1,0:T(8,128)(2,1)S(1)}, bf16[608,384]{1,0:T(8,128)(2,1)S(1)}, u32[]{:S(2)}, u32[]{:S(2)}) collective-permute-start(bf16[608,384]{1,0:T(8,128)(2,1)S(1)} %get-tuple-element.25), channel_id=1, source_target_pairs={{0,0},{1,2},{2,1},{3,4},{4,3},{5,6},{6,5},{7,7},{8,8},{9,10},{10,9... | collective-permute-start | bytes 1400840 | tf_op jit(solution)/shard_map/ppermute | solution.py:549
  5.4 0.0 slice-done
  5.4 0.0 slice-done.1
  5.4 0.1 copy-done.3
  5.5 0.0 copy-done.6
  5.5 5.4 %shard_map.101 = (f32[8,160,384]{2,1,0:T(8,128)S(1)}, bf16[480,384]{1,0:T(8,128)(2,1)S(1)}, bf16[480,384]{1,0:T(8,128)(2,1)S(1)}, bf16[3456,384]{1,0:T(8,128)(2,...) custom-call(s32[4]{0:T(128)S(1)} %get-tuple-element.20.info, ...), custom_call_target="tpu_custom_call" | custom-call | flops 4000000000 | bytes 1048576 | tf_op jit(solution)/shard_map/pallas_call | solution.py:553
  11.0 4.0 %collective-permute-start.2 = (bf16[480,384]{1,0:T(8,128)(2,1)S(1)}, bf16[480,384]{1,0:T(8,128)(2,1)S(1)}, u32[]{:S(2)}, u32[]{:S(2)}) collective-permute-start(bf16[480,384]{1,0:T(8,128)(2,1)S(1)} %get-tuple-element.29), channel_id=1, source_target_pairs={{0,1},{1,0},{2,3},{3,2},{4,5},{5,4},{6,7},{7,6},{8,9},{9,8},{10,11... | collective-permute-start | bytes 1105928 | tf_op jit(solution)/shard_map/ppermute | solution.py:561
  15.0 0.7 %collective-permute-start.3 = (bf16[480,384]{1,0:T(8,128)(2,1)S(1)}, bf16[480,384]{1,0:T(8,128)(2,1)S(1)}, u32[]{:S(2)}, u32[]{:S(2)}) collective-permute-start(bf16[480,384]{1,0:T(8,128)(2,1)S(1)} %get-tuple-element.30), channel_id=1, source_target_pairs={{0,0},{1,2},{2,1},{3,4},{4,3},{5,6},{6,5},{7,7},{8,8},{9,10},{10,9... | collective-permute-start | bytes 1105928 | tf_op jit(solution)/shard_map/ppermute | solution.py:562
  15.7 0.0 copy-done.7
  15.7 0.0 copy-done
  15.8 0.0 copy-done.8
  15.8 0.1 maximum_multiply_fusion.half_out
  15.9 0.0 collective-permute-done.got_even.packed_even
  15.9 0.0 collective-permute-done.1.got_odd.packed_odd
  15.9 7.4 %shard_map.103 = (bf16[10,160,384]{2,1,0:T(8,128)(2,1)S(1)}, f32[8,160,384]{2,1,0:T(8,128)S(1)}) custom-call(s32[4]{0:T(128)S(1)} %get-tuple-element.20.info, bf16[4,16,160]{2,1,0:T(8,128)(2,1)S(1)} %bitcast.27, bf16[2,4,16,160]{3,2,1,0:T(8,128)(2,1)S(1)} %bitcast.25, bf16[608,384]{1,0:T(8,128)(2,1)S(1)} %collective-permute-done.got_even.packed_even, ...), custom_call_target="tpu_custom_call" | custom-call | flops 5000000000 | bytes 1048576 | tf_op jit(solution)/shard_map/pallas_call | solution.py:564
  23.3 0.0 collective-permute-done.2.got_even
  23.3 0.0 collective-permute-done.3.got_odd
  23.3 13.2 %shard_map.104 = bf16[8,16,128]{2,1,0:T(8,128)(2,1)S(1)} custom-call(s32[4]{0:T(128)S(1)} %get-tuple-element.20.info, bf16[10,160,384]{2,1,0:T(8,128)(2,1)S(1)} %get-tuple-element.26.hidden, f32[8,160,384]{2,1,0:T(8,128)S(1)} %get-tuple-element.27.conv, f32[8,160,384]{2,1,0:T(8,128)S(1)} %get-tuple-element.28.acc, ...), custom_call_target="tpu_custom_call" | custom-call | flops 8000000000 | bytes 1048576 | tf_op jit(solution)/shard_map/pallas_call | solution.py:578
  36.5 11.7 %all_to_all.5.got = bf16[8,16,128]{2,1,0:T(8,128)(2,1)S(1)} all-to-all(bf16[8,16,128]{2,1,0:T(8,128)(2,1)S(1)} %shard_map.104), channel_id=1, replica_groups=mesh['prompt'=4,'tile'=8] {'tile'}, dimensions={0} | all-to-all | bytes 65536 | tf_op jit(solution)/shard_map/all_to_all | solution.py:604
  48.3 1.0 %shard_map.105 = f32[64,160]{1,0:T(8,128)} custom-call(bf16[8,128,640]{2,1,0:T(8,128)(2,1)S(1)} %get-tuple-element.23.sel, bf16[8,16,128]{2,1,0:T(8,128)(2,1)S(1)} %all_to_all.5.got), custom_call_target="tpu_custom_call" | custom-call | flops 10000000 | bytes 1048576 | tf_op jit(solution)/shard_map/pallas_call | solution.py:605
  (12 shorter events, 0.0 us)
Async XLA Ops:
  0.1 1.3 %copy-start.1 = (bf16[3,3,384,192]{2,3,1,0:T(8,128)(2,1)S(1)}, bf16[3,3,384,192]{2,3,1,0:T(8,128)(2,1)}, u32[]{:S(2)}) copy-start(bf16[3,3,384,192]{2,3,1,0:T(8,128)(2,1)} %param.16) | copy-start | bytes 3981316
  1.4 1.3 %copy-start.2 = (bf16[8,320,192]{1,2,0:T(8,128)(2,1)S(1)}, bf16[8,320,192]{1,2,0:T(8,128)(2,1)}, u32[]{:S(2)}) copy-start(bf16[8,320,192]{1,2,0:T(8,128)(2,1)} %param.13) | copy-start | bytes 2949124
  1.4 1.3 %copy-start.4 = (bf16[2,4,160,16]{2,3,1,0:T(8,128)(2,1)S(1)}, bf16[2,4,160,16]{2,3,1,0:T(8,128)(2,1)}, u32[]{:S(2)}) copy-start(bf16[2,4,160,16]{2,3,1,0:T(8,128)(2,1)} %param.11) | copy-start | bytes 122884
  1.4 1.3 %copy-start.5 = (bf16[4,160,16]{1,2,0:T(8,128)(2,1)S(1)}, bf16[4,160,16]{1,2,0:T(8,128)(2,1)}, u32[]{:S(2)}) copy-start(bf16[4,160,16]{1,2,0:T(8,128)(2,1)} %param.10) | copy-start | bytes 61444
  1.4 4.0 %slice-start = ((s8[7962624]{0:T(1024)(128)(4,1)}), s8[4194304]{0:T(1024)(128)(4,1)S(1)}, s32[]{:S(2)}) async-start(s8[7962624]{0:T(1024)(128)(4,1)} %bitcast.17), calls=%async_computation.1 | async-start | bytes 8388608
  2.7 2.7 %slice-start.1 = ((s8[7962624]{0:T(1024)(128)(4,1)}), s8[3768320]{0:T(1024)(128)(4,1)S(1)}, s32[]{:S(2)}) async-start(s8[7962624]{0:T(1024)(128)(4,1)} %bitcast.17), calls=%async_computation.2 | async-start | bytes 7536640
  2.7 2.8 %copy-start.3 = (bf16[2,4,160,384]{3,2,1,0:T(8,128)(2,1)S(1)}, bf16[2,4,160,384]{3,2,1,0:T(8,128)(2,1)}, u32[]{:S(2)}) copy-start(bf16[2,4,160,384]{3,2,1,0:T(8,128)(2,1)} %features.1) | copy-start | bytes 2949124
  2.7 2.8 %copy-start.6 = (s32[8]{0:T(128)S(1)}, s32[8]{0:T(128)}, u32[]{:S(2)}) copy-start(s32[8]{0:T(128)} %order.1) | copy-start | bytes 100
  4.2 11.7 %collective-permute-start = (bf16[608,384]{1,0:T(8,128)(2,1)S(1)}, bf16[608,384]{1,0:T(8,128)(2,1)S(1)}, u32[]{:S(2)}, u32[]{:S(2)}) collective-permute-start(bf16[608,384]{1,0:T(8,128)(2,1)S(1)} %get-tuple-element.24), channel_id=1, source_target_pairs={{0,1},{1,0},{2,3},{3,2},{4,5},{5,4},{6,7},{7,6},{8,9},{9,8},{10,11... | collective-permute-start | bytes 1400840 | tf_op jit(solution)/shard_map/ppermute | solution.py:548
  4.7 11.2 %collective-permute-start.1 = (bf16[608,384]{1,0:T(8,128)(2,1)S(1)}, bf16[608,384]{1,0:T(8,128)(2,1)S(1)}, u32[]{:S(2)}, u32[]{:S(2)}) collective-permute-start(bf16[608,384]{1,0:T(8,128)(2,1)S(1)} %get-tuple-element.25), channel_id=1, source_target_pairs={{0,0},{1,2},{2,1},{3,4},{4,3},{5,6},{6,5},{7,7},{8,8},{9,10},{10,9... | collective-permute-start | bytes 1400840 | tf_op jit(solution)/shard_map/ppermute | solution.py:549
  5.5 10.2 %copy-start.7 = (f32[384]{0:T(512)S(1)}, f32[384]{0:T(512)}, u32[]{:S(2)}) copy-start(f32[384]{0:T(512)} %param.17) | copy-start | bytes 4612
  5.5 10.2 %copy-start = (bf16[3,3,3,16,384]{4,3,2,1,0:T(8,128)(2,1)S(1)}, bf16[3,3,3,16,384]{4,3,2,1,0:T(8,128)(2,1)}, u32[]{:S(2)}) copy-start(bf16[3,3,3,16,384]{4,3,2,1,0:T(8,128)(2,1)} %param.14) | copy-start | bytes 995332
  5.5 10.2 %copy-start.8 = (f32[192]{0:T(256)S(1)}, f32[192]{0:T(256)}, u32[]{:S(2)}) copy-start(f32[192]{0:T(256)} %param.18) | copy-start | bytes 2308
  11.0 12.3 %collective-permute-start.2 = (bf16[480,384]{1,0:T(8,128)(2,1)S(1)}, bf16[480,384]{1,0:T(8,128)(2,1)S(1)}, u32[]{:S(2)}, u32[]{:S(2)}) collective-permute-start(bf16[480,384]{1,0:T(8,128)(2,1)S(1)} %get-tuple-element.29), channel_id=1, source_target_pairs={{0,1},{1,0},{2,3},{3,2},{4,5},{5,4},{6,7},{7,6},{8,9},{9,8},{10,11... | collective-permute-start | bytes 1105928 | tf_op jit(solution)/shard_map/ppermute | solution.py:561
  15.0 8.3 %collective-permute-start.3 = (bf16[480,384]{1,0:T(8,128)(2,1)S(1)}, bf16[480,384]{1,0:T(8,128)(2,1)S(1)}, u32[]{:S(2)}, u32[]{:S(2)}) collective-permute-start(bf16[480,384]{1,0:T(8,128)(2,1)S(1)} %get-tuple-element.30), channel_id=1, source_target_pairs={{0,0},{1,2},{2,1},{3,4},{4,3},{5,6},{6,5},{7,7},{8,8},{9,10},{10,9... | collective-permute-start | bytes 1105928 | tf_op jit(solution)/shard_map/ppermute | solution.py:562

commit v9 on v8

--- a/solution.py
+++ b/solution.py
@@ -275,18 +275,25 @@
             for lanes in range(0, 384, 128):
                 beside(wide.at[k], 0, lanes, plain[k % 2, :, lanes : lanes + 128], False)
 
-        def conv_rows(p, number, lanes):
+        def conv_rows(p, number):
             lhs = [wide[p + i : p + i + number].reshape(number * cols, 1152) for i in range(3)]
-            total = mm(jnp.concatenate(lhs, axis=1), mid[2, :, :, lanes].reshape(3456, lanes.stop - lanes.start))
-            conv[p : p + number, :, lanes] = total.reshape(number, cols, lanes.stop - lanes.start)
-
-        def convs(p, number):
-            return steps(conv_rows, (p, number, slice(0, 256)), (p, number, slice(256, 384)))
+            total = mm(jnp.concatenate(lhs, axis=1), mid[2, :, :, 0:256].reshape(3456, 256))
+            conv[p : p + number, :, 0:256] = total.reshape(number, cols, 256)
 
         for k in range(rows + 2):
             hidden_row(k)
-        weave(steps(hidden_row, *[(k,) for k in range(rows + 2, rows + 6)]), convs(0, rows))
-        weave(convs(rows, 4))
+        conv_rows(0, rows)
+        for k in range(rows + 2, rows + 6):
+            hidden_row(k)
+        conv_rows(rows, 4)
+        both = mm(
+            wide[0 : rows + 5].reshape((rows + 5) * cols, 1152),
+            jnp.concatenate([mid[2, 0, :, 256:384], mid[2, 1, :, 256:384]], axis=1),
+        )
+        rest = mm(wide[2 : rows + 6].reshape((rows + 4) * cols, 1152), mid[2, 2, :, 256:384])
+        for p in range(rows + 4):
+            at, after = slice(p * cols, (p + 1) * cols), slice((p + 1) * cols, (p + 2) * cols)
+            conv[p, :, 256:384] = both[at, :128] + both[after, 128:] + rest[at]
 
     return body
 
@@ -343,16 +350,18 @@
                     x = x + edge[k, :, at]
                 beside(wide.at[k], 0, lanes, inside(x, k, 2, rows + 2), False)
 
-        def up_rows(k, number, b, n):
-            x = wide[k : k + number, :, b * 384 : b * 384 + 768].reshape(number * cols, 768)
+        def up_rows(first, last, b, n):
+            count = last - first
+            x = wide[first:last, :, b * 384 : b * 384 + 768].reshape(count * cols, 768)
             lanes = slice(n * 256, n * 256 + 256)
-            (p0, p1)[b][k : k + number, :, lanes] = mm(x, fwd[b, :, lanes]).reshape(number, cols, 256)
-
-        def down_rows(k, number, odd, n):
+            (p0, p1)[b][first:last, :, lanes] = mm(x, fwd[b, :, lanes]).reshape(count, cols, 256)
+
+        def down_rows(first, last, odd, n):
+            count = last - first
             g, kernel, t = (g_odd, back_odd, t_odd) if odd else (g_even, back_even, t_even)
             lanes = slice(n * 256, n * 256 + 256)
-            x = g[k : k + number].reshape(number * cols, 768)
-            t[k : k + number, :, lanes] = mm(x, kernel[:, lanes]).reshape(number, cols, 256)
+            x = g[first:last].reshape(count * cols, 768)
+            t[first:last, :, lanes] = mm(x, kernel[:, lanes]).reshape(count, cols, 256)
 
         low = lax.broadcasted_iota(jnp.int32, (CHUNK, 128), 1) < 64
         tall_low = lax.broadcasted_iota(jnp.int32, (cols, 128), 1) < 64
@@ -417,26 +426,32 @@
                 dv = inv * (d - s * jnp.mean(d * s, axis=1, keepdims=True))
                 hid[k, at] = (back[k + 1, at, 384:768].astype(F32) + dv).astype(BF16)
 
-        def each(f, first, last):
-            return steps(f, *[(k,) for k in range(first, last)])
-
-        def ups(k, number):
-            return steps(up_rows, *[(k, number, b, n) for n in range(3) for b in range(2)])
-
-        def downs(k, number):
-            return steps(down_rows, *[(k, number, odd, n) for n in range(3) for odd in (True, False)])
-
-        def pulls(first, last):
-            return steps(pull_row, *[(k, odd) for k in range(first, last) for odd in (True, False)])
-
-        weave(each(state_row, 0, rows))
-        weave(each(state_row, rows, rows + 4), ups(0, rows))
-        weave(pulls(0, rows - 1), ups(rows, 4))
-        weave(pulls(rows - 1, rows + 3), downs(0, rows - 1))
-        weave(each(block_row, 0, rows - 2), downs(rows - 1, 4))
-        weave(each(block_row, rows - 2, rows + 2))
+        fine = rows + 3
+        for k in range(rows + 4):
+            state_row(k)
+        for b in range(2):
+            up_rows(1, rows + 4, b, 0)
+            up_rows(0, rows + 3, b, 1)
+            up_rows(0, rows + 4, b, 2)
+        for k in range(fine):
+            pull_row(k, True)
+            pull_row(k, False)
+        for odd in (True, False):
+            down_rows(1 if odd else 0, fine if odd else fine - 1, odd, 0)
+            down_rows(0, fine, odd, 1)
+            down_rows(0 if odd else 1, fine - 1 if odd else fine, odd, 2)
+        for k in range(rows + 2):
+            block_row(k)
         lhs = [back[2 - i : 2 - i + rows].reshape(size, 1152) for i in range(3)]
-        act_grad[...] = mm(jnp.concatenate(lhs, axis=1), mid_t[...]).reshape(rows, cols, 384)
+        act_grad[:, :, 0:256] = mm(jnp.concatenate(lhs, axis=1), mid_t[:, 0:256]).reshape(rows, cols, 256)
+        both = mm(
+            back[1 : rows + 2].reshape((rows + 1) * cols, 1152),
+            jnp.concatenate([mid_t[1152:2304, 256:384], mid_t[0:1152, 256:384]], axis=1),
+        )
+        rest = mm(back[0:rows].reshape(size, 1152), mid_t[2304:3456, 256:384])
+        for p in range(rows):
+            at, after = slice(p * cols, (p + 1) * cols), slice((p + 1) * cols, (p + 2) * cols)
+            act_grad[p, :, 256:384] = both[at, :128] + both[after, 128:] + rest[at]
         for k in range(rows):
             hidden_pull(k)
 

time: 49.5 us -> 48.3 us (0.976)
  Pallas kernels: 29.7 us -> 28.5 us
    pallas_call x1, Pallas kernels: 13.2 us -> 12.6 us  [shards(): call(back_body(rows, cols, chan, count, o), [((count, chan, 128), BF16)],...]
    pallas_call x1, Pallas kernels: 7.44 us -> 6.9 us  [shards(): call(current_body(rows, cols, chan), [((rows + 6, cols, 384), BF16), ((ro...]
where the time goes in v9:
time: 48.3 us; the launch traced here: 48.1 us
  Pallas kernels  28.5 us (59%)
  blocking collectives  11.7 us (24%)
  starting transfers between devices  5.95 us (12%)
  local copies, waits for them, and re-layouts  1.58 us (3%)
    pallas_call x1, Pallas kernels, shards(): call(back_body(rows, cols, chan, count, o), [((count, chan, 128), BF16)],...  12.6 us
    all_to_all x1, blocking collectives, shards(): lax.all_to_all(payload, 'tile', split_axis=0, concat_axis=0, tiled=True)  11.7 us
    pallas_call x1, Pallas kernels, shards(): call(current_body(rows, cols, chan), [((rows + 6, cols, 384), BF16), ((ro...  6.9 us
    pallas_call x1, Pallas kernels, shards(): call(cached_body(rows, cols, count, width, tokens, o), [((rows + 4, cols,...  5.43 us
    ppermute x1, starting transfers between devices, shards(): got_even = lax.ppermute(part_even, 'tile', within)  4.05 us
    unnamed x22, local copies, waits for them, and re-layouts  1.56 us
    pallas_call x1, Pallas kernels, shards(): call(pack_body(rows, cols, o, chan), [((6, cols, 384), BF16), ((edge_rows...  1.45 us
    pallas_call x1, Pallas kernels, shards(): call(taps_body, [((4,), jnp.int32), ((768, 768), BF16), ((768, 768), BF16...  1.15 us
  transfers between devices with their start and end apart: 4, of which 0 were waited for; matrix products, arithmetic and copies ran while one was open for 0% of the time, Pallas kernels for 26%

profile of v9, /device:TPU:0, one launch (start us, length us, event | category | flops | bytes accessed | tf_op | source)
XLA Modules:
  0.0 48.1 jit_solution(9886514103460289203)
XLA Ops:
  0.0 0.1 pad_add_fusion.info
  0.1 0.0 copy-start.1
  0.1 1.3 %copy-done.1 = bf16[3,3,384,192]{2,3,1,0:T(8,128)(2,1)S(1)} copy-done((bf16[3,3,384,192]{2,3,1,0:T(8,128)(2,1)S(1)}, bf16[3,3,384,192]{2,3,1,0:T(8,128)(2,1)}, u32[]{:S(2)}) %copy-start.1) | copy-done | bytes 1327128
  1.4 0.0 copy-start.2
  1.4 0.0 copy-start.4
  1.4 1.1 %shard_map.100 = (s32[4]{0:T(128)S(1)}, bf16[768,768]{1,0:T(8,128)(2,1)S(1)}, bf16[768,768]{1,0:T(8,128)(2,1)S(1)}) custom-call(s32[4]{0:T(128)S(1)} %pad_add_fusion.info, bf16[3,3,192,384]{3,2,1,0:T(8,128)(2,1)S(1)} %bitcast.21), custom_call_target="tpu_custom_call" | custom-call | flops 10000000000 | bytes 1048576 | tf_op jit(solution)/shard_map/pallas_call | solution.py:552
  2.6 0.1 copy-done.2
  2.7 0.0 copy-done.4
  2.7 0.0 copy-done.5
  2.7 0.0 copy-start.6
  2.7 1.5 %shard_map.102 = (bf16[6,160,384]{2,1,0:T(8,128)(2,1)S(1)}, bf16[608,384]{1,0:T(8,128)(2,1)S(1)}, bf16[608,384]{1,0:T(8,128)(2,1)S(1)}) custom-call(s32[4]{0:T(128)S(1)} %get-tuple-element.20.info, bf16[8,192,320]{2,1,0:T(8,128)(2,1)S(1)} %bitcast.22, bf16[4,16,160]{2,1,0:T(8,128)(2,1)S(1)} %bitcast.26, bf16[2,4,16,160]{3,2,1,0:T(8,128)(2,1)S(1)} %bitcast.24), custom_call_target="tpu_custom_call" | custom-call | flops 10000000000 | bytes 1048576 | tf_op jit(solution)/shard_map/pallas_call | solution.py:558
  4.2 0.5 %collective-permute-start = (bf16[608,384]{1,0:T(8,128)(2,1)S(1)}, bf16[608,384]{1,0:T(8,128)(2,1)S(1)}, u32[]{:S(2)}, u32[]{:S(2)}) collective-permute-start(bf16[608,384]{1,0:T(8,128)(2,1)S(1)} %get-tuple-element.24), channel_id=1, source_target_pairs={{0,1},{1,0},{2,3},{3,2},{4,5},{5,4},{6,7},{7,6},{8,9},{9,8},{10,11... | collective-permute-start | bytes 1400840 | tf_op jit(solution)/shard_map/ppermute | solution.py:563
  4.7 0.7 %collective-permute-start.1 = (bf16[608,384]{1,0:T(8,128)(2,1)S(1)}, bf16[608,384]{1,0:T(8,128)(2,1)S(1)}, u32[]{:S(2)}, u32[]{:S(2)}) collective-permute-start(bf16[608,384]{1,0:T(8,128)(2,1)S(1)} %get-tuple-element.25), channel_id=1, source_target_pairs={{0,0},{1,2},{2,1},{3,4},{4,3},{5,6},{6,5},{7,7},{8,8},{9,10},{10,9... | collective-permute-start | bytes 1400840 | tf_op jit(solution)/shard_map/ppermute | solution.py:564
  5.4 0.0 slice-done
  5.4 0.0 slice-done.1
  5.4 0.1 copy-done.3
  5.5 0.0 copy-done.6
  5.5 5.4 %shard_map.101 = (f32[8,160,384]{2,1,0:T(8,128)S(1)}, bf16[480,384]{1,0:T(8,128)(2,1)S(1)}, bf16[480,384]{1,0:T(8,128)(2,1)S(1)}, bf16[3456,384]{1,0:T(8,128)(2,...) custom-call(s32[4]{0:T(128)S(1)} %get-tuple-element.20.info, ...), custom_call_target="tpu_custom_call" | custom-call | flops 4000000000 | bytes 1048576 | tf_op jit(solution)/shard_map/pallas_call | solution.py:568
  11.0 4.0 %collective-permute-start.2 = (bf16[480,384]{1,0:T(8,128)(2,1)S(1)}, bf16[480,384]{1,0:T(8,128)(2,1)S(1)}, u32[]{:S(2)}, u32[]{:S(2)}) collective-permute-start(bf16[480,384]{1,0:T(8,128)(2,1)S(1)} %get-tuple-element.29), channel_id=1, source_target_pairs={{0,1},{1,0},{2,3},{3,2},{4,5},{5,4},{6,7},{7,6},{8,9},{9,8},{10,11... | collective-permute-start | bytes 1105928 | tf_op jit(solution)/shard_map/ppermute | solution.py:576
  15.0 0.7 %collective-permute-start.3 = (bf16[480,384]{1,0:T(8,128)(2,1)S(1)}, bf16[480,384]{1,0:T(8,128)(2,1)S(1)}, u32[]{:S(2)}, u32[]{:S(2)}) collective-permute-start(bf16[480,384]{1,0:T(8,128)(2,1)S(1)} %get-tuple-element.30), channel_id=1, source_target_pairs={{0,0},{1,2},{2,1},{3,4},{4,3},{5,6},{6,5},{7,7},{8,8},{9,10},{10,9... | collective-permute-start | bytes 1105928 | tf_op jit(solution)/shard_map/ppermute | solution.py:577
  15.7 0.0 copy-done.7
  15.7 0.0 copy-done
  15.8 0.0 copy-done.8
  15.8 0.1 maximum_multiply_fusion.half_out
  15.9 0.0 collective-permute-done.got_even.packed_even
  15.9 0.0 collective-permute-done.1.got_odd.packed_odd
  15.9 6.9 %shard_map.103 = (bf16[10,160,384]{2,1,0:T(8,128)(2,1)S(1)}, f32[8,160,384]{2,1,0:T(8,128)S(1)}) custom-call(s32[4]{0:T(128)S(1)} %get-tuple-element.20.info, bf16[4,16,160]{2,1,0:T(8,128)(2,1)S(1)} %bitcast.27, bf16[2,4,16,160]{3,2,1,0:T(8,128)(2,1)S(1)} %bitcast.25, bf16[608,384]{1,0:T(8,128)(2,1)S(1)} %collective-permute-done.got_even.packed_even, ...), custom_call_target="tpu_custom_call" | custom-call | flops 5000000000 | bytes 1048576 | tf_op jit(solution)/shard_map/pallas_call | solution.py:579
  22.8 0.0 collective-permute-done.2.got_even
  22.8 0.0 collective-permute-done.3.got_odd
  22.8 12.6 %shard_map.104 = bf16[8,16,128]{2,1,0:T(8,128)(2,1)S(1)} custom-call(s32[4]{0:T(128)S(1)} %get-tuple-element.20.info, bf16[10,160,384]{2,1,0:T(8,128)(2,1)S(1)} %get-tuple-element.26.hidden, f32[8,160,384]{2,1,0:T(8,128)S(1)} %get-tuple-element.27.conv, f32[8,160,384]{2,1,0:T(8,128)S(1)} %get-tuple-element.28.acc, ...), custom_call_target="tpu_custom_call" | custom-call | flops 8000000000 | bytes 1048576 | tf_op jit(solution)/shard_map/pallas_call | solution.py:593
  35.4 11.7 %all_to_all.5.got = bf16[8,16,128]{2,1,0:T(8,128)(2,1)S(1)} all-to-all(bf16[8,16,128]{2,1,0:T(8,128)(2,1)S(1)} %shard_map.104), channel_id=1, replica_groups=mesh['prompt'=4,'tile'=8] {'tile'}, dimensions={0} | all-to-all | bytes 65536 | tf_op jit(solution)/shard_map/all_to_all | solution.py:619
  47.1 1.0 %shard_map.105 = f32[64,160]{1,0:T(8,128)} custom-call(bf16[8,128,640]{2,1,0:T(8,128)(2,1)S(1)} %get-tuple-element.23.sel, bf16[8,16,128]{2,1,0:T(8,128)(2,1)S(1)} %all_to_all.5.got), custom_call_target="tpu_custom_call" | custom-call | flops 10000000 | bytes 1048576 | tf_op jit(solution)/shard_map/pallas_call | solution.py:620
  (12 shorter events, 0.0 us)
Async XLA Ops:
  0.1 1.3 %copy-start.1 = (bf16[3,3,384,192]{2,3,1,0:T(8,128)(2,1)S(1)}, bf16[3,3,384,192]{2,3,1,0:T(8,128)(2,1)}, u32[]{:S(2)}) copy-start(bf16[3,3,384,192]{2,3,1,0:T(8,128)(2,1)} %param.16) | copy-start | bytes 3981316
  1.4 1.3 %copy-start.2 = (bf16[8,320,192]{1,2,0:T(8,128)(2,1)S(1)}, bf16[8,320,192]{1,2,0:T(8,128)(2,1)}, u32[]{:S(2)}) copy-start(bf16[8,320,192]{1,2,0:T(8,128)(2,1)} %param.13) | copy-start | bytes 2949124
  1.4 1.3 %copy-start.4 = (bf16[2,4,160,16]{2,3,1,0:T(8,128)(2,1)S(1)}, bf16[2,4,160,16]{2,3,1,0:T(8,128)(2,1)}, u32[]{:S(2)}) copy-start(bf16[2,4,160,16]{2,3,1,0:T(8,128)(2,1)} %param.11) | copy-start | bytes 122884
  1.4 1.3 %copy-start.5 = (bf16[4,160,16]{1,2,0:T(8,128)(2,1)S(1)}, bf16[4,160,16]{1,2,0:T(8,128)(2,1)}, u32[]{:S(2)}) copy-start(bf16[4,160,16]{1,2,0:T(8,128)(2,1)} %param.10) | copy-start | bytes 61444
  1.4 4.0 %slice-start = ((s8[7962624]{0:T(1024)(128)(4,1)}), s8[4194304]{0:T(1024)(128)(4,1)S(1)}, s32[]{:S(2)}) async-start(s8[7962624]{0:T(1024)(128)(4,1)} %bitcast.17), calls=%async_computation.1 | async-start | bytes 8388608
  2.7 2.7 %slice-start.1 = ((s8[7962624]{0:T(1024)(128)(4,1)}), s8[3768320]{0:T(1024)(128)(4,1)S(1)}, s32[]{:S(2)}) async-start(s8[7962624]{0:T(1024)(128)(4,1)} %bitcast.17), calls=%async_computation.2 | async-start | bytes 7536640
  2.7 2.8 %copy-start.3 = (bf16[2,4,160,384]{3,2,1,0:T(8,128)(2,1)S(1)}, bf16[2,4,160,384]{3,2,1,0:T(8,128)(2,1)}, u32[]{:S(2)}) copy-start(bf16[2,4,160,384]{3,2,1,0:T(8,128)(2,1)} %features.1) | copy-start | bytes 2949124
  2.7 2.8 %copy-start.6 = (s32[8]{0:T(128)S(1)}, s32[8]{0:T(128)}, u32[]{:S(2)}) copy-start(s32[8]{0:T(128)} %order.1) | copy-start | bytes 100
  4.2 11.7 %collective-permute-start = (bf16[608,384]{1,0:T(8,128)(2,1)S(1)}, bf16[608,384]{1,0:T(8,128)(2,1)S(1)}, u32[]{:S(2)}, u32[]{:S(2)}) collective-permute-start(bf16[608,384]{1,0:T(8,128)(2,1)S(1)} %get-tuple-element.24), channel_id=1, source_target_pairs={{0,1},{1,0},{2,3},{3,2},{4,5},{5,4},{6,7},{7,6},{8,9},{9,8},{10,11... | collective-permute-start | bytes 1400840 | tf_op jit(solution)/shard_map/ppermute | solution.py:563
  4.7 11.2 %collective-permute-start.1 = (bf16[608,384]{1,0:T(8,128)(2,1)S(1)}, bf16[608,384]{1,0:T(8,128)(2,1)S(1)}, u32[]{:S(2)}, u32[]{:S(2)}) collective-permute-start(bf16[608,384]{1,0:T(8,128)(2,1)S(1)} %get-tuple-element.25), channel_id=1, source_target_pairs={{0,0},{1,2},{2,1},{3,4},{4,3},{5,6},{6,5},{7,7},{8,8},{9,10},{10,9... | collective-permute-start | bytes 1400840 | tf_op jit(solution)/shard_map/ppermute | solution.py:564
  5.5 10.2 %copy-start.7 = (f32[384]{0:T(512)S(1)}, f32[384]{0:T(512)}, u32[]{:S(2)}) copy-start(f32[384]{0:T(512)} %param.17) | copy-start | bytes 4612
  5.5 10.2 %copy-start = (bf16[3,3,3,16,384]{4,3,2,1,0:T(8,128)(2,1)S(1)}, bf16[3,3,3,16,384]{4,3,2,1,0:T(8,128)(2,1)}, u32[]{:S(2)}) copy-start(bf16[3,3,3,16,384]{4,3,2,1,0:T(8,128)(2,1)} %param.14) | copy-start | bytes 995332
  5.5 10.2 %copy-start.8 = (f32[192]{0:T(256)S(1)}, f32[192]{0:T(256)}, u32[]{:S(2)}) copy-start(f32[192]{0:T(256)} %param.18) | copy-start | bytes 2308
  11.0 11.8 %collective-permute-start.2 = (bf16[480,384]{1,0:T(8,128)(2,1)S(1)}, bf16[480,384]{1,0:T(8,128)(2,1)S(1)}, u32[]{:S(2)}, u32[]{:S(2)}) collective-permute-start(bf16[480,384]{1,0:T(8,128)(2,1)S(1)} %get-tuple-element.29), channel_id=1, source_target_pairs={{0,1},{1,0},{2,3},{3,2},{4,5},{5,4},{6,7},{7,6},{8,9},{9,8},{10,11... | collective-permute-start | bytes 1105928 | tf_op jit(solution)/shard_map/ppermute | solution.py:576
  15.0 7.8 %collective-permute-start.3 = (bf16[480,384]{1,0:T(8,128)(2,1)S(1)}, bf16[480,384]{1,0:T(8,128)(2,1)S(1)}, u32[]{:S(2)}, u32[]{:S(2)}) collective-permute-start(bf16[480,384]{1,0:T(8,128)(2,1)S(1)} %get-tuple-element.30), channel_id=1, source_target_pairs={{0,0},{1,2},{2,1},{3,4},{4,3},{5,6},{6,5},{7,7},{8,8},{9,10},{10,9... | collective-permute-start | bytes 1105928 | tf_op jit(solution)/shard_map/ppermute | solution.py:577

commit v10 on v8

--- a/solution.py
+++ b/solution.py
@@ -20,6 +20,16 @@
             while done[n] * total < (k + 1) * len(g):
                 g[done[n]]()
                 done[n] += 1
+
+
+def joined(refs, lanes=slice(None)):
+    return jnp.concatenate([ref[:, lanes] for ref in refs], axis=0)
+
+
+def shared(refs, lanes, value):
+    size = refs[0].shape[0]
+    for k, ref in enumerate(refs):
+        ref[:, lanes] = value[k * size : (k + 1) * size]
 
 
 def steps(f, *keys):
@@ -214,8 +224,9 @@
     per = chan * rows
     base = 3 * cols
 
-    def body(info, latent, cached, got_even, got_odd, w_in, mid, half_gain, hidden, conv, lat, tall, wide, w_order, plain):
+    def body(info, latent, cached, got_even, got_odd, w_in, mid, half_gain, hidden, conv, lat, tall, w_order, *buffers):
         even = info[0] == 0
+        wide, plain = buffers[: rows + 6], buffers[rows + 6 :]
         lat[...] = jnp.zeros_like(lat)
 
         def fill(first_row, got, ok):
@@ -258,10 +269,10 @@
         def hidden_row(k):
             lhs = tall[k : k + 3].reshape(27 * chan, 256)[:, 0:cols]
             h = lax.dot_general(lhs, w_order[...], (((0,), (0,)), ((), ())), preferred_element_type=F32)
-            plain[k % 2] = h
+            plain[k][...] = h
             for c in range(0, cols, CHUNK):
                 at = slice(c, c + CHUNK)
-                v = plain[k % 2, at].astype(BF16)
+                v = plain[k][at].astype(BF16)
                 hidden[k, at] = v
                 v = v.astype(F32)
                 inv = lax.rsqrt(jnp.mean(v * v, axis=1, keepdims=True) + EPS)
@@ -271,22 +282,24 @@
                     act = act * flag(info, 1)
                 if k >= rows + 3:
                     act = act * flag(info, 2)
-                plain[k % 2, at] = act
+                plain[k][at] = act
             for lanes in range(0, 384, 128):
-                beside(wide.at[k], 0, lanes, plain[k % 2, :, lanes : lanes + 128], False)
-
-        def conv_rows(p, number, lanes):
-            lhs = [wide[p + i : p + i + number].reshape(number * cols, 1152) for i in range(3)]
-            total = mm(jnp.concatenate(lhs, axis=1), mid[2, :, :, lanes].reshape(3456, lanes.stop - lanes.start))
-            conv[p : p + number, :, lanes] = total.reshape(number, cols, lanes.stop - lanes.start)
-
-        def convs(p, number):
-            return steps(conv_rows, (p, number, slice(0, 256)), (p, number, slice(256, 384)))
-
-        for k in range(rows + 2):
+                beside(wide[k], 0, lanes, plain[k][:, lanes : lanes + 128], False)
+
+        def conv_rows(p, number):
+            lhs = [joined(wide[p + i : p + i + number]) for i in range(3)]
+            total = mm(jnp.concatenate(lhs, axis=1), mid[2, :, :, 0:256].reshape(3456, 256))
+            conv[p : p + number, :, 0:256] = total.reshape(number, cols, 256)
+
+        for k in range(rows + 1):
             hidden_row(k)
-        weave(steps(hidden_row, *[(k,) for k in range(rows + 2, rows + 6)]), convs(0, rows))
-        weave(convs(rows, 4))
+        weave(steps(hidden_row, *[(k,) for k in range(rows + 1, rows + 6)]), steps(conv_rows, (0, rows - 1)))
+        conv_rows(rows - 1, 5)
+        both = mm(joined(wide[0 : rows + 5]), jnp.concatenate([mid[2, 0, :, 256:384], mid[2, 1, :, 256:384]], axis=1))
+        rest = mm(joined(wide[2 : rows + 6]), mid[2, 2, :, 256:384])
+        for p in range(rows + 4):
+            at, after = slice(p * cols, (p + 1) * cols), slice((p + 1) * cols, (p + 2) * cols)
+            conv[p, :, 256:384] = both[at, :128] + both[after, 128:] + rest[at]
 
     return body
 
@@ -303,8 +316,20 @@
 
     def body(
         info, hidden, conv, acc, got_even, got_odd, packed_even, packed_odd, own, own_mid, fwd, back_odd, back_even, mid_t, w_in, half_gain,
-        half_out, payload, reward, edge, p0, p1, g_odd, g_even, wide, t_odd, t_even, back, act_grad, hid, tmp_odd, tmp_even, lines,
+        half_out, payload, reward, edge, lines, *buffers
     ):
+        fine = rows + 3
+        buffers = list(buffers)
+
+        def part(count):
+            taken = buffers[:count]
+            del buffers[:count]
+            return taken
+
+        p0, p1, wide = part(rows + 4), part(rows + 4), part(rows + 4)
+        g_odd, g_even, t_odd, t_even = part(fine), part(fine), part(fine), part(fine)
+        tmp_odd, tmp_even, back = part(fine), part(fine), part(rows + 2)
+        act_grad, hid = part(rows), part(rows)
         even = info[0] == 0
         top, bottom = flag(info, 1), flag(info, 2)
 
@@ -341,18 +366,17 @@
                     x = x + acc[k, :, at]
                 if k < 3 or k > rows:
                     x = x + edge[k, :, at]
-                beside(wide.at[k], 0, lanes, inside(x, k, 2, rows + 2), False)
-
-        def up_rows(k, number, b, n):
-            x = wide[k : k + number, :, b * 384 : b * 384 + 768].reshape(number * cols, 768)
+                beside(wide[k], 0, lanes, inside(x, k, 2, rows + 2), False)
+
+        def up_rows(first, last, b, n):
             lanes = slice(n * 256, n * 256 + 256)
-            (p0, p1)[b][k : k + number, :, lanes] = mm(x, fwd[b, :, lanes]).reshape(number, cols, 256)
-
-        def down_rows(k, number, odd, n):
+            x = joined(wide[first:last], slice(b * 384, b * 384 + 768))
+            shared((p0, p1)[b][first:last], lanes, mm(x, fwd[b, :, lanes]))
+
+        def down_rows(first, last, odd, n):
             g, kernel, t = (g_odd, back_odd, t_odd) if odd else (g_even, back_even, t_even)
             lanes = slice(n * 256, n * 256 + 256)
-            x = g[k : k + number].reshape(number * cols, 768)
-            t[k : k + number, :, lanes] = mm(x, kernel[:, lanes]).reshape(number, cols, 256)
+            shared(t[first:last], lanes, mm(joined(g[first:last]), kernel[:, lanes]))
 
         low = lax.broadcasted_iota(jnp.int32, (CHUNK, 128), 1) < 64
         tall_low = lax.broadcasted_iota(jnp.int32, (cols, 128), 1) < 64
@@ -381,31 +405,31 @@
             for c in range(0, cols, CHUNK):
                 at = slice(c, c + CHUNK)
                 if odd:
-                    v0 = p0[k, at, 256:384] + p0[k + 1, at, 0:128]
-                    v1 = p1[k, at, 256:384] + p1[k + 1, at, 0:128]
-                    m0 = p0[k, at, 640:768] + p0[k + 1, at, 512:640]
-                    m1 = p1[k, at, 640:768] + p1[k + 1, at, 512:640]
+                    v0 = p0[k][at, 256:384] + p0[k + 1][at, 0:128]
+                    v1 = p1[k][at, 256:384] + p1[k + 1][at, 0:128]
+                    m0 = p0[k][at, 640:768] + p0[k + 1][at, 512:640]
+                    m1 = p1[k][at, 640:768] + p1[k + 1][at, 512:640]
                 else:
-                    v0 = p0[k + 1, at, 128:256] + p0[k, at, 384:512]
-                    v1 = p1[k + 1, at, 128:256] + p1[k, at, 384:512]
-                    m0 = p1[k + 1, at, 512:640] + p1[k, at, 640:768]
-                    m1 = p0[k + 1, at, 512:640] + p0[k, at, 640:768]
+                    v0 = p0[k + 1][at, 128:256] + p0[k][at, 384:512]
+                    v1 = p1[k + 1][at, 128:256] + p1[k][at, 384:512]
+                    m0 = p1[k + 1][at, 512:640] + p1[k][at, 640:768]
+                    m1 = p0[k + 1][at, 512:640] + p0[k][at, 640:768]
                 out = pull(v0, v1, jnp.where(low, m0, m1), reward[2 * k + (0 if odd else 1), at], odd)
                 for n, value in enumerate(out):
                     lanes = slice(n * 128, n * 128 + 128)
-                    target[k, at, lanes] = value.astype(BF16)
-                    tmp[k % 2, at, lanes] = value
-            target[k, :, 384:512] = from_right(tmp[k % 2, :, 0:128]).astype(BF16)
-            target[k, :, 512:640] = from_left(tmp[k % 2, :, 128:256]).astype(BF16)
-            x = tmp[k % 2, :, 256:384]
+                    target[k][at, lanes] = value.astype(BF16)
+                    tmp[k][at, lanes] = value
+            target[k][:, 384:512] = from_right(tmp[k][:, 0:128]).astype(BF16)
+            target[k][:, 512:640] = from_left(tmp[k][:, 128:256]).astype(BF16)
+            x = tmp[k][:, 256:384]
             sides = (from_right(x), from_left(x)) if odd else (from_left(x), from_right(x))
-            target[k, :, 640:768] = jnp.where(tall_low, *sides).astype(BF16)
+            target[k][:, 640:768] = jnp.where(tall_low, *sides).astype(BF16)
 
         def block_row(k):
             for lanes in range(0, 384, 128):
                 at, far = slice(lanes, lanes + 128), slice(lanes + 384, lanes + 512)
-                x = t_odd[k + 1, :, at] + t_odd[k, :, far] + t_even[k, :, at] + t_even[k + 1, :, far]
-                beside(back.at[k], 0, lanes, inside(x, k, 1, rows + 1), True)
+                x = t_odd[k + 1][:, at] + t_odd[k][:, far] + t_even[k][:, at] + t_even[k + 1][:, far]
+                beside(back[k], 0, lanes, inside(x, k, 1, rows + 1), True)
 
         def hidden_pull(k):
             for c in range(0, cols, CHUNK):
@@ -413,34 +437,62 @@
                 v = hidden[k + 3, at].astype(F32)
                 inv = lax.rsqrt(jnp.mean(v * v, axis=1, keepdims=True) + EPS)
                 s = v * inv
-                d = pulled(s, half_gain[...], act_grad[k, at])
+                d = pulled(s, half_gain[...], act_grad[k][at])
                 dv = inv * (d - s * jnp.mean(d * s, axis=1, keepdims=True))
-                hid[k, at] = (back[k + 1, at, 384:768].astype(F32) + dv).astype(BF16)
+                hid[k][at] = (back[k + 1][at, 384:768].astype(F32) + dv).astype(BF16)
+
+        def mid_rows(p, number):
+            lhs = [joined(back[p + 2 - i : p + 2 - i + number]) for i in range(3)]
+            shared(act_grad[p : p + number], slice(0, 256), mm(jnp.concatenate(lhs, axis=1), mid_t[:, 0:256]))
+
+        def mid_rest(p, number):
+            pair = jnp.concatenate([mid_t[1152:2304, 256:384], mid_t[0:1152, 256:384]], axis=1)
+            both = mm(joined(back[p + 1 : p + number + 2]), pair)
+            rest = mm(joined(back[p : p + number]), mid_t[2304:3456, 256:384])
+            for k in range(number):
+                at, after = slice(k * cols, (k + 1) * cols), slice((k + 1) * cols, (k + 2) * cols)
+                act_grad[p + k][:, 256:384] = both[at, :128] + both[after, 128:] + rest[at]
 
         def each(f, first, last):
             return steps(f, *[(k,) for k in range(first, last)])
 
-        def ups(k, number):
-            return steps(up_rows, *[(k, number, b, n) for n in range(3) for b in range(2)])
-
-        def downs(k, number):
-            return steps(down_rows, *[(k, number, odd, n) for n in range(3) for odd in (True, False)])
+        def ups(first, last):
+            full = rows + 4
+            return steps(
+                up_rows,
+                *[
+                    key
+                    for b in range(2)
+                    for key in (
+                        (max(first, 1), last, b, 0), (first, min(last, full - 1), b, 1), (first, last, b, 2),
+                    )
+                ],
+            )
+
+        def downs(first, last):
+            keys = []
+            for odd in (True, False):
+                skip_first, skip_last = max(first, 1), min(last, fine - 1)
+                keys.append((skip_first, last, odd, 0) if odd else (first, skip_last, odd, 0))
+                keys.append((first, last, odd, 1))
+                keys.append((first, skip_last, odd, 2) if odd else (skip_first, last, odd, 2))
+            return steps(down_rows, *keys)
 
         def pulls(first, last):
             return steps(pull_row, *[(k, odd) for k in range(first, last) for odd in (True, False)])
 
         weave(each(state_row, 0, rows))
         weave(each(state_row, rows, rows + 4), ups(0, rows))
-        weave(pulls(0, rows - 1), ups(rows, 4))
-        weave(pulls(rows - 1, rows + 3), downs(0, rows - 1))
-        weave(each(block_row, 0, rows - 2), downs(rows - 1, 4))
+        weave(pulls(0, rows - 1), ups(rows, rows + 4))
+        weave(pulls(rows - 1, fine), downs(0, rows - 1))
+        weave(each(block_row, 0, rows - 2), downs(rows - 1, fine))
         weave(each(block_row, rows - 2, rows + 2))
-        lhs = [back[2 - i : 2 - i + rows].reshape(size, 1152) for i in range(3)]
-        act_grad[...] = mm(jnp.concatenate(lhs, axis=1), mid_t[...]).reshape(rows, cols, 384)
+        mid_rows(0, rows)
+        mid_rest(0, rows)
         for k in range(rows):
             hidden_pull(k)
 
-        z = mm_t(w_in[...], hid[...].reshape(size, 384))
+        z = mm_t(w_in[...], joined(hid))
         place = lax.broadcasted_iota(jnp.int32, (chan, size), 1)
         col = lax.rem(place, cols)
         sums = []
@@ -568,10 +620,10 @@
         [
             pltpu.VMEM((9 * rows * chan, 256), F32),
             pltpu.VMEM((3 * rows, 9 * chan, 256), BF16),
-            pltpu.VMEM((rows + 6, cols, 1152), BF16),
             pltpu.VMEM((27 * chan, 384), BF16),
-            pltpu.VMEM((2, cols, 384), F32),
-        ],
+        ]
+        + [pltpu.VMEM((cols, 1152), BF16)] * (rows + 6)
+        + [pltpu.VMEM((cols, 384), F32)] * (rows + 6),
         5e9, 14,
     )(info, lat, lat_cached, packed_even, packed_odd, w_in, mid, gain)
 
@@ -582,21 +634,17 @@
         [
             pltpu.VMEM((2 * rows + 6, cols, 384), BF16),
             pltpu.VMEM((rows + 4, cols, 384), F32),
-            pltpu.VMEM((rows + 4, cols, 768), F32),
-            pltpu.VMEM((rows + 4, cols, 768), F32),
-            pltpu.VMEM((rows + 3, cols, 768), BF16),
-            pltpu.VMEM((rows + 3, cols, 768), BF16),
-            pltpu.VMEM((rows + 4, cols, 1152), BF16),
-            pltpu.VMEM((rows + 3, cols, 768), F32),
-            pltpu.VMEM((rows + 3, cols, 768), F32),
-            pltpu.VMEM((rows + 2, cols, 1152), BF16),
-            pltpu.VMEM((rows, cols, 384), F32),
-            pltpu.VMEM((rows, cols, 384), BF16),
-            pltpu.VMEM((2, cols, 384), F32),
-            pltpu.VMEM((2, cols, 384), F32),
             pltpu.VMEM((3 * chan, size), F32),
-        ],
-        8e9, 34,
+        ]
+        + [pltpu.VMEM((cols, 768), F32)] * (2 * (rows + 4))
+        + [pltpu.VMEM((cols, 1152), BF16)] * (rows + 4)
+        + [pltpu.VMEM((cols, 768), BF16)] * (2 * (rows + 3))
+        + [pltpu.VMEM((cols, 768), F32)] * (2 * (rows + 3))
+        + [pltpu.VMEM((cols, 384), F32)] * (2 * (rows + 3))
+        + [pltpu.VMEM((cols, 1152), BF16)] * (rows + 2)
+        + [pltpu.VMEM((cols, 384), F32)] * rows
+        + [pltpu.VMEM((cols, 384), BF16)] * rows,
+        8e9, 36,
     )(
         info, hidden, conv, acc, got_even, got_odd, packed_even, packed_odd, own, own_mid, fwd, back_odd, back_even, mid_t,
         w_in[2].reshape(9 * chan, mid_chan), gain, gain_out,

time: 49.5 us -> 48.3 us (0.976)
  Pallas kernels: 29.7 us -> 28.5 us
    pallas_call x1, Pallas kernels: 13.2 us -> 12.5 us  [shards(): call(back_body(rows, cols, chan, count, o), [((count, chan, 128), BF16)],...]
where the time goes in v10:
time: 48.3 us; the launch traced here: 48.1 us
  Pallas kernels  28.5 us (59%)
  blocking collectives  11.7 us (24%)
  starting transfers between devices  5.95 us (12%)
  local copies, waits for them, and re-layouts  1.58 us (3%)
    pallas_call x1, Pallas kernels, shards(): call(back_body(rows, cols, chan, count, o), [((count, chan, 128), BF16)],...  12.5 us
    all_to_all x1, blocking collectives, shards(): lax.all_to_all(payload, 'tile', split_axis=0, concat_axis=0, tiled=True)  11.7 us
    pallas_call x1, Pallas kernels, shards(): call(current_body(rows, cols, chan), [((rows + 6, cols, 384), BF16), ((ro...  7.01 us
    pallas_call x1, Pallas kernels, shards(): call(cached_body(rows, cols, count, width, tokens, o), [((rows + 4, cols,...  5.43 us
    ppermute x1, starting transfers between devices, shards(): got_even = lax.ppermute(part_even, 'tile', within)  4.05 us
    unnamed x22, local copies, waits for them, and re-layouts  1.56 us
    pallas_call x1, Pallas kernels, shards(): call(pack_body(rows, cols, o, chan), [((6, cols, 384), BF16), ((edge_rows...  1.45 us
    pallas_call x1, Pallas kernels, shards(): call(taps_body, [((4,), jnp.int32), ((768, 768), BF16), ((768, 768), BF16...  1.15 us
  transfers between devices with their start and end apart: 4, of which 0 were waited for; matrix products, arithmetic and copies ran while one was open for 0% of the time, Pallas kernels for 26%

profile of v10, /device:TPU:0, one launch (start us, length us, event | category | flops | bytes accessed | tf_op | source)
XLA Modules:
  0.0 48.1 jit_solution(6725896348009631123)
XLA Ops:
  0.0 0.1 pad_add_fusion.info
  0.1 0.0 copy-start.1
  0.1 1.3 %copy-done.1 = bf16[3,3,384,192]{2,3,1,0:T(8,128)(2,1)S(1)} copy-done((bf16[3,3,384,192]{2,3,1,0:T(8,128)(2,1)S(1)}, bf16[3,3,384,192]{2,3,1,0:T(8,128)(2,1)}, u32[]{:S(2)}) %copy-start.1) | copy-done | bytes 1327128
  1.4 0.0 copy-start.2
  1.4 0.0 copy-start.4
  1.4 1.1 %shard_map.100 = (s32[4]{0:T(128)S(1)}, bf16[768,768]{1,0:T(8,128)(2,1)S(1)}, bf16[768,768]{1,0:T(8,128)(2,1)S(1)}) custom-call(s32[4]{0:T(128)S(1)} %pad_add_fusion.info, bf16[3,3,192,384]{3,2,1,0:T(8,128)(2,1)S(1)} %bitcast.21), custom_call_target="tpu_custom_call" | custom-call | flops 10000000000 | bytes 1048576 | tf_op jit(solution)/shard_map/pallas_call | solution.py:589
  2.6 0.1 copy-done.2
  2.7 0.0 copy-done.4
  2.7 0.0 copy-done.5
  2.7 0.0 copy-start.6
  2.7 1.5 %shard_map.102 = (bf16[6,160,384]{2,1,0:T(8,128)(2,1)S(1)}, bf16[608,384]{1,0:T(8,128)(2,1)S(1)}, bf16[608,384]{1,0:T(8,128)(2,1)S(1)}) custom-call(s32[4]{0:T(128)S(1)} %get-tuple-element.20.info, bf16[8,192,320]{2,1,0:T(8,128)(2,1)S(1)} %bitcast.22, bf16[4,16,160]{2,1,0:T(8,128)(2,1)S(1)} %bitcast.26, bf16[2,4,16,160]{3,2,1,0:T(8,128)(2,1)S(1)} %bitcast.24), custom_call_target="tpu_custom_call" | custom-call | flops 10000000000 | bytes 1048576 | tf_op jit(solution)/shard_map/pallas_call | solution.py:595
  4.2 0.5 %collective-permute-start = (bf16[608,384]{1,0:T(8,128)(2,1)S(1)}, bf16[608,384]{1,0:T(8,128)(2,1)S(1)}, u32[]{:S(2)}, u32[]{:S(2)}) collective-permute-start(bf16[608,384]{1,0:T(8,128)(2,1)S(1)} %get-tuple-element.24), channel_id=1, source_target_pairs={{0,1},{1,0},{2,3},{3,2},{4,5},{5,4},{6,7},{7,6},{8,9},{9,8},{10,11... | collective-permute-start | bytes 1400840 | tf_op jit(solution)/shard_map/ppermute | solution.py:600
  4.7 0.7 %collective-permute-start.1 = (bf16[608,384]{1,0:T(8,128)(2,1)S(1)}, bf16[608,384]{1,0:T(8,128)(2,1)S(1)}, u32[]{:S(2)}, u32[]{:S(2)}) collective-permute-start(bf16[608,384]{1,0:T(8,128)(2,1)S(1)} %get-tuple-element.25), channel_id=1, source_target_pairs={{0,0},{1,2},{2,1},{3,4},{4,3},{5,6},{6,5},{7,7},{8,8},{9,10},{10,9... | collective-permute-start | bytes 1400840 | tf_op jit(solution)/shard_map/ppermute | solution.py:601
  5.4 0.0 slice-done
  5.4 0.0 slice-done.1
  5.4 0.1 copy-done.3
  5.5 0.0 copy-done.6
  5.5 5.4 %shard_map.101 = (f32[8,160,384]{2,1,0:T(8,128)S(1)}, bf16[480,384]{1,0:T(8,128)(2,1)S(1)}, bf16[480,384]{1,0:T(8,128)(2,1)S(1)}, bf16[3456,384]{1,0:T(8,128)(2,...) custom-call(s32[4]{0:T(128)S(1)} %get-tuple-element.20.info, ...), custom_call_target="tpu_custom_call" | custom-call | flops 4000000000 | bytes 1048576 | tf_op jit(solution)/shard_map/pallas_call | solution.py:605
  11.0 4.0 %collective-permute-start.2 = (bf16[480,384]{1,0:T(8,128)(2,1)S(1)}, bf16[480,384]{1,0:T(8,128)(2,1)S(1)}, u32[]{:S(2)}, u32[]{:S(2)}) collective-permute-start(bf16[480,384]{1,0:T(8,128)(2,1)S(1)} %get-tuple-element.29), channel_id=1, source_target_pairs={{0,1},{1,0},{2,3},{3,2},{4,5},{5,4},{6,7},{7,6},{8,9},{9,8},{10,11... | collective-permute-start | bytes 1105928 | tf_op jit(solution)/shard_map/ppermute | solution.py:613
  15.0 0.7 %collective-permute-start.3 = (bf16[480,384]{1,0:T(8,128)(2,1)S(1)}, bf16[480,384]{1,0:T(8,128)(2,1)S(1)}, u32[]{:S(2)}, u32[]{:S(2)}) collective-permute-start(bf16[480,384]{1,0:T(8,128)(2,1)S(1)} %get-tuple-element.30), channel_id=1, source_target_pairs={{0,0},{1,2},{2,1},{3,4},{4,3},{5,6},{6,5},{7,7},{8,8},{9,10},{10,9... | collective-permute-start | bytes 1105928 | tf_op jit(solution)/shard_map/ppermute | solution.py:614
  15.7 0.0 copy-done.7
  15.7 0.0 copy-done
  15.8 0.0 copy-done.8
  15.8 0.1 maximum_multiply_fusion.half_out
  15.9 0.0 collective-permute-done.got_even.packed_even
  15.9 0.0 collective-permute-done.1.got_odd.packed_odd
  15.9 7.0 %shard_map.103 = (bf16[10,160,384]{2,1,0:T(8,128)(2,1)S(1)}, f32[8,160,384]{2,1,0:T(8,128)S(1)}) custom-call(s32[4]{0:T(128)S(1)} %get-tuple-element.20.info, bf16[4,16,160]{2,1,0:T(8,128)(2,1)S(1)} %bitcast.27, bf16[2,4,16,160]{3,2,1,0:T(8,128)(2,1)S(1)} %bitcast.25, bf16[608,384]{1,0:T(8,128)(2,1)S(1)} %collective-permute-done.got_even.packed_even, ...), custom_call_target="tpu_custom_call" | custom-call | flops 5000000000 | bytes 1048576 | tf_op jit(solution)/shard_map/pallas_call | solution.py:616
  22.9 0.0 collective-permute-done.2.got_even
  22.9 0.0 collective-permute-done.3.got_odd
  22.9 12.5 %shard_map.104 = bf16[8,16,128]{2,1,0:T(8,128)(2,1)S(1)} custom-call(s32[4]{0:T(128)S(1)} %get-tuple-element.20.info, bf16[10,160,384]{2,1,0:T(8,128)(2,1)S(1)} %get-tuple-element.26.hidden, f32[8,160,384]{2,1,0:T(8,128)S(1)} %get-tuple-element.27.conv, f32[8,160,384]{2,1,0:T(8,128)S(1)} %get-tuple-element.28.acc, ...), custom_call_target="tpu_custom_call" | custom-call | flops 8000000000 | bytes 1048576 | tf_op jit(solution)/shard_map/pallas_call | solution.py:630
  35.4 11.7 %all_to_all.5.got = bf16[8,16,128]{2,1,0:T(8,128)(2,1)S(1)} all-to-all(bf16[8,16,128]{2,1,0:T(8,128)(2,1)S(1)} %shard_map.104), channel_id=1, replica_groups=mesh['prompt'=4,'tile'=8] {'tile'}, dimensions={0} | all-to-all | bytes 65536 | tf_op jit(solution)/shard_map/all_to_all | solution.py:652
  47.1 1.0 %shard_map.105 = f32[64,160]{1,0:T(8,128)} custom-call(bf16[8,128,640]{2,1,0:T(8,128)(2,1)S(1)} %get-tuple-element.23.sel, bf16[8,16,128]{2,1,0:T(8,128)(2,1)S(1)} %all_to_all.5.got), custom_call_target="tpu_custom_call" | custom-call | flops 10000000 | bytes 1048576 | tf_op jit(solution)/shard_map/pallas_call | solution.py:653
  (12 shorter events, 0.0 us)
Async XLA Ops:
  0.1 1.3 %copy-start.1 = (bf16[3,3,384,192]{2,3,1,0:T(8,128)(2,1)S(1)}, bf16[3,3,384,192]{2,3,1,0:T(8,128)(2,1)}, u32[]{:S(2)}) copy-start(bf16[3,3,384,192]{2,3,1,0:T(8,128)(2,1)} %param.16) | copy-start | bytes 3981316
  1.4 1.3 %copy-start.2 = (bf16[8,320,192]{1,2,0:T(8,128)(2,1)S(1)}, bf16[8,320,192]{1,2,0:T(8,128)(2,1)}, u32[]{:S(2)}) copy-start(bf16[8,320,192]{1,2,0:T(8,128)(2,1)} %param.13) | copy-start | bytes 2949124
  1.4 1.3 %copy-start.4 = (bf16[2,4,160,16]{2,3,1,0:T(8,128)(2,1)S(1)}, bf16[2,4,160,16]{2,3,1,0:T(8,128)(2,1)}, u32[]{:S(2)}) copy-start(bf16[2,4,160,16]{2,3,1,0:T(8,128)(2,1)} %param.11) | copy-start | bytes 122884
  1.4 1.3 %copy-start.5 = (bf16[4,160,16]{1,2,0:T(8,128)(2,1)S(1)}, bf16[4,160,16]{1,2,0:T(8,128)(2,1)}, u32[]{:S(2)}) copy-start(bf16[4,160,16]{1,2,0:T(8,128)(2,1)} %param.10) | copy-start | bytes 61444
  1.4 4.0 %slice-start = ((s8[7962624]{0:T(1024)(128)(4,1)}), s8[4194304]{0:T(1024)(128)(4,1)S(1)}, s32[]{:S(2)}) async-start(s8[7962624]{0:T(1024)(128)(4,1)} %bitcast.17), calls=%async_computation.1 | async-start | bytes 8388608
  2.7 2.7 %slice-start.1 = ((s8[7962624]{0:T(1024)(128)(4,1)}), s8[3768320]{0:T(1024)(128)(4,1)S(1)}, s32[]{:S(2)}) async-start(s8[7962624]{0:T(1024)(128)(4,1)} %bitcast.17), calls=%async_computation.2 | async-start | bytes 7536640
  2.7 2.8 %copy-start.3 = (bf16[2,4,160,384]{3,2,1,0:T(8,128)(2,1)S(1)}, bf16[2,4,160,384]{3,2,1,0:T(8,128)(2,1)}, u32[]{:S(2)}) copy-start(bf16[2,4,160,384]{3,2,1,0:T(8,128)(2,1)} %features.1) | copy-start | bytes 2949124
  2.7 2.8 %copy-start.6 = (s32[8]{0:T(128)S(1)}, s32[8]{0:T(128)}, u32[]{:S(2)}) copy-start(s32[8]{0:T(128)} %order.1) | copy-start | bytes 100
  4.2 11.7 %collective-permute-start = (bf16[608,384]{1,0:T(8,128)(2,1)S(1)}, bf16[608,384]{1,0:T(8,128)(2,1)S(1)}, u32[]{:S(2)}, u32[]{:S(2)}) collective-permute-start(bf16[608,384]{1,0:T(8,128)(2,1)S(1)} %get-tuple-element.24), channel_id=1, source_target_pairs={{0,1},{1,0},{2,3},{3,2},{4,5},{5,4},{6,7},{7,6},{8,9},{9,8},{10,11... | collective-permute-start | bytes 1400840 | tf_op jit(solution)/shard_map/ppermute | solution.py:600
  4.7 11.2 %collective-permute-start.1 = (bf16[608,384]{1,0:T(8,128)(2,1)S(1)}, bf16[608,384]{1,0:T(8,128)(2,1)S(1)}, u32[]{:S(2)}, u32[]{:S(2)}) collective-permute-start(bf16[608,384]{1,0:T(8,128)(2,1)S(1)} %get-tuple-element.25), channel_id=1, source_target_pairs={{0,0},{1,2},{2,1},{3,4},{4,3},{5,6},{6,5},{7,7},{8,8},{9,10},{10,9... | collective-permute-start | bytes 1400840 | tf_op jit(solution)/shard_map/ppermute | solution.py:601
  5.5 10.2 %copy-start.7 = (f32[384]{0:T(512)S(1)}, f32[384]{0:T(512)}, u32[]{:S(2)}) copy-start(f32[384]{0:T(512)} %param.17) | copy-start | bytes 4612
  5.5 10.2 %copy-start = (bf16[3,3,3,16,384]{4,3,2,1,0:T(8,128)(2,1)S(1)}, bf16[3,3,3,16,384]{4,3,2,1,0:T(8,128)(2,1)}, u32[]{:S(2)}) copy-start(bf16[3,3,3,16,384]{4,3,2,1,0:T(8,128)(2,1)} %param.14) | copy-start | bytes 995332
  5.5 10.2 %copy-start.8 = (f32[192]{0:T(256)S(1)}, f32[192]{0:T(256)}, u32[]{:S(2)}) copy-start(f32[192]{0:T(256)} %param.18) | copy-start | bytes 2308
  11.0 11.9 %collective-permute-start.2 = (bf16[480,384]{1,0:T(8,128)(2,1)S(1)}, bf16[480,384]{1,0:T(8,128)(2,1)S(1)}, u32[]{:S(2)}, u32[]{:S(2)}) collective-permute-start(bf16[480,384]{1,0:T(8,128)(2,1)S(1)} %get-tuple-element.29), channel_id=1, source_target_pairs={{0,1},{1,0},{2,3},{3,2},{4,5},{5,4},{6,7},{7,6},{8,9},{9,8},{10,11... | collective-permute-start | bytes 1105928 | tf_op jit(solution)/shard_map/ppermute | solution.py:613
  15.0 7.9 %collective-permute-start.3 = (bf16[480,384]{1,0:T(8,128)(2,1)S(1)}, bf16[480,384]{1,0:T(8,128)(2,1)S(1)}, u32[]{:S(2)}, u32[]{:S(2)}) collective-permute-start(bf16[480,384]{1,0:T(8,128)(2,1)S(1)} %get-tuple-element.30), channel_id=1, source_target_pairs={{0,0},{1,2},{2,1},{3,4},{4,3},{5,6},{6,5},{7,7},{8,8},{9,10},{10,9... | collective-permute-start | bytes 1105928 | tf_op jit(solution)/shard_map/ppermute | solution.py:614

commit v11 on v9

--- a/solution.py
+++ b/solution.py
@@ -53,22 +53,24 @@
 
 def from_left(x):
     moved = pltpu.roll(x, 1, 0)
-    first = lax.broadcasted_iota(jnp.int32, (8, x.shape[1]), 0) == 0
-    return jnp.concatenate([jnp.where(first, 0.0, moved[:8]), moved[8:]], axis=0)
+    first = lax.broadcasted_iota(jnp.int32, (16, x.shape[1]), 0) == 0
+    head = jnp.where(first, 0.0, moved[:16].astype(F32)).astype(BF16)
+    return jnp.concatenate([head, moved[16:]], axis=0)
 
 
 def from_right(x):
     size = x.shape[0]
     moved = pltpu.roll(x, size - 1, 0)
-    last = lax.broadcasted_iota(jnp.int32, (8, x.shape[1]), 0) == 7
-    return jnp.concatenate([moved[: size - 8], jnp.where(last, 0.0, moved[size - 8 :])], axis=0)
+    last = lax.broadcasted_iota(jnp.int32, (16, x.shape[1]), 0) == 15
+    tail = jnp.where(last, 0.0, moved[size - 16 :].astype(F32)).astype(BF16)
+    return jnp.concatenate([moved[: size - 16], tail], axis=0)
 
 
 def beside(target, base, lanes, x, ahead):
     sides = (from_right, from_left) if ahead else (from_left, from_right)
     for group, value in enumerate((sides[0](x), x, sides[1](x))):
         at = base + group * 384 + lanes
-        target[:, at : at + 128] = value.astype(BF16)
+        target[:, at : at + 128] = value
 
 
 CHUNK = 32
@@ -172,7 +174,7 @@
         for t in range(2):
             for r in range(rows):
                 for lanes in range(0, 384, 128):
-                    x = features[t, r, :, lanes : lanes + 128].astype(F32)
+                    x = features[t, r, :, lanes : lanes + 128]
                     beside(wide.at[r * cols : (r + 1) * cols], t * 1152, lanes, x, False)
         def product(i, lanes):
             parts[i, :, lanes] = mm(wide[...], jnp.concatenate([mid[0, i, :, lanes], mid[1, i, :, lanes]], axis=0))
@@ -271,9 +273,9 @@
                     act = act * flag(info, 1)
                 if k >= rows + 3:
                     act = act * flag(info, 2)
-                plain[k % 2, at] = act
+                wide[k, at, 384:768] = act.astype(BF16)
             for lanes in range(0, 384, 128):
-                beside(wide.at[k], 0, lanes, plain[k % 2, :, lanes : lanes + 128], False)
+                beside(wide.at[k], 0, lanes, wide[k, :, 384 + lanes : 512 + lanes], False)
 
         def conv_rows(p, number):
             lhs = [wide[p + i : p + i + number].reshape(number * cols, 1152) for i in range(3)]
@@ -310,7 +312,7 @@
 
     def body(
         info, hidden, conv, acc, got_even, got_odd, packed_even, packed_odd, own, own_mid, fwd, back_odd, back_even, mid_t, w_in, half_gain,
-        half_out, payload, reward, edge, p0, p1, g_odd, g_even, wide, t_odd, t_even, back, act_grad, hid, tmp_odd, tmp_even, lines,
+        half_out, payload, reward, edge, p0, p1, g_odd, g_even, wide, t_odd, t_even, back, act_grad, hid, lines,
     ):
         even = info[0] == 0
         top, bottom = flag(info, 1), flag(info, 2)
@@ -348,7 +350,7 @@
                     x = x + acc[k, :, at]
                 if k < 3 or k > rows:
                     x = x + edge[k, :, at]
-                beside(wide.at[k], 0, lanes, inside(x, k, 2, rows + 2), False)
+                beside(wide.at[k], 0, lanes, inside(x, k, 2, rows + 2).astype(BF16), False)
 
         def up_rows(first, last, b, n):
             count = last - first
@@ -364,7 +366,6 @@
             t[first:last, :, lanes] = mm(x, kernel[:, lanes]).reshape(count, cols, 256)
 
         low = lax.broadcasted_iota(jnp.int32, (CHUNK, 128), 1) < 64
-        tall_low = lax.broadcasted_iota(jnp.int32, (cols, 128), 1) < 64
         gains = [half_out[:, 0:128], half_out[:, 128:256]]
 
         def pull(v0, v1, vm, r, zero_low):
@@ -386,7 +387,7 @@
             return [i * (d - s * m) for (s, d), i, m in zip(out, (i0, i1, im), (m0, m1, mx))]
 
         def pull_row(k, odd):
-            target, tmp = (g_odd, tmp_odd) if odd else (g_even, tmp_even)
+            target = g_odd if odd else g_even
             for c in range(0, cols, CHUNK):
                 at = slice(c, c + CHUNK)
                 if odd:
@@ -403,18 +404,18 @@
                 for n, value in enumerate(out):
                     lanes = slice(n * 128, n * 128 + 128)
                     target[k, at, lanes] = value.astype(BF16)
-                    tmp[k % 2, at, lanes] = value
-            target[k, :, 384:512] = from_right(tmp[k % 2, :, 0:128]).astype(BF16)
-            target[k, :, 512:640] = from_left(tmp[k % 2, :, 128:256]).astype(BF16)
-            x = tmp[k % 2, :, 256:384]
+            target[k, :, 384:512] = from_right(target[k, :, 0:128])
+            target[k, :, 512:640] = from_left(target[k, :, 128:256])
+            x = target[k, :, 256:384]
             sides = (from_right(x), from_left(x)) if odd else (from_left(x), from_right(x))
-            target[k, :, 640:768] = jnp.where(tall_low, *sides).astype(BF16)
+            target[k, :, 640:704] = sides[0][:, 0:64]
+            target[k, :, 704:768] = sides[1][:, 64:128]
 
         def block_row(k):
             for lanes in range(0, 384, 128):
                 at, far = slice(lanes, lanes + 128), slice(lanes + 384, lanes + 512)
                 x = t_odd[k + 1, :, at] + t_odd[k, :, far] + t_even[k, :, at] + t_even[k + 1, :, far]
-                beside(back.at[k], 0, lanes, inside(x, k, 1, rows + 1), True)
+                beside(back.at[k], 0, lanes, inside(x, k, 1, rows + 1).astype(BF16), True)
 
         def hidden_pull(k):
             for c in range(0, cols, CHUNK):
@@ -607,8 +608,6 @@
             pltpu.VMEM((rows + 2, cols, 1152), BF16),
             pltpu.VMEM((rows, cols, 384), F32),
             pltpu.VMEM((rows, cols, 384), BF16),
-            pltpu.VMEM((2, cols, 384), F32),
-            pltpu.VMEM((2, cols, 384), F32),
             pltpu.VMEM((3 * chan, size), F32),
         ],
         8e9, 34,

time: 48.3 us -> 48.8 us (1.010)
  Pallas kernels: 28.5 us -> 29 us
where the time goes in v11:
time: 48.8 us; the launch traced here: 48.6 us
  Pallas kernels  29 us (59%)
  blocking collectives  11.7 us (24%)
  starting transfers between devices  5.94 us (12%)
  local copies, waits for them, and re-layouts  1.58 us (3%)
    pallas_call x1, Pallas kernels, shards(): call(back_body(rows, cols, chan, count, o), [((count, chan, 128), BF16)],...  12.9 us
    all_to_all x1, blocking collectives, shards(): lax.all_to_all(payload, 'tile', split_axis=0, concat_axis=0, tiled=True)  11.7 us
    pallas_call x1, Pallas kernels, shards(): call(current_body(rows, cols, chan), [((rows + 6, cols, 384), BF16), ((ro...  7.04 us
    pallas_call x1, Pallas kernels, shards(): call(cached_body(rows, cols, count, width, tokens, o), [((rows + 4, cols,...  5.46 us
    ppermute x1, starting transfers between devices, shards(): got_even = lax.ppermute(part_even, 'tile', within)  4.05 us
    unnamed x22, local copies, waits for them, and re-layouts  1.56 us
    pallas_call x1, Pallas kernels, shards(): call(pack_body(rows, cols, o, chan), [((6, cols, 384), BF16), ((edge_rows...  1.45 us
    pallas_call x1, Pallas kernels, shards(): call(taps_body, [((4,), jnp.int32), ((768, 768), BF16), ((768, 768), BF16...  1.15 us
  transfers between devices with their start and end apart: 4, of which 0 were waited for; matrix products, arithmetic and copies ran while one was open for 0% of the time, Pallas kernels for 26%

profile of v11, /device:TPU:0, one launch (start us, length us, event | category | flops | bytes accessed | tf_op | source)
XLA Modules:
  0.0 48.6 jit_solution(11799049506453606936)
XLA Ops:
  0.0 0.1 pad_add_fusion.info
  0.1 0.0 copy-start.1
  0.1 1.3 %copy-done.1 = bf16[3,3,384,192]{2,3,1,0:T(8,128)(2,1)S(1)} copy-done((bf16[3,3,384,192]{2,3,1,0:T(8,128)(2,1)S(1)}, bf16[3,3,384,192]{2,3,1,0:T(8,128)(2,1)}, u32[]{:S(2)}) %copy-start.1) | copy-done | bytes 1327128
  1.4 0.0 copy-start.2
  1.4 0.0 copy-start.4
  1.4 1.1 %shard_map.100 = (s32[4]{0:T(128)S(1)}, bf16[768,768]{1,0:T(8,128)(2,1)S(1)}, bf16[768,768]{1,0:T(8,128)(2,1)S(1)}) custom-call(s32[4]{0:T(128)S(1)} %pad_add_fusion.info, bf16[3,3,192,384]{3,2,1,0:T(8,128)(2,1)S(1)} %bitcast.21), custom_call_target="tpu_custom_call" | custom-call | flops 10000000000 | bytes 1048576 | tf_op jit(solution)/shard_map/pallas_call | solution.py:553
  2.6 0.1 copy-done.2
  2.7 0.0 copy-done.4
  2.7 0.0 copy-done.5
  2.7 0.0 copy-start.6
  2.7 1.5 %shard_map.102 = (bf16[6,160,384]{2,1,0:T(8,128)(2,1)S(1)}, bf16[608,384]{1,0:T(8,128)(2,1)S(1)}, bf16[608,384]{1,0:T(8,128)(2,1)S(1)}) custom-call(s32[4]{0:T(128)S(1)} %get-tuple-element.20.info, bf16[8,192,320]{2,1,0:T(8,128)(2,1)S(1)} %bitcast.22, bf16[4,16,160]{2,1,0:T(8,128)(2,1)S(1)} %bitcast.26, bf16[2,4,16,160]{3,2,1,0:T(8,128)(2,1)S(1)} %bitcast.24), custom_call_target="tpu_custom_call" | custom-call | flops 10000000000 | bytes 1048576 | tf_op jit(solution)/shard_map/pallas_call | solution.py:559
  4.2 0.5 %collective-permute-start = (bf16[608,384]{1,0:T(8,128)(2,1)S(1)}, bf16[608,384]{1,0:T(8,128)(2,1)S(1)}, u32[]{:S(2)}, u32[]{:S(2)}) collective-permute-start(bf16[608,384]{1,0:T(8,128)(2,1)S(1)} %get-tuple-element.24), channel_id=1, source_target_pairs={{0,1},{1,0},{2,3},{3,2},{4,5},{5,4},{6,7},{7,6},{8,9},{9,8},{10,11... | collective-permute-start | bytes 1400840 | tf_op jit(solution)/shard_map/ppermute | solution.py:564
  4.7 0.7 %collective-permute-start.1 = (bf16[608,384]{1,0:T(8,128)(2,1)S(1)}, bf16[608,384]{1,0:T(8,128)(2,1)S(1)}, u32[]{:S(2)}, u32[]{:S(2)}) collective-permute-start(bf16[608,384]{1,0:T(8,128)(2,1)S(1)} %get-tuple-element.25), channel_id=1, source_target_pairs={{0,0},{1,2},{2,1},{3,4},{4,3},{5,6},{6,5},{7,7},{8,8},{9,10},{10,9... | collective-permute-start | bytes 1400840 | tf_op jit(solution)/shard_map/ppermute | solution.py:565
  5.4 0.0 slice-done
  5.4 0.0 slice-done.1
  5.4 0.1 copy-done.3
  5.5 0.0 copy-done.6
  5.5 5.5 %shard_map.101 = (f32[8,160,384]{2,1,0:T(8,128)S(1)}, bf16[480,384]{1,0:T(8,128)(2,1)S(1)}, bf16[480,384]{1,0:T(8,128)(2,1)S(1)}, bf16[3456,384]{1,0:T(8,128)(2,...) custom-call(s32[4]{0:T(128)S(1)} %get-tuple-element.20.info, ...), custom_call_target="tpu_custom_call" | custom-call | flops 4000000000 | bytes 1048576 | tf_op jit(solution)/shard_map/pallas_call | solution.py:569
  11.0 4.0 %collective-permute-start.2 = (bf16[480,384]{1,0:T(8,128)(2,1)S(1)}, bf16[480,384]{1,0:T(8,128)(2,1)S(1)}, u32[]{:S(2)}, u32[]{:S(2)}) collective-permute-start(bf16[480,384]{1,0:T(8,128)(2,1)S(1)} %get-tuple-element.29), channel_id=1, source_target_pairs={{0,1},{1,0},{2,3},{3,2},{4,5},{5,4},{6,7},{7,6},{8,9},{9,8},{10,11... | collective-permute-start | bytes 1105928 | tf_op jit(solution)/shard_map/ppermute | solution.py:577
  15.0 0.7 %collective-permute-start.3 = (bf16[480,384]{1,0:T(8,128)(2,1)S(1)}, bf16[480,384]{1,0:T(8,128)(2,1)S(1)}, u32[]{:S(2)}, u32[]{:S(2)}) collective-permute-start(bf16[480,384]{1,0:T(8,128)(2,1)S(1)} %get-tuple-element.30), channel_id=1, source_target_pairs={{0,0},{1,2},{2,1},{3,4},{4,3},{5,6},{6,5},{7,7},{8,8},{9,10},{10,9... | collective-permute-start | bytes 1105928 | tf_op jit(solution)/shard_map/ppermute | solution.py:578
  15.7 0.0 copy-done.7
  15.8 0.0 copy-done
  15.8 0.0 copy-done.8
  15.8 0.1 maximum_multiply_fusion.half_out
  15.9 0.0 collective-permute-done.got_even.packed_even
  15.9 0.0 collective-permute-done.1.got_odd.packed_odd
  15.9 7.0 %shard_map.103 = (bf16[10,160,384]{2,1,0:T(8,128)(2,1)S(1)}, f32[8,160,384]{2,1,0:T(8,128)S(1)}) custom-call(s32[4]{0:T(128)S(1)} %get-tuple-element.20.info, bf16[4,16,160]{2,1,0:T(8,128)(2,1)S(1)} %bitcast.27, bf16[2,4,16,160]{3,2,1,0:T(8,128)(2,1)S(1)} %bitcast.25, bf16[608,384]{1,0:T(8,128)(2,1)S(1)} %collective-permute-done.got_even.packed_even, ...), custom_call_target="tpu_custom_call" | custom-call | flops 5000000000 | bytes 1048576 | tf_op jit(solution)/shard_map/pallas_call | solution.py:580
  22.9 0.0 collective-permute-done.2.got_even
  23.0 0.0 collective-permute-done.3.got_odd
  23.0 12.9 %shard_map.104 = bf16[8,16,128]{2,1,0:T(8,128)(2,1)S(1)} custom-call(s32[4]{0:T(128)S(1)} %get-tuple-element.20.info, bf16[10,160,384]{2,1,0:T(8,128)(2,1)S(1)} %get-tuple-element.26.hidden, f32[8,160,384]{2,1,0:T(8,128)S(1)} %get-tuple-element.27.conv, f32[8,160,384]{2,1,0:T(8,128)S(1)} %get-tuple-element.28.acc, ...), custom_call_target="tpu_custom_call" | custom-call | flops 8000000000 | bytes 1048576 | tf_op jit(solution)/shard_map/pallas_call | solution.py:594
  35.8 11.7 %all_to_all.5.got = bf16[8,16,128]{2,1,0:T(8,128)(2,1)S(1)} all-to-all(bf16[8,16,128]{2,1,0:T(8,128)(2,1)S(1)} %shard_map.104), channel_id=1, replica_groups=mesh['prompt'=4,'tile'=8] {'tile'}, dimensions={0} | all-to-all | bytes 65536 | tf_op jit(solution)/shard_map/all_to_all | solution.py:618
  47.6 1.0 %shard_map.105 = f32[64,160]{1,0:T(8,128)} custom-call(bf16[8,128,640]{2,1,0:T(8,128)(2,1)S(1)} %get-tuple-element.23.sel, bf16[8,16,128]{2,1,0:T(8,128)(2,1)S(1)} %all_to_all.5.got), custom_call_target="tpu_custom_call" | custom-call | flops 10000000 | bytes 1048576 | tf_op jit(solution)/shard_map/pallas_call | solution.py:619
  (12 shorter events, 0.0 us)
Async XLA Ops:
  0.1 1.3 %copy-start.1 = (bf16[3,3,384,192]{2,3,1,0:T(8,128)(2,1)S(1)}, bf16[3,3,384,192]{2,3,1,0:T(8,128)(2,1)}, u32[]{:S(2)}) copy-start(bf16[3,3,384,192]{2,3,1,0:T(8,128)(2,1)} %param.16) | copy-start | bytes 3981316
  1.4 1.3 %copy-start.2 = (bf16[8,320,192]{1,2,0:T(8,128)(2,1)S(1)}, bf16[8,320,192]{1,2,0:T(8,128)(2,1)}, u32[]{:S(2)}) copy-start(bf16[8,320,192]{1,2,0:T(8,128)(2,1)} %param.13) | copy-start | bytes 2949124
  1.4 1.3 %copy-start.4 = (bf16[2,4,160,16]{2,3,1,0:T(8,128)(2,1)S(1)}, bf16[2,4,160,16]{2,3,1,0:T(8,128)(2,1)}, u32[]{:S(2)}) copy-start(bf16[2,4,160,16]{2,3,1,0:T(8,128)(2,1)} %param.11) | copy-start | bytes 122884
  1.4 1.3 %copy-start.5 = (bf16[4,160,16]{1,2,0:T(8,128)(2,1)S(1)}, bf16[4,160,16]{1,2,0:T(8,128)(2,1)}, u32[]{:S(2)}) copy-start(bf16[4,160,16]{1,2,0:T(8,128)(2,1)} %param.10) | copy-start | bytes 61444
  1.4 4.0 %slice-start = ((s8[7962624]{0:T(1024)(128)(4,1)}), s8[4194304]{0:T(1024)(128)(4,1)S(1)}, s32[]{:S(2)}) async-start(s8[7962624]{0:T(1024)(128)(4,1)} %bitcast.17), calls=%async_computation.1 | async-start | bytes 8388608
  2.7 2.7 %slice-start.1 = ((s8[7962624]{0:T(1024)(128)(4,1)}), s8[3768320]{0:T(1024)(128)(4,1)S(1)}, s32[]{:S(2)}) async-start(s8[7962624]{0:T(1024)(128)(4,1)} %bitcast.17), calls=%async_computation.2 | async-start | bytes 7536640
  2.7 2.8 %copy-start.3 = (bf16[2,4,160,384]{3,2,1,0:T(8,128)(2,1)S(1)}, bf16[2,4,160,384]{3,2,1,0:T(8,128)(2,1)}, u32[]{:S(2)}) copy-start(bf16[2,4,160,384]{3,2,1,0:T(8,128)(2,1)} %features.1) | copy-start | bytes 2949124
  2.7 2.8 %copy-start.6 = (s32[8]{0:T(128)S(1)}, s32[8]{0:T(128)}, u32[]{:S(2)}) copy-start(s32[8]{0:T(128)} %order.1) | copy-start | bytes 100
  4.2 11.7 %collective-permute-start = (bf16[608,384]{1,0:T(8,128)(2,1)S(1)}, bf16[608,384]{1,0:T(8,128)(2,1)S(1)}, u32[]{:S(2)}, u32[]{:S(2)}) collective-permute-start(bf16[608,384]{1,0:T(8,128)(2,1)S(1)} %get-tuple-element.24), channel_id=1, source_target_pairs={{0,1},{1,0},{2,3},{3,2},{4,5},{5,4},{6,7},{7,6},{8,9},{9,8},{10,11... | collective-permute-start | bytes 1400840 | tf_op jit(solution)/shard_map/ppermute | solution.py:564
  4.7 11.2 %collective-permute-start.1 = (bf16[608,384]{1,0:T(8,128)(2,1)S(1)}, bf16[608,384]{1,0:T(8,128)(2,1)S(1)}, u32[]{:S(2)}, u32[]{:S(2)}) collective-permute-start(bf16[608,384]{1,0:T(8,128)(2,1)S(1)} %get-tuple-element.25), channel_id=1, source_target_pairs={{0,0},{1,2},{2,1},{3,4},{4,3},{5,6},{6,5},{7,7},{8,8},{9,10},{10,9... | collective-permute-start | bytes 1400840 | tf_op jit(solution)/shard_map/ppermute | solution.py:565
  5.5 10.2 %copy-start.7 = (f32[384]{0:T(512)S(1)}, f32[384]{0:T(512)}, u32[]{:S(2)}) copy-start(f32[384]{0:T(512)} %param.17) | copy-start | bytes 4612
  5.5 10.2 %copy-start = (bf16[3,3,3,16,384]{4,3,2,1,0:T(8,128)(2,1)S(1)}, bf16[3,3,3,16,384]{4,3,2,1,0:T(8,128)(2,1)}, u32[]{:S(2)}) copy-start(bf16[3,3,3,16,384]{4,3,2,1,0:T(8,128)(2,1)} %param.14) | copy-start | bytes 995332
  5.5 10.3 %copy-start.8 = (f32[192]{0:T(256)S(1)}, f32[192]{0:T(256)}, u32[]{:S(2)}) copy-start(f32[192]{0:T(256)} %param.18) | copy-start | bytes 2308
  11.0 11.9 %collective-permute-start.2 = (bf16[480,384]{1,0:T(8,128)(2,1)S(1)}, bf16[480,384]{1,0:T(8,128)(2,1)S(1)}, u32[]{:S(2)}, u32[]{:S(2)}) collective-permute-start(bf16[480,384]{1,0:T(8,128)(2,1)S(1)} %get-tuple-element.29), channel_id=1, source_target_pairs={{0,1},{1,0},{2,3},{3,2},{4,5},{5,4},{6,7},{7,6},{8,9},{9,8},{10,11... | collective-permute-start | bytes 1105928 | tf_op jit(solution)/shard_map/ppermute | solution.py:577
  15.0 7.9 %collective-permute-start.3 = (bf16[480,384]{1,0:T(8,128)(2,1)S(1)}, bf16[480,384]{1,0:T(8,128)(2,1)S(1)}, u32[]{:S(2)}, u32[]{:S(2)}) collective-permute-start(bf16[480,384]{1,0:T(8,128)(2,1)S(1)} %get-tuple-element.30), channel_id=1, source_target_pairs={{0,0},{1,2},{2,1},{3,4},{4,3},{5,6},{6,5},{7,7},{8,8},{9,10},{10,9... | collective-permute-start | bytes 1105928 | tf_op jit(solution)/shard_map/ppermute | solution.py:578

commit v12 on v9

--- a/solution.py
+++ b/solution.py
@@ -96,7 +96,9 @@
 
 
 def pack_body(rows, cols, o, chan):
-    def body(info, reward, latent, cached, own, send_even, send_odd):
+    def body(info, reward, latents, info_out, own, send_even, send_odd):
+        for k in range(4):
+            info_out[k] = info[k]
         one = picker(cols, o)
         for k in range(6):
             one(reward, k if k < 3 else 2 * rows - 6 + k, own, k)
@@ -107,8 +109,7 @@
             for k in range(3):
                 send[k * cols : (k + 1) * cols] = own[begin + k]
             for t in range(3):
-                src = cached[t] if t < 2 else latent[...]
-                lat = src.reshape(per, cols)
+                lat = latents[t].reshape(per, cols)
                 send[base : base + per, t * 128 : t * 128 + 128] = lat[:, :128]
                 send[base + per : base + 2 * per, t * 128 : t * 128 + cols - 128] = lat[:, 128:]
 
@@ -146,28 +147,27 @@
     return steps(one, *[(b, side, lanes) for b in range(2) for side in range(2) for lanes in range(0, 384, 128)])
 
 
-def taps_body(info, up, info_out, back_odd, back_even):
-    for k in range(4):
-        info_out[k] = info[k]
-
+def summing(up, back_odd, back_even):
     parts = ((2,), (1, 2), (0, 1), (0,))
     targets = ((back_odd, 1), (back_even, 0), (back_odd, 0), (back_even, 1))
 
-    for tile in range(3):
-        for lanes in range(0, 384, 128):
-            w = [[up[i, j, tile * 64 : tile * 64 + 64, lanes : lanes + 128].astype(F32) for j in range(3)] for i in range(3)]
-            for q in range(4):
-                c = [w[parts[q][0]][j] + w[parts[q][1]][j] if len(parts[q]) > 1 else w[parts[q][0]][j] for j in range(3)]
-                for p, tap in enumerate((c[2], c[1] + c[2], c[0] + c[1], c[0])):
-                    target, row, side = home(targets, q, p, tile)
-                    target[row : row + 64, side + lanes : side + lanes + 128] = tap.astype(BF16)
+    def one(tile, lanes):
+        w = [[up[i, j, tile * 64 : tile * 64 + 64, lanes : lanes + 128].astype(F32) for j in range(3)] for i in range(3)]
+        for q in range(4):
+            c = [w[parts[q][0]][j] + w[parts[q][1]][j] if len(parts[q]) > 1 else w[parts[q][0]][j] for j in range(3)]
+            for p, tap in enumerate((c[2], c[1] + c[2], c[0] + c[1], c[0])):
+                target, row, side = home(targets, q, p, tile)
+                target[row : row + 64, side + lanes : side + lanes + 128] = tap.astype(BF16)
+
+    return steps(one, *[(tile, lanes) for tile in range(3) for lanes in range(0, 384, 128)])
 
 
 def cached_body(rows, cols, count, width, tokens, o):
     size = rows * cols
 
     def body(
-        info, order, features, mid, back_odd, back_even, reward, acc, send_even, send_odd, mid_t, sel, fwd, own, wide, parts
+        info, order, features, mid, up, reward, acc, send_even, send_odd, mid_t, sel, fwd, own, back_odd, back_even, wide,
+        parts,
     ):
         for t in range(2):
             for r in range(rows):
@@ -192,7 +192,7 @@
         products = steps(product, (0, most), (1, most)) + steps(double, ()) + steps(product, (2, most), (2, rest))
         one = picker(cols, o)
         others = steps(turn, *[(i, j) for i in range(3) for j in range(3)])
-        others += turning(back_odd, back_even, fwd)
+        others += summing(up, back_odd, back_even) + turning(back_odd, back_even, fwd)
         others += steps(placing(info, order, sel, count, width, tokens), *[(t,) for t in range(count)])
         others += steps(one, (reward, rows - 1, own, 0), (reward, rows, own, 1))
         weave(others, products)
@@ -214,7 +214,7 @@
     per = chan * rows
     base = 3 * cols
 
-    def body(info, latent, cached, got_even, got_odd, w_in, mid, half_gain, hidden, conv, lat, tall, wide, w_order, plain):
+    def body(info, latents, got_even, got_odd, w_in, mid, half_gain, hidden, conv, lat, tall, wide, w_order, plain):
         even = info[0] == 0
         lat[...] = jnp.zeros_like(lat)
 
@@ -241,7 +241,7 @@
         for t in range(3):
             for r in range(rows):
                 at = pl.ds((rows + r) * 3 * chan + t * chan, chan)
-                lat[at, 0:cols] = (cached[t, r] if t < 2 else latent[r]).astype(F32)
+                lat[at, 0:cols] = latents[t, r].astype(F32)
 
         for r in range(3 * rows):
             for t in range(3):
@@ -310,29 +310,22 @@
 
     def body(
         info, hidden, conv, acc, got_even, got_odd, packed_even, packed_odd, own, own_mid, fwd, back_odd, back_even, mid_t, w_in, half_gain,
-        half_out, payload, reward, edge, p0, p1, g_odd, g_even, wide, t_odd, t_even, back, act_grad, hid, tmp_odd, tmp_even, lines,
+        half_out, payload, reward, p0, p1, g_odd, g_even, wide, t_odd, t_even, back, act_grad, hid, tmp_odd, tmp_even, lines,
     ):
-        even = info[0] == 0
         top, bottom = flag(info, 1), flag(info, 2)
-
-        def take(got, packed, before):
-            ok = top if before else bottom
-            place = 0 if before else rows + 1
-            for k in range(3):
-                at = slice(k * cols, (k + 1) * cols)
-                edge[place + k] = got[at].astype(F32) * ok
-                reward[k if before else 2 * rows + 3 + k] = (packed[at].astype(F32) * ok).astype(BF16)
-
-        @pl.when(even)
-        def _():
-            take(got_odd, packed_odd, True)
-            take(got_even, packed_even, False)
-
-        @pl.when(jnp.logical_not(even))
-        def _():
-            take(got_even, packed_even, True)
-            take(got_odd, packed_odd, False)
-
+        odd_tile = flag(info, 0)
+        above = (top * odd_tile, top * (1.0 - odd_tile))
+        below = (bottom * (1.0 - odd_tile), bottom * odd_tile)
+
+        def halo(of_even, of_odd, k, lanes, before):
+            scale = above if before else below
+            at = slice(k * cols, (k + 1) * cols)
+            return of_even[at, lanes].astype(F32) * scale[0] + of_odd[at, lanes].astype(F32) * scale[1]
+
+        for k in range(3):
+            for lanes in (slice(0, 128), slice(128, 256), slice(256, 384)):
+                reward[k, :, lanes] = halo(packed_even, packed_odd, k, lanes, True).astype(BF16)
+                reward[2 * rows + 3 + k, :, lanes] = halo(packed_even, packed_odd, k, lanes, False).astype(BF16)
         reward[3:6] = own[0:3]
         reward[6 : 2 * rows] = own_mid[...]
         reward[2 * rows : 2 * rows + 3] = own[3:6]
@@ -346,8 +339,10 @@
                 x = hidden[k + 1, :, at].astype(F32) + conv[k, :, at]
                 if 1 <= k <= rows + 2:
                     x = x + acc[k, :, at]
-                if k < 3 or k > rows:
-                    x = x + edge[k, :, at]
+                if k < 3:
+                    x = x + halo(got_even, got_odd, k, at, True)
+                if k > rows:
+                    x = x + halo(got_even, got_odd, k - rows - 1, at, False)
                 beside(wide.at[k], 0, lanes, inside(x, k, 2, rows + 2), False)
 
         def up_rows(first, last, b, n):
@@ -403,10 +398,10 @@
                 for n, value in enumerate(out):
                     lanes = slice(n * 128, n * 128 + 128)
                     target[k, at, lanes] = value.astype(BF16)
-                    tmp[k % 2, at, lanes] = value
-            target[k, :, 384:512] = from_right(tmp[k % 2, :, 0:128]).astype(BF16)
-            target[k, :, 512:640] = from_left(tmp[k % 2, :, 128:256]).astype(BF16)
-            x = tmp[k % 2, :, 256:384]
+                    tmp[0, at, lanes] = value
+            target[k, :, 384:512] = from_right(tmp[0, :, 0:128]).astype(BF16)
+            target[k, :, 512:640] = from_left(tmp[0, :, 128:256]).astype(BF16)
+            x = tmp[0, :, 256:384]
             sides = (from_right(x), from_left(x)) if odd else (from_left(x), from_right(x))
             target[k, :, 640:768] = jnp.where(tall_low, *sides).astype(BF16)
 
@@ -433,9 +428,12 @@
             up_rows(1, rows + 4, b, 0)
             up_rows(0, rows + 3, b, 1)
             up_rows(0, rows + 4, b, 2)
-        for k in range(fine):
+
+        @pl.loop(0, fine)
+        def _(k):
             pull_row(k, True)
             pull_row(k, False)
+
         for odd in (True, False):
             down_rows(1 if odd else 0, fine if odd else fine - 1, odd, 0)
             down_rows(0, fine, odd, 1)
@@ -502,16 +500,17 @@
         valid = jnp.logical_and(step >= 0, step < count)
         beside = jnp.where(valid, piece * order[jnp.clip(step, 0, count - 1)], -9999)
         begin = jnp.where(group == 2, beside, piece * order[t])
-        sel[t] = (fixed + begin == 0).astype(F32).astype(BF16)
+        sel[t // 2, t % 2 * 128 : t % 2 * 128 + 128] = (fixed + begin == 0).astype(F32).astype(BF16)
 
     return one
 
 
 def place_body(count, chan, tokens):
     def body(sel, got, out):
-        total = mm(got[0], sel[0])
-        for t in range(1, count):
-            total += mm(got[t], sel[t])
+        total = None
+        for t in range(count // 2):
+            x = mm(jnp.concatenate([got[2 * t], got[2 * t + 1]], axis=1), sel[t])
+            total = x if total is None else total + x
         for k in range(4):
             out[k * chan : (k + 1) * chan] = total[:, k * tokens : (k + 1) * tokens]
 
@@ -537,8 +536,7 @@
     info = jnp.stack(
         [tile % 2, (tile > 0).astype(jnp.int32), (tile < count - 1).astype(jnp.int32), (tile >= count // 2).astype(jnp.int32)]
     ).astype(jnp.int32)
-    lat = jnp.transpose(latent, (0, 2, 1))
-    lat_cached = jnp.transpose(cached_latent, (0, 1, 3, 2))
+    latents = jnp.concatenate([jnp.transpose(cached_latent, (0, 1, 3, 2)), jnp.transpose(latent, (0, 2, 1))[None]], axis=0)
     reward_t = jnp.transpose(reward_grad, (0, 2, 1))
     up_t = jnp.transpose(conv_up_weight, (0, 1, 3, 2))
     mid = conv_mid_weight.reshape(3, 3, 3 * mid_chan, mid_chan)
@@ -549,37 +547,32 @@
     size = rows * cols
     edge_rows = 3 * cols + 2 * chan * rows
 
-    info, back_odd, back_even = call(
-        taps_body,
-        [((4,), jnp.int32), ((768, 768), BF16), ((768, 768), BF16)],
-        1, 1, [], 1e10, 8, 1,
-    )(info, up_t)
-
-    own, send_even, send_odd = call(
+    info, own, send_even, send_odd = call(
         pack_body(rows, cols, o, chan),
-        [((6, cols, 384), BF16), ((edge_rows, 384), BF16), ((edge_rows, 384), BF16)],
-        1, 3, [], 1e10, 8,
-    )(info, reward_t, lat, lat_cached)
+        [((4,), jnp.int32), ((6, cols, 384), BF16), ((edge_rows, 384), BF16), ((edge_rows, 384), BF16)],
+        1, 2, [], 2e10, 8, 1,
+    )(info, reward_t, latents)
     packed_even = lax.ppermute(send_even, "tile", within)
     packed_odd = lax.ppermute(send_odd, "tile", across)
 
     width = 2 * cols // count
     tokens = size // 4
-    acc, part_even, part_odd, mid_t, sel, fwd, own_mid = call(
+    acc, part_even, part_odd, mid_t, sel, fwd, own_mid, back_odd, back_even = call(
         cached_body(rows, cols, count, width, tokens, o),
         [
             ((rows + 4, cols, 384), F32), ((3 * cols, 384), BF16), ((3 * cols, 384), BF16), ((3456, 384), BF16),
-            ((count, 128, 4 * tokens), BF16), ((2, 768, 768), BF16), ((2, cols, 384), BF16),
+            ((count // 2, 256, 4 * tokens), BF16), ((2, 768, 768), BF16), ((2, cols, 384), BF16),
+            ((768, 768), BF16), ((768, 768), BF16),
         ],
-        2, 5, [pltpu.VMEM((size, 2304), BF16), pltpu.VMEM((3, size, 384), F32)], 4e9, 14,
-    )(info, shard_order, cached_features, mid, back_odd, back_even, reward_t)
+        2, 4, [pltpu.VMEM((size, 2304), BF16), pltpu.VMEM((3, size, 384), F32)], 4e9, 14,
+    )(info, shard_order, cached_features, mid, up_t, reward_t)
     got_even = lax.ppermute(part_even, "tile", within)
     got_odd = lax.ppermute(part_odd, "tile", across)
 
     hidden, conv = call(
         current_body(rows, cols, chan),
         [((rows + 6, cols, 384), BF16), ((rows + 4, cols, 384), F32)],
-        1, 7,
+        1, 6,
         [
             pltpu.VMEM((9 * rows * chan, 256), F32),
             pltpu.VMEM((3 * rows, 9 * chan, 256), BF16),
@@ -588,7 +581,7 @@
             pltpu.VMEM((2, cols, 384), F32),
         ],
         5e9, 14,
-    )(info, lat, lat_cached, packed_even, packed_odd, w_in, mid, gain)
+    )(info, latents, packed_even, packed_odd, w_in, mid, gain)
 
     (payload,) = call(
         back_body(rows, cols, chan, count, o),
@@ -596,7 +589,6 @@
         1, 16,
         [
             pltpu.VMEM((2 * rows + 6, cols, 384), BF16),
-            pltpu.VMEM((rows + 4, cols, 384), F32),
             pltpu.VMEM((rows + 4, cols, 768), F32),
             pltpu.VMEM((rows + 4, cols, 768), F32),
             pltpu.VMEM((rows + 3, cols, 768), BF16),

time: 48.3 us -> 61 us (1.26)
  blocking collectives: 11.7 us -> 19.1 us
  local copies, waits for them, and re-layouts: 1.58 us -> 4 us
  Pallas kernels: 28.5 us -> 30 us
  other arithmetic: 0.16 us -> 1.04 us
    all_to_all x1, blocking collectives: 11.7 us -> 19.1 us  [shards(): lax.all_to_all(payload, 'tile', split_axis=0, concat_axis=0, tiled=True)]
    ppermute x1, starting transfers between devices: 4.05 us -> 0.52 us  [shards(): got_even = lax.ppermute(part_even, 'tile', within)]
    ppermute x1, starting transfers between devices: 0.55 us -> 4 us  [shards(): packed_even = lax.ppermute(send_even, 'tile', within)]
    unnamed x22 -> x18, local copies, waits for them, and re-layouts: 1.56 us -> 3.98 us
    pallas_call x1, Pallas kernels: 12.6 us -> 14.5 us  [shards(): call(back_body(rows, cols, chan, count, o), [((count, chan, 128), BF16)],...]
    pallas_call x2 -> x1, Pallas kernels: 2.6 us -> 1.47 us  [shards(): call(pack_body(rows, cols, o, chan), [((4,), jnp.int32), ((6, cols, 384),...]
    concatenate x0 -> x1, other arithmetic: none -> 0.88 us  [shards(): jnp.concatenate([jnp.transpose(cached_latent, (0, 1, 3, 2)), jnp.transpos...]
  transfers between devices with their start and end apart: 4 -> 4, of which waited for: 0 -> 1; matrix products, arithmetic and copies ran while one was open for 0% -> 0% of each run, Pallas kernels for 26% -> 12%
where the time goes in v12:
time: 61 us; the launch traced here: 60.8 us
  Pallas kernels  30 us (49%)
  blocking collectives  19.1 us (31%)
  starting transfers between devices  5.87 us (10%)
  local copies, waits for them, and re-layouts  4 us (7%)
  other arithmetic  1.04 us (2%)
  waiting for transfers between devices  0.61 us (1%)
    all_to_all x1, blocking collectives, shards(): lax.all_to_all(payload, 'tile', split_axis=0, concat_axis=0, tiled=True)  19.1 us
    pallas_call x1, Pallas kernels, shards(): call(back_body(rows, cols, chan, count, o), [((count, chan, 128), BF16)],...  14.5 us
    pallas_call x1, Pallas kernels, shards(): call(current_body(rows, cols, chan), [((rows + 6, cols, 384), BF16), ((ro...  7.09 us
    pallas_call x1, Pallas kernels, shards(): call(cached_body(rows, cols, count, width, tokens, o), [((rows + 4, cols,...  5.99 us
    ppermute x1, starting transfers between devices, shards(): packed_even = lax.ppermute(send_even, 'tile', within)  4 us
    unnamed x18, local copies, waits for them, and re-layouts  3.98 us
    pallas_call x1, Pallas kernels, shards(): call(pack_body(rows, cols, o, chan), [((4,), jnp.int32), ((6, cols, 384),...  1.47 us
  transfers between devices with their start and end apart: 4, of which 1 were waited for; matrix products, arithmetic and copies ran while one was open for 0% of the time, Pallas kernels for 12%

profile of v12, /device:TPU:0, one launch (start us, length us, event | category | flops | bytes accessed | tf_op | source)
XLA Modules:
  0.0 60.8 jit_solution(14647678014583468658)
XLA Ops:
  0.0 0.9 %pad_maximum_fusion.latents = bf16[3,4,16,160]{3,2,1,0:T(8,128)(2,1)S(1)} fusion(bf16[1,4,16,160]{3,2,1,0:T(8,128)(2,1)} %bitcast.25, bf16[2,4,16,160]{3,2,1,0:T(8,128)(2,1)} %bitcast.24), kind=kLoop, calls=%fused_computation | loop fusion | flops 30720 | bytes 122880 | tf_op jit(solution)/shard_map/concatenate | solution.py:539
  0.9 0.1 pad_add_fusion.info
  1.0 0.0 copy-start.3
  1.0 1.3 %copy-done.3 = bf16[8,320,192]{1,2,0:T(8,128)(2,1)S(1)} copy-done((bf16[8,320,192]{1,2,0:T(8,128)(2,1)S(1)}, bf16[8,320,192]{1,2,0:T(8,128)(2,1)}, u32[]{:S(2)}) %copy-start.3) | copy-done | bytes 983064
  2.2 0.0 copy-start.1
  2.2 0.0 copy-start.2
  2.2 0.0 copy-start.4
  2.2 0.0 copy-start.5
  2.2 0.0 copy-start.6
  2.3 1.5 %shard_map.100 = (s32[4]{0:T(128)S(1)}, bf16[6,160,384]{2,1,0:T(8,128)(2,1)S(1)}, bf16[608,384]{1,0:T(8,128)(2,1)S(1)}, bf16[608,384]{1,0:T(8,128)(2,1)S(1)}) custom-call(s32[4]{0:T(128)S(1)} %pad_add_fusion.info, bf16[8,192,320]{2,1,0:T(8,128)(2,1)S(1)} %bitcast.22, bf16[3,4,16,160]{3,2,1,0:T(8,128)(2,1)S(1)} %pad_maximum_fusion.latents), custom_call_target="tpu_custom_call" | custom-call | flops 20000000000 | bytes 1048576 | tf_op jit(solution)/shard_map/pallas_call | solution.py:550
  3.7 1.8 %copy-done.1 = bf16[3,3,3,384,384]{4,3,2,1,0:T(8,128)(2,1)S(1)} copy-done((bf16[3,3,3,384,384]{4,3,2,1,0:T(8,128)(2,1)S(1)}, bf16[3,3,3,384,384]{4,3,2,1,0:T(8,128)(2,1)}, u32[]{:S(2)}) %copy-start.1) | copy-done | bytes 7962648
  5.5 0.3 copy-done.2
  5.8 0.3 copy-done.4
  6.2 0.3 copy-done.5
  6.4 0.0 copy-done.6
  6.4 6.0 %shard_map.101 = (f32[8,160,384]{2,1,0:T(8,128)S(1)}, bf16[480,384]{1,0:T(8,128)(2,1)S(1)}, bf16[480,384]{1,0:T(8,128)(2,1)S(1)}, bf16[3456,384]{1,0:T(8,128)(2,...) custom-call(s32[4]{0:T(128)S(1)} %get-tuple-element.20.info, ...), custom_call_target="tpu_custom_call" | custom-call | flops 4000000000 | bytes 1048576 | tf_op jit(solution)/shard_map/pallas_call | solution.py:560
  12.4 0.5 collective-permute-start.2
  12.9 0.7 %collective-permute-start.3 = (bf16[480,384]{1,0:T(8,128)(2,1)S(1)}, bf16[480,384]{1,0:T(8,128)(2,1)S(1)}, u32[]{:S(2)}, u32[]{:S(2)}) collective-permute-start(bf16[480,384]{1,0:T(8,128)(2,1)S(1)} %get-tuple-element.28), channel_id=1, source_target_pairs={{0,0},{1,2},{2,1},{3,4},{4,3},{5,6},{6,5},{7,7},{8,8},{9,10},{10,9... | collective-permute-start | bytes 1105928 | tf_op jit(solution)/shard_map/ppermute | solution.py:570
  13.6 4.0 %collective-permute-start = (bf16[608,384]{1,0:T(8,128)(2,1)S(1)}, bf16[608,384]{1,0:T(8,128)(2,1)S(1)}, u32[]{:S(2)}, u32[]{:S(2)}) collective-permute-start(bf16[608,384]{1,0:T(8,128)(2,1)S(1)} %get-tuple-element.22), channel_id=1, source_target_pairs={{0,1},{1,0},{2,3},{3,2},{4,5},{5,4},{6,7},{7,6},{8,9},{9,8},{10,11... | collective-permute-start | bytes 1400840 | tf_op jit(solution)/shard_map/ppermute | solution.py:555
  17.6 0.7 %collective-permute-start.1 = (bf16[608,384]{1,0:T(8,128)(2,1)S(1)}, bf16[608,384]{1,0:T(8,128)(2,1)S(1)}, u32[]{:S(2)}, u32[]{:S(2)}) collective-permute-start(bf16[608,384]{1,0:T(8,128)(2,1)S(1)} %get-tuple-element.23), channel_id=1, source_target_pairs={{0,0},{1,2},{2,1},{3,4},{4,3},{5,6},{6,5},{7,7},{8,8},{9,10},{10,9... | collective-permute-start | bytes 1400840 | tf_op jit(solution)/shard_map/ppermute | solution.py:556
  18.3 0.0 copy-done.7
  18.3 0.0 copy-done
  18.4 0.0 copy-done.8
  18.4 0.1 maximum_multiply_fusion.half_out
  18.5 0.6 collective-permute-done.got_even.packed_even
  19.1 0.0 collective-permute-done.1.got_odd.packed_odd
  19.1 7.1 %shard_map.102 = (bf16[10,160,384]{2,1,0:T(8,128)(2,1)S(1)}, f32[8,160,384]{2,1,0:T(8,128)S(1)}) custom-call(s32[4]{0:T(128)S(1)} %get-tuple-element.20.info, bf16[3,4,16,160]{3,2,1,0:T(8,128)(2,1)S(1)} %pad_maximum_fusion.latents, bf16[608,384]{1,0:T(8,128)(2,1)S(1)} %collective-permute-done.got_even.packed_even, ...), custom_call_target="tpu_custom_call" | custom-call | flops 5000000000 | bytes 1048576 | tf_op jit(solution)/shard_map/pallas_call | solution.py:572
  26.2 0.0 collective-permute-done.2.got_even
  26.2 0.0 collective-permute-done.3.got_odd
  26.2 14.5 %shard_map.103 = bf16[8,16,128]{2,1,0:T(8,128)(2,1)S(1)} custom-call(s32[4]{0:T(128)S(1)} %get-tuple-element.20.info, bf16[10,160,384]{2,1,0:T(8,128)(2,1)S(1)} %get-tuple-element.24.hidden, f32[8,160,384]{2,1,0:T(8,128)S(1)} %get-tuple-element.25.conv, f32[8,160,384]{2,1,0:T(8,128)S(1)} %get-tuple-element.26.acc, ...), custom_call_target="tpu_custom_call" | custom-call | flops 8000000000 | bytes 1048576 | tf_op jit(solution)/shard_map/pallas_call | solution.py:586
  40.7 19.1 %all_to_all.5.got = bf16[8,16,128]{2,1,0:T(8,128)(2,1)S(1)} all-to-all(bf16[8,16,128]{2,1,0:T(8,128)(2,1)S(1)} %shard_map.103), channel_id=1, replica_groups=mesh['prompt'=4,'tile'=8] {'tile'}, dimensions={0} | all-to-all | bytes 65536 | tf_op jit(solution)/shard_map/all_to_all | solution.py:611
  59.8 1.0 %shard_map.104 = f32[64,160]{1,0:T(8,128)} custom-call(bf16[4,256,640]{2,1,0:T(8,128)(2,1)S(1)} %get-tuple-element.21.sel, bf16[8,16,128]{2,1,0:T(8,128)(2,1)S(1)} %all_to_all.5.got), custom_call_target="tpu_custom_call" | custom-call | flops 10000000 | bytes 1048576 | tf_op jit(solution)/shard_map/pallas_call | solution.py:612
  (7 shorter events, 0.0 us)
Async XLA Ops:
  1.0 1.3 %copy-start.3 = (bf16[8,320,192]{1,2,0:T(8,128)(2,1)S(1)}, bf16[8,320,192]{1,2,0:T(8,128)(2,1)}, u32[]{:S(2)}) copy-start(bf16[8,320,192]{1,2,0:T(8,128)(2,1)} %param.13) | copy-start | bytes 2949124
  2.2 3.3 %copy-start.1 = (bf16[3,3,3,384,384]{4,3,2,1,0:T(8,128)(2,1)S(1)}, bf16[3,3,3,384,384]{4,3,2,1,0:T(8,128)(2,1)}, u32[]{:S(2)}) copy-start(bf16[3,3,3,384,384]{4,3,2,1,0:T(8,128)(2,1)} %param.15) | copy-start | bytes 23887876
  2.2 3.6 %copy-start.2 = (bf16[3,3,384,192]{2,3,1,0:T(8,128)(2,1)S(1)}, bf16[3,3,384,192]{2,3,1,0:T(8,128)(2,1)}, u32[]{:S(2)}) copy-start(bf16[3,3,384,192]{2,3,1,0:T(8,128)(2,1)} %param.16) | copy-start | bytes 3981316
  2.2 3.9 %copy-start.4 = (bf16[8,320,192]{1,2,0:T(8,128)(2,1)S(1)}, bf16[8,320,192]{1,2,0:T(8,128)(2,1)}, u32[]{:S(2)}) copy-start(bf16[8,320,192]{1,2,0:T(8,128)(2,1)} %param.13) | copy-start | bytes 2949124
  2.2 4.2 %copy-start.5 = (bf16[2,4,160,384]{3,2,1,0:T(8,128)(2,1)S(1)}, bf16[2,4,160,384]{3,2,1,0:T(8,128)(2,1)}, u32[]{:S(2)}) copy-start(bf16[2,4,160,384]{3,2,1,0:T(8,128)(2,1)} %features.1) | copy-start | bytes 2949124
  2.2 4.2 %copy-start.6 = (s32[8]{0:T(128)S(1)}, s32[8]{0:T(128)}, u32[]{:S(2)}) copy-start(s32[8]{0:T(128)} %order.1) | copy-start | bytes 100
  6.4 11.9 %copy-start.7 = (f32[384]{0:T(512)S(1)}, f32[384]{0:T(512)}, u32[]{:S(2)}) copy-start(f32[384]{0:T(512)} %param.17) | copy-start | bytes 4612
  6.4 11.9 %copy-start = (bf16[3,3,3,16,384]{4,3,2,1,0:T(8,128)(2,1)S(1)}, bf16[3,3,3,16,384]{4,3,2,1,0:T(8,128)(2,1)}, u32[]{:S(2)}) copy-start(bf16[3,3,3,16,384]{4,3,2,1,0:T(8,128)(2,1)} %param.14) | copy-start | bytes 995332
  6.4 12.0 %copy-start.8 = (f32[192]{0:T(256)S(1)}, f32[192]{0:T(256)}, u32[]{:S(2)}) copy-start(f32[192]{0:T(256)} %param.18) | copy-start | bytes 2308
  12.4 13.8 %collective-permute-start.2 = (bf16[480,384]{1,0:T(8,128)(2,1)S(1)}, bf16[480,384]{1,0:T(8,128)(2,1)S(1)}, u32[]{:S(2)}, u32[]{:S(2)}) collective-permute-start(bf16[480,384]{1,0:T(8,128)(2,1)S(1)} %get-tuple-element.27), channel_id=1, source_target_pairs={{0,1},{1,0},{2,3},{3,2},{4,5},{5,4},{6,7},{7,6},{8,9},{9,8},{10,11... | collective-permute-start | bytes 1105928 | tf_op jit(solution)/shard_map/ppermute | solution.py:569
  12.9 13.3 %collective-permute-start.3 = (bf16[480,384]{1,0:T(8,128)(2,1)S(1)}, bf16[480,384]{1,0:T(8,128)(2,1)S(1)}, u32[]{:S(2)}, u32[]{:S(2)}) collective-permute-start(bf16[480,384]{1,0:T(8,128)(2,1)S(1)} %get-tuple-element.28), channel_id=1, source_target_pairs={{0,0},{1,2},{2,1},{3,4},{4,3},{5,6},{6,5},{7,7},{8,8},{9,10},{10,9... | collective-permute-start | bytes 1105928 | tf_op jit(solution)/shard_map/ppermute | solution.py:570
  13.6 5.5 %collective-permute-start = (bf16[608,384]{1,0:T(8,128)(2,1)S(1)}, bf16[608,384]{1,0:T(8,128)(2,1)S(1)}, u32[]{:S(2)}, u32[]{:S(2)}) collective-permute-start(bf16[608,384]{1,0:T(8,128)(2,1)S(1)} %get-tuple-element.22), channel_id=1, source_target_pairs={{0,1},{1,0},{2,3},{3,2},{4,5},{5,4},{6,7},{7,6},{8,9},{9,8},{10,11... | collective-permute-start | bytes 1400840 | tf_op jit(solution)/shard_map/ppermute | solution.py:555
  17.6 1.5 %collective-permute-start.1 = (bf16[608,384]{1,0:T(8,128)(2,1)S(1)}, bf16[608,384]{1,0:T(8,128)(2,1)S(1)}, u32[]{:S(2)}, u32[]{:S(2)}) collective-permute-start(bf16[608,384]{1,0:T(8,128)(2,1)S(1)} %get-tuple-element.23), channel_id=1, source_target_pairs={{0,0},{1,2},{2,1},{3,4},{4,3},{5,6},{6,5},{7,7},{8,8},{9,10},{10,9... | collective-permute-start | bytes 1400840 | tf_op jit(solution)/shard_map/ppermute | solution.py:556

commit v13 on v10

--- a/solution.py
+++ b/solution.py
@@ -266,10 +266,12 @@
                 at = (i * 3 + t) * 3 * chan
                 w_order[at : at + 3 * chan] = w_in[t, i]
 
-        def hidden_row(k):
+        def hidden_product(k):
             lhs = tall[k : k + 3].reshape(27 * chan, 256)[:, 0:cols]
             h = lax.dot_general(lhs, w_order[...], (((0,), (0,)), ((), ())), preferred_element_type=F32)
             plain[k][...] = h
+
+        def hidden_norm(k):
             for c in range(0, cols, CHUNK):
                 at = slice(c, c + CHUNK)
                 v = plain[k][at].astype(BF16)
@@ -291,9 +293,13 @@
             total = mm(jnp.concatenate(lhs, axis=1), mid[2, :, :, 0:256].reshape(3456, 256))
             conv[p : p + number, :, 0:256] = total.reshape(number, cols, 256)
 
-        for k in range(rows + 1):
-            hidden_row(k)
-        weave(steps(hidden_row, *[(k,) for k in range(rows + 1, rows + 6)]), steps(conv_rows, (0, rows - 1)))
+        full = rows + 6
+        early = rows + 1
+        for k in range(full):
+            hidden_product(k)
+            if 2 <= k < early + 2:
+                hidden_norm(k - 2)
+        weave(steps(conv_rows, (0, rows - 1)), steps(hidden_norm, *[(k,) for k in range(early, full)]))
         conv_rows(rows - 1, 5)
         both = mm(joined(wide[0 : rows + 5]), jnp.concatenate([mid[2, 0, :, 256:384], mid[2, 1, :, 256:384]], axis=1))
         rest = mm(joined(wide[2 : rows + 6]), mid[2, 2, :, 256:384])
@@ -316,7 +322,7 @@
 
     def body(
         info, hidden, conv, acc, got_even, got_odd, packed_even, packed_odd, own, own_mid, fwd, back_odd, back_even, mid_t, w_in, half_gain,
-        half_out, payload, reward, edge, lines, *buffers
+        half_out, payload, reward, lines, *buffers
     ):
         fine = rows + 3
         buffers = list(buffers)
@@ -330,27 +336,20 @@
         g_odd, g_even, t_odd, t_even = part(fine), part(fine), part(fine), part(fine)
         tmp_odd, tmp_even, back = part(fine), part(fine), part(rows + 2)
         act_grad, hid = part(rows), part(rows)
-        even = info[0] == 0
         top, bottom = flag(info, 1), flag(info, 2)
-
-        def take(got, packed, before):
-            ok = top if before else bottom
-            place = 0 if before else rows + 1
-            for k in range(3):
-                at = slice(k * cols, (k + 1) * cols)
-                edge[place + k] = got[at].astype(F32) * ok
-                reward[k if before else 2 * rows + 3 + k] = (packed[at].astype(F32) * ok).astype(BF16)
-
-        @pl.when(even)
-        def _():
-            take(got_odd, packed_odd, True)
-            take(got_even, packed_even, False)
-
-        @pl.when(jnp.logical_not(even))
-        def _():
-            take(got_even, packed_even, True)
-            take(got_odd, packed_odd, False)
-
+        odd_tile = flag(info, 0)
+        above = (top * odd_tile, top * (1.0 - odd_tile))
+        below = (bottom * (1.0 - odd_tile), bottom * odd_tile)
+
+        def halo(of_even, of_odd, k, lanes, before):
+            scale = above if before else below
+            at = slice(k * cols, (k + 1) * cols)
+            return of_even[at, lanes].astype(F32) * scale[0] + of_odd[at, lanes].astype(F32) * scale[1]
+
+        for k in range(3):
+            for lanes in (slice(0, 128), slice(128, 256), slice(256, 384)):
+                reward[k, :, lanes] = halo(packed_even, packed_odd, k, lanes, True).astype(BF16)
+                reward[2 * rows + 3 + k, :, lanes] = halo(packed_even, packed_odd, k, lanes, False).astype(BF16)
         reward[3:6] = own[0:3]
         reward[6 : 2 * rows] = own_mid[...]
         reward[2 * rows : 2 * rows + 3] = own[3:6]
@@ -364,8 +363,10 @@
                 x = hidden[k + 1, :, at].astype(F32) + conv[k, :, at]
                 if 1 <= k <= rows + 2:
                     x = x + acc[k, :, at]
-                if k < 3 or k > rows:
-                    x = x + edge[k, :, at]
+                if k < 3:
+                    x = x + halo(got_even, got_odd, k, at, True)
+                if k > rows:
+                    x = x + halo(got_even, got_odd, k - rows - 1, at, False)
                 beside(wide[k], 0, lanes, inside(x, k, 2, rows + 2), False)
 
         def up_rows(first, last, b, n):
@@ -487,9 +488,10 @@
         weave(pulls(rows - 1, fine), downs(0, rows - 1))
         weave(each(block_row, 0, rows - 2), downs(rows - 1, fine))
         weave(each(block_row, rows - 2, rows + 2))
-        mid_rows(0, rows)
         mid_rest(0, rows)
-        for k in range(rows):
+        mid_rows(0, 2)
+        weave(steps(mid_rows, (2, rows - 2)), each(hidden_pull, 0, 2))
+        for k in range(2, rows):
             hidden_pull(k)
 
         z = mm_t(w_in[...], joined(hid))
@@ -633,7 +635,6 @@
         1, 16,
         [
             pltpu.VMEM((2 * rows + 6, cols, 384), BF16),
-            pltpu.VMEM((rows + 4, cols, 384), F32),
             pltpu.VMEM((3 * chan, size), F32),
         ]
         + [pltpu.VMEM((cols, 768), F32)] * (2 * (rows + 4))

time: 48.3 us -> 49.2 us (1.019)
  Pallas kernels: 28.5 us -> 29.4 us
    pallas_call x1, Pallas kernels: 7.01 us -> 7.64 us  [shards(): call(current_body(rows, cols, chan), [((rows + 6, cols, 384), BF16), ((ro...]
  transfers between devices with their start and end apart: 4 -> 4, of which waited for: 0 -> 0; matrix products, arithmetic and copies ran while one was open for 0% -> 0% of each run, Pallas kernels for 26% -> 27%
where the time goes in v13:
time: 49.2 us; the launch traced here: 49 us
  Pallas kernels  29.4 us (60%)
  blocking collectives  11.7 us (24%)
  starting transfers between devices  5.95 us (12%)
  local copies, waits for them, and re-layouts  1.58 us (3%)
    pallas_call x1, Pallas kernels, shards(): call(back_body(rows, cols, chan, count, o), [((count, chan, 128), BF16)],...  12.7 us
    all_to_all x1, blocking collectives, shards(): lax.all_to_all(payload, 'tile', split_axis=0, concat_axis=0, tiled=True)  11.7 us
    pallas_call x1, Pallas kernels, shards(): call(current_body(rows, cols, chan), [((rows + 6, cols, 384), BF16), ((ro...  7.64 us
    pallas_call x1, Pallas kernels, shards(): call(cached_body(rows, cols, count, width, tokens, o), [((rows + 4, cols,...  5.43 us
    ppermute x1, starting transfers between devices, shards(): got_even = lax.ppermute(part_even, 'tile', within)  4.05 us
    unnamed x22, local copies, waits for them, and re-layouts  1.56 us
    pallas_call x1, Pallas kernels, shards(): call(pack_body(rows, cols, o, chan), [((6, cols, 384), BF16), ((edge_rows...  1.45 us
    pallas_call x1, Pallas kernels, shards(): call(taps_body, [((4,), jnp.int32), ((768, 768), BF16), ((768, 768), BF16...  1.15 us
  transfers between devices with their start and end apart: 4, of which 0 were waited for; matrix products, arithmetic and copies ran while one was open for 0% of the time, Pallas kernels for 27%

profile of v13, /device:TPU:0, one launch (start us, length us, event | category | flops | bytes accessed | tf_op | source)
XLA Modules:
  0.0 49.0 jit_solution(15135586453826142374)
XLA Ops:
  0.0 0.1 pad_add_fusion.info
  0.1 0.0 copy-start.1
  0.1 1.3 %copy-done.1 = bf16[3,3,384,192]{2,3,1,0:T(8,128)(2,1)S(1)} copy-done((bf16[3,3,384,192]{2,3,1,0:T(8,128)(2,1)S(1)}, bf16[3,3,384,192]{2,3,1,0:T(8,128)(2,1)}, u32[]{:S(2)}) %copy-start.1) | copy-done | bytes 1327128
  1.4 0.0 copy-start.2
  1.4 0.0 copy-start.4
  1.4 1.1 %shard_map.100 = (s32[4]{0:T(128)S(1)}, bf16[768,768]{1,0:T(8,128)(2,1)S(1)}, bf16[768,768]{1,0:T(8,128)(2,1)S(1)}) custom-call(s32[4]{0:T(128)S(1)} %pad_add_fusion.info, bf16[3,3,192,384]{3,2,1,0:T(8,128)(2,1)S(1)} %bitcast.21), custom_call_target="tpu_custom_call" | custom-call | flops 10000000000 | bytes 1048576 | tf_op jit(solution)/shard_map/pallas_call | solution.py:591
  2.6 0.1 copy-done.2
  2.7 0.0 copy-done.4
  2.7 0.0 copy-done.5
  2.7 0.0 copy-start.6
  2.7 1.5 %shard_map.102 = (bf16[6,160,384]{2,1,0:T(8,128)(2,1)S(1)}, bf16[608,384]{1,0:T(8,128)(2,1)S(1)}, bf16[608,384]{1,0:T(8,128)(2,1)S(1)}) custom-call(s32[4]{0:T(128)S(1)} %get-tuple-element.20.info, bf16[8,192,320]{2,1,0:T(8,128)(2,1)S(1)} %bitcast.22, bf16[4,16,160]{2,1,0:T(8,128)(2,1)S(1)} %bitcast.26, bf16[2,4,16,160]{3,2,1,0:T(8,128)(2,1)S(1)} %bitcast.24), custom_call_target="tpu_custom_call" | custom-call | flops 10000000000 | bytes 1048576 | tf_op jit(solution)/shard_map/pallas_call | solution.py:597
  4.2 0.5 %collective-permute-start = (bf16[608,384]{1,0:T(8,128)(2,1)S(1)}, bf16[608,384]{1,0:T(8,128)(2,1)S(1)}, u32[]{:S(2)}, u32[]{:S(2)}) collective-permute-start(bf16[608,384]{1,0:T(8,128)(2,1)S(1)} %get-tuple-element.24), channel_id=1, source_target_pairs={{0,1},{1,0},{2,3},{3,2},{4,5},{5,4},{6,7},{7,6},{8,9},{9,8},{10,11... | collective-permute-start | bytes 1400840 | tf_op jit(solution)/shard_map/ppermute | solution.py:602
  4.7 0.7 %collective-permute-start.1 = (bf16[608,384]{1,0:T(8,128)(2,1)S(1)}, bf16[608,384]{1,0:T(8,128)(2,1)S(1)}, u32[]{:S(2)}, u32[]{:S(2)}) collective-permute-start(bf16[608,384]{1,0:T(8,128)(2,1)S(1)} %get-tuple-element.25), channel_id=1, source_target_pairs={{0,0},{1,2},{2,1},{3,4},{4,3},{5,6},{6,5},{7,7},{8,8},{9,10},{10,9... | collective-permute-start | bytes 1400840 | tf_op jit(solution)/shard_map/ppermute | solution.py:603
  5.4 0.0 slice-done
  5.4 0.0 slice-done.1
  5.4 0.1 copy-done.3
  5.5 0.0 copy-done.6
  5.5 5.4 %shard_map.101 = (f32[8,160,384]{2,1,0:T(8,128)S(1)}, bf16[480,384]{1,0:T(8,128)(2,1)S(1)}, bf16[480,384]{1,0:T(8,128)(2,1)S(1)}, bf16[3456,384]{1,0:T(8,128)(2,...) custom-call(s32[4]{0:T(128)S(1)} %get-tuple-element.20.info, ...), custom_call_target="tpu_custom_call" | custom-call | flops 4000000000 | bytes 1048576 | tf_op jit(solution)/shard_map/pallas_call | solution.py:607
  11.0 4.0 %collective-permute-start.2 = (bf16[480,384]{1,0:T(8,128)(2,1)S(1)}, bf16[480,384]{1,0:T(8,128)(2,1)S(1)}, u32[]{:S(2)}, u32[]{:S(2)}) collective-permute-start(bf16[480,384]{1,0:T(8,128)(2,1)S(1)} %get-tuple-element.29), channel_id=1, source_target_pairs={{0,1},{1,0},{2,3},{3,2},{4,5},{5,4},{6,7},{7,6},{8,9},{9,8},{10,11... | collective-permute-start | bytes 1105928 | tf_op jit(solution)/shard_map/ppermute | solution.py:615
  15.0 0.7 %collective-permute-start.3 = (bf16[480,384]{1,0:T(8,128)(2,1)S(1)}, bf16[480,384]{1,0:T(8,128)(2,1)S(1)}, u32[]{:S(2)}, u32[]{:S(2)}) collective-permute-start(bf16[480,384]{1,0:T(8,128)(2,1)S(1)} %get-tuple-element.30), channel_id=1, source_target_pairs={{0,0},{1,2},{2,1},{3,4},{4,3},{5,6},{6,5},{7,7},{8,8},{9,10},{10,9... | collective-permute-start | bytes 1105928 | tf_op jit(solution)/shard_map/ppermute | solution.py:616
  15.7 0.0 copy-done.7
  15.7 0.0 copy-done
  15.8 0.0 copy-done.8
  15.8 0.1 maximum_multiply_fusion.half_out
  15.9 0.0 collective-permute-done.got_even.packed_even
  15.9 0.0 collective-permute-done.1.got_odd.packed_odd
  15.9 7.6 %shard_map.103 = (bf16[10,160,384]{2,1,0:T(8,128)(2,1)S(1)}, f32[8,160,384]{2,1,0:T(8,128)S(1)}) custom-call(s32[4]{0:T(128)S(1)} %get-tuple-element.20.info, bf16[4,16,160]{2,1,0:T(8,128)(2,1)S(1)} %bitcast.27, bf16[2,4,16,160]{3,2,1,0:T(8,128)(2,1)S(1)} %bitcast.25, bf16[608,384]{1,0:T(8,128)(2,1)S(1)} %collective-permute-done.got_even.packed_even, ...), custom_call_target="tpu_custom_call" | custom-call | flops 5000000000 | bytes 1048576 | tf_op jit(solution)/shard_map/pallas_call | solution.py:618
  23.5 0.0 collective-permute-done.2.got_even
  23.5 0.0 collective-permute-done.3.got_odd
  23.5 12.7 %shard_map.104 = bf16[8,16,128]{2,1,0:T(8,128)(2,1)S(1)} custom-call(s32[4]{0:T(128)S(1)} %get-tuple-element.20.info, bf16[10,160,384]{2,1,0:T(8,128)(2,1)S(1)} %get-tuple-element.26.hidden, f32[8,160,384]{2,1,0:T(8,128)S(1)} %get-tuple-element.27.conv, f32[8,160,384]{2,1,0:T(8,128)S(1)} %get-tuple-element.28.acc, ...), custom_call_target="tpu_custom_call" | custom-call | flops 8000000000 | bytes 1048576 | tf_op jit(solution)/shard_map/pallas_call | solution.py:632
  36.3 11.7 %all_to_all.5.got = bf16[8,16,128]{2,1,0:T(8,128)(2,1)S(1)} all-to-all(bf16[8,16,128]{2,1,0:T(8,128)(2,1)S(1)} %shard_map.104), channel_id=1, replica_groups=mesh['prompt'=4,'tile'=8] {'tile'}, dimensions={0} | all-to-all | bytes 65536 | tf_op jit(solution)/shard_map/all_to_all | solution.py:653
  48.0 1.0 %shard_map.105 = f32[64,160]{1,0:T(8,128)} custom-call(bf16[8,128,640]{2,1,0:T(8,128)(2,1)S(1)} %get-tuple-element.23.sel, bf16[8,16,128]{2,1,0:T(8,128)(2,1)S(1)} %all_to_all.5.got), custom_call_target="tpu_custom_call" | custom-call | flops 10000000 | bytes 1048576 | tf_op jit(solution)/shard_map/pallas_call | solution.py:654
  (12 shorter events, 0.0 us)
Async XLA Ops:
  0.1 1.3 %copy-start.1 = (bf16[3,3,384,192]{2,3,1,0:T(8,128)(2,1)S(1)}, bf16[3,3,384,192]{2,3,1,0:T(8,128)(2,1)}, u32[]{:S(2)}) copy-start(bf16[3,3,384,192]{2,3,1,0:T(8,128)(2,1)} %param.16) | copy-start | bytes 3981316
  1.4 1.3 %copy-start.2 = (bf16[8,320,192]{1,2,0:T(8,128)(2,1)S(1)}, bf16[8,320,192]{1,2,0:T(8,128)(2,1)}, u32[]{:S(2)}) copy-start(bf16[8,320,192]{1,2,0:T(8,128)(2,1)} %param.13) | copy-start | bytes 2949124
  1.4 1.3 %copy-start.4 = (bf16[2,4,160,16]{2,3,1,0:T(8,128)(2,1)S(1)}, bf16[2,4,160,16]{2,3,1,0:T(8,128)(2,1)}, u32[]{:S(2)}) copy-start(bf16[2,4,160,16]{2,3,1,0:T(8,128)(2,1)} %param.11) | copy-start | bytes 122884
  1.4 1.3 %copy-start.5 = (bf16[4,160,16]{1,2,0:T(8,128)(2,1)S(1)}, bf16[4,160,16]{1,2,0:T(8,128)(2,1)}, u32[]{:S(2)}) copy-start(bf16[4,160,16]{1,2,0:T(8,128)(2,1)} %param.10) | copy-start | bytes 61444
  1.4 4.0 %slice-start = ((s8[7962624]{0:T(1024)(128)(4,1)}), s8[4194304]{0:T(1024)(128)(4,1)S(1)}, s32[]{:S(2)}) async-start(s8[7962624]{0:T(1024)(128)(4,1)} %bitcast.17), calls=%async_computation.1 | async-start | bytes 8388608
  2.7 2.7 %slice-start.1 = ((s8[7962624]{0:T(1024)(128)(4,1)}), s8[3768320]{0:T(1024)(128)(4,1)S(1)}, s32[]{:S(2)}) async-start(s8[7962624]{0:T(1024)(128)(4,1)} %bitcast.17), calls=%async_computation.2 | async-start | bytes 7536640
  2.7 2.8 %copy-start.3 = (bf16[2,4,160,384]{3,2,1,0:T(8,128)(2,1)S(1)}, bf16[2,4,160,384]{3,2,1,0:T(8,128)(2,1)}, u32[]{:S(2)}) copy-start(bf16[2,4,160,384]{3,2,1,0:T(8,128)(2,1)} %features.1) | copy-start | bytes 2949124
  2.7 2.8 %copy-start.6 = (s32[8]{0:T(128)S(1)}, s32[8]{0:T(128)}, u32[]{:S(2)}) copy-start(s32[8]{0:T(128)} %order.1) | copy-start | bytes 100
  4.2 11.7 %collective-permute-start = (bf16[608,384]{1,0:T(8,128)(2,1)S(1)}, bf16[608,384]{1,0:T(8,128)(2,1)S(1)}, u32[]{:S(2)}, u32[]{:S(2)}) collective-permute-start(bf16[608,384]{1,0:T(8,128)(2,1)S(1)} %get-tuple-element.24), channel_id=1, source_target_pairs={{0,1},{1,0},{2,3},{3,2},{4,5},{5,4},{6,7},{7,6},{8,9},{9,8},{10,11... | collective-permute-start | bytes 1400840 | tf_op jit(solution)/shard_map/ppermute | solution.py:602
  4.7 11.2 %collective-permute-start.1 = (bf16[608,384]{1,0:T(8,128)(2,1)S(1)}, bf16[608,384]{1,0:T(8,128)(2,1)S(1)}, u32[]{:S(2)}, u32[]{:S(2)}) collective-permute-start(bf16[608,384]{1,0:T(8,128)(2,1)S(1)} %get-tuple-element.25), channel_id=1, source_target_pairs={{0,0},{1,2},{2,1},{3,4},{4,3},{5,6},{6,5},{7,7},{8,8},{9,10},{10,9... | collective-permute-start | bytes 1400840 | tf_op jit(solution)/shard_map/ppermute | solution.py:603
  5.5 10.2 %copy-start.7 = (f32[384]{0:T(512)S(1)}, f32[384]{0:T(512)}, u32[]{:S(2)}) copy-start(f32[384]{0:T(512)} %param.17) | copy-start | bytes 4612
  5.5 10.2 %copy-start = (bf16[3,3,3,16,384]{4,3,2,1,0:T(8,128)(2,1)S(1)}, bf16[3,3,3,16,384]{4,3,2,1,0:T(8,128)(2,1)}, u32[]{:S(2)}) copy-start(bf16[3,3,3,16,384]{4,3,2,1,0:T(8,128)(2,1)} %param.14) | copy-start | bytes 995332
  5.5 10.2 %copy-start.8 = (f32[192]{0:T(256)S(1)}, f32[192]{0:T(256)}, u32[]{:S(2)}) copy-start(f32[192]{0:T(256)} %param.18) | copy-start | bytes 2308
  11.0 12.5 %collective-permute-start.2 = (bf16[480,384]{1,0:T(8,128)(2,1)S(1)}, bf16[480,384]{1,0:T(8,128)(2,1)S(1)}, u32[]{:S(2)}, u32[]{:S(2)}) collective-permute-start(bf16[480,384]{1,0:T(8,128)(2,1)S(1)} %get-tuple-element.29), channel_id=1, source_target_pairs={{0,1},{1,0},{2,3},{3,2},{4,5},{5,4},{6,7},{7,6},{8,9},{9,8},{10,11... | collective-permute-start | bytes 1105928 | tf_op jit(solution)/shard_map/ppermute | solution.py:615
  15.0 8.5 %collective-permute-start.3 = (bf16[480,384]{1,0:T(8,128)(2,1)S(1)}, bf16[480,384]{1,0:T(8,128)(2,1)S(1)}, u32[]{:S(2)}, u32[]{:S(2)}) collective-permute-start(bf16[480,384]{1,0:T(8,128)(2,1)S(1)} %get-tuple-element.30), channel_id=1, source_target_pairs={{0,0},{1,2},{2,1},{3,4},{4,3},{5,6},{6,5},{7,7},{8,8},{9,10},{10,9... | collective-permute-start | bytes 1105928 | tf_op jit(solution)/shard_map/ppermute | solution.py:616

commit v14 on v9

--- a/solution.py
+++ b/solution.py
@@ -280,12 +280,13 @@
             total = mm(jnp.concatenate(lhs, axis=1), mid[2, :, :, 0:256].reshape(3456, 256))
             conv[p : p + number, :, 0:256] = total.reshape(number, cols, 256)
 
-        for k in range(rows + 2):
+        for k in range(4):
             hidden_row(k)
-        conv_rows(0, rows)
-        for k in range(rows + 2, rows + 6):
-            hidden_row(k)
-        conv_rows(rows, 4)
+        for p in range(0, rows + 4, 2):
+            conv_rows(p, 2)
+            for k in (p + 4, p + 5):
+                if k < rows + 6:
+                    hidden_row(k)
         both = mm(
             wide[0 : rows + 5].reshape((rows + 5) * cols, 1152),
             jnp.concatenate([mid[2, 0, :, 256:384], mid[2, 1, :, 256:384]], axis=1),
@@ -502,16 +503,17 @@
         valid = jnp.logical_and(step >= 0, step < count)
         beside = jnp.where(valid, piece * order[jnp.clip(step, 0, count - 1)], -9999)
         begin = jnp.where(group == 2, beside, piece * order[t])
-        sel[t] = (fixed + begin == 0).astype(F32).astype(BF16)
+        sel[t // 2, t % 2 * 128 : t % 2 * 128 + 128] = (fixed + begin == 0).astype(F32).astype(BF16)
 
     return one
 
 
 def place_body(count, chan, tokens):
     def body(sel, got, out):
-        total = mm(got[0], sel[0])
-        for t in range(1, count):
-            total += mm(got[t], sel[t])
+        total = None
+        for t in range(count // 2):
+            x = mm(jnp.concatenate([got[2 * t], got[2 * t + 1]], axis=1), sel[t])
+            total = x if total is None else total + x
         for k in range(4):
             out[k * chan : (k + 1) * chan] = total[:, k * tokens : (k + 1) * tokens]
 
@@ -569,7 +571,7 @@
         cached_body(rows, cols, count, width, tokens, o),
         [
             ((rows + 4, cols, 384), F32), ((3 * cols, 384), BF16), ((3 * cols, 384), BF16), ((3456, 384), BF16),
-            ((count, 128, 4 * tokens), BF16), ((2, 768, 768), BF16), ((2, cols, 384), BF16),
+            ((count // 2, 256, 4 * tokens), BF16), ((2, 768, 768), BF16), ((2, cols, 384), BF16),
         ],
         2, 5, [pltpu.VMEM((size, 2304), BF16), pltpu.VMEM((3, size, 384), F32)], 4e9, 14,
     )(info, shard_order, cached_features, mid, back_odd, back_even, reward_t)

time: 48.3 us -> 48.1 us (level)
  transfers between devices with their start and end apart: 4 -> 4, of which waited for: 0 -> 0; matrix products, arithmetic and copies ran while one was open for 0% -> 0% of each run, Pallas kernels for 26% -> 25%
where the time goes in v14:
time: 48.1 us; the launch traced here: 47.9 us
  Pallas kernels  28.3 us (59%)
  blocking collectives  11.7 us (24%)
  starting transfers between devices  5.95 us (12%)
  local copies, waits for them, and re-layouts  1.58 us (3%)
    pallas_call x1, Pallas kernels, shards(): call(back_body(rows, cols, chan, count, o), [((count, chan, 128), BF16)],...  12.6 us
    all_to_all x1, blocking collectives, shards(): lax.all_to_all(payload, 'tile', split_axis=0, concat_axis=0, tiled=True)  11.7 us
    pallas_call x1, Pallas kernels, shards(): call(current_body(rows, cols, chan), [((rows + 6, cols, 384), BF16), ((ro...  6.72 us
    pallas_call x1, Pallas kernels, shards(): call(cached_body(rows, cols, count, width, tokens, o), [((rows + 4, cols,...  5.43 us
    ppermute x1, starting transfers between devices, shards(): got_even = lax.ppermute(part_even, 'tile', within)  4.05 us
    unnamed x22, local copies, waits for them, and re-layouts  1.56 us
    pallas_call x1, Pallas kernels, shards(): call(pack_body(rows, cols, o, chan), [((6, cols, 384), BF16), ((edge_rows...  1.45 us
    pallas_call x1, Pallas kernels, shards(): call(taps_body, [((4,), jnp.int32), ((768, 768), BF16), ((768, 768), BF16...  1.15 us
  transfers between devices with their start and end apart: 4, of which 0 were waited for; matrix products, arithmetic and copies ran while one was open for 0% of the time, Pallas kernels for 25%

profile of v14, /device:TPU:0, one launch (start us, length us, event | category | flops | bytes accessed | tf_op | source)
XLA Modules:
  0.0 47.9 jit_solution(8503345670269662032)
XLA Ops:
  0.0 0.1 pad_add_fusion.info
  0.1 0.0 copy-start.1
  0.1 1.3 %copy-done.1 = bf16[3,3,384,192]{2,3,1,0:T(8,128)(2,1)S(1)} copy-done((bf16[3,3,384,192]{2,3,1,0:T(8,128)(2,1)S(1)}, bf16[3,3,384,192]{2,3,1,0:T(8,128)(2,1)}, u32[]{:S(2)}) %copy-start.1) | copy-done | bytes 1327128
  1.4 0.0 copy-start.2
  1.4 0.0 copy-start.4
  1.4 1.1 %shard_map.100 = (s32[4]{0:T(128)S(1)}, bf16[768,768]{1,0:T(8,128)(2,1)S(1)}, bf16[768,768]{1,0:T(8,128)(2,1)S(1)}) custom-call(s32[4]{0:T(128)S(1)} %pad_add_fusion.info, bf16[3,3,192,384]{3,2,1,0:T(8,128)(2,1)S(1)} %bitcast.21), custom_call_target="tpu_custom_call" | custom-call | flops 10000000000 | bytes 1048576 | tf_op jit(solution)/shard_map/pallas_call | solution.py:554
  2.6 0.1 copy-done.2
  2.7 0.0 copy-done.4
  2.7 0.0 copy-done.5
  2.7 0.0 copy-start.6
  2.7 1.5 %shard_map.102 = (bf16[6,160,384]{2,1,0:T(8,128)(2,1)S(1)}, bf16[608,384]{1,0:T(8,128)(2,1)S(1)}, bf16[608,384]{1,0:T(8,128)(2,1)S(1)}) custom-call(s32[4]{0:T(128)S(1)} %get-tuple-element.20.info, bf16[8,192,320]{2,1,0:T(8,128)(2,1)S(1)} %bitcast.22, bf16[4,16,160]{2,1,0:T(8,128)(2,1)S(1)} %bitcast.26, bf16[2,4,16,160]{3,2,1,0:T(8,128)(2,1)S(1)} %bitcast.24), custom_call_target="tpu_custom_call" | custom-call | flops 10000000000 | bytes 1048576 | tf_op jit(solution)/shard_map/pallas_call | solution.py:560
  4.2 0.5 %collective-permute-start = (bf16[608,384]{1,0:T(8,128)(2,1)S(1)}, bf16[608,384]{1,0:T(8,128)(2,1)S(1)}, u32[]{:S(2)}, u32[]{:S(2)}) collective-permute-start(bf16[608,384]{1,0:T(8,128)(2,1)S(1)} %get-tuple-element.24), channel_id=1, source_target_pairs={{0,1},{1,0},{2,3},{3,2},{4,5},{5,4},{6,7},{7,6},{8,9},{9,8},{10,11... | collective-permute-start | bytes 1400840 | tf_op jit(solution)/shard_map/ppermute | solution.py:565
  4.7 0.7 %collective-permute-start.1 = (bf16[608,384]{1,0:T(8,128)(2,1)S(1)}, bf16[608,384]{1,0:T(8,128)(2,1)S(1)}, u32[]{:S(2)}, u32[]{:S(2)}) collective-permute-start(bf16[608,384]{1,0:T(8,128)(2,1)S(1)} %get-tuple-element.25), channel_id=1, source_target_pairs={{0,0},{1,2},{2,1},{3,4},{4,3},{5,6},{6,5},{7,7},{8,8},{9,10},{10,9... | collective-permute-start | bytes 1400840 | tf_op jit(solution)/shard_map/ppermute | solution.py:566
  5.4 0.0 slice-done
  5.4 0.0 slice-done.1
  5.4 0.1 copy-done.3
  5.5 0.0 copy-done.6
  5.5 5.4 %shard_map.101 = (f32[8,160,384]{2,1,0:T(8,128)S(1)}, bf16[480,384]{1,0:T(8,128)(2,1)S(1)}, bf16[480,384]{1,0:T(8,128)(2,1)S(1)}, bf16[3456,384]{1,0:T(8,128)(2,...) custom-call(s32[4]{0:T(128)S(1)} %get-tuple-element.20.info, ...), custom_call_target="tpu_custom_call" | custom-call | flops 4000000000 | bytes 1048576 | tf_op jit(solution)/shard_map/pallas_call | solution.py:570
  11.0 4.0 %collective-permute-start.2 = (bf16[480,384]{1,0:T(8,128)(2,1)S(1)}, bf16[480,384]{1,0:T(8,128)(2,1)S(1)}, u32[]{:S(2)}, u32[]{:S(2)}) collective-permute-start(bf16[480,384]{1,0:T(8,128)(2,1)S(1)} %get-tuple-element.29), channel_id=1, source_target_pairs={{0,1},{1,0},{2,3},{3,2},{4,5},{5,4},{6,7},{7,6},{8,9},{9,8},{10,11... | collective-permute-start | bytes 1105928 | tf_op jit(solution)/shard_map/ppermute | solution.py:578
  15.0 0.7 %collective-permute-start.3 = (bf16[480,384]{1,0:T(8,128)(2,1)S(1)}, bf16[480,384]{1,0:T(8,128)(2,1)S(1)}, u32[]{:S(2)}, u32[]{:S(2)}) collective-permute-start(bf16[480,384]{1,0:T(8,128)(2,1)S(1)} %get-tuple-element.30), channel_id=1, source_target_pairs={{0,0},{1,2},{2,1},{3,4},{4,3},{5,6},{6,5},{7,7},{8,8},{9,10},{10,9... | collective-permute-start | bytes 1105928 | tf_op jit(solution)/shard_map/ppermute | solution.py:579
  15.7 0.0 copy-done.7
  15.7 0.0 copy-done
  15.8 0.0 copy-done.8
  15.8 0.1 maximum_multiply_fusion.half_out
  15.9 0.0 collective-permute-done.got_even.packed_even
  15.9 0.0 collective-permute-done.1.got_odd.packed_odd
  15.9 6.7 %shard_map.103 = (bf16[10,160,384]{2,1,0:T(8,128)(2,1)S(1)}, f32[8,160,384]{2,1,0:T(8,128)S(1)}) custom-call(s32[4]{0:T(128)S(1)} %get-tuple-element.20.info, bf16[4,16,160]{2,1,0:T(8,128)(2,1)S(1)} %bitcast.27, bf16[2,4,16,160]{3,2,1,0:T(8,128)(2,1)S(1)} %bitcast.25, bf16[608,384]{1,0:T(8,128)(2,1)S(1)} %collective-permute-done.got_even.packed_even, ...), custom_call_target="tpu_custom_call" | custom-call | flops 5000000000 | bytes 1048576 | tf_op jit(solution)/shard_map/pallas_call | solution.py:581
  22.6 0.0 collective-permute-done.2.got_even
  22.6 0.0 collective-permute-done.3.got_odd
  22.6 12.6 %shard_map.104 = bf16[8,16,128]{2,1,0:T(8,128)(2,1)S(1)} custom-call(s32[4]{0:T(128)S(1)} %get-tuple-element.20.info, bf16[10,160,384]{2,1,0:T(8,128)(2,1)S(1)} %get-tuple-element.26.hidden, f32[8,160,384]{2,1,0:T(8,128)S(1)} %get-tuple-element.27.conv, f32[8,160,384]{2,1,0:T(8,128)S(1)} %get-tuple-element.28.acc, ...), custom_call_target="tpu_custom_call" | custom-call | flops 8000000000 | bytes 1048576 | tf_op jit(solution)/shard_map/pallas_call | solution.py:595
  35.2 11.7 %all_to_all.5.got = bf16[8,16,128]{2,1,0:T(8,128)(2,1)S(1)} all-to-all(bf16[8,16,128]{2,1,0:T(8,128)(2,1)S(1)} %shard_map.104), channel_id=1, replica_groups=mesh['prompt'=4,'tile'=8] {'tile'}, dimensions={0} | all-to-all | bytes 65536 | tf_op jit(solution)/shard_map/all_to_all | solution.py:621
  46.9 1.0 %shard_map.105 = f32[64,160]{1,0:T(8,128)} custom-call(bf16[4,256,640]{2,1,0:T(8,128)(2,1)S(1)} %get-tuple-element.23.sel, bf16[8,16,128]{2,1,0:T(8,128)(2,1)S(1)} %all_to_all.5.got), custom_call_target="tpu_custom_call" | custom-call | flops 10000000 | bytes 1048576 | tf_op jit(solution)/shard_map/pallas_call | solution.py:622
  (12 shorter events, 0.0 us)
Async XLA Ops:
  0.1 1.3 %copy-start.1 = (bf16[3,3,384,192]{2,3,1,0:T(8,128)(2,1)S(1)}, bf16[3,3,384,192]{2,3,1,0:T(8,128)(2,1)}, u32[]{:S(2)}) copy-start(bf16[3,3,384,192]{2,3,1,0:T(8,128)(2,1)} %param.16) | copy-start | bytes 3981316
  1.4 1.3 %copy-start.2 = (bf16[8,320,192]{1,2,0:T(8,128)(2,1)S(1)}, bf16[8,320,192]{1,2,0:T(8,128)(2,1)}, u32[]{:S(2)}) copy-start(bf16[8,320,192]{1,2,0:T(8,128)(2,1)} %param.13) | copy-start | bytes 2949124
  1.4 1.3 %copy-start.4 = (bf16[2,4,160,16]{2,3,1,0:T(8,128)(2,1)S(1)}, bf16[2,4,160,16]{2,3,1,0:T(8,128)(2,1)}, u32[]{:S(2)}) copy-start(bf16[2,4,160,16]{2,3,1,0:T(8,128)(2,1)} %param.11) | copy-start | bytes 122884
  1.4 1.3 %copy-start.5 = (bf16[4,160,16]{1,2,0:T(8,128)(2,1)S(1)}, bf16[4,160,16]{1,2,0:T(8,128)(2,1)}, u32[]{:S(2)}) copy-start(bf16[4,160,16]{1,2,0:T(8,128)(2,1)} %param.10) | copy-start | bytes 61444
  1.4 4.0 %slice-start = ((s8[7962624]{0:T(1024)(128)(4,1)}), s8[4194304]{0:T(1024)(128)(4,1)S(1)}, s32[]{:S(2)}) async-start(s8[7962624]{0:T(1024)(128)(4,1)} %bitcast.17), calls=%async_computation.1 | async-start | bytes 8388608
  2.7 2.7 %slice-start.1 = ((s8[7962624]{0:T(1024)(128)(4,1)}), s8[3768320]{0:T(1024)(128)(4,1)S(1)}, s32[]{:S(2)}) async-start(s8[7962624]{0:T(1024)(128)(4,1)} %bitcast.17), calls=%async_computation.2 | async-start | bytes 7536640
  2.7 2.8 %copy-start.3 = (bf16[2,4,160,384]{3,2,1,0:T(8,128)(2,1)S(1)}, bf16[2,4,160,384]{3,2,1,0:T(8,128)(2,1)}, u32[]{:S(2)}) copy-start(bf16[2,4,160,384]{3,2,1,0:T(8,128)(2,1)} %features.1) | copy-start | bytes 2949124
  2.7 2.8 %copy-start.6 = (s32[8]{0:T(128)S(1)}, s32[8]{0:T(128)}, u32[]{:S(2)}) copy-start(s32[8]{0:T(128)} %order.1) | copy-start | bytes 100
  4.2 11.7 %collective-permute-start = (bf16[608,384]{1,0:T(8,128)(2,1)S(1)}, bf16[608,384]{1,0:T(8,128)(2,1)S(1)}, u32[]{:S(2)}, u32[]{:S(2)}) collective-permute-start(bf16[608,384]{1,0:T(8,128)(2,1)S(1)} %get-tuple-element.24), channel_id=1, source_target_pairs={{0,1},{1,0},{2,3},{3,2},{4,5},{5,4},{6,7},{7,6},{8,9},{9,8},{10,11... | collective-permute-start | bytes 1400840 | tf_op jit(solution)/shard_map/ppermute | solution.py:565
  4.7 11.2 %collective-permute-start.1 = (bf16[608,384]{1,0:T(8,128)(2,1)S(1)}, bf16[608,384]{1,0:T(8,128)(2,1)S(1)}, u32[]{:S(2)}, u32[]{:S(2)}) collective-permute-start(bf16[608,384]{1,0:T(8,128)(2,1)S(1)} %get-tuple-element.25), channel_id=1, source_target_pairs={{0,0},{1,2},{2,1},{3,4},{4,3},{5,6},{6,5},{7,7},{8,8},{9,10},{10,9... | collective-permute-start | bytes 1400840 | tf_op jit(solution)/shard_map/ppermute | solution.py:566
  5.5 10.2 %copy-start.7 = (f32[384]{0:T(512)S(1)}, f32[384]{0:T(512)}, u32[]{:S(2)}) copy-start(f32[384]{0:T(512)} %param.17) | copy-start | bytes 4612
  5.5 10.2 %copy-start = (bf16[3,3,3,16,384]{4,3,2,1,0:T(8,128)(2,1)S(1)}, bf16[3,3,3,16,384]{4,3,2,1,0:T(8,128)(2,1)}, u32[]{:S(2)}) copy-start(bf16[3,3,3,16,384]{4,3,2,1,0:T(8,128)(2,1)} %param.14) | copy-start | bytes 995332
  5.5 10.2 %copy-start.8 = (f32[192]{0:T(256)S(1)}, f32[192]{0:T(256)}, u32[]{:S(2)}) copy-start(f32[192]{0:T(256)} %param.18) | copy-start | bytes 2308
  11.0 11.6 %collective-permute-start.2 = (bf16[480,384]{1,0:T(8,128)(2,1)S(1)}, bf16[480,384]{1,0:T(8,128)(2,1)S(1)}, u32[]{:S(2)}, u32[]{:S(2)}) collective-permute-start(bf16[480,384]{1,0:T(8,128)(2,1)S(1)} %get-tuple-element.29), channel_id=1, source_target_pairs={{0,1},{1,0},{2,3},{3,2},{4,5},{5,4},{6,7},{7,6},{8,9},{9,8},{10,11... | collective-permute-start | bytes 1105928 | tf_op jit(solution)/shard_map/ppermute | solution.py:578
  15.0 7.6 %collective-permute-start.3 = (bf16[480,384]{1,0:T(8,128)(2,1)S(1)}, bf16[480,384]{1,0:T(8,128)(2,1)S(1)}, u32[]{:S(2)}, u32[]{:S(2)}) collective-permute-start(bf16[480,384]{1,0:T(8,128)(2,1)S(1)} %get-tuple-element.30), channel_id=1, source_target_pairs={{0,0},{1,2},{2,1},{3,4},{4,3},{5,6},{6,5},{7,7},{8,8},{9,10},{10,9... | collective-permute-start | bytes 1105928 | tf_op jit(solution)/shard_map/ppermute | solution.py:579

commit v15 on v14

--- a/solution.py
+++ b/solution.py
@@ -311,7 +311,8 @@
 
     def body(
         info, hidden, conv, acc, got_even, got_odd, packed_even, packed_odd, own, own_mid, fwd, back_odd, back_even, mid_t, w_in, half_gain,
-        half_out, payload, reward, edge, p0, p1, g_odd, g_even, wide, t_odd, t_even, back, act_grad, hid, tmp_odd, tmp_even, lines,
+        half_out, payload, reward, edge, p0, p1, g_odd, g_even, wide, t_odd, t_even, main, back, act_grad, hid, tmp_odd, tmp_even,
+        lines,
     ):
         even = info[0] == 0
         top, bottom = flag(info, 1), flag(info, 2)
@@ -356,13 +357,6 @@
             x = wide[first:last, :, b * 384 : b * 384 + 768].reshape(count * cols, 768)
             lanes = slice(n * 256, n * 256 + 256)
             (p0, p1)[b][first:last, :, lanes] = mm(x, fwd[b, :, lanes]).reshape(count, cols, 256)
-
-        def down_rows(first, last, odd, n):
-            count = last - first
-            g, kernel, t = (g_odd, back_odd, t_odd) if odd else (g_even, back_even, t_even)
-            lanes = slice(n * 256, n * 256 + 256)
-            x = g[first:last].reshape(count * cols, 768)
-            t[first:last, :, lanes] = mm(x, kernel[:, lanes]).reshape(count, cols, 256)
 
         low = lax.broadcasted_iota(jnp.int32, (CHUNK, 128), 1) < 64
         tall_low = lax.broadcasted_iota(jnp.int32, (cols, 128), 1) < 64
@@ -413,8 +407,10 @@
 
         def block_row(k):
             for lanes in range(0, 384, 128):
-                at, far = slice(lanes, lanes + 128), slice(lanes + 384, lanes + 512)
-                x = t_odd[k + 1, :, at] + t_odd[k, :, far] + t_even[k, :, at] + t_even[k + 1, :, far]
+                if lanes < 256:
+                    x = main[k, :, lanes : lanes + 128]
+                else:
+                    x = t_odd[k + 1, :, 0:128] + t_odd[k, :, 128:256] + t_even[k, :, 0:128] + t_even[k + 1, :, 128:256]
                 beside(back.at[k], 0, lanes, inside(x, k, 1, rows + 1), True)
 
         def hidden_pull(k):
@@ -437,10 +433,13 @@
         for k in range(fine):
             pull_row(k, True)
             pull_row(k, False)
-        for odd in (True, False):
-            down_rows(1 if odd else 0, fine if odd else fine - 1, odd, 0)
-            down_rows(0, fine, odd, 1)
-            down_rows(0 if odd else 1, fine - 1 if odd else fine, odd, 2)
+        number = rows + 2
+        lhs = [x.reshape(number * cols, 768) for x in (g_odd[1:fine], g_odd[0:number], g_even[0:number], g_even[1:fine])]
+        rhs = [back_odd[:, 0:256], back_odd[:, 384:640], back_even[:, 0:256], back_even[:, 384:640]]
+        main[...] = mm(jnp.concatenate(lhs, axis=1), jnp.concatenate(rhs, axis=0)).reshape(number, cols, 256)
+        for g, kernel, t in ((g_odd, back_odd, t_odd), (g_even, back_even, t_even)):
+            pair = jnp.concatenate([kernel[:, 256:384], kernel[:, 640:768]], axis=1)
+            t[...] = mm(g[...].reshape(fine * cols, 768), pair).reshape(fine, cols, 256)
         for k in range(rows + 2):
             block_row(k)
         lhs = [back[2 - i : 2 - i + rows].reshape(size, 1152) for i in range(3)]
@@ -604,8 +603,9 @@
             pltpu.VMEM((rows + 3, cols, 768), BF16),
             pltpu.VMEM((rows + 3, cols, 768), BF16),
             pltpu.VMEM((rows + 4, cols, 1152), BF16),
-            pltpu.VMEM((rows + 3, cols, 768), F32),
-            pltpu.VMEM((rows + 3, cols, 768), F32),
+            pltpu.VMEM((rows + 3, cols, 256), F32),
+            pltpu.VMEM((rows + 3, cols, 256), F32),
+            pltpu.VMEM((rows + 2, cols, 256), F32),
             pltpu.VMEM((rows + 2, cols, 1152), BF16),
             pltpu.VMEM((rows, cols, 384), F32),
             pltpu.VMEM((rows, cols, 384), BF16),

time: 48.1 us -> 48.6 us (1.010)
  Pallas kernels: 28.3 us -> 28.8 us
    pallas_call x1, Pallas kernels: 12.6 us -> 13.1 us  [shards(): call(back_body(rows, cols, chan, count, o), [((count, chan, 128), BF16)],...]
where the time goes in v15:
time: 48.6 us; the launch traced here: 48.4 us
  Pallas kernels  28.8 us (59%)
  blocking collectives  11.7 us (24%)
  starting transfers between devices  5.95 us (12%)
  local copies, waits for them, and re-layouts  1.58 us (3%)
    pallas_call x1, Pallas kernels, shards(): call(back_body(rows, cols, chan, count, o), [((count, chan, 128), BF16)],...  13.1 us
    all_to_all x1, blocking collectives, shards(): lax.all_to_all(payload, 'tile', split_axis=0, concat_axis=0, tiled=True)  11.7 us
    pallas_call x1, Pallas kernels, shards(): call(current_body(rows, cols, chan), [((rows + 6, cols, 384), BF16), ((ro...  6.72 us
    pallas_call x1, Pallas kernels, shards(): call(cached_body(rows, cols, count, width, tokens, o), [((rows + 4, cols,...  5.43 us
    ppermute x1, starting transfers between devices, shards(): got_even = lax.ppermute(part_even, 'tile', within)  4.05 us
    unnamed x22, local copies, waits for them, and re-layouts  1.56 us
    pallas_call x1, Pallas kernels, shards(): call(pack_body(rows, cols, o, chan), [((6, cols, 384), BF16), ((edge_rows...  1.45 us
    pallas_call x1, Pallas kernels, shards(): call(taps_body, [((4,), jnp.int32), ((768, 768), BF16), ((768, 768), BF16...  1.15 us
  transfers between devices with their start and end apart: 4, of which 0 were waited for; matrix products, arithmetic and copies ran while one was open for 0% of the time, Pallas kernels for 25%

profile of v15, /device:TPU:0, one launch (start us, length us, event | category | flops | bytes accessed | tf_op | source)
XLA Modules:
  0.0 48.4 jit_solution(15401852419860523166)
XLA Ops:
  0.0 0.1 pad_add_fusion.info
  0.1 0.0 copy-start.1
  0.1 1.3 %copy-done.1 = bf16[3,3,384,192]{2,3,1,0:T(8,128)(2,1)S(1)} copy-done((bf16[3,3,384,192]{2,3,1,0:T(8,128)(2,1)S(1)}, bf16[3,3,384,192]{2,3,1,0:T(8,128)(2,1)}, u32[]{:S(2)}) %copy-start.1) | copy-done | bytes 1327128
  1.4 0.0 copy-start.2
  1.4 0.0 copy-start.4
  1.4 1.1 %shard_map.100 = (s32[4]{0:T(128)S(1)}, bf16[768,768]{1,0:T(8,128)(2,1)S(1)}, bf16[768,768]{1,0:T(8,128)(2,1)S(1)}) custom-call(s32[4]{0:T(128)S(1)} %pad_add_fusion.info, bf16[3,3,192,384]{3,2,1,0:T(8,128)(2,1)S(1)} %bitcast.21), custom_call_target="tpu_custom_call" | custom-call | flops 10000000000 | bytes 1048576 | tf_op jit(solution)/shard_map/pallas_call | solution.py:553
  2.6 0.1 copy-done.2
  2.7 0.0 copy-done.4
  2.7 0.0 copy-done.5
  2.7 0.0 copy-start.6
  2.7 1.5 %shard_map.102 = (bf16[6,160,384]{2,1,0:T(8,128)(2,1)S(1)}, bf16[608,384]{1,0:T(8,128)(2,1)S(1)}, bf16[608,384]{1,0:T(8,128)(2,1)S(1)}) custom-call(s32[4]{0:T(128)S(1)} %get-tuple-element.20.info, bf16[8,192,320]{2,1,0:T(8,128)(2,1)S(1)} %bitcast.22, bf16[4,16,160]{2,1,0:T(8,128)(2,1)S(1)} %bitcast.26, bf16[2,4,16,160]{3,2,1,0:T(8,128)(2,1)S(1)} %bitcast.24), custom_call_target="tpu_custom_call" | custom-call | flops 10000000000 | bytes 1048576 | tf_op jit(solution)/shard_map/pallas_call | solution.py:559
  4.2 0.5 %collective-permute-start = (bf16[608,384]{1,0:T(8,128)(2,1)S(1)}, bf16[608,384]{1,0:T(8,128)(2,1)S(1)}, u32[]{:S(2)}, u32[]{:S(2)}) collective-permute-start(bf16[608,384]{1,0:T(8,128)(2,1)S(1)} %get-tuple-element.24), channel_id=1, source_target_pairs={{0,1},{1,0},{2,3},{3,2},{4,5},{5,4},{6,7},{7,6},{8,9},{9,8},{10,11... | collective-permute-start | bytes 1400840 | tf_op jit(solution)/shard_map/ppermute | solution.py:564
  4.7 0.7 %collective-permute-start.1 = (bf16[608,384]{1,0:T(8,128)(2,1)S(1)}, bf16[608,384]{1,0:T(8,128)(2,1)S(1)}, u32[]{:S(2)}, u32[]{:S(2)}) collective-permute-start(bf16[608,384]{1,0:T(8,128)(2,1)S(1)} %get-tuple-element.25), channel_id=1, source_target_pairs={{0,0},{1,2},{2,1},{3,4},{4,3},{5,6},{6,5},{7,7},{8,8},{9,10},{10,9... | collective-permute-start | bytes 1400840 | tf_op jit(solution)/shard_map/ppermute | solution.py:565
  5.4 0.0 slice-done
  5.4 0.0 slice-done.1
  5.4 0.1 copy-done.3
  5.5 0.0 copy-done.6
  5.5 5.4 %shard_map.101 = (f32[8,160,384]{2,1,0:T(8,128)S(1)}, bf16[480,384]{1,0:T(8,128)(2,1)S(1)}, bf16[480,384]{1,0:T(8,128)(2,1)S(1)}, bf16[3456,384]{1,0:T(8,128)(2,...) custom-call(s32[4]{0:T(128)S(1)} %get-tuple-element.20.info, ...), custom_call_target="tpu_custom_call" | custom-call | flops 4000000000 | bytes 1048576 | tf_op jit(solution)/shard_map/pallas_call | solution.py:569
  11.0 4.0 %collective-permute-start.2 = (bf16[480,384]{1,0:T(8,128)(2,1)S(1)}, bf16[480,384]{1,0:T(8,128)(2,1)S(1)}, u32[]{:S(2)}, u32[]{:S(2)}) collective-permute-start(bf16[480,384]{1,0:T(8,128)(2,1)S(1)} %get-tuple-element.29), channel_id=1, source_target_pairs={{0,1},{1,0},{2,3},{3,2},{4,5},{5,4},{6,7},{7,6},{8,9},{9,8},{10,11... | collective-permute-start | bytes 1105928 | tf_op jit(solution)/shard_map/ppermute | solution.py:577
  15.0 0.7 %collective-permute-start.3 = (bf16[480,384]{1,0:T(8,128)(2,1)S(1)}, bf16[480,384]{1,0:T(8,128)(2,1)S(1)}, u32[]{:S(2)}, u32[]{:S(2)}) collective-permute-start(bf16[480,384]{1,0:T(8,128)(2,1)S(1)} %get-tuple-element.30), channel_id=1, source_target_pairs={{0,0},{1,2},{2,1},{3,4},{4,3},{5,6},{6,5},{7,7},{8,8},{9,10},{10,9... | collective-permute-start | bytes 1105928 | tf_op jit(solution)/shard_map/ppermute | solution.py:578
  15.7 0.0 copy-done.7
  15.7 0.0 copy-done
  15.8 0.0 copy-done.8
  15.8 0.1 maximum_multiply_fusion.half_out
  15.9 0.0 collective-permute-done.got_even.packed_even
  15.9 0.0 collective-permute-done.1.got_odd.packed_odd
  15.9 6.7 %shard_map.103 = (bf16[10,160,384]{2,1,0:T(8,128)(2,1)S(1)}, f32[8,160,384]{2,1,0:T(8,128)S(1)}) custom-call(s32[4]{0:T(128)S(1)} %get-tuple-element.20.info, bf16[4,16,160]{2,1,0:T(8,128)(2,1)S(1)} %bitcast.27, bf16[2,4,16,160]{3,2,1,0:T(8,128)(2,1)S(1)} %bitcast.25, bf16[608,384]{1,0:T(8,128)(2,1)S(1)} %collective-permute-done.got_even.packed_even, ...), custom_call_target="tpu_custom_call" | custom-call | flops 5000000000 | bytes 1048576 | tf_op jit(solution)/shard_map/pallas_call | solution.py:580
  22.6 0.0 collective-permute-done.2.got_even
  22.6 0.0 collective-permute-done.3.got_odd
  22.6 13.1 %shard_map.104 = bf16[8,16,128]{2,1,0:T(8,128)(2,1)S(1)} custom-call(s32[4]{0:T(128)S(1)} %get-tuple-element.20.info, bf16[10,160,384]{2,1,0:T(8,128)(2,1)S(1)} %get-tuple-element.26.hidden, f32[8,160,384]{2,1,0:T(8,128)S(1)} %get-tuple-element.27.conv, f32[8,160,384]{2,1,0:T(8,128)S(1)} %get-tuple-element.28.acc, ...), custom_call_target="tpu_custom_call" | custom-call | flops 8000000000 | bytes 1048576 | tf_op jit(solution)/shard_map/pallas_call | solution.py:594
  35.7 11.7 %all_to_all.5.got = bf16[8,16,128]{2,1,0:T(8,128)(2,1)S(1)} all-to-all(bf16[8,16,128]{2,1,0:T(8,128)(2,1)S(1)} %shard_map.104), channel_id=1, replica_groups=mesh['prompt'=4,'tile'=8] {'tile'}, dimensions={0} | all-to-all | bytes 65536 | tf_op jit(solution)/shard_map/all_to_all | solution.py:621
  47.4 1.0 %shard_map.105 = f32[64,160]{1,0:T(8,128)} custom-call(bf16[4,256,640]{2,1,0:T(8,128)(2,1)S(1)} %get-tuple-element.23.sel, bf16[8,16,128]{2,1,0:T(8,128)(2,1)S(1)} %all_to_all.5.got), custom_call_target="tpu_custom_call" | custom-call | flops 10000000 | bytes 1048576 | tf_op jit(solution)/shard_map/pallas_call | solution.py:622
  (12 shorter events, 0.0 us)
Async XLA Ops:
  0.1 1.3 %copy-start.1 = (bf16[3,3,384,192]{2,3,1,0:T(8,128)(2,1)S(1)}, bf16[3,3,384,192]{2,3,1,0:T(8,128)(2,1)}, u32[]{:S(2)}) copy-start(bf16[3,3,384,192]{2,3,1,0:T(8,128)(2,1)} %param.16) | copy-start | bytes 3981316
  1.4 1.3 %copy-start.2 = (bf16[8,320,192]{1,2,0:T(8,128)(2,1)S(1)}, bf16[8,320,192]{1,2,0:T(8,128)(2,1)}, u32[]{:S(2)}) copy-start(bf16[8,320,192]{1,2,0:T(8,128)(2,1)} %param.13) | copy-start | bytes 2949124
  1.4 1.3 %copy-start.4 = (bf16[2,4,160,16]{2,3,1,0:T(8,128)(2,1)S(1)}, bf16[2,4,160,16]{2,3,1,0:T(8,128)(2,1)}, u32[]{:S(2)}) copy-start(bf16[2,4,160,16]{2,3,1,0:T(8,128)(2,1)} %param.11) | copy-start | bytes 122884
  1.4 1.3 %copy-start.5 = (bf16[4,160,16]{1,2,0:T(8,128)(2,1)S(1)}, bf16[4,160,16]{1,2,0:T(8,128)(2,1)}, u32[]{:S(2)}) copy-start(bf16[4,160,16]{1,2,0:T(8,128)(2,1)} %param.10) | copy-start | bytes 61444
  1.4 4.0 %slice-start = ((s8[7962624]{0:T(1024)(128)(4,1)}), s8[4194304]{0:T(1024)(128)(4,1)S(1)}, s32[]{:S(2)}) async-start(s8[7962624]{0:T(1024)(128)(4,1)} %bitcast.17), calls=%async_computation.1 | async-start | bytes 8388608
  2.7 2.7 %slice-start.1 = ((s8[7962624]{0:T(1024)(128)(4,1)}), s8[3768320]{0:T(1024)(128)(4,1)S(1)}, s32[]{:S(2)}) async-start(s8[7962624]{0:T(1024)(128)(4,1)} %bitcast.17), calls=%async_computation.2 | async-start | bytes 7536640
  2.7 2.8 %copy-start.3 = (bf16[2,4,160,384]{3,2,1,0:T(8,128)(2,1)S(1)}, bf16[2,4,160,384]{3,2,1,0:T(8,128)(2,1)}, u32[]{:S(2)}) copy-start(bf16[2,4,160,384]{3,2,1,0:T(8,128)(2,1)} %features.1) | copy-start | bytes 2949124
  2.7 2.8 %copy-start.6 = (s32[8]{0:T(128)S(1)}, s32[8]{0:T(128)}, u32[]{:S(2)}) copy-start(s32[8]{0:T(128)} %order.1) | copy-start | bytes 100
  4.2 11.7 %collective-permute-start = (bf16[608,384]{1,0:T(8,128)(2,1)S(1)}, bf16[608,384]{1,0:T(8,128)(2,1)S(1)}, u32[]{:S(2)}, u32[]{:S(2)}) collective-permute-start(bf16[608,384]{1,0:T(8,128)(2,1)S(1)} %get-tuple-element.24), channel_id=1, source_target_pairs={{0,1},{1,0},{2,3},{3,2},{4,5},{5,4},{6,7},{7,6},{8,9},{9,8},{10,11... | collective-permute-start | bytes 1400840 | tf_op jit(solution)/shard_map/ppermute | solution.py:564
  4.7 11.2 %collective-permute-start.1 = (bf16[608,384]{1,0:T(8,128)(2,1)S(1)}, bf16[608,384]{1,0:T(8,128)(2,1)S(1)}, u32[]{:S(2)}, u32[]{:S(2)}) collective-permute-start(bf16[608,384]{1,0:T(8,128)(2,1)S(1)} %get-tuple-element.25), channel_id=1, source_target_pairs={{0,0},{1,2},{2,1},{3,4},{4,3},{5,6},{6,5},{7,7},{8,8},{9,10},{10,9... | collective-permute-start | bytes 1400840 | tf_op jit(solution)/shard_map/ppermute | solution.py:565
  5.5 10.2 %copy-start.7 = (f32[384]{0:T(512)S(1)}, f32[384]{0:T(512)}, u32[]{:S(2)}) copy-start(f32[384]{0:T(512)} %param.17) | copy-start | bytes 4612
  5.5 10.2 %copy-start = (bf16[3,3,3,16,384]{4,3,2,1,0:T(8,128)(2,1)S(1)}, bf16[3,3,3,16,384]{4,3,2,1,0:T(8,128)(2,1)}, u32[]{:S(2)}) copy-start(bf16[3,3,3,16,384]{4,3,2,1,0:T(8,128)(2,1)} %param.14) | copy-start | bytes 995332
  5.5 10.2 %copy-start.8 = (f32[192]{0:T(256)S(1)}, f32[192]{0:T(256)}, u32[]{:S(2)}) copy-start(f32[192]{0:T(256)} %param.18) | copy-start | bytes 2308
  11.0 11.6 %collective-permute-start.2 = (bf16[480,384]{1,0:T(8,128)(2,1)S(1)}, bf16[480,384]{1,0:T(8,128)(2,1)S(1)}, u32[]{:S(2)}, u32[]{:S(2)}) collective-permute-start(bf16[480,384]{1,0:T(8,128)(2,1)S(1)} %get-tuple-element.29), channel_id=1, source_target_pairs={{0,1},{1,0},{2,3},{3,2},{4,5},{5,4},{6,7},{7,6},{8,9},{9,8},{10,11... | collective-permute-start | bytes 1105928 | tf_op jit(solution)/shard_map/ppermute | solution.py:577
  15.0 7.6 %collective-permute-start.3 = (bf16[480,384]{1,0:T(8,128)(2,1)S(1)}, bf16[480,384]{1,0:T(8,128)(2,1)S(1)}, u32[]{:S(2)}, u32[]{:S(2)}) collective-permute-start(bf16[480,384]{1,0:T(8,128)(2,1)S(1)} %get-tuple-element.30), channel_id=1, source_target_pairs={{0,0},{1,2},{2,1},{3,4},{4,3},{5,6},{6,5},{7,7},{8,8},{9,10},{10,9... | collective-permute-start | bytes 1105928 | tf_op jit(solution)/shard_map/ppermute | solution.py:578

commit v16 on v14

--- a/solution.py
+++ b/solution.py
@@ -174,22 +174,27 @@
                 for lanes in range(0, 384, 128):
                     x = features[t, r, :, lanes : lanes + 128].astype(F32)
                     beside(wide.at[r * cols : (r + 1) * cols], t * 1152, lanes, x, False)
-        def product(i, lanes):
-            parts[i, :, lanes] = mm(wide[...], jnp.concatenate([mid[0, i, :, lanes], mid[1, i, :, lanes]], axis=0))
-
-        def double():
+        def product(r, i, lanes):
+            at = slice(r * cols, (r + 1) * cols)
+            parts[i, at, lanes] = mm(wide[at], jnp.concatenate([mid[0, i, :, lanes], mid[1, i, :, lanes]], axis=0))
+
+        def double(r):
+            at = slice(r * cols, (r + 1) * cols)
             left = jnp.concatenate([mid[0, 0, :, 256:384], mid[1, 0, :, 256:384]], axis=0)
             right = jnp.concatenate([mid[0, 1, :, 256:384], mid[1, 1, :, 256:384]], axis=0)
-            both = mm(wide[...], jnp.concatenate([left, right], axis=1))
-            parts[0, :, 256:384] = both[:, :128]
-            parts[1, :, 256:384] = both[:, 128:]
+            both = mm(wide[at], jnp.concatenate([left, right], axis=1))
+            parts[0, at, 256:384] = both[:, :128]
+            parts[1, at, 256:384] = both[:, 128:]
 
         def turn(i, j):
             at = (i * 3 + j) * 384
             mid_t[at : at + 384] = mid[2, i, j * 384 : (j + 1) * 384].T
 
         most, rest = slice(0, 256), slice(256, 384)
-        products = steps(product, (0, most), (1, most)) + steps(double, ()) + steps(product, (2, most), (2, rest))
+        products = []
+        for r in range(rows):
+            products += steps(product, (r, 0, most), (r, 1, most)) + steps(double, (r,))
+            products += steps(product, (r, 2, most), (r, 2, rest))
         one = picker(cols, o)
         others = steps(turn, *[(i, j) for i in range(3) for j in range(3)])
         others += turning(back_odd, back_even, fwd)
@@ -283,10 +288,10 @@
         for k in range(4):
             hidden_row(k)
         for p in range(0, rows + 4, 2):
-            conv_rows(p, 2)
-            for k in (p + 4, p + 5):
-                if k < rows + 6:
-                    hidden_row(k)
+            for k in (p, p + 1):
+                conv_rows(k, 1)
+                if k + 4 < rows + 6:
+                    hidden_row(k + 4)
         both = mm(
             wide[0 : rows + 5].reshape((rows + 5) * cols, 1152),
             jnp.concatenate([mid[2, 0, :, 256:384], mid[2, 1, :, 256:384]], axis=1),
@@ -443,8 +448,9 @@
             down_rows(0 if odd else 1, fine - 1 if odd else fine, odd, 2)
         for k in range(rows + 2):
             block_row(k)
-        lhs = [back[2 - i : 2 - i + rows].reshape(size, 1152) for i in range(3)]
-        act_grad[:, :, 0:256] = mm(jnp.concatenate(lhs, axis=1), mid_t[:, 0:256]).reshape(rows, cols, 256)
+        for p in range(rows):
+            lhs = jnp.concatenate([back[p + 2], back[p + 1], back[p]], axis=1)
+            act_grad[p, :, 0:256] = mm(lhs, mid_t[:, 0:256])
         both = mm(
             back[1 : rows + 2].reshape((rows + 1) * cols, 1152),
             jnp.concatenate([mid_t[1152:2304, 256:384], mid_t[0:1152, 256:384]], axis=1),

time: 48.1 us -> 48.7 us (1.012)
  Pallas kernels: 28.3 us -> 28.9 us
  transfers between devices with their start and end apart: 4 -> 4, of which waited for: 0 -> 0; matrix products, arithmetic and copies ran while one was open for 0% -> 0% of each run, Pallas kernels for 25% -> 27%
where the time goes in v16:
time: 48.7 us; the launch traced here: 48.5 us
  Pallas kernels  28.9 us (59%)
  blocking collectives  11.7 us (24%)
  starting transfers between devices  5.95 us (12%)
  local copies, waits for them, and re-layouts  1.58 us (3%)
    pallas_call x1, Pallas kernels, shards(): call(back_body(rows, cols, chan, count, o), [((count, chan, 128), BF16)],...  12.5 us
    all_to_all x1, blocking collectives, shards(): lax.all_to_all(payload, 'tile', split_axis=0, concat_axis=0, tiled=True)  11.7 us
    pallas_call x1, Pallas kernels, shards(): call(current_body(rows, cols, chan), [((rows + 6, cols, 384), BF16), ((ro...  7.06 us
    pallas_call x1, Pallas kernels, shards(): call(cached_body(rows, cols, count, width, tokens, o), [((rows + 4, cols,...  5.83 us
    ppermute x1, starting transfers between devices, shards(): got_even = lax.ppermute(part_even, 'tile', within)  4.05 us
    unnamed x22, local copies, waits for them, and re-layouts  1.56 us
    pallas_call x1, Pallas kernels, shards(): call(pack_body(rows, cols, o, chan), [((6, cols, 384), BF16), ((edge_rows...  1.45 us
    pallas_call x1, Pallas kernels, shards(): call(taps_body, [((4,), jnp.int32), ((768, 768), BF16), ((768, 768), BF16...  1.15 us
  transfers between devices with their start and end apart: 4, of which 0 were waited for; matrix products, arithmetic and copies ran while one was open for 0% of the time, Pallas kernels for 27%

profile of v16, /device:TPU:0, one launch (start us, length us, event | category | flops | bytes accessed | tf_op | source)
XLA Modules:
  0.0 48.5 jit_solution(4229985154103316448)
XLA Ops:
  0.0 0.1 pad_add_fusion.info
  0.1 0.0 copy-start.1
  0.1 1.3 %copy-done.1 = bf16[3,3,384,192]{2,3,1,0:T(8,128)(2,1)S(1)} copy-done((bf16[3,3,384,192]{2,3,1,0:T(8,128)(2,1)S(1)}, bf16[3,3,384,192]{2,3,1,0:T(8,128)(2,1)}, u32[]{:S(2)}) %copy-start.1) | copy-done | bytes 1327128
  1.4 0.0 copy-start.2
  1.4 0.0 copy-start.4
  1.4 1.1 %shard_map.100 = (s32[4]{0:T(128)S(1)}, bf16[768,768]{1,0:T(8,128)(2,1)S(1)}, bf16[768,768]{1,0:T(8,128)(2,1)S(1)}) custom-call(s32[4]{0:T(128)S(1)} %pad_add_fusion.info, bf16[3,3,192,384]{3,2,1,0:T(8,128)(2,1)S(1)} %bitcast.21), custom_call_target="tpu_custom_call" | custom-call | flops 10000000000 | bytes 1048576 | tf_op jit(solution)/shard_map/pallas_call | solution.py:560
  2.6 0.1 copy-done.2
  2.7 0.0 copy-done.4
  2.7 0.0 copy-done.5
  2.7 0.0 copy-start.6
  2.7 1.5 %shard_map.102 = (bf16[6,160,384]{2,1,0:T(8,128)(2,1)S(1)}, bf16[608,384]{1,0:T(8,128)(2,1)S(1)}, bf16[608,384]{1,0:T(8,128)(2,1)S(1)}) custom-call(s32[4]{0:T(128)S(1)} %get-tuple-element.20.info, bf16[8,192,320]{2,1,0:T(8,128)(2,1)S(1)} %bitcast.22, bf16[4,16,160]{2,1,0:T(8,128)(2,1)S(1)} %bitcast.26, bf16[2,4,16,160]{3,2,1,0:T(8,128)(2,1)S(1)} %bitcast.24), custom_call_target="tpu_custom_call" | custom-call | flops 10000000000 | bytes 1048576 | tf_op jit(solution)/shard_map/pallas_call | solution.py:566
  4.2 0.5 %collective-permute-start = (bf16[608,384]{1,0:T(8,128)(2,1)S(1)}, bf16[608,384]{1,0:T(8,128)(2,1)S(1)}, u32[]{:S(2)}, u32[]{:S(2)}) collective-permute-start(bf16[608,384]{1,0:T(8,128)(2,1)S(1)} %get-tuple-element.24), channel_id=1, source_target_pairs={{0,1},{1,0},{2,3},{3,2},{4,5},{5,4},{6,7},{7,6},{8,9},{9,8},{10,11... | collective-permute-start | bytes 1400840 | tf_op jit(solution)/shard_map/ppermute | solution.py:571
  4.7 0.7 %collective-permute-start.1 = (bf16[608,384]{1,0:T(8,128)(2,1)S(1)}, bf16[608,384]{1,0:T(8,128)(2,1)S(1)}, u32[]{:S(2)}, u32[]{:S(2)}) collective-permute-start(bf16[608,384]{1,0:T(8,128)(2,1)S(1)} %get-tuple-element.25), channel_id=1, source_target_pairs={{0,0},{1,2},{2,1},{3,4},{4,3},{5,6},{6,5},{7,7},{8,8},{9,10},{10,9... | collective-permute-start | bytes 1400840 | tf_op jit(solution)/shard_map/ppermute | solution.py:572
  5.4 0.0 slice-done
  5.4 0.0 slice-done.1
  5.4 0.1 copy-done.3
  5.5 0.0 copy-done.6
  5.5 5.8 %shard_map.101 = (f32[8,160,384]{2,1,0:T(8,128)S(1)}, bf16[480,384]{1,0:T(8,128)(2,1)S(1)}, bf16[480,384]{1,0:T(8,128)(2,1)S(1)}, bf16[3456,384]{1,0:T(8,128)(2,...) custom-call(s32[4]{0:T(128)S(1)} %get-tuple-element.20.info, ...), custom_call_target="tpu_custom_call" | custom-call | flops 4000000000 | bytes 1048576 | tf_op jit(solution)/shard_map/pallas_call | solution.py:576
  11.4 4.0 %collective-permute-start.2 = (bf16[480,384]{1,0:T(8,128)(2,1)S(1)}, bf16[480,384]{1,0:T(8,128)(2,1)S(1)}, u32[]{:S(2)}, u32[]{:S(2)}) collective-permute-start(bf16[480,384]{1,0:T(8,128)(2,1)S(1)} %get-tuple-element.29), channel_id=1, source_target_pairs={{0,1},{1,0},{2,3},{3,2},{4,5},{5,4},{6,7},{7,6},{8,9},{9,8},{10,11... | collective-permute-start | bytes 1105928 | tf_op jit(solution)/shard_map/ppermute | solution.py:584
  15.4 0.7 %collective-permute-start.3 = (bf16[480,384]{1,0:T(8,128)(2,1)S(1)}, bf16[480,384]{1,0:T(8,128)(2,1)S(1)}, u32[]{:S(2)}, u32[]{:S(2)}) collective-permute-start(bf16[480,384]{1,0:T(8,128)(2,1)S(1)} %get-tuple-element.30), channel_id=1, source_target_pairs={{0,0},{1,2},{2,1},{3,4},{4,3},{5,6},{6,5},{7,7},{8,8},{9,10},{10,9... | collective-permute-start | bytes 1105928 | tf_op jit(solution)/shard_map/ppermute | solution.py:585
  16.1 0.0 copy-done.7
  16.1 0.0 copy-done
  16.2 0.0 copy-done.8
  16.2 0.1 maximum_multiply_fusion.half_out
  16.3 0.0 collective-permute-done.got_even.packed_even
  16.3 0.0 collective-permute-done.1.got_odd.packed_odd
  16.3 7.1 %shard_map.103 = (bf16[10,160,384]{2,1,0:T(8,128)(2,1)S(1)}, f32[8,160,384]{2,1,0:T(8,128)S(1)}) custom-call(s32[4]{0:T(128)S(1)} %get-tuple-element.20.info, bf16[4,16,160]{2,1,0:T(8,128)(2,1)S(1)} %bitcast.27, bf16[2,4,16,160]{3,2,1,0:T(8,128)(2,1)S(1)} %bitcast.25, bf16[608,384]{1,0:T(8,128)(2,1)S(1)} %collective-permute-done.got_even.packed_even, ...), custom_call_target="tpu_custom_call" | custom-call | flops 5000000000 | bytes 1048576 | tf_op jit(solution)/shard_map/pallas_call | solution.py:587
  23.3 0.0 collective-permute-done.2.got_even
  23.3 0.0 collective-permute-done.3.got_odd
  23.4 12.5 %shard_map.104 = bf16[8,16,128]{2,1,0:T(8,128)(2,1)S(1)} custom-call(s32[4]{0:T(128)S(1)} %get-tuple-element.20.info, bf16[10,160,384]{2,1,0:T(8,128)(2,1)S(1)} %get-tuple-element.26.hidden, f32[8,160,384]{2,1,0:T(8,128)S(1)} %get-tuple-element.27.conv, f32[8,160,384]{2,1,0:T(8,128)S(1)} %get-tuple-element.28.acc, ...), custom_call_target="tpu_custom_call" | custom-call | flops 8000000000 | bytes 1048576 | tf_op jit(solution)/shard_map/pallas_call | solution.py:601
  35.8 11.7 %all_to_all.5.got = bf16[8,16,128]{2,1,0:T(8,128)(2,1)S(1)} all-to-all(bf16[8,16,128]{2,1,0:T(8,128)(2,1)S(1)} %shard_map.104), channel_id=1, replica_groups=mesh['prompt'=4,'tile'=8] {'tile'}, dimensions={0} | all-to-all | bytes 65536 | tf_op jit(solution)/shard_map/all_to_all | solution.py:627
  47.5 1.0 %shard_map.105 = f32[64,160]{1,0:T(8,128)} custom-call(bf16[4,256,640]{2,1,0:T(8,128)(2,1)S(1)} %get-tuple-element.23.sel, bf16[8,16,128]{2,1,0:T(8,128)(2,1)S(1)} %all_to_all.5.got), custom_call_target="tpu_custom_call" | custom-call | flops 10000000 | bytes 1048576 | tf_op jit(solution)/shard_map/pallas_call | solution.py:628
  (12 shorter events, 0.0 us)
Async XLA Ops:
  0.1 1.3 %copy-start.1 = (bf16[3,3,384,192]{2,3,1,0:T(8,128)(2,1)S(1)}, bf16[3,3,384,192]{2,3,1,0:T(8,128)(2,1)}, u32[]{:S(2)}) copy-start(bf16[3,3,384,192]{2,3,1,0:T(8,128)(2,1)} %param.16) | copy-start | bytes 3981316
  1.4 1.3 %copy-start.2 = (bf16[8,320,192]{1,2,0:T(8,128)(2,1)S(1)}, bf16[8,320,192]{1,2,0:T(8,128)(2,1)}, u32[]{:S(2)}) copy-start(bf16[8,320,192]{1,2,0:T(8,128)(2,1)} %param.13) | copy-start | bytes 2949124
  1.4 1.3 %copy-start.4 = (bf16[2,4,160,16]{2,3,1,0:T(8,128)(2,1)S(1)}, bf16[2,4,160,16]{2,3,1,0:T(8,128)(2,1)}, u32[]{:S(2)}) copy-start(bf16[2,4,160,16]{2,3,1,0:T(8,128)(2,1)} %param.11) | copy-start | bytes 122884
  1.4 1.3 %copy-start.5 = (bf16[4,160,16]{1,2,0:T(8,128)(2,1)S(1)}, bf16[4,160,16]{1,2,0:T(8,128)(2,1)}, u32[]{:S(2)}) copy-start(bf16[4,160,16]{1,2,0:T(8,128)(2,1)} %param.10) | copy-start | bytes 61444
  1.4 4.0 %slice-start = ((s8[7962624]{0:T(1024)(128)(4,1)}), s8[4194304]{0:T(1024)(128)(4,1)S(1)}, s32[]{:S(2)}) async-start(s8[7962624]{0:T(1024)(128)(4,1)} %bitcast.17), calls=%async_computation.1 | async-start | bytes 8388608
  2.7 2.7 %slice-start.1 = ((s8[7962624]{0:T(1024)(128)(4,1)}), s8[3768320]{0:T(1024)(128)(4,1)S(1)}, s32[]{:S(2)}) async-start(s8[7962624]{0:T(1024)(128)(4,1)} %bitcast.17), calls=%async_computation.2 | async-start | bytes 7536640
  2.7 2.8 %copy-start.3 = (bf16[2,4,160,384]{3,2,1,0:T(8,128)(2,1)S(1)}, bf16[2,4,160,384]{3,2,1,0:T(8,128)(2,1)}, u32[]{:S(2)}) copy-start(bf16[2,4,160,384]{3,2,1,0:T(8,128)(2,1)} %features.1) | copy-start | bytes 2949124
  2.7 2.8 %copy-start.6 = (s32[8]{0:T(128)S(1)}, s32[8]{0:T(128)}, u32[]{:S(2)}) copy-start(s32[8]{0:T(128)} %order.1) | copy-start | bytes 100
  4.2 12.1 %collective-permute-start = (bf16[608,384]{1,0:T(8,128)(2,1)S(1)}, bf16[608,384]{1,0:T(8,128)(2,1)S(1)}, u32[]{:S(2)}, u32[]{:S(2)}) collective-permute-start(bf16[608,384]{1,0:T(8,128)(2,1)S(1)} %get-tuple-element.24), channel_id=1, source_target_pairs={{0,1},{1,0},{2,3},{3,2},{4,5},{5,4},{6,7},{7,6},{8,9},{9,8},{10,11... | collective-permute-start | bytes 1400840 | tf_op jit(solution)/shard_map/ppermute | solution.py:571
  4.7 11.6 %collective-permute-start.1 = (bf16[608,384]{1,0:T(8,128)(2,1)S(1)}, bf16[608,384]{1,0:T(8,128)(2,1)S(1)}, u32[]{:S(2)}, u32[]{:S(2)}) collective-permute-start(bf16[608,384]{1,0:T(8,128)(2,1)S(1)} %get-tuple-element.25), channel_id=1, source_target_pairs={{0,0},{1,2},{2,1},{3,4},{4,3},{5,6},{6,5},{7,7},{8,8},{9,10},{10,9... | collective-permute-start | bytes 1400840 | tf_op jit(solution)/shard_map/ppermute | solution.py:572
  5.5 10.6 %copy-start.7 = (f32[384]{0:T(512)S(1)}, f32[384]{0:T(512)}, u32[]{:S(2)}) copy-start(f32[384]{0:T(512)} %param.17) | copy-start | bytes 4612
  5.5 10.6 %copy-start = (bf16[3,3,3,16,384]{4,3,2,1,0:T(8,128)(2,1)S(1)}, bf16[3,3,3,16,384]{4,3,2,1,0:T(8,128)(2,1)}, u32[]{:S(2)}) copy-start(bf16[3,3,3,16,384]{4,3,2,1,0:T(8,128)(2,1)} %param.14) | copy-start | bytes 995332
  5.5 10.6 %copy-start.8 = (f32[192]{0:T(256)S(1)}, f32[192]{0:T(256)}, u32[]{:S(2)}) copy-start(f32[192]{0:T(256)} %param.18) | copy-start | bytes 2308
  11.4 12.0 %collective-permute-start.2 = (bf16[480,384]{1,0:T(8,128)(2,1)S(1)}, bf16[480,384]{1,0:T(8,128)(2,1)S(1)}, u32[]{:S(2)}, u32[]{:S(2)}) collective-permute-start(bf16[480,384]{1,0:T(8,128)(2,1)S(1)} %get-tuple-element.29), channel_id=1, source_target_pairs={{0,1},{1,0},{2,3},{3,2},{4,5},{5,4},{6,7},{7,6},{8,9},{9,8},{10,11... | collective-permute-start | bytes 1105928 | tf_op jit(solution)/shard_map/ppermute | solution.py:584
  15.4 7.9 %collective-permute-start.3 = (bf16[480,384]{1,0:T(8,128)(2,1)S(1)}, bf16[480,384]{1,0:T(8,128)(2,1)S(1)}, u32[]{:S(2)}, u32[]{:S(2)}) collective-permute-start(bf16[480,384]{1,0:T(8,128)(2,1)S(1)} %get-tuple-element.30), channel_id=1, source_target_pairs={{0,0},{1,2},{2,1},{3,4},{4,3},{5,6},{6,5},{7,7},{8,8},{9,10},{10,9... | collective-permute-start | bytes 1105928 | tf_op jit(solution)/shard_map/ppermute | solution.py:585

commit v17 on v14

--- a/solution.py
+++ b/solution.py
@@ -428,19 +428,41 @@
                 hid[k, at] = (back[k + 1, at, 384:768].astype(F32) + dv).astype(BF16)
 
         fine = rows + 3
-        for k in range(rows + 4):
-            state_row(k)
-        for b in range(2):
-            up_rows(1, rows + 4, b, 0)
-            up_rows(0, rows + 3, b, 1)
-            up_rows(0, rows + 4, b, 2)
-        for k in range(fine):
-            pull_row(k, True)
-            pull_row(k, False)
-        for odd in (True, False):
-            down_rows(1 if odd else 0, fine if odd else fine - 1, odd, 0)
-            down_rows(0, fine, odd, 1)
-            down_rows(0 if odd else 1, fine - 1 if odd else fine, odd, 2)
+        def ups(first, last):
+            for b in range(2):
+                up_rows(max(first, 1), last, b, 0)
+                up_rows(first, min(last, rows + 3), b, 1)
+                up_rows(first, last, b, 2)
+
+        def downs(first, last):
+            for odd in (True, False):
+                down_rows(max(first, 1) if odd else first, last if odd else min(last, fine - 1), odd, 0)
+                down_rows(first, last, odd, 1)
+                down_rows(first if odd else max(first, 1), min(last, fine - 1) if odd else last, odd, 2)
+
+        def states(first, last):
+            for k in range(first, last):
+                state_row(k)
+
+        def pulls(first, last):
+            for k in range(first, last):
+                pull_row(k, True)
+                pull_row(k, False)
+
+        states(0, rows)
+        ups(0, 2)
+        states(rows, rows + 2)
+        ups(2, rows)
+        states(rows + 2, rows + 4)
+        ups(rows, rows + 2)
+        pulls(0, 2)
+        ups(rows + 2, rows + 4)
+        pulls(2, rows)
+        downs(0, 2)
+        pulls(rows, rows + 2)
+        downs(2, rows)
+        pulls(rows + 2, fine)
+        downs(rows, fine)
         for k in range(rows + 2):
             block_row(k)
         lhs = [back[2 - i : 2 - i + rows].reshape(size, 1152) for i in range(3)]

time: 48.1 us -> 47.6 us (0.990)
  Pallas kernels: 28.3 us -> 27.8 us
  transfers between devices with their start and end apart: 4 -> 4, of which waited for: 0 -> 0; matrix products, arithmetic and copies ran while one was open for 0% -> 0% of each run, Pallas kernels for 25% -> 26%
where the time goes in v17:
time: 47.6 us; the launch traced here: 47.4 us
  Pallas kernels  27.8 us (58%)
  blocking collectives  11.7 us (25%)
  starting transfers between devices  5.95 us (12%)
  local copies, waits for them, and re-layouts  1.58 us (3%)
    pallas_call x1, Pallas kernels, shards(): call(back_body(rows, cols, chan, count, o), [((count, chan, 128), BF16)],...  12.1 us
    all_to_all x1, blocking collectives, shards(): lax.all_to_all(payload, 'tile', split_axis=0, concat_axis=0, tiled=True)  11.7 us
    pallas_call x1, Pallas kernels, shards(): call(current_body(rows, cols, chan), [((rows + 6, cols, 384), BF16), ((ro...  6.72 us
    pallas_call x1, Pallas kernels, shards(): call(cached_body(rows, cols, count, width, tokens, o), [((rows + 4, cols,...  5.43 us
    ppermute x1, starting transfers between devices, shards(): got_even = lax.ppermute(part_even, 'tile', within)  4.05 us
    unnamed x22, local copies, waits for them, and re-layouts  1.56 us
    pallas_call x1, Pallas kernels, shards(): call(pack_body(rows, cols, o, chan), [((6, cols, 384), BF16), ((edge_rows...  1.45 us
    pallas_call x1, Pallas kernels, shards(): call(taps_body, [((4,), jnp.int32), ((768, 768), BF16), ((768, 768), BF16...  1.15 us
  transfers between devices with their start and end apart: 4, of which 0 were waited for; matrix products, arithmetic and copies ran while one was open for 0% of the time, Pallas kernels for 26%

profile of v17, /device:TPU:0, one launch (start us, length us, event | category | flops | bytes accessed | tf_op | source)
XLA Modules:
  0.0 47.4 jit_solution(14336953335794179884)
XLA Ops:
  0.0 0.1 pad_add_fusion.info
  0.1 0.0 copy-start.1
  0.1 1.3 %copy-done.1 = bf16[3,3,384,192]{2,3,1,0:T(8,128)(2,1)S(1)} copy-done((bf16[3,3,384,192]{2,3,1,0:T(8,128)(2,1)S(1)}, bf16[3,3,384,192]{2,3,1,0:T(8,128)(2,1)}, u32[]{:S(2)}) %copy-start.1) | copy-done | bytes 1327128
  1.4 0.0 copy-start.2
  1.4 0.0 copy-start.4
  1.4 1.1 %shard_map.100 = (s32[4]{0:T(128)S(1)}, bf16[768,768]{1,0:T(8,128)(2,1)S(1)}, bf16[768,768]{1,0:T(8,128)(2,1)S(1)}) custom-call(s32[4]{0:T(128)S(1)} %pad_add_fusion.info, bf16[3,3,192,384]{3,2,1,0:T(8,128)(2,1)S(1)} %bitcast.21), custom_call_target="tpu_custom_call" | custom-call | flops 10000000000 | bytes 1048576 | tf_op jit(solution)/shard_map/pallas_call | solution.py:576
  2.6 0.1 copy-done.2
  2.7 0.0 copy-done.4
  2.7 0.0 copy-done.5
  2.7 0.0 copy-start.6
  2.7 1.5 %shard_map.102 = (bf16[6,160,384]{2,1,0:T(8,128)(2,1)S(1)}, bf16[608,384]{1,0:T(8,128)(2,1)S(1)}, bf16[608,384]{1,0:T(8,128)(2,1)S(1)}) custom-call(s32[4]{0:T(128)S(1)} %get-tuple-element.20.info, bf16[8,192,320]{2,1,0:T(8,128)(2,1)S(1)} %bitcast.22, bf16[4,16,160]{2,1,0:T(8,128)(2,1)S(1)} %bitcast.26, bf16[2,4,16,160]{3,2,1,0:T(8,128)(2,1)S(1)} %bitcast.24), custom_call_target="tpu_custom_call" | custom-call | flops 10000000000 | bytes 1048576 | tf_op jit(solution)/shard_map/pallas_call | solution.py:582
  4.2 0.5 %collective-permute-start = (bf16[608,384]{1,0:T(8,128)(2,1)S(1)}, bf16[608,384]{1,0:T(8,128)(2,1)S(1)}, u32[]{:S(2)}, u32[]{:S(2)}) collective-permute-start(bf16[608,384]{1,0:T(8,128)(2,1)S(1)} %get-tuple-element.24), channel_id=1, source_target_pairs={{0,1},{1,0},{2,3},{3,2},{4,5},{5,4},{6,7},{7,6},{8,9},{9,8},{10,11... | collective-permute-start | bytes 1400840 | tf_op jit(solution)/shard_map/ppermute | solution.py:587
  4.7 0.7 %collective-permute-start.1 = (bf16[608,384]{1,0:T(8,128)(2,1)S(1)}, bf16[608,384]{1,0:T(8,128)(2,1)S(1)}, u32[]{:S(2)}, u32[]{:S(2)}) collective-permute-start(bf16[608,384]{1,0:T(8,128)(2,1)S(1)} %get-tuple-element.25), channel_id=1, source_target_pairs={{0,0},{1,2},{2,1},{3,4},{4,3},{5,6},{6,5},{7,7},{8,8},{9,10},{10,9... | collective-permute-start | bytes 1400840 | tf_op jit(solution)/shard_map/ppermute | solution.py:588
  5.4 0.0 slice-done
  5.4 0.0 slice-done.1
  5.4 0.1 copy-done.3
  5.5 0.0 copy-done.6
  5.5 5.4 %shard_map.101 = (f32[8,160,384]{2,1,0:T(8,128)S(1)}, bf16[480,384]{1,0:T(8,128)(2,1)S(1)}, bf16[480,384]{1,0:T(8,128)(2,1)S(1)}, bf16[3456,384]{1,0:T(8,128)(2,...) custom-call(s32[4]{0:T(128)S(1)} %get-tuple-element.20.info, ...), custom_call_target="tpu_custom_call" | custom-call | flops 4000000000 | bytes 1048576 | tf_op jit(solution)/shard_map/pallas_call | solution.py:592
  11.0 4.0 %collective-permute-start.2 = (bf16[480,384]{1,0:T(8,128)(2,1)S(1)}, bf16[480,384]{1,0:T(8,128)(2,1)S(1)}, u32[]{:S(2)}, u32[]{:S(2)}) collective-permute-start(bf16[480,384]{1,0:T(8,128)(2,1)S(1)} %get-tuple-element.29), channel_id=1, source_target_pairs={{0,1},{1,0},{2,3},{3,2},{4,5},{5,4},{6,7},{7,6},{8,9},{9,8},{10,11... | collective-permute-start | bytes 1105928 | tf_op jit(solution)/shard_map/ppermute | solution.py:600
  15.0 0.7 %collective-permute-start.3 = (bf16[480,384]{1,0:T(8,128)(2,1)S(1)}, bf16[480,384]{1,0:T(8,128)(2,1)S(1)}, u32[]{:S(2)}, u32[]{:S(2)}) collective-permute-start(bf16[480,384]{1,0:T(8,128)(2,1)S(1)} %get-tuple-element.30), channel_id=1, source_target_pairs={{0,0},{1,2},{2,1},{3,4},{4,3},{5,6},{6,5},{7,7},{8,8},{9,10},{10,9... | collective-permute-start | bytes 1105928 | tf_op jit(solution)/shard_map/ppermute | solution.py:601
  15.7 0.0 copy-done.7
  15.7 0.0 copy-done
  15.8 0.0 copy-done.8
  15.8 0.1 maximum_multiply_fusion.half_out
  15.9 0.0 collective-permute-done.got_even.packed_even
  15.9 0.0 collective-permute-done.1.got_odd.packed_odd
  15.9 6.7 %shard_map.103 = (bf16[10,160,384]{2,1,0:T(8,128)(2,1)S(1)}, f32[8,160,384]{2,1,0:T(8,128)S(1)}) custom-call(s32[4]{0:T(128)S(1)} %get-tuple-element.20.info, bf16[4,16,160]{2,1,0:T(8,128)(2,1)S(1)} %bitcast.27, bf16[2,4,16,160]{3,2,1,0:T(8,128)(2,1)S(1)} %bitcast.25, bf16[608,384]{1,0:T(8,128)(2,1)S(1)} %collective-permute-done.got_even.packed_even, ...), custom_call_target="tpu_custom_call" | custom-call | flops 5000000000 | bytes 1048576 | tf_op jit(solution)/shard_map/pallas_call | solution.py:603
  22.6 0.0 collective-permute-done.2.got_even
  22.6 0.0 collective-permute-done.3.got_odd
  22.6 12.1 %shard_map.104 = bf16[8,16,128]{2,1,0:T(8,128)(2,1)S(1)} custom-call(s32[4]{0:T(128)S(1)} %get-tuple-element.20.info, bf16[10,160,384]{2,1,0:T(8,128)(2,1)S(1)} %get-tuple-element.26.hidden, f32[8,160,384]{2,1,0:T(8,128)S(1)} %get-tuple-element.27.conv, f32[8,160,384]{2,1,0:T(8,128)S(1)} %get-tuple-element.28.acc, ...), custom_call_target="tpu_custom_call" | custom-call | flops 8000000000 | bytes 1048576 | tf_op jit(solution)/shard_map/pallas_call | solution.py:617
  34.7 11.7 %all_to_all.5.got = bf16[8,16,128]{2,1,0:T(8,128)(2,1)S(1)} all-to-all(bf16[8,16,128]{2,1,0:T(8,128)(2,1)S(1)} %shard_map.104), channel_id=1, replica_groups=mesh['prompt'=4,'tile'=8] {'tile'}, dimensions={0} | all-to-all | bytes 65536 | tf_op jit(solution)/shard_map/all_to_all | solution.py:643
  46.5 1.0 %shard_map.105 = f32[64,160]{1,0:T(8,128)} custom-call(bf16[4,256,640]{2,1,0:T(8,128)(2,1)S(1)} %get-tuple-element.23.sel, bf16[8,16,128]{2,1,0:T(8,128)(2,1)S(1)} %all_to_all.5.got), custom_call_target="tpu_custom_call" | custom-call | flops 10000000 | bytes 1048576 | tf_op jit(solution)/shard_map/pallas_call | solution.py:644
  (12 shorter events, 0.0 us)
Async XLA Ops:
  0.1 1.3 %copy-start.1 = (bf16[3,3,384,192]{2,3,1,0:T(8,128)(2,1)S(1)}, bf16[3,3,384,192]{2,3,1,0:T(8,128)(2,1)}, u32[]{:S(2)}) copy-start(bf16[3,3,384,192]{2,3,1,0:T(8,128)(2,1)} %param.16) | copy-start | bytes 3981316
  1.4 1.3 %copy-start.2 = (bf16[8,320,192]{1,2,0:T(8,128)(2,1)S(1)}, bf16[8,320,192]{1,2,0:T(8,128)(2,1)}, u32[]{:S(2)}) copy-start(bf16[8,320,192]{1,2,0:T(8,128)(2,1)} %param.13) | copy-start | bytes 2949124
  1.4 1.3 %copy-start.4 = (bf16[2,4,160,16]{2,3,1,0:T(8,128)(2,1)S(1)}, bf16[2,4,160,16]{2,3,1,0:T(8,128)(2,1)}, u32[]{:S(2)}) copy-start(bf16[2,4,160,16]{2,3,1,0:T(8,128)(2,1)} %param.11) | copy-start | bytes 122884
  1.4 1.3 %copy-start.5 = (bf16[4,160,16]{1,2,0:T(8,128)(2,1)S(1)}, bf16[4,160,16]{1,2,0:T(8,128)(2,1)}, u32[]{:S(2)}) copy-start(bf16[4,160,16]{1,2,0:T(8,128)(2,1)} %param.10) | copy-start | bytes 61444
  1.4 4.0 %slice-start = ((s8[7962624]{0:T(1024)(128)(4,1)}), s8[4194304]{0:T(1024)(128)(4,1)S(1)}, s32[]{:S(2)}) async-start(s8[7962624]{0:T(1024)(128)(4,1)} %bitcast.17), calls=%async_computation.1 | async-start | bytes 8388608
  2.7 2.7 %slice-start.1 = ((s8[7962624]{0:T(1024)(128)(4,1)}), s8[3768320]{0:T(1024)(128)(4,1)S(1)}, s32[]{:S(2)}) async-start(s8[7962624]{0:T(1024)(128)(4,1)} %bitcast.17), calls=%async_computation.2 | async-start | bytes 7536640
  2.7 2.8 %copy-start.3 = (bf16[2,4,160,384]{3,2,1,0:T(8,128)(2,1)S(1)}, bf16[2,4,160,384]{3,2,1,0:T(8,128)(2,1)}, u32[]{:S(2)}) copy-start(bf16[2,4,160,384]{3,2,1,0:T(8,128)(2,1)} %features.1) | copy-start | bytes 2949124
  2.7 2.8 %copy-start.6 = (s32[8]{0:T(128)S(1)}, s32[8]{0:T(128)}, u32[]{:S(2)}) copy-start(s32[8]{0:T(128)} %order.1) | copy-start | bytes 100
  4.2 11.7 %collective-permute-start = (bf16[608,384]{1,0:T(8,128)(2,1)S(1)}, bf16[608,384]{1,0:T(8,128)(2,1)S(1)}, u32[]{:S(2)}, u32[]{:S(2)}) collective-permute-start(bf16[608,384]{1,0:T(8,128)(2,1)S(1)} %get-tuple-element.24), channel_id=1, source_target_pairs={{0,1},{1,0},{2,3},{3,2},{4,5},{5,4},{6,7},{7,6},{8,9},{9,8},{10,11... | collective-permute-start | bytes 1400840 | tf_op jit(solution)/shard_map/ppermute | solution.py:587
  4.7 11.2 %collective-permute-start.1 = (bf16[608,384]{1,0:T(8,128)(2,1)S(1)}, bf16[608,384]{1,0:T(8,128)(2,1)S(1)}, u32[]{:S(2)}, u32[]{:S(2)}) collective-permute-start(bf16[608,384]{1,0:T(8,128)(2,1)S(1)} %get-tuple-element.25), channel_id=1, source_target_pairs={{0,0},{1,2},{2,1},{3,4},{4,3},{5,6},{6,5},{7,7},{8,8},{9,10},{10,9... | collective-permute-start | bytes 1400840 | tf_op jit(solution)/shard_map/ppermute | solution.py:588
  5.5 10.2 %copy-start.7 = (f32[384]{0:T(512)S(1)}, f32[384]{0:T(512)}, u32[]{:S(2)}) copy-start(f32[384]{0:T(512)} %param.17) | copy-start | bytes 4612
  5.5 10.2 %copy-start = (bf16[3,3,3,16,384]{4,3,2,1,0:T(8,128)(2,1)S(1)}, bf16[3,3,3,16,384]{4,3,2,1,0:T(8,128)(2,1)}, u32[]{:S(2)}) copy-start(bf16[3,3,3,16,384]{4,3,2,1,0:T(8,128)(2,1)} %param.14) | copy-start | bytes 995332
  5.5 10.2 %copy-start.8 = (f32[192]{0:T(256)S(1)}, f32[192]{0:T(256)}, u32[]{:S(2)}) copy-start(f32[192]{0:T(256)} %param.18) | copy-start | bytes 2308
  11.0 11.6 %collective-permute-start.2 = (bf16[480,384]{1,0:T(8,128)(2,1)S(1)}, bf16[480,384]{1,0:T(8,128)(2,1)S(1)}, u32[]{:S(2)}, u32[]{:S(2)}) collective-permute-start(bf16[480,384]{1,0:T(8,128)(2,1)S(1)} %get-tuple-element.29), channel_id=1, source_target_pairs={{0,1},{1,0},{2,3},{3,2},{4,5},{5,4},{6,7},{7,6},{8,9},{9,8},{10,11... | collective-permute-start | bytes 1105928 | tf_op jit(solution)/shard_map/ppermute | solution.py:600
  15.0 7.6 %collective-permute-start.3 = (bf16[480,384]{1,0:T(8,128)(2,1)S(1)}, bf16[480,384]{1,0:T(8,128)(2,1)S(1)}, u32[]{:S(2)}, u32[]{:S(2)}) collective-permute-start(bf16[480,384]{1,0:T(8,128)(2,1)S(1)} %get-tuple-element.30), channel_id=1, source_target_pairs={{0,0},{1,2},{2,1},{3,4},{4,3},{5,6},{6,5},{7,7},{8,8},{9,10},{10,9... | collective-permute-start | bytes 1105928 | tf_op jit(solution)/shard_map/ppermute | solution.py:601

commit v18 on v17

--- a/solution.py
+++ b/solution.py
@@ -449,6 +449,15 @@
                 pull_row(k, True)
                 pull_row(k, False)
 
+        def blocks(first, last):
+            for k in range(first, last):
+                block_row(k)
+
+        def mid_rows(p, number):
+            lhs = [back[p + 2 - i : p + 2 - i + number].reshape(number * cols, 1152) for i in range(3)]
+            total = mm(jnp.concatenate(lhs, axis=1), mid_t[:, 0:256])
+            act_grad[p : p + number, :, 0:256] = total.reshape(number, cols, 256)
+
         states(0, rows)
         ups(0, 2)
         states(rows, rows + 2)
@@ -462,11 +471,12 @@
         pulls(rows, rows + 2)
         downs(2, rows)
         pulls(rows + 2, fine)
+        blocks(0, rows - 1)
         downs(rows, fine)
-        for k in range(rows + 2):
-            block_row(k)
-        lhs = [back[2 - i : 2 - i + rows].reshape(size, 1152) for i in range(3)]
-        act_grad[:, :, 0:256] = mm(jnp.concatenate(lhs, axis=1), mid_t[:, 0:256]).reshape(rows, cols, 256)
+        blocks(rows - 1, rows)
+        mid_rows(0, 2)
+        blocks(rows, rows + 2)
+        mid_rows(2, rows - 2)
         both = mm(
             back[1 : rows + 2].reshape((rows + 1) * cols, 1152),
             jnp.concatenate([mid_t[1152:2304, 256:384], mid_t[0:1152, 256:384]], axis=1),

time: 47.6 us -> 47.7 us (level)
  no operation moved by 1% of the time
where the time goes in v18:
time: 47.7 us; the launch traced here: 47.5 us
  Pallas kernels  27.9 us (58%)
  blocking collectives  11.7 us (25%)
  starting transfers between devices  5.95 us (12%)
  local copies, waits for them, and re-layouts  1.58 us (3%)
    pallas_call x1, Pallas kernels, shards(): call(back_body(rows, cols, chan, count, o), [((count, chan, 128), BF16)],...  12.2 us
    all_to_all x1, blocking collectives, shards(): lax.all_to_all(payload, 'tile', split_axis=0, concat_axis=0, tiled=True)  11.7 us
    pallas_call x1, Pallas kernels, shards(): call(current_body(rows, cols, chan), [((rows + 6, cols, 384), BF16), ((ro...  6.72 us
    pallas_call x1, Pallas kernels, shards(): call(cached_body(rows, cols, count, width, tokens, o), [((rows + 4, cols,...  5.43 us
    ppermute x1, starting transfers between devices, shards(): got_even = lax.ppermute(part_even, 'tile', within)  4.05 us
    unnamed x22, local copies, waits for them, and re-layouts  1.56 us
    pallas_call x1, Pallas kernels, shards(): call(pack_body(rows, cols, o, chan), [((6, cols, 384), BF16), ((edge_rows...  1.45 us
    pallas_call x1, Pallas kernels, shards(): call(taps_body, [((4,), jnp.int32), ((768, 768), BF16), ((768, 768), BF16...  1.15 us
  transfers between devices with their start and end apart: 4, of which 0 were waited for; matrix products, arithmetic and copies ran while one was open for 0% of the time, Pallas kernels for 26%

profile of v18, /device:TPU:0, one launch (start us, length us, event | category | flops | bytes accessed | tf_op | source)
XLA Modules:
  0.0 47.5 jit_solution(5414369466826061937)
XLA Ops:
  0.0 0.1 pad_add_fusion.info
  0.1 0.0 copy-start.1
  0.1 1.3 %copy-done.1 = bf16[3,3,384,192]{2,3,1,0:T(8,128)(2,1)S(1)} copy-done((bf16[3,3,384,192]{2,3,1,0:T(8,128)(2,1)S(1)}, bf16[3,3,384,192]{2,3,1,0:T(8,128)(2,1)}, u32[]{:S(2)}) %copy-start.1) | copy-done | bytes 1327128
  1.4 0.0 copy-start.2
  1.4 0.0 copy-start.4
  1.4 1.1 %shard_map.100 = (s32[4]{0:T(128)S(1)}, bf16[768,768]{1,0:T(8,128)(2,1)S(1)}, bf16[768,768]{1,0:T(8,128)(2,1)S(1)}) custom-call(s32[4]{0:T(128)S(1)} %pad_add_fusion.info, bf16[3,3,192,384]{3,2,1,0:T(8,128)(2,1)S(1)} %bitcast.21), custom_call_target="tpu_custom_call" | custom-call | flops 10000000000 | bytes 1048576 | tf_op jit(solution)/shard_map/pallas_call | solution.py:586
  2.6 0.1 copy-done.2
  2.7 0.0 copy-done.4
  2.7 0.0 copy-done.5
  2.7 0.0 copy-start.6
  2.7 1.5 %shard_map.102 = (bf16[6,160,384]{2,1,0:T(8,128)(2,1)S(1)}, bf16[608,384]{1,0:T(8,128)(2,1)S(1)}, bf16[608,384]{1,0:T(8,128)(2,1)S(1)}) custom-call(s32[4]{0:T(128)S(1)} %get-tuple-element.20.info, bf16[8,192,320]{2,1,0:T(8,128)(2,1)S(1)} %bitcast.22, bf16[4,16,160]{2,1,0:T(8,128)(2,1)S(1)} %bitcast.26, bf16[2,4,16,160]{3,2,1,0:T(8,128)(2,1)S(1)} %bitcast.24), custom_call_target="tpu_custom_call" | custom-call | flops 10000000000 | bytes 1048576 | tf_op jit(solution)/shard_map/pallas_call | solution.py:592
  4.2 0.5 %collective-permute-start = (bf16[608,384]{1,0:T(8,128)(2,1)S(1)}, bf16[608,384]{1,0:T(8,128)(2,1)S(1)}, u32[]{:S(2)}, u32[]{:S(2)}) collective-permute-start(bf16[608,384]{1,0:T(8,128)(2,1)S(1)} %get-tuple-element.24), channel_id=1, source_target_pairs={{0,1},{1,0},{2,3},{3,2},{4,5},{5,4},{6,7},{7,6},{8,9},{9,8},{10,11... | collective-permute-start | bytes 1400840 | tf_op jit(solution)/shard_map/ppermute | solution.py:597
  4.7 0.7 %collective-permute-start.1 = (bf16[608,384]{1,0:T(8,128)(2,1)S(1)}, bf16[608,384]{1,0:T(8,128)(2,1)S(1)}, u32[]{:S(2)}, u32[]{:S(2)}) collective-permute-start(bf16[608,384]{1,0:T(8,128)(2,1)S(1)} %get-tuple-element.25), channel_id=1, source_target_pairs={{0,0},{1,2},{2,1},{3,4},{4,3},{5,6},{6,5},{7,7},{8,8},{9,10},{10,9... | collective-permute-start | bytes 1400840 | tf_op jit(solution)/shard_map/ppermute | solution.py:598
  5.4 0.0 slice-done
  5.4 0.0 slice-done.1
  5.4 0.1 copy-done.3
  5.5 0.0 copy-done.6
  5.5 5.4 %shard_map.101 = (f32[8,160,384]{2,1,0:T(8,128)S(1)}, bf16[480,384]{1,0:T(8,128)(2,1)S(1)}, bf16[480,384]{1,0:T(8,128)(2,1)S(1)}, bf16[3456,384]{1,0:T(8,128)(2,...) custom-call(s32[4]{0:T(128)S(1)} %get-tuple-element.20.info, ...), custom_call_target="tpu_custom_call" | custom-call | flops 4000000000 | bytes 1048576 | tf_op jit(solution)/shard_map/pallas_call | solution.py:602
  11.0 4.0 %collective-permute-start.2 = (bf16[480,384]{1,0:T(8,128)(2,1)S(1)}, bf16[480,384]{1,0:T(8,128)(2,1)S(1)}, u32[]{:S(2)}, u32[]{:S(2)}) collective-permute-start(bf16[480,384]{1,0:T(8,128)(2,1)S(1)} %get-tuple-element.29), channel_id=1, source_target_pairs={{0,1},{1,0},{2,3},{3,2},{4,5},{5,4},{6,7},{7,6},{8,9},{9,8},{10,11... | collective-permute-start | bytes 1105928 | tf_op jit(solution)/shard_map/ppermute | solution.py:610
  15.0 0.7 %collective-permute-start.3 = (bf16[480,384]{1,0:T(8,128)(2,1)S(1)}, bf16[480,384]{1,0:T(8,128)(2,1)S(1)}, u32[]{:S(2)}, u32[]{:S(2)}) collective-permute-start(bf16[480,384]{1,0:T(8,128)(2,1)S(1)} %get-tuple-element.30), channel_id=1, source_target_pairs={{0,0},{1,2},{2,1},{3,4},{4,3},{5,6},{6,5},{7,7},{8,8},{9,10},{10,9... | collective-permute-start | bytes 1105928 | tf_op jit(solution)/shard_map/ppermute | solution.py:611
  15.7 0.0 copy-done.7
  15.7 0.0 copy-done
  15.8 0.0 copy-done.8
  15.8 0.1 maximum_multiply_fusion.half_out
  15.9 0.0 collective-permute-done.got_even.packed_even
  15.9 0.0 collective-permute-done.1.got_odd.packed_odd
  15.9 6.7 %shard_map.103 = (bf16[10,160,384]{2,1,0:T(8,128)(2,1)S(1)}, f32[8,160,384]{2,1,0:T(8,128)S(1)}) custom-call(s32[4]{0:T(128)S(1)} %get-tuple-element.20.info, bf16[4,16,160]{2,1,0:T(8,128)(2,1)S(1)} %bitcast.27, bf16[2,4,16,160]{3,2,1,0:T(8,128)(2,1)S(1)} %bitcast.25, bf16[608,384]{1,0:T(8,128)(2,1)S(1)} %collective-permute-done.got_even.packed_even, ...), custom_call_target="tpu_custom_call" | custom-call | flops 5000000000 | bytes 1048576 | tf_op jit(solution)/shard_map/pallas_call | solution.py:613
  22.6 0.0 collective-permute-done.2.got_even
  22.6 0.0 collective-permute-done.3.got_odd
  22.6 12.2 %shard_map.104 = bf16[8,16,128]{2,1,0:T(8,128)(2,1)S(1)} custom-call(s32[4]{0:T(128)S(1)} %get-tuple-element.20.info, bf16[10,160,384]{2,1,0:T(8,128)(2,1)S(1)} %get-tuple-element.26.hidden, f32[8,160,384]{2,1,0:T(8,128)S(1)} %get-tuple-element.27.conv, f32[8,160,384]{2,1,0:T(8,128)S(1)} %get-tuple-element.28.acc, ...), custom_call_target="tpu_custom_call" | custom-call | flops 8000000000 | bytes 1048576 | tf_op jit(solution)/shard_map/pallas_call | solution.py:627
  34.8 11.7 %all_to_all.5.got = bf16[8,16,128]{2,1,0:T(8,128)(2,1)S(1)} all-to-all(bf16[8,16,128]{2,1,0:T(8,128)(2,1)S(1)} %shard_map.104), channel_id=1, replica_groups=mesh['prompt'=4,'tile'=8] {'tile'}, dimensions={0} | all-to-all | bytes 65536 | tf_op jit(solution)/shard_map/all_to_all | solution.py:653
  46.5 1.0 %shard_map.105 = f32[64,160]{1,0:T(8,128)} custom-call(bf16[4,256,640]{2,1,0:T(8,128)(2,1)S(1)} %get-tuple-element.23.sel, bf16[8,16,128]{2,1,0:T(8,128)(2,1)S(1)} %all_to_all.5.got), custom_call_target="tpu_custom_call" | custom-call | flops 10000000 | bytes 1048576 | tf_op jit(solution)/shard_map/pallas_call | solution.py:654
  (12 shorter events, 0.0 us)
Async XLA Ops:
  0.1 1.3 %copy-start.1 = (bf16[3,3,384,192]{2,3,1,0:T(8,128)(2,1)S(1)}, bf16[3,3,384,192]{2,3,1,0:T(8,128)(2,1)}, u32[]{:S(2)}) copy-start(bf16[3,3,384,192]{2,3,1,0:T(8,128)(2,1)} %param.16) | copy-start | bytes 3981316
  1.4 1.3 %copy-start.2 = (bf16[8,320,192]{1,2,0:T(8,128)(2,1)S(1)}, bf16[8,320,192]{1,2,0:T(8,128)(2,1)}, u32[]{:S(2)}) copy-start(bf16[8,320,192]{1,2,0:T(8,128)(2,1)} %param.13) | copy-start | bytes 2949124
  1.4 1.3 %copy-start.4 = (bf16[2,4,160,16]{2,3,1,0:T(8,128)(2,1)S(1)}, bf16[2,4,160,16]{2,3,1,0:T(8,128)(2,1)}, u32[]{:S(2)}) copy-start(bf16[2,4,160,16]{2,3,1,0:T(8,128)(2,1)} %param.11) | copy-start | bytes 122884
  1.4 1.3 %copy-start.5 = (bf16[4,160,16]{1,2,0:T(8,128)(2,1)S(1)}, bf16[4,160,16]{1,2,0:T(8,128)(2,1)}, u32[]{:S(2)}) copy-start(bf16[4,160,16]{1,2,0:T(8,128)(2,1)} %param.10) | copy-start | bytes 61444
  1.4 4.0 %slice-start = ((s8[7962624]{0:T(1024)(128)(4,1)}), s8[4194304]{0:T(1024)(128)(4,1)S(1)}, s32[]{:S(2)}) async-start(s8[7962624]{0:T(1024)(128)(4,1)} %bitcast.17), calls=%async_computation.1 | async-start | bytes 8388608
  2.7 2.7 %slice-start.1 = ((s8[7962624]{0:T(1024)(128)(4,1)}), s8[3768320]{0:T(1024)(128)(4,1)S(1)}, s32[]{:S(2)}) async-start(s8[7962624]{0:T(1024)(128)(4,1)} %bitcast.17), calls=%async_computation.2 | async-start | bytes 7536640
  2.7 2.8 %copy-start.3 = (bf16[2,4,160,384]{3,2,1,0:T(8,128)(2,1)S(1)}, bf16[2,4,160,384]{3,2,1,0:T(8,128)(2,1)}, u32[]{:S(2)}) copy-start(bf16[2,4,160,384]{3,2,1,0:T(8,128)(2,1)} %features.1) | copy-start | bytes 2949124
  2.7 2.8 %copy-start.6 = (s32[8]{0:T(128)S(1)}, s32[8]{0:T(128)}, u32[]{:S(2)}) copy-start(s32[8]{0:T(128)} %order.1) | copy-start | bytes 100
  4.2 11.7 %collective-permute-start = (bf16[608,384]{1,0:T(8,128)(2,1)S(1)}, bf16[608,384]{1,0:T(8,128)(2,1)S(1)}, u32[]{:S(2)}, u32[]{:S(2)}) collective-permute-start(bf16[608,384]{1,0:T(8,128)(2,1)S(1)} %get-tuple-element.24), channel_id=1, source_target_pairs={{0,1},{1,0},{2,3},{3,2},{4,5},{5,4},{6,7},{7,6},{8,9},{9,8},{10,11... | collective-permute-start | bytes 1400840 | tf_op jit(solution)/shard_map/ppermute | solution.py:597
  4.7 11.2 %collective-permute-start.1 = (bf16[608,384]{1,0:T(8,128)(2,1)S(1)}, bf16[608,384]{1,0:T(8,128)(2,1)S(1)}, u32[]{:S(2)}, u32[]{:S(2)}) collective-permute-start(bf16[608,384]{1,0:T(8,128)(2,1)S(1)} %get-tuple-element.25), channel_id=1, source_target_pairs={{0,0},{1,2},{2,1},{3,4},{4,3},{5,6},{6,5},{7,7},{8,8},{9,10},{10,9... | collective-permute-start | bytes 1400840 | tf_op jit(solution)/shard_map/ppermute | solution.py:598
  5.5 10.2 %copy-start.7 = (f32[384]{0:T(512)S(1)}, f32[384]{0:T(512)}, u32[]{:S(2)}) copy-start(f32[384]{0:T(512)} %param.17) | copy-start | bytes 4612
  5.5 10.2 %copy-start = (bf16[3,3,3,16,384]{4,3,2,1,0:T(8,128)(2,1)S(1)}, bf16[3,3,3,16,384]{4,3,2,1,0:T(8,128)(2,1)}, u32[]{:S(2)}) copy-start(bf16[3,3,3,16,384]{4,3,2,1,0:T(8,128)(2,1)} %param.14) | copy-start | bytes 995332
  5.5 10.2 %copy-start.8 = (f32[192]{0:T(256)S(1)}, f32[192]{0:T(256)}, u32[]{:S(2)}) copy-start(f32[192]{0:T(256)} %param.18) | copy-start | bytes 2308
  11.0 11.6 %collective-permute-start.2 = (bf16[480,384]{1,0:T(8,128)(2,1)S(1)}, bf16[480,384]{1,0:T(8,128)(2,1)S(1)}, u32[]{:S(2)}, u32[]{:S(2)}) collective-permute-start(bf16[480,384]{1,0:T(8,128)(2,1)S(1)} %get-tuple-element.29), channel_id=1, source_target_pairs={{0,1},{1,0},{2,3},{3,2},{4,5},{5,4},{6,7},{7,6},{8,9},{9,8},{10,11... | collective-permute-start | bytes 1105928 | tf_op jit(solution)/shard_map/ppermute | solution.py:610
  15.0 7.6 %collective-permute-start.3 = (bf16[480,384]{1,0:T(8,128)(2,1)S(1)}, bf16[480,384]{1,0:T(8,128)(2,1)S(1)}, u32[]{:S(2)}, u32[]{:S(2)}) collective-permute-start(bf16[480,384]{1,0:T(8,128)(2,1)S(1)} %get-tuple-element.30), channel_id=1, source_target_pairs={{0,0},{1,2},{2,1},{3,4},{4,3},{5,6},{6,5},{7,7},{8,8},{9,10},{10,9... | collective-permute-start | bytes 1105928 | tf_op jit(solution)/shard_map/ppermute | solution.py:611
